TPU v7x, 32 devices: a whole 2x2x4 slice. The times are simulated.
32 devices in a mesh: fsdp: 2 (over core), expert: 16 (over z, y, x).
Axes of the slice: x: 2, y: 2, z: 4, core: 2. Of those that a mesh axis runs over, the one named last changes fastest.
Arguments:
- tokens: bfloat16 [16, 384, 2048], P('expert', 'fsdp'), may hold values from -6 to 6
- segments: int32 [16, 384], P('expert'), may hold values from 0 to 1, as said below
- routes: int32 [16, 384, 6], P('expert', 'fsdp'), may hold values from 0 to 15, as said below
- slot_index: int32 [16, 384, 6], P('expert', 'fsdp'), may hold values from -1 to 71, as said below
- cotangent: bfloat16 [16, 384, 2048], P('expert', 'fsdp'), may hold values from -6 to 6
- attention_norm: bfloat16 [2048], P(('fsdp', 'expert')), may hold values from 0.5 to 1.5
- query_weight: bfloat16 [2048, 3072], P(('fsdp', 'expert')), may hold values from -0.1875 to 0.1875
- latent_down: bfloat16 [2048, 576], P(('fsdp', 'expert')), may hold values from -0.125 to 0.125
- latent_norm: bfloat16 [512], P(('fsdp', 'expert')), may hold values from 0.5 to 1.5
- latent_up: bfloat16 [512, 4096], P(('fsdp', 'expert')), may hold values from -0.25 to 0.25
- output_weight: bfloat16 [2048, 2048], P(('fsdp', 'expert')), may hold values from -0.5 to 0.5
- feed_norm: bfloat16 [2048], P(('fsdp', 'expert')), may hold values from 0.5 to 1.5
- router_weight: bfloat16 [2048, 16], P(('fsdp', 'expert')), may hold values from -0.0625 to 0.0625
- shared_gate: bfloat16 [2048, 2816], P(('fsdp', 'expert')), may hold values from -0.125 to 0.125
- shared_up: bfloat16 [2048, 2816], P(('fsdp', 'expert')), may hold values from -0.125 to 0.125
- shared_down: bfloat16 [2816, 2048], P(('fsdp', 'expert')), may hold values from -0.15625 to 0.15625
- expert_gate: bfloat16 [16, 2048, 1408], P('expert', 'fsdp'), may hold values from -0.125 to 0.125
- expert_up: bfloat16 [16, 2048, 1408], P('expert', 'fsdp'), may hold values from -0.125 to 0.125
- expert_down: bfloat16 [16, 1408, 2048], P('expert', None, 'fsdp'), may hold values from -6 to 6
Outputs:
- output: bfloat16 [16, 384, 2048], P('expert', 'fsdp')
- token_grad: float32 [16, 384, 2048], P('expert', 'fsdp')
- grad_attention_norm: float32 [2048], P(('fsdp', 'expert'))
- grad_query_weight: float32 [2048, 3072], P(('fsdp', 'expert'))
- grad_latent_down: float32 [2048, 576], P(('fsdp', 'expert'))
- grad_latent_norm: float32 [512], P(('fsdp', 'expert'))
- grad_latent_up: float32 [512, 4096], P(('fsdp', 'expert'))
- grad_output_weight: float32 [2048, 2048], P(('fsdp', 'expert'))
- grad_feed_norm: float32 [2048], P(('fsdp', 'expert'))
- grad_router_weight: float32 [2048, 16], P(('fsdp', 'expert'))
- grad_shared_gate: float32 [2048, 2816], P(('fsdp', 'expert'))
- grad_shared_up: float32 [2048, 2816], P(('fsdp', 'expert'))
- grad_shared_down: float32 [2816, 2048], P(('fsdp', 'expert'))
- grad_expert_gate: float32 [16, 2048, 1408], P('expert', 'fsdp')
- grad_expert_up: float32 [16, 2048, 1408], P('expert', 'fsdp')
- grad_expert_down: float32 [16, 1408, 2048], P('expert', None, 'fsdp')
Inputs may be any that keep to these rules, and one draw needn't show every extreme that they name: `segments`: each sequence holds two documents: document 0 from its first token up to a place after token 192, and document 1, cut at the sequence's end, after it. The numbers never change between token k * 192 - 1 and token k * 192. `routes`: each token names 6 different experts. `slot_index`: for the rows of one device (192 tokens in a row, pairs taken token by token, then in route order), a pair's slot is the number of earlier pairs naming the same expert if that is below 72, else -1. In every draw some expert has all 72 slots filled on every device.
All inputs are finite; a program needn't handle non-finite values.
Results may differ from a plain program's by a relative error of at most 0.023.
Values may be sent and summed in bfloat16 or wider, within the bound.
A program may use at most 384 MiB of HBM per device.

v0:
```python
import math

import jax
import jax.numpy as jnp
from jax import lax
from jax.sharding import PartitionSpec as P

D = 2048
HEADS = 16
NOPE = 128
ROPE = 64
VALUE = 128
LATENT = 512
TOPK = 6


EPSILON = 1e-06
FLOOR_SCORE = -1e30


def passed_along(value, axis, steps):
    count = lax.axis_size(axis)
    first, last = (max(0, -steps), min(count, count - steps))
    return lax.ppermute(value, axis, [(source, source + steps) for source in range(first, last)])


def norm_rows(values, gain):
    return values * lax.rsqrt(jnp.mean(values * values, axis=-1, keepdims=True) + EPSILON) * gain


def norm_back(values, gain, incoming):
    primal_out, pullback = jax.vjp(norm_rows, values, gain)
    return pullback(incoming)


def swiglu_back(gate_part, up_portion, incoming):
    primal_out, pullback = jax.vjp(
        lambda former, latter: jax.nn.silu(former) * latter, gate_part, up_portion
    )
    return pullback(incoming)


def rotary_table(row_total, offset, rope_width):
    frequency_steps = jnp.arange(rope_width // 2, dtype=jnp.float32)
    inverse = jnp.exp(frequency_steps * (-2.0 * math.log(10000.0) / rope_width))
    places = (offset + jnp.arange(row_total)).astype(jnp.float32)
    angles = places[:, None] * inverse[None, :]
    return (jnp.cos(angles), jnp.sin(angles))


def rotate_forward(values, cosine, sine_table):
    middle = values.shape[-1] // 2
    front_half = values[..., :middle]
    back_half = values[..., middle:]
    return jnp.concatenate(
        [
            front_half * cosine - back_half * sine_table,
            back_half * cosine + front_half * sine_table,
        ],
        axis=-1,
    )


def rotate_backward(values, cosine, sine_table):
    middle = values.shape[-1] // 2
    front_half = values[..., :middle]
    back_half = values[..., middle:]
    return jnp.concatenate(
        [
            front_half * cosine + back_half * sine_table,
            back_half * cosine - front_half * sine_table,
        ],
        axis=-1,
    )


def matmul(former, latter):
    return jnp.dot(former, latter, preferred_element_type=jnp.float32)


def left_matmul(former, latter):
    return lax.dot_general(
        former, latter, (((0,), (0,)), ((), ())), preferred_element_type=jnp.float32
    )


def right_matmul(former, latter):
    return lax.dot_general(
        former, latter, (((1,), (1,)), ((), ())), preferred_element_type=jnp.float32
    )


def attention_scores(queries, expanded, keys_rope, visible, score_scale):
    scores = jnp.einsum(
        "qhd,khd->hqk",
        queries[..., :NOPE],
        expanded[..., :NOPE],
        preferred_element_type=jnp.float32,
    )
    scores = scores + jnp.einsum(
        "qhd,kd->hqk", queries[..., NOPE:], keys_rope, preferred_element_type=jnp.float32
    )
    return jnp.where(visible[None], scores * score_scale, FLOOR_SCORE)


def body(
    tokens,
    segments,
    routes,
    slot_index,
    cotangent,
    attention_norm,
    query_weight,
    latent_down,
    latent_norm,
    latent_up,
    output_weight,
    feed_norm,
    router_weight,
    shared_gate,
    shared_up,
    shared_down,
    expert_gate,
    expert_up,
    expert_down,
):
    row_count = tokens.shape[1]
    device_half = lax.axis_index("fsdp")
    inputs = tokens[0].astype(jnp.float32)
    gain_one, query_full, down_full, gain_latent, up_full, output_full = (
        lax.all_gather(attention_norm, ("fsdp", "expert"), axis=0, tiled=True),
        lax.all_gather(query_weight, ("fsdp", "expert"), axis=0, tiled=True),
        lax.all_gather(latent_down, ("fsdp", "expert"), axis=0, tiled=True),
        lax.all_gather(latent_norm, ("fsdp", "expert"), axis=0, tiled=True),
        lax.all_gather(latent_up, ("fsdp", "expert"), axis=0, tiled=True),
        lax.all_gather(output_weight, ("fsdp", "expert"), axis=0, tiled=True),
    )
    cosine, sine_table = rotary_table(row_count, device_half * row_count, ROPE)
    score_scale = (NOPE + ROPE) ** (-0.5)
    gain_first = gain_one.astype(jnp.float32)
    normed_low = norm_rows(inputs, gain_first).astype(jnp.bfloat16)
    query_raw = matmul(normed_low, query_full).reshape(row_count, HEADS, NOPE + ROPE)
    queries = jnp.concatenate(
        [
            query_raw[..., :NOPE],
            rotate_forward(query_raw[..., NOPE:], cosine[:, None, :], sine_table[:, None, :]),
        ],
        axis=-1,
    ).astype(jnp.bfloat16)
    compressed = matmul(normed_low, down_full)
    latent_gain = gain_latent.astype(jnp.float32)
    latent = norm_rows(compressed[:, :LATENT], latent_gain).astype(jnp.bfloat16)
    key_rope = rotate_forward(compressed[:, LATENT:], cosine, sine_table).astype(jnp.bfloat16)
    prior_latent, prior_rope = passed_along((latent, key_rope), "fsdp", 1)
    key_latent = jnp.concatenate([prior_latent, latent], axis=0)
    keys_rope = jnp.concatenate([prior_rope, key_rope], axis=0)
    expanded = (
        matmul(key_latent, up_full).astype(jnp.bfloat16).reshape(2 * row_count, HEADS, NOPE + VALUE)
    )
    query_place = device_half * row_count + jnp.arange(row_count)
    key_place = (device_half - 1) * row_count + jnp.arange(2 * row_count)
    padded_segments = jnp.concatenate([jnp.full((row_count,), -1, jnp.int32), segments[0]])
    key_segment = lax.dynamic_slice_in_dim(padded_segments, device_half * row_count, 2 * row_count)
    query_segment = lax.dynamic_slice_in_dim(segments[0], device_half * row_count, row_count)
    visible = (key_place[None, :] <= query_place[:, None]) & (
        key_segment[None, :] == query_segment[:, None]
    )
    scores = attention_scores(queries, expanded, keys_rope, visible, score_scale)
    top_score = jnp.max(scores, axis=-1, keepdims=True)
    log_total = top_score + jnp.log(jnp.sum(jnp.exp(scores - top_score), axis=-1, keepdims=True))
    weight_low = jnp.exp(scores - log_total).astype(jnp.bfloat16)
    mixed_heads = (
        jnp.einsum(
            "hqk,khd->qhd", weight_low, expanded[..., NOPE:], preferred_element_type=jnp.float32
        )
        .reshape(row_count, HEADS * VALUE)
        .astype(jnp.bfloat16)
    )
    residual = inputs + matmul(mixed_heads, output_full)
    gain_feed, router_full, sgate_full, sup_full, sdown_full = (
        lax.all_gather(feed_norm, ("fsdp", "expert"), axis=0, tiled=True),
        lax.all_gather(router_weight, ("fsdp", "expert"), axis=0, tiled=True),
        lax.all_gather(shared_gate, ("fsdp", "expert"), axis=0, tiled=True),
        lax.all_gather(shared_up, ("fsdp", "expert"), axis=0, tiled=True),
        lax.all_gather(shared_down, ("fsdp", "expert"), axis=0, tiled=True),
    )
    expert_gate_gathered, expert_up_gathered, expert_down_gathered = (
        lax.all_gather(expert_gate, "fsdp", axis=1, tiled=True),
        lax.all_gather(expert_up, "fsdp", axis=1, tiled=True),
        lax.all_gather(expert_down, "fsdp", axis=2, tiled=True),
    )
    feed_gain = gain_feed.astype(jnp.float32)
    mixed_low = norm_rows(residual, feed_gain).astype(jnp.bfloat16)
    logits = matmul(mixed_low, router_full)
    expert_count = logits.shape[1]
    capacity = row_count * TOPK // expert_count
    probabilities = jax.nn.softmax(logits, axis=-1)
    route_rows = routes[0]
    slot_rows = slot_index[0]
    choose = (route_rows[..., None] == jnp.arange(expert_count)[None, None, :]).astype(jnp.float32)
    gate_values = jnp.sum(probabilities[:, None, :] * choose, axis=-1)
    kept_pairs = (slot_rows >= 0).astype(jnp.float32)
    target_row = jnp.where(
        slot_rows >= 0, route_rows * capacity + slot_rows, expert_count * capacity
    ).reshape(-1)
    safe_row = jnp.minimum(target_row, expert_count * capacity - 1)
    pair_rows = jnp.repeat(mixed_low, TOPK, axis=0)
    dispatch_buffer = (
        jnp.zeros((expert_count * capacity, D), jnp.bfloat16)
        .at[target_row]
        .set(pair_rows, mode="drop")
        .reshape(expert_count, capacity, D)
    )
    received_rows = lax.all_to_all(
        dispatch_buffer, "expert", split_axis=0, concat_axis=1, tiled=True
    )
    gate_part = jnp.einsum(
        "pjh,phy->pjy", received_rows, expert_gate_gathered, preferred_element_type=jnp.float32
    )
    up_portion = jnp.einsum(
        "pjh,phy->pjy", received_rows, expert_up_gathered, preferred_element_type=jnp.float32
    )
    hidden = (jax.nn.silu(gate_part) * up_portion).astype(jnp.bfloat16)
    expert_out = jnp.einsum(
        "erf,efd->erd", hidden, expert_down_gathered, preferred_element_type=jnp.float32
    ).astype(jnp.bfloat16)
    returned = lax.all_to_all(expert_out, "expert", split_axis=1, concat_axis=0, tiled=True)
    gathered = returned.reshape(expert_count * capacity, D)[safe_row].reshape(row_count, TOPK, D)
    pair_weight = gate_values * kept_pairs
    routed = jnp.sum(pair_weight[..., None] * gathered, axis=1)
    shared_gate_part = matmul(mixed_low, sgate_full)
    shared_up_part = matmul(mixed_low, sup_full)
    shared_hidden = (jax.nn.silu(shared_gate_part) * shared_up_part).astype(jnp.bfloat16)
    output = (residual + routed + matmul(shared_hidden, sdown_full)).astype(jnp.bfloat16)
    out_grad = cotangent[0].astype(jnp.float32)
    grad_low = cotangent[0]
    gate_grad_pairs = jnp.sum(out_grad[:, None, :] * gathered, axis=-1) * kept_pairs
    pair_grad = (
        (pair_weight[..., None] * out_grad[:, None, :])
        .astype(jnp.bfloat16)
        .reshape(row_count * TOPK, D)
    )
    grad_buffer = (
        jnp.zeros((expert_count * capacity, D), jnp.bfloat16)
        .at[target_row]
        .set(pair_grad, mode="drop")
        .reshape(expert_count, capacity, D)
    )
    grad_received = lax.all_to_all(grad_buffer, "expert", split_axis=0, concat_axis=1, tiled=True)
    hidden_grad = jnp.einsum(
        "erd,efd->erf", grad_received, expert_down_gathered, preferred_element_type=jnp.float32
    )
    edown_grad = jnp.einsum(
        "erf,erd->efd", hidden, grad_received, preferred_element_type=jnp.float32
    )
    gate_part_grad, up_part_grad = swiglu_back(gate_part, up_portion, hidden_grad)
    gate_low = gate_part_grad.astype(jnp.bfloat16)
    up_reduced = up_part_grad.astype(jnp.bfloat16)
    input_grad = (
        jnp.einsum(
            "jsx,jzx->jsz", gate_low, expert_gate_gathered, preferred_element_type=jnp.float32
        )
        + jnp.einsum(
            "jsx,jzx->jsz", up_reduced, expert_up_gathered, preferred_element_type=jnp.float32
        )
    ).astype(jnp.bfloat16)
    egate_grad = jnp.einsum(
        "siq,siy->sqy", received_rows, gate_low, preferred_element_type=jnp.float32
    )
    expert_up_gradient = jnp.einsum(
        "siq,siy->sqy", received_rows, up_reduced, preferred_element_type=jnp.float32
    )
    expert_gate_piece, expert_up_piece, expert_down_piece = (
        lax.psum_scatter(
            egate_grad.astype(jnp.bfloat16), "fsdp", scatter_dimension=1, tiled=True
        ).astype(jnp.float32),
        lax.psum_scatter(
            expert_up_gradient.astype(jnp.bfloat16), "fsdp", scatter_dimension=1, tiled=True
        ).astype(jnp.float32),
        lax.psum_scatter(
            edown_grad.astype(jnp.bfloat16), "fsdp", scatter_dimension=2, tiled=True
        ).astype(jnp.float32),
    )
    back_rows = lax.all_to_all(input_grad, "expert", split_axis=1, concat_axis=0, tiled=True)
    pair_back = back_rows.reshape(expert_count * capacity, D)[safe_row].reshape(row_count, TOPK, D)
    routed_grad = jnp.sum(kept_pairs[..., None] * pair_back, axis=1)
    prob_grad = jnp.sum(gate_grad_pairs[..., None] * choose, axis=1)
    logit_low = (
        probabilities * (prob_grad - jnp.sum(probabilities * prob_grad, axis=-1, keepdims=True))
    ).astype(jnp.bfloat16)
    router_grad = left_matmul(mixed_low, logit_low)
    shared_hidden_grad = right_matmul(grad_low, sdown_full)
    sdown_grad = left_matmul(shared_hidden, grad_low)
    shared_gate_grad, shared_up_grad = swiglu_back(
        shared_gate_part, shared_up_part, shared_hidden_grad
    )
    shared_gate_low = shared_gate_grad.astype(jnp.bfloat16)
    shared_up_low = shared_up_grad.astype(jnp.bfloat16)
    sgate_grad = left_matmul(mixed_low, shared_gate_low)
    sup_grad = left_matmul(mixed_low, shared_up_low)
    mixed_grad = (
        right_matmul(logit_low, router_full)
        + right_matmul(shared_gate_low, sgate_full)
        + right_matmul(shared_up_low, sup_full)
        + routed_grad
    )
    residual_add, feed_gain_grad = norm_back(residual, feed_gain, mixed_grad)
    residual_grad = out_grad + residual_add
    attended_low = residual_grad.astype(jnp.bfloat16)
    output_grad = left_matmul(mixed_heads, attended_low)
    heads_low = (
        right_matmul(attended_low, output_full)
        .astype(jnp.bfloat16)
        .reshape(row_count, HEADS, VALUE)
    )
    scores_again = attention_scores(queries, expanded, keys_rope, visible, score_scale)
    probs_again = jnp.exp(scores_again - log_total)
    weights_again = probs_again.astype(jnp.bfloat16)
    weight_grad = jnp.einsum(
        "qhd,khd->hqk", heads_low, expanded[..., NOPE:], preferred_element_type=jnp.float32
    )
    value_grad = jnp.einsum(
        "hqk,qhd->khd", weights_again, heads_low, preferred_element_type=jnp.float32
    )
    delta_rows = jnp.sum(probs_again * weight_grad, axis=-1, keepdims=True)
    score_low = (probs_again * (weight_grad - delta_rows)).astype(jnp.bfloat16)
    query_nope_grad = (
        jnp.einsum(
            "hqk,khd->qhd", score_low, expanded[..., :NOPE], preferred_element_type=jnp.float32
        )
        * score_scale
    )
    query_rope_grad = (
        jnp.einsum("hqk,kd->qhd", score_low, keys_rope, preferred_element_type=jnp.float32)
        * score_scale
    )
    key_nope_grad = (
        jnp.einsum(
            "hqk,qhd->khd", score_low, queries[..., :NOPE], preferred_element_type=jnp.float32
        )
        * score_scale
    )
    key_rope_grad = (
        jnp.einsum(
            "hqk,qhd->kd", score_low, queries[..., NOPE:], preferred_element_type=jnp.float32
        )
        * score_scale
    )
    expanded_grad = jnp.concatenate([key_nope_grad, value_grad], axis=-1).reshape(
        2 * row_count, HEADS * (NOPE + VALUE)
    )
    returned_expanded, returned_rope = (
        passed_along(expanded_grad[:row_count].astype(jnp.bfloat16), "fsdp", -1).astype(
            jnp.float32
        ),
        passed_along(key_rope_grad[:row_count].astype(jnp.bfloat16), "fsdp", -1).astype(
            jnp.float32
        ),
    )
    expanded_low = (expanded_grad[row_count:] + returned_expanded).astype(jnp.bfloat16)
    own_rope = key_rope_grad[row_count:] + returned_rope
    latent_grad = right_matmul(expanded_low, up_full)
    up_weight_grad = left_matmul(latent, expanded_low)
    compressed_latent_grad, latent_gain_grad = norm_back(
        compressed[:, :LATENT], latent_gain, latent_grad
    )
    compressed_low = jnp.concatenate(
        [compressed_latent_grad, rotate_backward(own_rope, cosine, sine_table)], axis=-1
    ).astype(jnp.bfloat16)
    query_low = (
        jnp.concatenate(
            [
                query_nope_grad,
                rotate_backward(query_rope_grad, cosine[:, None, :], sine_table[:, None, :]),
            ],
            axis=-1,
        )
        .reshape(row_count, HEADS * (NOPE + ROPE))
        .astype(jnp.bfloat16)
    )
    normed_grad = right_matmul(query_low, query_full) + right_matmul(compressed_low, down_full)
    query_weight_grad = left_matmul(normed_low, query_low)
    down_weight_grad = left_matmul(normed_low, compressed_low)
    input_add, first_gain_grad = norm_back(inputs, gain_first, normed_grad)
    token_grad = residual_grad + input_add
    all_shards = (
        lax.psum_scatter(first_gain_grad, ("fsdp", "expert"), scatter_dimension=0, tiled=True),
        lax.psum_scatter(query_weight_grad, ("fsdp", "expert"), scatter_dimension=0, tiled=True),
        lax.psum_scatter(down_weight_grad, ("fsdp", "expert"), scatter_dimension=0, tiled=True),
        lax.psum_scatter(latent_gain_grad, ("fsdp", "expert"), scatter_dimension=0, tiled=True),
        lax.psum_scatter(up_weight_grad, ("fsdp", "expert"), scatter_dimension=0, tiled=True),
        lax.psum_scatter(output_grad, ("fsdp", "expert"), scatter_dimension=0, tiled=True),
        lax.psum_scatter(feed_gain_grad, ("fsdp", "expert"), scatter_dimension=0, tiled=True),
        lax.psum_scatter(router_grad, ("fsdp", "expert"), scatter_dimension=0, tiled=True),
        lax.psum_scatter(sgate_grad, ("fsdp", "expert"), scatter_dimension=0, tiled=True),
        lax.psum_scatter(sup_grad, ("fsdp", "expert"), scatter_dimension=0, tiled=True),
        lax.psum_scatter(sdown_grad, ("fsdp", "expert"), scatter_dimension=0, tiled=True),
    )
    return (
        output[None],
        token_grad[None],
        all_shards[0],
        all_shards[1],
        all_shards[2],
        all_shards[3],
        all_shards[4],
        all_shards[5],
        all_shards[6],
        all_shards[7],
        all_shards[8],
        all_shards[9],
        all_shards[10],
        expert_gate_piece,
        expert_up_piece,
        expert_down_piece,
    )


def solution(mesh):
    return jax.shard_map(
        body,
        mesh=mesh,
        in_specs=(
            P("expert", "fsdp", None),
            P("expert", None),
            P("expert", "fsdp", None),
            P("expert", "fsdp", None),
            P("expert", "fsdp", None),
            P(("fsdp", "expert")),
            P(("fsdp", "expert"), None),
            P(("fsdp", "expert"), None),
            P(("fsdp", "expert")),
            P(("fsdp", "expert"), None),
            P(("fsdp", "expert"), None),
            P(("fsdp", "expert")),
            P(("fsdp", "expert"), None),
            P(("fsdp", "expert"), None),
            P(("fsdp", "expert"), None),
            P(("fsdp", "expert"), None),
            P("expert", "fsdp", None),
            P("expert", "fsdp", None),
            P("expert", None, "fsdp"),
        ),
        out_specs=(
            P("expert", "fsdp", None),
            P("expert", "fsdp", None),
            P(("fsdp", "expert")),
            P(("fsdp", "expert"), None),
            P(("fsdp", "expert"), None),
            P(("fsdp", "expert")),
            P(("fsdp", "expert"), None),
            P(("fsdp", "expert"), None),
            P(("fsdp", "expert")),
            P(("fsdp", "expert"), None),
            P(("fsdp", "expert"), None),
            P(("fsdp", "expert"), None),
            P(("fsdp", "expert"), None),
            P("expert", "fsdp", None),
            P("expert", "fsdp", None),
            P("expert", None, "fsdp"),
        ),
        check_vma=False,
    )
```

profile of v0, /device:TPU:0, one launch (start us, length us, event | category | flops | bytes accessed | tf_op | source)
XLA Modules:
  0.0 3791.5 jit_solution(753623551358739924)
XLA Ops:
  14.2 42.3 %all-reduce.8 = (bf16[2048]{0:T(1024)(128)(2,1)S(1)}, bf16[512]{0:T(512)(128)(2,1)S(1)}, bf16[2048]{0:T(1024)(128)(2,1)S(1)}) all-reduce(bf16[2048]{0:T(1024)(128)(2,1)S(1)} %dynamic-update-slice, bf16[512]{0:T(512)(128)(2,1)S(1)} %dynamic-update-slice.1, ...), channel_id=1, replica_groups=mesh['fsdp'=2,'expert'=16] {'fsdp','expert'}, use_global_device_ids=true, to_apply=%add.1 | all-reduce | flops 4608 | bytes 18432
  58.1 13.5 all-gather.12.cloned.1.call-done
  78.5 57.1 %all-gather.14.cloned.1.call-done = bf16[512,4096]{1,0:T(8,128)(2,1)} async-done(((bf16[16,4096]{1,0:T(8,128)(2,1)}), bf16[512,4096]{1,0:T(8,128)(2,1)}) %all-gather.14.cloned.1.call-update) | async-done | bytes 4194320 | tf_op jit(solution)/shard_map/all_gather | solution.py:135
  142.3 90.7 %all-gather.16.cloned.1.call-done = bf16[2048,3072]{1,0:T(8,128)(2,1)} async-done(((bf16[64,3072]{1,0:T(8,128)(2,1)}), bf16[2048,3072]{1,0:T(8,128)(2,1)}) %all-gather.16.cloned.1.call-update) | async-done | bytes 12582928 | tf_op jit(solution)/shard_map/all_gather | solution.py:132
  233.0 16.9 copy.164
  250.0 6.8 fusion.73
  264.2 47.4 %all-gather.18.cloned.1.call-done = bf16[2048,2048]{1,0:T(8,128)(2,1)} async-done(((bf16[64,2048]{1,0:T(8,128)(2,1)}), bf16[2048,2048]{1,0:T(8,128)(2,1)}) %all-gather.18.cloned.1.call-update) | async-done | bytes 8388624 | tf_op jit(solution)/shard_map/all_gather | solution.py:136
  321.4 8.8 reshape.542
  330.2 14.0 scatter_custom_fusion
  349.1 206.4 %all-gather = bf16[32,64,16]{1,2,0:T(8,128)(2,1)S(1)} all-gather(bf16[1,64,16]{1,2,0:T(8,128)(2,1)S(1)} %bitcast.221), channel_id=1, replica_groups=mesh['fsdp'=2,'expert'=16] {'fsdp','expert'}, dimensions={0}, use_global_device_ids=true | all-gather | bytes 67584 | tf_op jit(solution)/shard_map/all_gather | solution.py:182
  556.0 6.2 mul.553
  562.2 11.9 mul.569
  574.9 19.6 scatter_custom_fusion.1
  594.4 6.7 all-to-all-start.2
  601.8 13.4 fusion.13
  615.2 12.7 fusion.17
  627.9 73.8 %all-to-all-done.2 = bf16[16,72,2048]{2,1,0:T(8,128)(2,1)} async-done(((bf16[16,72,2048]{2,1,0:T(8,128)(2,1)}), bf16[16,72,2048]{2,1,0:T(8,128)(2,1)}, u32[]{:S(2)}, u32[]{:S(2)}) %all-to-all-start.2) | async-done | bytes 4718624 | tf_op jit(solution)/shard_map/all_to_all | solution.py:249
  701.7 17.7 multiply_convert_fusion.1
  719.4 10.8 fusion
  730.2 27.8 copy.254
  758.5 29.8 reduce.9
  788.3 13.3 reshape.574
  801.5 56.0 %all-to-all-start.1 = ((bf16[16,2,73728]{2,1,0:T(2,128)(2,1)}), bf16[16,2,73728]{2,1,0:T(2,128)(2,1)}, u32[]{:S(2)}, u32[]{:S(2)}) async-start(bf16[16,2,73728]{2,1,0:T(2,128)(2,1)} %reshape.574), calls=%async_computation.1 | async-start | bytes 9437184 | tf_op jit(solution)/shard_map/all_to_all | solution.py:227
  857.7 85.4 %all-to-all-done.1 = bf16[16,2,73728]{2,1,0:T(2,128)(2,1)} async-done(((bf16[16,2,73728]{2,1,0:T(2,128)(2,1)}), bf16[16,2,73728]{2,1,0:T(2,128)(2,1)}, u32[]{:S(2)}, u32[]{:S(2)}) %all-to-all-start.1) | async-done | bytes 4718624 | tf_op jit(solution)/shard_map/all_to_all | solution.py:227
  943.1 12.8 reshape.575
  955.9 8.8 copy.252
  964.8 13.6 gather_fusion
  978.4 9.2 reshape.520
  987.6 9.6 multiply_reduce_fusion.1
  999.0 12.1 fusion.3
  1011.2 12.9 fusion.1
  1024.2 10.8 fusion.15
  1035.0 9.3 fusion.4
  1044.3 27.6 copy.253
  1071.9 30.2 reduce.10
  1102.1 13.3 reshape.576
  1115.4 20.6 all-to-all-start.3
  1136.2 12.7 fusion.2
  1150.1 9.6 fusion.71
  1159.7 8.1 fusion.132
  1167.7 12.3 fusion.35
  1180.0 10.1 fusion.133
  1195.3 29.0 all-to-all-done.3
  1224.3 13.2 reshape.577
  1237.5 8.8 copy.251
  1246.4 13.6 gather_fusion.1
  1260.0 9.2 reshape.521
  1269.2 10.8 multiply_reduce_fusion
  1284.2 7.1 fusion.59
  1330.7 7.0 fusion.126
  1337.8 10.6 fusion.136
  1348.5 10.6 fusion.137
  1360.2 10.7 fusion.69
  1372.0 9.6 fusion.64
  1392.7 10.4 fusion.75
  1403.2 10.2 fusion.135
  1413.5 7.9 fusion.29
  1427.4 58.5 %all-reduce.7 = (f32[2048]{0:T(1024)S(1)}, f32[512]{0:T(512)S(1)}, f32[2048]{0:T(1024)S(1)}) all-reduce(f32[2048]{0:T(1024)S(1)} %get-tuple-element.20, f32[512]{0:T(512)S(1)} %get-tuple-element.22, f32[2048]{0:T(1024)S(1)} %copy-done.62), channel_id=2, replica_groups=mesh['fsdp'=2,'expert'=16] {'fsdp','expert'}, use_global_device_ids=true, to_apply=%region_20.21.clone | all-reduce | flops 4608 | bytes 36864
  1505.2 176.8 %reduce-scatter.18.cloned.1.call-done = f32[16,4096]{1,0:T(8,128)} async-done(((f32[512,4096]{1,0:T(8,128)}), f32[16,4096]{1,0:T(8,128)}) %reduce-scatter.18.cloned.1.call-update) | async-done | bytes 262160 | tf_op jit(solution)/shard_map/reduce_scatter | solution.py:391
  1682.0 491.5 %reduce-scatter.22.cloned.1.call-done = f32[64,2816]{1,0:T(8,128)} async-done(((f32[2048,2816]{1,0:T(8,128)}), f32[64,2816]{1,0:T(8,128)}) %reduce-scatter.22.cloned.1.call-update) | async-done | bytes 720912 | tf_op jit(solution)/shard_map/reduce_scatter | solution.py:395
  2173.5 495.5 %reduce-scatter.24.cloned.1.call-done = f32[64,2816]{1,0:T(8,128)} async-done(((f32[2048,2816]{1,0:T(8,128)}), f32[64,2816]{1,0:T(8,128)}) %reduce-scatter.24.cloned.1.call-update) | async-done | bytes 720912 | tf_op jit(solution)/shard_map/reduce_scatter | solution.py:396
  2668.9 495.6 %reduce-scatter.26.cloned.1.call-done = f32[88,2048]{1,0:T(8,128)} async-done(((f32[2816,2048]{1,0:T(8,128)}), f32[88,2048]{1,0:T(8,128)}) %reduce-scatter.26.cloned.1.call-update) | async-done | bytes 720912 | tf_op jit(solution)/shard_map/reduce_scatter | solution.py:397
  3164.5 364.7 %reduce-scatter.20.cloned.1.call-done = f32[64,2048]{1,0:T(8,128)} async-done(((f32[2048,2048]{1,0:T(8,128)}), f32[64,2048]{1,0:T(8,128)}) %reduce-scatter.20.cloned.1.call-update) | async-done | bytes 524304 | tf_op jit(solution)/shard_map/reduce_scatter | solution.py:392
  3529.3 255.1 %reduce-scatter.14.cloned.1.call-done = f32[64,3072]{1,0:T(8,128)} async-done(((f32[2048,3072]{1,0:T(8,128)}), f32[64,3072]{1,0:T(8,128)}) %reduce-scatter.14.cloned.1.call-update) | async-done | bytes 786448 | tf_op jit(solution)/shard_map/reduce_scatter | solution.py:388
  (358 shorter events, 136.3 us)
Async XLA Ops:
  7.2 64.4 %all-gather.12.cloned.1.call-start = ((), (), s32[]{:S(2)}) async-start(), calls=%async_computation.15 | async-start | bytes 2703360 | tf_op jit(solution)/shard_map/all_gather | solution.py:133
  7.9 127.7 %all-gather.14.cloned.1.call-start = ((), (), s32[]{:S(2)}) async-start(), calls=%async_computation.16 | async-start | bytes 4325376 | tf_op jit(solution)/shard_map/all_gather | solution.py:135
  8.7 224.4 %all-gather.16.cloned.1.call-start = ((), (), s32[]{:S(2)}) async-start(), calls=%async_computation.17 | async-start | bytes 12976128 | tf_op jit(solution)/shard_map/all_gather | solution.py:132
  9.4 302.2 %all-gather.18.cloned.1.call-start = ((), (), s32[]{:S(2)}) async-start(), calls=%async_computation.18 | async-start | bytes 8650752 | tf_op jit(solution)/shard_map/all_gather | solution.py:136
  10.0 591.8 %all-gather.22.cloned.1.call-start = ((), (), s32[]{:S(2)}) async-start(), calls=%async_computation.20 | async-start | bytes 8650752 | tf_op jit(solution)/shard_map/all_gather | solution.py:189
  10.6 45.9 %copy-start.73 = (s32[1,384]{1,0:T(1,128)S(1)}, s32[1,384]{1,0:T(1,128)}, u32[]{:S(2)}) copy-start(s32[1,384]{1,0:T(1,128)} %param.20) | copy-start | bytes 4612
  10.6 46.0 %copy-start.63 = (s32[1,192,6]{1,0,2:T(1,128)S(1)}, s32[1,192,6]{1,0,2:T(1,128)}, u32[]{:S(2)}) copy-start(s32[1,192,6]{1,0,2:T(1,128)} %param.22) | copy-start | bytes 13828
  10.6 46.6 %copy-start.72 = (s32[1,192,6]{1,0,2:T(1,128)S(1)}, s32[1,192,6]{1,0,2:T(1,128)}, u32[]{:S(2)}) copy-start(s32[1,192,6]{1,0,2:T(1,128)} %param.21) | copy-start | bytes 13828
  10.6 47.1 %copy-start.3 = (bf16[1,192,2048]{2,1,0:T(8,128)(2,1)S(1)}, bf16[1,192,2048]{2,1,0:T(8,128)(2,1)}, u32[]{:S(2)}) copy-start(bf16[1,192,2048]{2,1,0:T(8,128)(2,1)} %param.19) | copy-start | bytes 2359300
  10.6 604.5 %all-gather.20.cloned.1.call-start = ((), (), s32[]{:S(2)}) async-start(), calls=%async_computation.19 | async-start | bytes 8650752 | tf_op jit(solution)/shard_map/all_gather | solution.py:188
  11.2 616.6 %all-gather.24.cloned.1.call-start = ((), (), s32[]{:S(2)}) async-start(), calls=%async_computation.21 | async-start | bytes 8650752 | tf_op jit(solution)/shard_map/all_gather | solution.py:190
  12.0 1137.3 %all-gather.30.cloned.1.call-start = ((), (), s32[]{:S(2)}) async-start(), calls=%async_computation.24 | async-start | bytes 11894784 | tf_op jit(solution)/shard_map/all_gather | solution.py:185
  12.7 1146.9 %all-gather.28.cloned.1.call-start = ((), (), s32[]{:S(2)}) async-start(), calls=%async_computation.23 | async-start | bytes 11894784 | tf_op jit(solution)/shard_map/all_gather | solution.py:184
  56.5 193.5 %copy-start.35 = (f32[2048]{0:T(1024)}, f32[2048]{0:T(1024)S(1)}, u32[]{:S(2)}) copy-start(f32[2048]{0:T(1024)S(1)} %convert_element_type.200) | copy-start | bytes 24580
  56.5 17.8 copy-start.59
  56.6 260.4 %copy-start.55 = (f32[2048]{0:T(1024)}, f32[2048]{0:T(1024)S(1)}, u32[]{:S(2)}) copy-start(f32[2048]{0:T(1024)S(1)} %convert_element_type.213) | copy-start | bytes 24580
  57.5 19.4 copy-start.79
  57.5 19.4 copy-start.74
  58.0 16.2 copy-start.68
  58.0 192.0 %copy-start.57 = (f32[192]{0:T(256)}, f32[192]{0:T(256)S(1)}, u32[]{:S(2)}) copy-start(f32[192]{0:T(256)S(1)} %fusion.116) | copy-start | bytes 2308
  74.5 65.1 %copy-start.33 = (bf16[192,512]{1,0:T(8,128)(2,1)}, bf16[192,512]{1,0:T(8,128)(2,1)S(1)}, u32[]{:S(2)}) copy-start(bf16[192,512]{1,0:T(8,128)(2,1)S(1)} %multiply_convert_fusion.8) | copy-start | bytes 589828
  74.5 4.0 collective-permute-start
  77.1 180.7 %copy-start.45 = (f32[192,32]{0,1:T(8,128)}, f32[192,32]{0,1:T(8,128)S(1)}, u32[]{:S(2)}) copy-start(f32[192,32]{0,1:T(8,128)S(1)} %get-tuple-element.54) | copy-start | bytes 73732
  77.1 180.7 %copy-start.47 = (f32[192,32]{0,1:T(8,128)}, f32[192,32]{0,1:T(8,128)S(1)}, u32[]{:S(2)}) copy-start(f32[192,32]{0,1:T(8,128)S(1)} %get-tuple-element.55) | copy-start | bytes 73732
  77.2 181.5 %copy-start.49 = (bf16[192,32]{0,1:T(8,128)(2,1)}, bf16[192,32]{0,1:T(8,128)(2,1)S(1)}, u32[]{:S(2)}) copy-start(bf16[192,32]{0,1:T(8,128)(2,1)S(1)} %get-tuple-element.50) | copy-start | bytes 36868
  77.2 181.5 %copy-start.51 = (bf16[192,32]{0,1:T(8,128)(2,1)}, bf16[192,32]{0,1:T(8,128)(2,1)S(1)}, u32[]{:S(2)}) copy-start(bf16[192,32]{0,1:T(8,128)(2,1)S(1)} %get-tuple-element.51) | copy-start | bytes 36868
  77.2 181.4 %collective-permute-start.1 = (bf16[192,64]{0,1:T(8,128)(2,1)S(1)}, bf16[192,64]{0,1:T(8,128)(2,1)S(1)}, u32[]{:S(2)}, u32[]{:S(2)}) collective-permute-start(bf16[192,64]{0,1:T(8,128)(2,1)S(1)} %pad_maximum_fusion.7), channel_id=1, source_target_pairs={{0,16},{1,17},{2,18},{3,19},{4,20},{5,21},{6,22},{7,23},{8,24},{9,... | collective-permute-start | bytes 73736 | tf_op jit(solution)/shard_map/ppermute | solution.py:24
  142.3 119.5 %copy-start.6 = (bf16[384,16,128]{2,1,0:T(8,128)(2,1)}, bf16[384,16,128]{2,1,0:T(8,128)(2,1)S(1)}, u32[]{:S(2)}) copy-start(bf16[384,16,128]{2,1,0:T(8,128)(2,1)S(1)} %get-tuple-element.43) | copy-start | bytes 4718596
  264.2 52.7 %copy-start.21 = (bf16[16,24,8,128]{3,2,1,0:T(8,128)(2,1)}, bf16[16,24,8,128]{3,2,1,0:T(8,128)(2,1)S(1)}, u32[]{:S(2)}) copy-start(bf16[16,24,8,128]{3,2,1,0:T(8,128)(2,1)S(1)} %fusion.60) | copy-start | bytes 2359300
  344.2 211.7 %copy-start.15 = (bf16[1,192,2048]{2,1,0:T(8,128)(2,1)S(1)}, bf16[1,192,2048]{2,1,0:T(8,128)(2,1)}, u32[]{:S(2)}) copy-start(bf16[1,192,2048]{2,1,0:T(8,128)(2,1)} %param.23) | copy-start | bytes 2359300
  344.2 250.2 %all-to-all-start = ((bf16[16,72,2048]{2,1,0:T(8,128)(2,1)}), bf16[16,72,2048]{2,1,0:T(8,128)(2,1)}, u32[]{:S(2)}, u32[]{:S(2)}) async-start(bf16[16,72,2048]{2,1,0:T(8,128)(2,1)} %bitcast.212), calls=%async_computation | async-start | bytes 9437184 | tf_op jit(solution)/shard_map/all_to_all | solution.py:214
  555.7 18.5 copy-start.37
  594.4 107.3 %all-to-all-start.2 = ((bf16[16,72,2048]{2,1,0:T(8,128)(2,1)}), bf16[16,72,2048]{2,1,0:T(8,128)(2,1)}, u32[]{:S(2)}, u32[]{:S(2)}) async-start(bf16[16,72,2048]{2,1,0:T(8,128)(2,1)} %bitcast.213), calls=%async_computation.2 | async-start | bytes 9437184 | tf_op jit(solution)/shard_map/all_to_all | solution.py:249
  601.2 566.6 %all-gather.26.cloned.1.call-start = ((), (), s32[]{:S(2)}) async-start(), calls=%async_computation.22 | async-start | bytes 11894784 | tf_op jit(solution)/shard_map/all_gather | solution.py:183
  719.4 10.8 copy-start.84
  801.5 141.6 %all-to-all-start.1 = ((bf16[16,2,73728]{2,1,0:T(2,128)(2,1)}), bf16[16,2,73728]{2,1,0:T(2,128)(2,1)}, u32[]{:S(2)}, u32[]{:S(2)}) async-start(bf16[16,2,73728]{2,1,0:T(2,128)(2,1)} %reshape.574), calls=%async_computation.1 | async-start | bytes 9437184 | tf_op jit(solution)/shard_map/all_to_all | solution.py:227
  857.5 563.8 %reduce-scatter.34.cloned.1.call-start = ((), (), s32[]{:S(2)}) async-start(), calls=%async_computation.35 | async-start | bytes 1081344
  999.0 491.7 %reduce-scatter.32.cloned.1.call-start = ((), (), s32[]{:S(2)}) async-start(), calls=%async_computation.34 | async-start | bytes 8650752 | tf_op jit(solution)/shard_map/reduce_scatter | solution.py:280
  1011.2 484.6 %reduce-scatter.28.cloned.1.call-start = ((), (), s32[]{:S(2)}) async-start(), calls=%async_computation.32 | async-start | bytes 8650752 | tf_op jit(solution)/shard_map/reduce_scatter | solution.py:274
  1024.2 10.8 slice-start.5
  1024.2 10.8 slice-start.6
  1115.4 20.7 copy-start.61
  1115.4 108.9 %all-to-all-start.3 = ((bf16[16,2,73728]{2,1,0:T(2,128)(2,1)}), bf16[16,2,73728]{2,1,0:T(2,128)(2,1)}, u32[]{:S(2)}, u32[]{:S(2)}) async-start(bf16[16,2,73728]{2,1,0:T(2,128)(2,1)} %reshape.576), calls=%async_computation.3 | async-start | bytes 9437184 | tf_op jit(solution)/shard_map/all_to_all | solution.py:284
  1136.1 364.4 %reduce-scatter.30.cloned.1.call-start = ((), (), s32[]{:S(2)}) async-start(), calls=%async_computation.33 | async-start | bytes 8650752 | tf_op jit(solution)/shard_map/reduce_scatter | solution.py:277
  1149.0 356.2 %reduce-scatter.16.cloned.1.call-start = ((), (), s32[]{:S(2)}) async-start(), calls=%async_computation.26 | async-start | bytes 5406720 | tf_op jit(solution)/shard_map/reduce_scatter | solution.py:389
  1167.7 22.4 slice-start.2
  1167.7 22.4 slice-start.3
  1269.2 10.8 copy-start.9
  1269.2 10.8 copy-start.38
  1269.2 10.8 copy-start.56
  1269.2 10.8 copy-start.67
  1304.4 15.7 collective-permute-start.2
  1307.2 12.2 collective-permute-start.3
  1329.8 352.2 %reduce-scatter.18.cloned.1.call-start = ((), (), s32[]{:S(2)}) async-start(), calls=%async_computation.27 | async-start | bytes 8650752 | tf_op jit(solution)/shard_map/reduce_scatter | solution.py:391
  1337.7 835.7 %reduce-scatter.22.cloned.1.call-start = ((), (), s32[]{:S(2)}) async-start(), calls=%async_computation.29 | async-start | bytes 23789568 | tf_op jit(solution)/shard_map/reduce_scatter | solution.py:395
  1348.4 1320.5 %reduce-scatter.24.cloned.1.call-start = ((), (), s32[]{:S(2)}) async-start(), calls=%async_computation.30 | async-start | bytes 23789568 | tf_op jit(solution)/shard_map/reduce_scatter | solution.py:396
  1359.1 1805.4 %reduce-scatter.26.cloned.1.call-start = ((), (), s32[]{:S(2)}) async-start(), calls=%async_computation.31 | async-start | bytes 23789568 | tf_op jit(solution)/shard_map/reduce_scatter | solution.py:397
  1370.9 2158.3 %reduce-scatter.20.cloned.1.call-start = ((), (), s32[]{:S(2)}) async-start(), calls=%async_computation.28 | async-start | bytes 17301504 | tf_op jit(solution)/shard_map/reduce_scatter | solution.py:392
  1381.7 2402.7 %reduce-scatter.14.cloned.1.call-start = ((), (), s32[]{:S(2)}) async-start(), calls=%async_computation.25 | async-start | bytes 25952256 | tf_op jit(solution)/shard_map/reduce_scatter | solution.py:388
  1403.2 10.2 copy-start.10
  1403.2 10.2 copy-start.29
  1403.2 10.2 copy-start.30
  1422.8 64.9 %copy-start.69 = (f32[192]{0:T(256)S(1)}, f32[192]{0:T(256)}, u32[]{:S(2)}) copy-start(f32[192]{0:T(256)} %copy-done.68) | copy-start | bytes 2308
  1422.8 64.9 %copy-start.12 = (f32[192,2048]{1,0:T(8,128)S(1)}, f32[192,2048]{1,0:T(8,128)}, u32[]{:S(2)}) copy-start(f32[192,2048]{1,0:T(8,128)} %copy-done.11) | copy-start | bytes 4718596
  (57 other events, 247.2 us)
Sparse Core Ops, SparseCore 0:
  10.9 60.6 all-gather.11
  74.6 60.9 all-gather.13
  138.5 94.5 all-gather.15
  235.8 75.7 all-gather.17
  313.0 14.5 all-gather.21
  329.0 17.1 all-gather.19
  347.7 17.1 all-gather.23
  367.8 144.9 all-gather.29
  515.6 119.7 all-gather.27
  638.1 128.0 all-gather.25
  999.1 154.9 reduce-scatter.33
  1156.9 21.0 reduce-scatter.31
  1180.9 15.0 reduce-scatter.27
  1198.2 15.0 reduce-scatter.29
  1329.9 165.5 reduce-scatter.15
  1498.3 183.6 reduce-scatter.17
  1684.7 488.7 reduce-scatter.21
  2176.2 492.6 reduce-scatter.23
  2671.8 492.6 reduce-scatter.25
  3167.3 361.9 reduce-scatter.19
  3536.3 248.0 reduce-scatter.13
where the time goes:
time: 3800 us; the launch traced here: 3790 us
  waiting for transfers between devices  2680 us (71%)
  blocking collectives  307 us (8%)
  matrix products  293 us (8%)
  local copies, waits for them, and re-layouts  265 us (7%)
  other arithmetic  132 us (3%)
  starting transfers between devices  95.3 us (3%)
    reduce_scatter x1, waiting for transfers between devices, body(): lax.psum_scatter(sdown_grad, ('fsdp', 'expert'), scatter_dimension=0, til...  496 us
    reduce_scatter x1, waiting for transfers between devices, body(): lax.psum_scatter(sup_grad, ('fsdp', 'expert'), scatter_dimension=0, tiled...  495 us
    reduce_scatter x1, waiting for transfers between devices, body(): lax.psum_scatter(sgate_grad, ('fsdp', 'expert'), scatter_dimension=0, til...  491 us
    reduce_scatter x1, waiting for transfers between devices, body(): lax.psum_scatter(output_grad, ('fsdp', 'expert'), scatter_dimension=0, ti...  365 us
    reduce_scatter x1, waiting for transfers between devices, body(): lax.psum_scatter(query_weight_grad, ('fsdp', 'expert'), scatter_dimension...  255 us
    all_gather x1, blocking collectives, body(): lax.all_gather(router_weight, ('fsdp', 'expert'), axis=0, tiled=True)  206 us
    reduce_scatter x1, waiting for transfers between devices, body(): lax.psum_scatter(up_weight_grad, ('fsdp', 'expert'), scatter_dimension=0,...  177 us
    unnamed x2, blocking collectives  101 us
  transfers between devices with their start and end apart: 29, of which 13 were waited for; matrix products, arithmetic and copies ran while one was open for 18% of the time, Pallas kernels for 0%

commit v1 on v0

--- a/solution.py
+++ b/solution.py
@@ -101,6 +101,26 @@
         "qhd,kd->hqk", queries[..., NOPE:], keys_rope, preferred_element_type=jnp.float32
     )
     return jnp.where(visible[None], scores * score_scale, FLOOR_SCORE)
+
+
+PLANE = 4
+
+
+def groups(count):
+    lines = count // PLANE
+    plane = [[row * PLANE + spot for spot in range(PLANE)] for row in range(lines)]
+    line = [[row * PLANE + spot for row in range(lines)] for spot in range(PLANE)]
+    return plane, line
+
+
+def gather_all(value):
+    part = lax.all_gather(value, "expert", axis=0, tiled=True)
+    return lax.all_gather(part, "fsdp", axis=0, tiled=True)
+
+
+def scatter_all(value):
+    part = lax.psum_scatter(value, "fsdp", scatter_dimension=0, tiled=True)
+    return lax.psum_scatter(part, "expert", scatter_dimension=0, tiled=True)
 
 
 def body(
@@ -125,16 +145,106 @@
     expert_down,
 ):
     row_count = tokens.shape[1]
+    expert_total = lax.axis_size("expert")
+    depth = expert_total // PLANE
+    plane, line = groups(expert_total)
+    place = lax.axis_index("expert")
+    level = place // PLANE
     device_half = lax.axis_index("fsdp")
+    capacity = row_count * TOPK // expert_total
+    line_rows = depth * row_count
     inputs = tokens[0].astype(jnp.float32)
-    gain_one, query_full, down_full, gain_latent, up_full, output_full = (
-        lax.all_gather(attention_norm, ("fsdp", "expert"), axis=0, tiled=True),
-        lax.all_gather(query_weight, ("fsdp", "expert"), axis=0, tiled=True),
-        lax.all_gather(latent_down, ("fsdp", "expert"), axis=0, tiled=True),
-        lax.all_gather(latent_norm, ("fsdp", "expert"), axis=0, tiled=True),
-        lax.all_gather(latent_up, ("fsdp", "expert"), axis=0, tiled=True),
-        lax.all_gather(output_weight, ("fsdp", "expert"), axis=0, tiled=True),
-    )
+
+    gain_width = attention_norm.shape[0]
+    latent_width = latent_norm.shape[0]
+    small = jnp.concatenate(
+        [attention_norm, latent_norm, feed_norm, router_weight.reshape(-1)]
+    )
+    small_full = gather_all(small[None])
+    cuts = [
+        0,
+        gain_width,
+        gain_width + latent_width,
+        2 * gain_width + latent_width,
+        small.shape[0],
+    ]
+    gain_one, gain_latent, gain_feed, router_full = (
+        small_full[:, cuts[0] : cuts[1]].reshape(-1),
+        small_full[:, cuts[1] : cuts[2]].reshape(-1),
+        small_full[:, cuts[2] : cuts[3]].reshape(-1),
+        small_full[:, cuts[3] : cuts[4]].reshape(-1, expert_total),
+    )
+    down_full = gather_all(latent_down)
+    query_full = gather_all(query_weight)
+    up_full = gather_all(latent_up)
+    output_full = gather_all(output_weight)
+
+    route_rows = routes[0]
+    slot_rows = slot_index[0]
+    target = jnp.where(
+        slot_rows >= 0, route_rows * capacity + slot_rows, expert_total * capacity
+    )
+    target_line = lax.all_gather(target, "expert", axis_index_groups=line, axis=0)
+    grad_line = lax.all_gather(
+        cotangent[0], "expert", axis_index_groups=line, axis=0, tiled=True
+    )
+    shared_width = shared_gate.shape[1] // (2 * depth)
+
+    def columns_to_levels(weight):
+        rows = weight.shape[0]
+        pieces = weight.reshape(rows, 2, depth, shared_width).transpose(2, 0, 1, 3)
+        moved = lax.all_to_all(
+            pieces.reshape(depth, rows, 2 * shared_width),
+            "expert",
+            split_axis=0,
+            concat_axis=0,
+            axis_index_groups=line,
+            tiled=True,
+        )
+        across = lax.all_gather(moved, "expert", axis_index_groups=plane, axis=0)
+        whole = lax.all_gather(across, "fsdp", axis=0)
+        return whole.transpose(0, 2, 1, 3, 4).reshape(-1, 2 * shared_width)
+
+    sgate_full = columns_to_levels(shared_gate)
+    sup_full = columns_to_levels(shared_up)
+    sdown_full = lax.all_gather(
+        lax.all_gather(shared_down, "expert", axis_index_groups=plane, axis=0, tiled=True),
+        "fsdp",
+        axis=0,
+        tiled=True,
+    )
+    expert_gate_full = lax.all_gather(expert_gate[0], "fsdp", axis=0, tiled=True)
+    expert_up_full = lax.all_gather(expert_up[0], "fsdp", axis=0, tiled=True)
+    expert_down_full = lax.all_gather(expert_down[0], "fsdp", axis=1, tiled=True)
+
+    slot_names = level * PLANE * capacity + jnp.arange(PLANE * capacity)
+    hits = target_line[:, None, :, :] == slot_names[None, :, None, None]
+    choose_rows = jnp.any(hits, axis=-1).astype(jnp.bfloat16)
+
+    def to_experts(rows_line):
+        placed = jnp.einsum(
+            "zst,ztd->zsd",
+            choose_rows,
+            rows_line.reshape(depth, row_count, D),
+            preferred_element_type=jnp.float32,
+        ).astype(jnp.bfloat16)
+        placed = placed.reshape(depth, PLANE, capacity, D).transpose(1, 0, 2, 3)
+        return lax.all_to_all(
+            placed, "expert", split_axis=0, concat_axis=0, axis_index_groups=plane, tiled=True
+        ).reshape(expert_total * capacity, D)
+
+    def from_experts(rows):
+        return lax.all_to_all(
+            rows.reshape(PLANE, depth, capacity, -1),
+            "expert",
+            split_axis=0,
+            concat_axis=0,
+            axis_index_groups=plane,
+            tiled=True,
+        )
+
+    grad_rows = to_experts(grad_line)
+
     cosine, sine_table = rotary_table(row_count, device_half * row_count, ROPE)
     score_scale = (NOPE + ROPE) ** (-0.5)
     gain_first = gain_one.astype(jnp.float32)
@@ -177,133 +287,119 @@
         .astype(jnp.bfloat16)
     )
     residual = inputs + matmul(mixed_heads, output_full)
-    gain_feed, router_full, sgate_full, sup_full, sdown_full = (
-        lax.all_gather(feed_norm, ("fsdp", "expert"), axis=0, tiled=True),
-        lax.all_gather(router_weight, ("fsdp", "expert"), axis=0, tiled=True),
-        lax.all_gather(shared_gate, ("fsdp", "expert"), axis=0, tiled=True),
-        lax.all_gather(shared_up, ("fsdp", "expert"), axis=0, tiled=True),
-        lax.all_gather(shared_down, ("fsdp", "expert"), axis=0, tiled=True),
-    )
-    expert_gate_gathered, expert_up_gathered, expert_down_gathered = (
-        lax.all_gather(expert_gate, "fsdp", axis=1, tiled=True),
-        lax.all_gather(expert_up, "fsdp", axis=1, tiled=True),
-        lax.all_gather(expert_down, "fsdp", axis=2, tiled=True),
-    )
     feed_gain = gain_feed.astype(jnp.float32)
     mixed_low = norm_rows(residual, feed_gain).astype(jnp.bfloat16)
-    logits = matmul(mixed_low, router_full)
-    expert_count = logits.shape[1]
-    capacity = row_count * TOPK // expert_count
-    probabilities = jax.nn.softmax(logits, axis=-1)
-    route_rows = routes[0]
-    slot_rows = slot_index[0]
-    choose = (route_rows[..., None] == jnp.arange(expert_count)[None, None, :]).astype(jnp.float32)
-    gate_values = jnp.sum(probabilities[:, None, :] * choose, axis=-1)
-    kept_pairs = (slot_rows >= 0).astype(jnp.float32)
-    target_row = jnp.where(
-        slot_rows >= 0, route_rows * capacity + slot_rows, expert_count * capacity
-    ).reshape(-1)
-    safe_row = jnp.minimum(target_row, expert_count * capacity - 1)
-    pair_rows = jnp.repeat(mixed_low, TOPK, axis=0)
-    dispatch_buffer = (
-        jnp.zeros((expert_count * capacity, D), jnp.bfloat16)
-        .at[target_row]
-        .set(pair_rows, mode="drop")
-        .reshape(expert_count, capacity, D)
-    )
-    received_rows = lax.all_to_all(
-        dispatch_buffer, "expert", split_axis=0, concat_axis=1, tiled=True
-    )
-    gate_part = jnp.einsum(
-        "pjh,phy->pjy", received_rows, expert_gate_gathered, preferred_element_type=jnp.float32
-    )
-    up_portion = jnp.einsum(
-        "pjh,phy->pjy", received_rows, expert_up_gathered, preferred_element_type=jnp.float32
-    )
-    hidden = (jax.nn.silu(gate_part) * up_portion).astype(jnp.bfloat16)
-    expert_out = jnp.einsum(
-        "erf,efd->erd", hidden, expert_down_gathered, preferred_element_type=jnp.float32
-    ).astype(jnp.bfloat16)
-    returned = lax.all_to_all(expert_out, "expert", split_axis=1, concat_axis=0, tiled=True)
-    gathered = returned.reshape(expert_count * capacity, D)[safe_row].reshape(row_count, TOPK, D)
-    pair_weight = gate_values * kept_pairs
-    routed = jnp.sum(pair_weight[..., None] * gathered, axis=1)
-    shared_gate_part = matmul(mixed_low, sgate_full)
-    shared_up_part = matmul(mixed_low, sup_full)
-    shared_hidden = (jax.nn.silu(shared_gate_part) * shared_up_part).astype(jnp.bfloat16)
-    output = (residual + routed + matmul(shared_hidden, sdown_full)).astype(jnp.bfloat16)
-    out_grad = cotangent[0].astype(jnp.float32)
-    grad_low = cotangent[0]
-    gate_grad_pairs = jnp.sum(out_grad[:, None, :] * gathered, axis=-1) * kept_pairs
-    pair_grad = (
-        (pair_weight[..., None] * out_grad[:, None, :])
-        .astype(jnp.bfloat16)
-        .reshape(row_count * TOPK, D)
-    )
-    grad_buffer = (
-        jnp.zeros((expert_count * capacity, D), jnp.bfloat16)
-        .at[target_row]
-        .set(pair_grad, mode="drop")
-        .reshape(expert_count, capacity, D)
-    )
-    grad_received = lax.all_to_all(grad_buffer, "expert", split_axis=0, concat_axis=1, tiled=True)
-    hidden_grad = jnp.einsum(
-        "erd,efd->erf", grad_received, expert_down_gathered, preferred_element_type=jnp.float32
-    )
-    edown_grad = jnp.einsum(
-        "erf,erd->efd", hidden, grad_received, preferred_element_type=jnp.float32
-    )
+    mixed_line = lax.all_gather(mixed_low, "expert", axis_index_groups=line, axis=0, tiled=True)
+    mixed_rows = to_experts(mixed_line)
+    probabilities_line = jax.nn.softmax(matmul(mixed_line, router_full), axis=-1).reshape(
+        depth, row_count, expert_total
+    )
+    level_probs = lax.dynamic_slice_in_dim(probabilities_line, level * PLANE, PLANE, axis=2)
+    hit_weights = choose_rows.astype(jnp.float32).reshape(depth, PLANE, capacity, row_count)
+    weighted = hit_weights * level_probs.transpose(0, 2, 1)[:, :, None, :]
+    slot_gate = jnp.sum(weighted, axis=-1).transpose(1, 0, 2).reshape(PLANE, depth, capacity, 1)
+    gate_column = from_experts(slot_gate).reshape(expert_total * capacity, 1)
+
+    gate_part = matmul(mixed_rows, expert_gate_full)
+    up_portion = matmul(mixed_rows, expert_up_full)
+    hidden_wide = jax.nn.silu(gate_part) * up_portion
+    hidden = hidden_wide.astype(jnp.bfloat16)
+    expert_out = matmul(hidden, expert_down_full).astype(jnp.bfloat16)
+    returned = from_experts(expert_out)
+    slot_grad = jnp.sum(
+        expert_out.astype(jnp.float32) * grad_rows.astype(jnp.float32), axis=-1, keepdims=True
+    )
+    slot_grad_back = from_experts(slot_grad)
+    hidden_grad = right_matmul(grad_rows, expert_down_full) * gate_column
     gate_part_grad, up_part_grad = swiglu_back(gate_part, up_portion, hidden_grad)
     gate_low = gate_part_grad.astype(jnp.bfloat16)
-    up_reduced = up_part_grad.astype(jnp.bfloat16)
+    up_low = up_part_grad.astype(jnp.bfloat16)
     input_grad = (
-        jnp.einsum(
-            "jsx,jzx->jsz", gate_low, expert_gate_gathered, preferred_element_type=jnp.float32
-        )
-        + jnp.einsum(
-            "jsx,jzx->jsz", up_reduced, expert_up_gathered, preferred_element_type=jnp.float32
-        )
+        right_matmul(gate_low, expert_gate_full) + right_matmul(up_low, expert_up_full)
     ).astype(jnp.bfloat16)
-    egate_grad = jnp.einsum(
-        "siq,siy->sqy", received_rows, gate_low, preferred_element_type=jnp.float32
-    )
-    expert_up_gradient = jnp.einsum(
-        "siq,siy->sqy", received_rows, up_reduced, preferred_element_type=jnp.float32
-    )
+    back_rows = from_experts(input_grad)
+    hidden_scaled = (hidden.astype(jnp.float32) * gate_column).astype(jnp.bfloat16)
+    egate_grad = left_matmul(mixed_rows, gate_low).astype(jnp.bfloat16)
+    eup_grad = left_matmul(mixed_rows, up_low).astype(jnp.bfloat16)
+    edown_grad = left_matmul(hidden_scaled, grad_rows).astype(jnp.bfloat16)
     expert_gate_piece, expert_up_piece, expert_down_piece = (
-        lax.psum_scatter(
-            egate_grad.astype(jnp.bfloat16), "fsdp", scatter_dimension=1, tiled=True
-        ).astype(jnp.float32),
-        lax.psum_scatter(
-            expert_up_gradient.astype(jnp.bfloat16), "fsdp", scatter_dimension=1, tiled=True
-        ).astype(jnp.float32),
-        lax.psum_scatter(
-            edown_grad.astype(jnp.bfloat16), "fsdp", scatter_dimension=2, tiled=True
-        ).astype(jnp.float32),
-    )
-    back_rows = lax.all_to_all(input_grad, "expert", split_axis=1, concat_axis=0, tiled=True)
-    pair_back = back_rows.reshape(expert_count * capacity, D)[safe_row].reshape(row_count, TOPK, D)
-    routed_grad = jnp.sum(kept_pairs[..., None] * pair_back, axis=1)
-    prob_grad = jnp.sum(gate_grad_pairs[..., None] * choose, axis=1)
+        lax.psum_scatter(egate_grad, "fsdp", scatter_dimension=0, tiled=True),
+        lax.psum_scatter(eup_grad, "fsdp", scatter_dimension=0, tiled=True),
+        lax.psum_scatter(edown_grad, "fsdp", scatter_dimension=1, tiled=True),
+    )
+
+    shared_gate_part = matmul(mixed_line, sgate_full)
+    shared_up_part = matmul(mixed_line, sup_full)
+    shared_hidden = (jax.nn.silu(shared_gate_part) * shared_up_part).astype(jnp.bfloat16)
+    shared_out = matmul(shared_hidden, sdown_full)
+    shared_hidden_grad = right_matmul(grad_line, sdown_full)
+    shared_gate_grad, shared_up_grad = swiglu_back(
+        shared_gate_part, shared_up_part, shared_hidden_grad
+    )
+    shared_gate_low = shared_gate_grad.astype(jnp.bfloat16)
+    shared_up_low = shared_up_grad.astype(jnp.bfloat16)
+    shared_back = right_matmul(shared_gate_low, sgate_full) + right_matmul(
+        shared_up_low, sup_full
+    )
+    sdown_grad = left_matmul(shared_hidden, grad_line).astype(jnp.bfloat16)
+    sgate_grad = left_matmul(mixed_line, shared_gate_low).astype(jnp.bfloat16)
+    sup_grad = left_matmul(mixed_line, shared_up_low).astype(jnp.bfloat16)
+
+    def scatter_plane(value):
+        part = lax.psum_scatter(value, "fsdp", scatter_dimension=0, tiled=True)
+        return lax.psum_scatter(
+            part, "expert", scatter_dimension=0, axis_index_groups=plane, tiled=True
+        )
+
+    def levels_to_columns(weight):
+        rows = D // (2 * expert_total)
+        pieces = weight.reshape(2, depth, PLANE, rows, 2 * shared_width).transpose(0, 2, 1, 3, 4)
+        summed = scatter_plane(pieces.reshape(2 * PLANE, depth, rows, 2 * shared_width))[0]
+        moved = lax.all_to_all(
+            summed, "expert", split_axis=0, concat_axis=0, axis_index_groups=line, tiled=True
+        )
+        return (
+            moved.reshape(depth, rows, 2, shared_width)
+            .transpose(1, 2, 0, 3)
+            .reshape(rows, -1)
+            .astype(jnp.float32)
+        )
+
+    sgate_piece = levels_to_columns(sgate_grad)
+    sup_piece = levels_to_columns(sup_grad)
+    sdown_piece = scatter_plane(sdown_grad).astype(jnp.float32)
+
+    choose_weighted = (
+        weighted.reshape(depth, PLANE * capacity, row_count).astype(jnp.bfloat16)
+    )
+
+    def combine(matrix, rows, add):
+        gathered = rows.transpose(1, 0, 2, 3).reshape(depth, PLANE * capacity, D)
+        mixed = jnp.einsum("zst,zsd->ztd", matrix, gathered, preferred_element_type=jnp.float32)
+        total = (mixed.reshape(line_rows, D) + add).astype(jnp.bfloat16)
+        return lax.psum_scatter(
+            total, "expert", scatter_dimension=0, axis_index_groups=line, tiled=True
+        ).astype(jnp.float32)
+
+    routed_and_shared = combine(choose_weighted, returned, shared_out)
+    back_and_shared = combine(choose_rows, back_rows, shared_back)
+    output = (residual + routed_and_shared).astype(jnp.bfloat16)
+    out_grad = cotangent[0].astype(jnp.float32)
+
+    slot_grads = slot_grad_back.transpose(1, 0, 2, 3).reshape(depth, PLANE, capacity, 1)
+    prob_part = jnp.sum(hit_weights * slot_grads, axis=2)
+    prob_wide = lax.dynamic_update_slice_in_dim(
+        jnp.zeros((depth, expert_total, row_count), jnp.float32), prob_part, level * PLANE, axis=1
+    )
+    prob_grad = lax.psum_scatter(
+        prob_wide, "expert", scatter_dimension=0, axis_index_groups=line, tiled=True
+    )[0].T
+    probabilities = lax.dynamic_index_in_dim(probabilities_line, level, axis=0, keepdims=False)
     logit_low = (
         probabilities * (prob_grad - jnp.sum(probabilities * prob_grad, axis=-1, keepdims=True))
     ).astype(jnp.bfloat16)
     router_grad = left_matmul(mixed_low, logit_low)
-    shared_hidden_grad = right_matmul(grad_low, sdown_full)
-    sdown_grad = left_matmul(shared_hidden, grad_low)
-    shared_gate_grad, shared_up_grad = swiglu_back(
-        shared_gate_part, shared_up_part, shared_hidden_grad
-    )
-    shared_gate_low = shared_gate_grad.astype(jnp.bfloat16)
-    shared_up_low = shared_up_grad.astype(jnp.bfloat16)
-    sgate_grad = left_matmul(mixed_low, shared_gate_low)
-    sup_grad = left_matmul(mixed_low, shared_up_low)
-    mixed_grad = (
-        right_matmul(logit_low, router_full)
-        + right_matmul(shared_gate_low, sgate_full)
-        + right_matmul(shared_up_low, sup_full)
-        + routed_grad
-    )
+    mixed_grad = right_matmul(logit_low, router_full) + back_and_shared
     residual_add, feed_gain_grad = norm_back(residual, feed_gain, mixed_grad)
     residual_grad = out_grad + residual_add
     attended_low = residual_grad.astype(jnp.bfloat16)
@@ -383,36 +479,37 @@
     down_weight_grad = left_matmul(normed_low, compressed_low)
     input_add, first_gain_grad = norm_back(inputs, gain_first, normed_grad)
     token_grad = residual_grad + input_add
-    all_shards = (
-        lax.psum_scatter(first_gain_grad, ("fsdp", "expert"), scatter_dimension=0, tiled=True),
-        lax.psum_scatter(query_weight_grad, ("fsdp", "expert"), scatter_dimension=0, tiled=True),
-        lax.psum_scatter(down_weight_grad, ("fsdp", "expert"), scatter_dimension=0, tiled=True),
-        lax.psum_scatter(latent_gain_grad, ("fsdp", "expert"), scatter_dimension=0, tiled=True),
-        lax.psum_scatter(up_weight_grad, ("fsdp", "expert"), scatter_dimension=0, tiled=True),
-        lax.psum_scatter(output_grad, ("fsdp", "expert"), scatter_dimension=0, tiled=True),
-        lax.psum_scatter(feed_gain_grad, ("fsdp", "expert"), scatter_dimension=0, tiled=True),
-        lax.psum_scatter(router_grad, ("fsdp", "expert"), scatter_dimension=0, tiled=True),
-        lax.psum_scatter(sgate_grad, ("fsdp", "expert"), scatter_dimension=0, tiled=True),
-        lax.psum_scatter(sup_grad, ("fsdp", "expert"), scatter_dimension=0, tiled=True),
-        lax.psum_scatter(sdown_grad, ("fsdp", "expert"), scatter_dimension=0, tiled=True),
-    )
+    small_grad = jnp.concatenate(
+        [
+            first_gain_grad.reshape(-1, gain_width),
+            latent_gain_grad.reshape(-1, latent_width),
+            feed_gain_grad.reshape(-1, gain_width),
+            router_grad.reshape(2 * expert_total, -1),
+        ],
+        axis=1,
+    )
+    small_piece = scatter_all(small_grad)[0]
+
+    def shard(value):
+        return scatter_all(value.astype(jnp.bfloat16)).astype(jnp.float32)
+
     return (
         output[None],
         token_grad[None],
-        all_shards[0],
-        all_shards[1],
-        all_shards[2],
-        all_shards[3],
-        all_shards[4],
-        all_shards[5],
-        all_shards[6],
-        all_shards[7],
-        all_shards[8],
-        all_shards[9],
-        all_shards[10],
-        expert_gate_piece,
-        expert_up_piece,
-        expert_down_piece,
+        small_piece[cuts[0] : cuts[1]],
+        shard(query_weight_grad),
+        shard(down_weight_grad),
+        small_piece[cuts[1] : cuts[2]],
+        shard(up_weight_grad),
+        shard(output_grad),
+        small_piece[cuts[2] : cuts[3]],
+        small_piece[cuts[3] : cuts[4]].reshape(gain_width, expert_total),
+        sgate_piece,
+        sup_piece,
+        sdown_piece,
+        expert_gate_piece.astype(jnp.float32)[None],
+        expert_up_piece.astype(jnp.float32)[None],
+        expert_down_piece.astype(jnp.float32)[None],
     )
 
 

time: 3800 us -> 1820 us (0.48)
  waiting for transfers between devices: 2680 us -> 1220 us
  blocking collectives: 307 us -> 117 us
  local copies, waits for them, and re-layouts: 265 us -> 110 us
  other arithmetic: 132 us -> 45.3 us
  starting transfers between devices: 95.3 us -> 50 us
    reduce_scatter x10 -> x17, waiting for transfers between devices: 2280 us -> 384 us  [the longest x3 321 us: scatter_all(): return lax.psum_scatter(part, 'expert', scatter_dimension=0, tiled=True)]
    unnamed x22 -> x46, waiting for transfers between devices: 6.42 us -> 283 us
    all_gather x10 -> x19, waiting for transfers between devices: 209 us -> 455 us  [the longest x4 295 us: gather_all(): part = lax.all_gather(value, 'expert', axis=0, tiled=True)]
    all_gather x1 -> x2, blocking collectives: 206 us -> 15.2 us  [the longest x1 13.4 us: body(): lax.all_gather(target, 'expert', axis_index_groups=line, axis=0)]
    dot_general x9 -> x4, matrix products: 112 us -> 10.2 us  [the longest x2 6.54 us: to_experts(): jnp.einsum('zst,ztd->zsd', choose_rows, rows_line.reshape(depth, row_coun...]
    all_to_all x4 -> x9, waiting for transfers between devices: 188 us -> 95.8 us  [the longest x4 81.8 us: from_experts(): lax.all_to_all(rows.reshape(PLANE, depth, capacity, -1), 'expert', split_...]
    unnamed x205 -> x233, local copies, waits for them, and re-layouts: 84.4 us -> 20.3 us
    unnamed x7 -> x4, other arithmetic: 60 us -> 0.02 us
  transfers between devices with their start and end apart: 29 -> 54, of which waited for: 13 -> 28; matrix products, arithmetic and copies ran while one was open for 18% -> 22% of each run, Pallas kernels for 0% -> 0%
where the time goes in v1:
time: 1820 us
  waiting for transfers between devices  1220 us (67%)
  matrix products  259 us (14%)
  blocking collectives  117 us (6%)
  local copies, waits for them, and re-layouts  110 us (6%)
  starting transfers between devices  50 us (3%)
  other arithmetic  45.3 us (2%)
    reduce_scatter x3, waiting for transfers between devices, scatter_all(): return lax.psum_scatter(part, 'expert', scatter_dimension=0, tiled=True)  321 us
    all_gather x4, waiting for transfers between devices, gather_all(): part = lax.all_gather(value, 'expert', axis=0, tiled=True)  295 us
    unnamed x46, waiting for transfers between devices  283 us
    dot_general x11, matrix products, right_matmul(): lax.dot_general(former, latter, (((1,), (1,)), ((), ())), preferred_eleme...  86.2 us
    all_to_all x4, waiting for transfers between devices, from_experts(): lax.all_to_all(rows.reshape(PLANE, depth, capacity, -1), 'expert', split_...  81.8 us
    unnamed x1, blocking collectives  76.3 us
    dot_general x11, matrix products, left_matmul(): lax.dot_general(former, latter, (((0,), (0,)), ((), ())), preferred_eleme...  76.1 us
    all_gather x1, waiting for transfers between devices, body(): lax.all_gather(cotangent[0], 'expert', axis_index_groups=line, axis=0, ti...  72.7 us
  transfers between devices with their start and end apart: 54, of which 28 were waited for; matrix products, arithmetic and copies ran while one was open for 22% of the time, Pallas kernels for 0%

profile of v1, /device:TPU:0, one launch (start us, length us, event | category | flops | bytes accessed | tf_op | source)
XLA Modules:
  0.0 1817.1 jit_solution(4817634317617043958)
XLA Ops:
  10.0 60.3 %all-gather.29.cloned.1.call-done = bf16[1024,576]{1,0:T(8,128)(2,1)} async-done(((bf16[64,576]{1,0:T(8,128)(2,1)}), bf16[1024,576]{1,0:T(8,128)(2,1)}) %all-gather.29.cloned.1.call-update) | async-done | bytes 1179664 | tf_op jit(solution)/shard_map/all_gather | solution.py:117
  70.4 62.3 %all-gather.33.cloned.1.call-done = bf16[256,4096]{1,0:T(8,128)(2,1)} async-done(((bf16[16,4096]{1,0:T(8,128)(2,1)}), bf16[256,4096]{1,0:T(8,128)(2,1)}) %all-gather.33.cloned.1.call-update) | async-done | bytes 2097168 | tf_op jit(solution)/shard_map/all_gather | solution.py:117
  132.8 95.5 %all-gather.37.cloned.1.call-done = bf16[1024,3072]{1,0:T(8,128)(2,1)} async-done(((bf16[64,3072]{1,0:T(8,128)(2,1)}), bf16[1024,3072]{1,0:T(8,128)(2,1)}) %all-gather.37.cloned.1.call-update) | async-done | bytes 6291472 | tf_op jit(solution)/shard_map/all_gather | solution.py:117
  228.4 76.9 %all-gather.41.cloned.1.call-done = bf16[1024,2048]{1,0:T(8,128)(2,1)} async-done(((bf16[64,2048]{1,0:T(8,128)(2,1)}), bf16[1024,2048]{1,0:T(8,128)(2,1)}) %all-gather.41.cloned.1.call-update) | async-done | bytes 4194320 | tf_op jit(solution)/shard_map/all_gather | solution.py:117
  312.7 76.3 %all-reduce.1 = bf16[18688]{0:T(1024)(128)(2,1)S(1)} all-reduce(bf16[18688]{0:T(1024)(128)(2,1)S(1)} %dynamic-update-slice), channel_id=2, replica_groups=mesh['fsdp'=2,'expert'=16] {'expert'}, use_global_device_ids=true, to_apply=%add.1 | all-reduce | flops 18688 | bytes 74752
  407.2 17.3 copy.224
  424.5 6.8 fusion.61
  438.6 5.6 multiply_reduce_fusion.4
  447.9 25.3 %all_to_all.50 = bf16[4,64,704]{2,1,0:T(8,128)(2,1)} all-to-all(bf16[4,64,704]{2,1,0:T(8,128)(2,1)S(1)} %reshape.454), channel_id=1, replica_groups={{0,4,8,12},{1,5,9,13},{2,6,10,14},{3,7,11,15},{16,20,24,28},{17,21,25,2..., dimensions={0} | all-to-all | bytes 720896 | tf_op jit(solution)/shard_map/all_to_all | solution.py:196
  476.5 13.4 all_gather.89
  490.9 23.3 %all-gather.45.cloned.1.call-done = bf16[768,2048]{1,0:T(8,128)(2,1)} async-done(((bf16[192,2048]{1,0:T(8,128)(2,1)}), bf16[768,2048]{1,0:T(8,128)(2,1)}) %all-gather.45.cloned.1.call-update) | async-done | bytes 3145744 | tf_op jit(solution)/shard_map/all_gather | solution.py:292
  520.0 5.1 all-to-all-start
  527.6 51.7 %all-gather.61.cloned.1.call-done = bf16[16,64,704]{2,1,0:T(8,128)(2,1)} async-done(((bf16[4,64,704]{2,1,0:T(8,128)(2,1)}), bf16[16,64,704]{2,1,0:T(8,128)(2,1)}) %all-gather.61.cloned.1.call-update) | async-done | bytes 1441808 | tf_op jit(solution)/shard_map/all_gather | solution.py:204
  579.3 72.7 %all-gather.65.cloned.1.call-done = bf16[1,768,2048]{2,1,0:T(8,128)(2,1)} async-done(((bf16[1,192,2048]{2,1,0:T(8,128)(2,1)}), bf16[1,768,2048]{2,1,0:T(8,128)(2,1)}) %all-gather.65.cloned.1.call-update) | async-done | bytes 3145744 | tf_op jit(solution)/shard_map/all_gather | solution.py:188
  660.2 5.6 all-to-all-start.4
  668.2 12.7 fusion.13
  680.9 5.9 all-gather.53.cloned.1.call-done
  686.8 14.4 multiply_convert_fusion.2
  701.2 4.2 all-gather.55.cloned.1.call-done
  705.4 14.0 all-to-all-done.4
  719.4 12.9 multiply_reduce_fusion
  736.3 4.6 all-to-all-done.5
  751.4 16.0 multiply_convert_fusion.1
  767.4 11.8 fusion.11
  779.2 11.9 add_convert_fusion
  791.1 5.0 all-to-all-start.7
  810.9 8.7 multiply_convert_fusion.5
  819.6 4.7 fusion.122
  825.4 21.8 %all-to-all-done.7 = bf16[4,4,72,2048]{3,2,1,0:T(8,128)(2,1)} async-done(((bf16[4,4,72,2048]{3,2,1,0:T(8,128)(2,1)}), bf16[4,4,72,2048]{3,2,1,0:T(8,128)(2,1)}, u32[]{:S(2)}, u32[]{:S(2)}) %all-to-all-start.7) | async-done | bytes 4718624 | tf_op jit(solution)/shard_map/all_to_all | solution.py:237
  853.0 4.7 fusion.4
  857.7 5.0 all-to-all-start.1
  863.7 51.5 %all-to-all-done.1 = bf16[4,4,72,2048]{3,2,1,0:T(8,128)(2,1)} async-done(((bf16[4,4,72,2048]{3,2,1,0:T(8,128)(2,1)}), bf16[4,4,72,2048]{3,2,1,0:T(8,128)(2,1)}, u32[]{:S(2)}, u32[]{:S(2)}) %all-to-all-start.1) | async-done | bytes 4718624 | tf_op jit(solution)/shard_map/all_to_all | solution.py:237
  920.1 4.4 fusion.5
  924.6 5.2 convolution_convert_fusion.11
  929.8 4.6 copy.258
  938.4 5.2 convolution_convert_fusion.10
  950.5 5.2 convolution_convert_fusion.12
  961.3 22.7 %reduce-scatter.30.cloned.1.call-done = bf16[192,2048]{1,0:T(8,128)(2,1)} async-done(((bf16[768,2048]{1,0:T(8,128)(2,1)}), bf16[192,2048]{1,0:T(8,128)(2,1)}) %reduce-scatter.30.cloned.1.call-update) | async-done | bytes 786448 | tf_op jit(solution)/shard_map/reduce_scatter | solution.py:380
  986.8 6.9 fusion.50
  1008.4 4.1 copy.253
  1021.7 11.3 fusion.123
  1041.3 5.1 multiply_reduce_fusion.7
  1055.4 4.7 convolution_convert_fusion.6
  1061.7 5.6 convolution_convert_fusion.5
  1068.9 6.6 convolution_convert_fusion
  1077.7 12.7 convolution_convert_fusion.3
  1090.6 13.0 convolution_convert_fusion.2
  1104.3 13.7 convolution_convert_fusion.1
  1122.5 13.3 reduce-scatter.38.cloned.1.call-done
  1135.8 35.4 %reduce-scatter.66.cloned.1.call-done = bf16[1,4,64,704]{3,2,1,0:T(8,128)(2,1)} async-done(((bf16[4,4,64,704]{3,2,1,0:T(8,128)(2,1)}), bf16[1,4,64,704]{3,2,1,0:T(8,128)(2,1)}) %reduce-scatter.66.cloned.1.call-update) | async-done | bytes 360464
  1171.2 4.6 all-to-all-start.8
  1175.8 29.6 %reduce-scatter.68.cloned.1.call-done = bf16[1,4,64,704]{3,2,1,0:T(8,128)(2,1)} async-done(((bf16[4,4,64,704]{3,2,1,0:T(8,128)(2,1)}), bf16[1,4,64,704]{3,2,1,0:T(8,128)(2,1)}) %reduce-scatter.68.cloned.1.call-update) | async-done | bytes 360464
  1205.4 4.8 all-to-all-start.9
  1210.2 28.4 %reduce-scatter.70.cloned.1.call-done = bf16[88,2048]{1,0:T(8,128)(2,1)} async-done(((bf16[352,2048]{1,0:T(8,128)(2,1)}), bf16[88,2048]{1,0:T(8,128)(2,1)}) %reduce-scatter.70.cloned.1.call-update) | async-done | bytes 360464
  1255.3 4.7 bitcast_convert_fusion.2
  1260.0 13.3 reduce-scatter.60.cloned.1.call-done
  1273.4 4.7 bitcast_convert_fusion.1
  1278.1 12.5 reduce-scatter.62.cloned.1.call-done
  1290.6 5.1 bitcast_convert_fusion
  1295.7 105.6 %all-reduce.8.cloned.1.call-done = f32[16,1168]{1,0:T(8,128)} async-done(((f32[16,1168]{1,0:T(8,128)}), f32[16,1168]{1,0:T(8,128)}) %all-reduce.8.cloned.1.call-update) | async-done | bytes 74768
  1407.4 74.6 %reduce-scatter.64.cloned.1.call-done = bf16[64,576]{1,0:T(8,128)(2,1)} async-done(((bf16[1024,576]{1,0:T(8,128)(2,1)}), bf16[64,576]{1,0:T(8,128)(2,1)}) %reduce-scatter.64.cloned.1.call-update) | async-done | bytes 73744
  1483.8 77.6 %reduce-scatter.46.cloned.1.call-done = bf16[16,4096]{1,0:T(8,128)(2,1)} async-done(((bf16[256,4096]{1,0:T(8,128)(2,1)}), bf16[16,4096]{1,0:T(8,128)(2,1)}) %reduce-scatter.46.cloned.1.call-update) | async-done | bytes 131088 | tf_op jit(solution)/shard_map/reduce_scatter | solution.py:123
  1563.0 93.3 %reduce-scatter.50.cloned.1.call-done = bf16[64,2048]{1,0:T(8,128)(2,1)} async-done(((bf16[1024,2048]{1,0:T(8,128)(2,1)}), bf16[64,2048]{1,0:T(8,128)(2,1)}) %reduce-scatter.50.cloned.1.call-update) | async-done | bytes 262160 | tf_op jit(solution)/shard_map/reduce_scatter | solution.py:123
  1658.1 150.0 %reduce-scatter.40.cloned.1.call-done = bf16[64,3072]{1,0:T(8,128)(2,1)} async-done(((bf16[1024,3072]{1,0:T(8,128)(2,1)}), bf16[64,3072]{1,0:T(8,128)(2,1)}) %reduce-scatter.40.cloned.1.call-update) | async-done | bytes 393232 | tf_op jit(solution)/shard_map/reduce_scatter | solution.py:123
  (483 shorter events, 203.3 us)
Async XLA Ops:
  7.2 63.2 %all-gather.29.cloned.1.call-start = ((), (), s32[]{:S(2)}) async-start(), calls=%async_computation.31 | async-start | bytes 1392640 | tf_op jit(solution)/shard_map/all_gather | solution.py:117
  7.9 124.8 %all-gather.33.cloned.1.call-start = ((), (), s32[]{:S(2)}) async-start(), calls=%async_computation.33 | async-start | bytes 2228224 | tf_op jit(solution)/shard_map/all_gather | solution.py:117
  8.7 219.7 %all-gather.37.cloned.1.call-start = ((), (), s32[]{:S(2)}) async-start(), calls=%async_computation.35 | async-start | bytes 6684672 | tf_op jit(solution)/shard_map/all_gather | solution.py:117
  9.4 296.0 %all-gather.41.cloned.1.call-start = ((), (), s32[]{:S(2)}) async-start(), calls=%async_computation.37 | async-start | bytes 4456448 | tf_op jit(solution)/shard_map/all_gather | solution.py:117
  10.0 382.9 %all-gather.31.cloned.1.call-start = ((), (), s32[]{:S(2)}) async-start(), calls=%async_computation.32 | async-start | bytes 3932160 | tf_op jit(solution)/shard_map/all_gather | solution.py:118
  70.4 330.0 %all-gather.35.cloned.1.call-start = ((), (), s32[]{:S(2)}) async-start(), calls=%async_computation.34 | async-start | bytes 6291456 | tf_op jit(solution)/shard_map/all_gather | solution.py:118
  132.8 274.4 %all-gather.39.cloned.1.call-start = ((), (), s32[]{:S(2)}) async-start(), calls=%async_computation.36 | async-start | bytes 18874368 | tf_op jit(solution)/shard_map/all_gather | solution.py:118
  228.4 77.1 %copy-start.49 = (bf16[64,2816]{1,0:T(8,128)(2,1)S(1)}, bf16[64,2816]{1,0:T(8,128)(2,1)}, u32[]{:S(2)}) copy-start(bf16[64,2816]{1,0:T(8,128)(2,1)} %param.32) | copy-start | bytes 1081348
  228.4 210.3 %all-gather.43.cloned.1.call-start = ((), (), s32[]{:S(2)}) async-start(), calls=%async_computation.38 | async-start | bytes 12582912 | tf_op jit(solution)/shard_map/all_gather | solution.py:118
  305.4 85.9 %copy-start.86 = (s32[1,384]{1,0:T(1,128)S(1)}, s32[1,384]{1,0:T(1,128)}, u32[]{:S(2)}) copy-start(s32[1,384]{1,0:T(1,128)} %param.20) | copy-start | bytes 4612
  305.4 86.2 %copy-start.6 = (bf16[1,192,2048]{2,1,0:T(8,128)(2,1)S(1)}, bf16[1,192,2048]{2,1,0:T(8,128)(2,1)}, u32[]{:S(2)}) copy-start(bf16[1,192,2048]{2,1,0:T(8,128)(2,1)} %param.19) | copy-start | bytes 2359300
  307.3 84.7 %all-to-all-start.2 = ((bf16[4,64,704]{2,1,0:T(8,128)(2,1)}), bf16[4,64,704]{2,1,0:T(8,128)(2,1)S(1)}, u32[]{:S(2)}, u32[]{:S(2)}) async-start(bf16[4,64,704]{2,1,0:T(8,128)(2,1)} %reshape.451), calls=%async_computation.2 | async-start | bytes 786432 | tf_op jit(solution)/shard_map/all_to_all | solution.py:196
  310.8 179.1 %all-gather.57.cloned.1.call-start = ((), (), s32[]{:S(2)}) async-start(), calls=%async_computation.62 | async-start | bytes 1966080 | tf_op jit(solution)/shard_map/all_gather | solution.py:204
  391.1 33.4 %copy-start.51 = (f32[2048]{0:T(1024)}, f32[2048]{0:T(1024)S(1)}, u32[]{:S(2)}) copy-start(f32[2048]{0:T(1024)S(1)} %reshape.474) | copy-start | bytes 24580
  391.4 52.9 %copy-start.67 = (f32[2048]{0:T(1024)}, f32[2048]{0:T(1024)S(1)}, u32[]{:S(2)}) copy-start(f32[2048]{0:T(1024)S(1)} %reshape.476) | copy-start | bytes 24580
  392.8 121.4 %all-gather.45.cloned.1.call-start = ((), (), s32[]{:S(2)}) async-start(), calls=%async_computation.39 | async-start | bytes 3932160 | tf_op jit(solution)/shard_map/all_gather | solution.py:292
  396.3 4.0 collective-permute-start
  398.8 33.6 %copy-start.53 = (f32[192,32]{0,1:T(8,128)}, f32[192,32]{0,1:T(8,128)S(1)}, u32[]{:S(2)}) copy-start(f32[192,32]{0,1:T(8,128)S(1)} %get-tuple-element.143) | copy-start | bytes 73732
  398.8 33.6 %copy-start.55 = (f32[192,32]{0,1:T(8,128)}, f32[192,32]{0,1:T(8,128)S(1)}, u32[]{:S(2)}) copy-start(f32[192,32]{0,1:T(8,128)S(1)} %get-tuple-element.144) | copy-start | bytes 73732
  398.8 34.3 %copy-start.57 = (bf16[192,32]{0,1:T(8,128)(2,1)}, bf16[192,32]{0,1:T(8,128)(2,1)S(1)}, u32[]{:S(2)}) copy-start(bf16[192,32]{0,1:T(8,128)(2,1)S(1)} %get-tuple-element.141) | copy-start | bytes 36868
  398.8 34.3 %copy-start.59 = (bf16[192,32]{0,1:T(8,128)(2,1)}, bf16[192,32]{0,1:T(8,128)(2,1)S(1)}, u32[]{:S(2)}) copy-start(bf16[192,32]{0,1:T(8,128)(2,1)S(1)} %get-tuple-element.142) | copy-start | bytes 36868
  398.9 34.2 %collective-permute-start.1 = (bf16[192,64]{0,1:T(8,128)(2,1)S(1)}, bf16[192,64]{0,1:T(8,128)(2,1)S(1)}, u32[]{:S(2)}, u32[]{:S(2)}) collective-permute-start(bf16[192,64]{0,1:T(8,128)(2,1)S(1)} %pad_maximum_fusion.7), channel_id=1, source_target_pairs={{0,16},{1,17},{2,18},{3,19},{4,20},{5,21},{6,22},{7,23},{8,24},{9,... | collective-permute-start | bytes 73736 | tf_op jit(solution)/shard_map/ppermute | solution.py:24
  446.5 132.8 %all-gather.61.cloned.1.call-start = ((), (), s32[]{:S(2)}) async-start(), calls=%async_computation.64 | async-start | bytes 1966080 | tf_op jit(solution)/shard_map/all_gather | solution.py:204
  473.3 178.7 %all-gather.65.cloned.1.call-start = ((), (), s32[]{:S(2)}) async-start(), calls=%async_computation.66 | async-start | bytes 3932160 | tf_op jit(solution)/shard_map/all_gather | solution.py:188
  473.9 194.4 %all-gather.51.cloned.1.call-start = ((), (), s32[]{:S(2)}) async-start(), calls=%async_computation.59 | async-start | bytes 8650752 | tf_op jit(solution)/shard_map/all_gather | solution.py:216
  474.6 212.2 %all-gather.53.cloned.1.call-start = ((), (), s32[]{:S(2)}) async-start(), calls=%async_computation.60 | async-start | bytes 8650752 | tf_op jit(solution)/shard_map/all_gather | solution.py:217
  475.2 230.2 %all-gather.55.cloned.1.call-start = ((), (), s32[]{:S(2)}) async-start(), calls=%async_computation.61 | async-start | bytes 8650752 | tf_op jit(solution)/shard_map/all_gather | solution.py:218
  475.8 271.0 %all-gather.47.cloned.1.call-start = ((), (), s32[]{:S(2)}) async-start(), calls=%async_computation.40 | async-start | bytes 1802240 | tf_op jit(solution)/shard_map/all_gather | solution.py:211
  476.4 320.0 %all-gather.59.cloned.1.call-start = ((), (), s32[]{:S(2)}) async-start(), calls=%async_computation.63 | async-start | bytes 4718592 | tf_op jit(solution)/shard_map/all_gather | solution.py:205
  520.0 140.2 %all-to-all-start = ((bf16[4,4,72,2048]{3,2,1,0:T(8,128)(2,1)}), bf16[4,4,72,2048]{3,2,1,0:T(8,128)(2,1)}, u32[]{:S(2)}, u32[]{:S(2)}) async-start(bf16[4,4,72,2048]{3,2,1,0:T(8,128)(2,1)} %bitcast.292), calls=%async_computation | async-start | bytes 9437184 | tf_op jit(solution)/shard_map/all_to_all | solution.py:232
  525.1 275.1 %all-gather.63.cloned.1.call-start = ((), (), s32[]{:S(2)}) async-start(), calls=%async_computation.65 | async-start | bytes 4718592 | tf_op jit(solution)/shard_map/all_gather | solution.py:205
  660.1 76.1 %copy-start.64 = (f32[4,192,16]{1,0,2:T(4,128)}, f32[4,192,16]{1,0,2:T(4,128)S(1)}, u32[]{:S(2)}) copy-start(f32[4,192,16]{1,0,2:T(4,128)S(1)} %reshape.443) | copy-start | bytes 147460
  660.2 59.2 %all-to-all-start.4 = ((bf16[4,4,72,2048]{3,2,1,0:T(8,128)(2,1)}), bf16[4,4,72,2048]{3,2,1,0:T(8,128)(2,1)}, u32[]{:S(2)}, u32[]{:S(2)}) async-start(bf16[4,4,72,2048]{3,2,1,0:T(8,128)(2,1)} %bitcast.293), calls=%async_computation.5 | async-start | bytes 9437184 | tf_op jit(solution)/shard_map/all_to_all | solution.py:232
  733.0 7.9 all-to-all-start.5
  743.3 7.9 all-to-all-start.6
  746.6 64.3 %all-gather.49.cloned.1.call-start = ((), (), s32[]{:S(2)}) async-start(), calls=%async_computation.41 | async-start | bytes 4325376 | tf_op jit(solution)/shard_map/all_gather | solution.py:210
  791.1 56.1 %all-to-all-start.7 = ((bf16[4,4,72,2048]{3,2,1,0:T(8,128)(2,1)}), bf16[4,4,72,2048]{3,2,1,0:T(8,128)(2,1)}, u32[]{:S(2)}, u32[]{:S(2)}) async-start(bf16[4,4,72,2048]{3,2,1,0:T(8,128)(2,1)} %bitcast.307), calls=%async_computation.9 | async-start | bytes 9437184 | tf_op jit(solution)/shard_map/all_to_all | solution.py:237
  796.1 159.8 %reduce-scatter.32.cloned.1.call-start = ((), (), s32[]{:S(2)}) async-start(), calls=%async_computation.43 | async-start | bytes 81920 | tf_op jit(solution)/shard_map/reduce_scatter | solution.py:394
  824.9 134.3 %reduce-scatter.34.cloned.1.call-start = ((), (), s32[]{:S(2)}) async-start(), calls=%async_computation.44 | async-start | bytes 3932160 | tf_op jit(solution)/shard_map/reduce_scatter | solution.py:380
  857.7 57.5 %all-to-all-start.1 = ((bf16[4,4,72,2048]{3,2,1,0:T(8,128)(2,1)}), bf16[4,4,72,2048]{3,2,1,0:T(8,128)(2,1)}, u32[]{:S(2)}, u32[]{:S(2)}) async-start(bf16[4,4,72,2048]{3,2,1,0:T(8,128)(2,1)} %bitcast.306), calls=%async_computation.1 | async-start | bytes 9437184 | tf_op jit(solution)/shard_map/all_to_all | solution.py:237
  862.7 121.3 %reduce-scatter.30.cloned.1.call-start = ((), (), s32[]{:S(2)}) async-start(), calls=%async_computation.42 | async-start | bytes 3932160 | tf_op jit(solution)/shard_map/reduce_scatter | solution.py:380
  924.6 151.0 %reduce-scatter.52.cloned.1.call-start = ((), (), s32[]{:S(2)}) async-start(), calls=%async_computation.53 | async-start | bytes 4718592 | tf_op jit(solution)/shard_map/reduce_scatter | solution.py:349
  938.3 138.0 %reduce-scatter.54.cloned.1.call-start = ((), (), s32[]{:S(2)}) async-start(), calls=%async_computation.54 | async-start | bytes 4718592 | tf_op jit(solution)/shard_map/reduce_scatter | solution.py:349
  948.6 128.4 %reduce-scatter.56.cloned.1.call-start = ((), (), s32[]{:S(2)}) async-start(), calls=%async_computation.55 | async-start | bytes 4325376 | tf_op jit(solution)/shard_map/reduce_scatter | solution.py:349
  955.8 162.3 %reduce-scatter.36.cloned.1.call-start = ((), (), s32[]{:S(2)}) async-start(), calls=%async_computation.45 | async-start | bytes 245760 | tf_op jit(solution)/shard_map/reduce_scatter | solution.py:122
  1012.5 28.8 %collective-permute-start.2 = (bf16[192,4096]{1,0:T(8,128)(2,1)}, bf16[192,4096]{1,0:T(8,128)(2,1)}, u32[]{:S(2)}, u32[]{:S(2)}) collective-permute-start(bf16[192,4096]{1,0:T(8,128)(2,1)} %copy.253), channel_id=1, source_target_pairs={{16,0},{17,1},{18,2},{19,3},{20,4},{21,5},{22,6},{23,7},{24,8},{25... | collective-permute-start | bytes 4718600 | tf_op jit(solution)/shard_map/ppermute | solution.py:24
  1020.2 19.9 %collective-permute-start.3 = (bf16[192,64]{0,1:T(8,128)(2,1)S(1)}, bf16[192,64]{0,1:T(8,128)(2,1)S(1)}, u32[]{:S(2)}, u32[]{:S(2)}) collective-permute-start(bf16[192,64]{0,1:T(8,128)(2,1)S(1)} %slice.185), channel_id=1, source_target_pairs={{16,0},{17,1},{18,2},{19,3},{20,4},{21,5},{22,6},{23,7},{24,8},{25... | collective-permute-start | bytes 73736 | tf_op jit(solution)/shard_map/ppermute | solution.py:24
  1051.3 67.4 %reduce-scatter.42.cloned.1.call-start = ((), (), s32[]{:S(2)}) async-start(), calls=%async_computation.48 | async-start | bytes 3538944 | tf_op jit(solution)/shard_map/reduce_scatter | solution.py:122
  1054.9 66.3 %reduce-scatter.44.cloned.1.call-start = ((), (), s32[]{:S(2)}) async-start(), calls=%async_computation.49 | async-start | bytes 6291456 | tf_op jit(solution)/shard_map/reduce_scatter | solution.py:122
  1060.1 61.7 %reduce-scatter.48.cloned.1.call-start = ((), (), s32[]{:S(2)}) async-start(), calls=%async_computation.51 | async-start | bytes 12582912 | tf_op jit(solution)/shard_map/reduce_scatter | solution.py:122
  1067.4 68.4 %reduce-scatter.38.cloned.1.call-start = ((), (), s32[]{:S(2)}) async-start(), calls=%async_computation.46 | async-start | bytes 18874368 | tf_op jit(solution)/shard_map/reduce_scatter | solution.py:122
  1075.5 95.7 %reduce-scatter.66.cloned.1.call-start = ((), (), s32[]{:S(2)}) async-start(), calls=%async_computation.69 | async-start | bytes 1966080
  1076.3 129.1 %reduce-scatter.68.cloned.1.call-start = ((), (), s32[]{:S(2)}) async-start(), calls=%async_computation.70 | async-start | bytes 1966080
  1077.0 161.6 %reduce-scatter.70.cloned.1.call-start = ((), (), s32[]{:S(2)}) async-start(), calls=%async_computation.71 | async-start | bytes 1802240
  1077.6 177.7 %reduce-scatter.58.cloned.1.call-start = ((), (), s32[]{:S(2)}) async-start(), calls=%async_computation.56 | async-start | bytes 8650752 | tf_op jit(solution)/shard_map/reduce_scatter | solution.py:326
  1090.4 183.0 %reduce-scatter.60.cloned.1.call-start = ((), (), s32[]{:S(2)}) async-start(), calls=%async_computation.57 | async-start | bytes 8650752 | tf_op jit(solution)/shard_map/reduce_scatter | solution.py:327
  1103.6 187.0 %reduce-scatter.62.cloned.1.call-start = ((), (), s32[]{:S(2)}) async-start(), calls=%async_computation.58 | async-start | bytes 8650752 | tf_op jit(solution)/shard_map/reduce_scatter | solution.py:328
  1118.0 283.2 %all-reduce.8.cloned.1.call-start = ((), (), s32[]{:S(2)}) async-start(), calls=%async_computation.68 | async-start | bytes 163840
  1118.6 363.4 %reduce-scatter.64.cloned.1.call-start = ((), (), s32[]{:S(2)}) async-start(), calls=%async_computation.67 | async-start | bytes 1392640
  1121.1 440.3 %reduce-scatter.46.cloned.1.call-start = ((), (), s32[]{:S(2)}) async-start(), calls=%async_computation.50 | async-start | bytes 2228224 | tf_op jit(solution)/shard_map/reduce_scatter | solution.py:123
  1121.7 534.6 %reduce-scatter.50.cloned.1.call-start = ((), (), s32[]{:S(2)}) async-start(), calls=%async_computation.52 | async-start | bytes 4456448 | tf_op jit(solution)/shard_map/reduce_scatter | solution.py:123
  1122.5 685.7 %reduce-scatter.40.cloned.1.call-start = ((), (), s32[]{:S(2)}) async-start(), calls=%async_computation.47 | async-start | bytes 6684672 | tf_op jit(solution)/shard_map/reduce_scatter | solution.py:123
  1171.2 34.2 %all-to-all-start.8 = ((bf16[4,64,704]{2,1,0:T(8,128)(2,1)}), bf16[4,64,704]{2,1,0:T(8,128)(2,1)S(1)}, u32[]{:S(2)}, u32[]{:S(2)}) async-start(bf16[4,64,704]{2,1,0:T(8,128)(2,1)} %bitcast.323), calls=%async_computation.20 | async-start | bytes 786432 | tf_op jit(solution)/shard_map/all_to_all | solution.py:358
  1205.4 39.7 %all-to-all-start.9 = ((bf16[4,64,704]{2,1,0:T(8,128)(2,1)}), bf16[4,64,704]{2,1,0:T(8,128)(2,1)}, u32[]{:S(2)}, u32[]{:S(2)}) async-start(bf16[4,64,704]{2,1,0:T(8,128)(2,1)} %bitcast.322), calls=%async_computation.22 | async-start | bytes 786432 | tf_op jit(solution)/shard_map/all_to_all | solution.py:358
  (101 other events, 516.7 us)
Sparse Core Ops, SparseCore 0:
  10.8 59.5 all-gather.28
  73.1 59.5 all-gather.32
  135.5 92.7 all-gather.36
  231.0 74.3 all-gather.40
  306.7 9.9 all-gather.30
  318.1 14.8 all-gather.34
  334.6 26.0 all-gather.38
  362.2 21.0 all-gather.42
  392.9 26.8 all-gather.56
  446.6 67.5 all-gather.44
  516.0 63.2 all-gather.60
  580.7 71.2 all-gather.64
  653.5 14.6 all-gather.50
  669.6 17.1 all-gather.52
  688.2 17.1 all-gather.54
  707.1 31.0 all-gather.46
  739.6 12.1 all-gather.58
  753.2 13.2 all-gather.62
  768.1 12.9 all-gather.48
  825.1 18.8 reduce-scatter.31
  857.8 59.2 reduce-scatter.33
  924.7 59.2 reduce-scatter.29
  986.3 10.9 reduce-scatter.51
  999.4 12.0 reduce-scatter.53
  1013.8 11.6 reduce-scatter.55
  1051.4 9.4 reduce-scatter.35
  1063.0 11.0 reduce-scatter.41
  1077.1 13.1 reduce-scatter.43
  1092.6 18.0 reduce-scatter.47
  1113.0 22.7 reduce-scatter.37
  1139.1 32.1 reduce-scatter.65
  1174.5 30.9 reduce-scatter.67
  1208.5 30.0 reduce-scatter.69
  1241.5 13.7 reduce-scatter.57
  1258.3 15.0 reduce-scatter.59
  1275.5 15.0 reduce-scatter.61
  1296.8 104.3 all-reduce.7
  1403.6 78.3 reduce-scatter.63
  1484.2 77.1 reduce-scatter.45
  1563.8 92.4 reduce-scatter.49
  1662.4 145.6 reduce-scatter.39

commit v2 on v1

--- a/solution.py
+++ b/solution.py
@@ -1,8 +1,11 @@
+import functools
 import math
 
 import jax
 import jax.numpy as jnp
 from jax import lax
+from jax.experimental import pallas as pl
+from jax.experimental.pallas import tpu as pltpu
 from jax.sharding import PartitionSpec as P
 
 D = 2048
@@ -104,6 +107,8 @@
 
 
 PLANE = 4
+MESH = pl.DeviceIdType.MESH
+MEBIBYTE = 1024 * 1024
 
 
 def groups(count):
@@ -113,14 +118,432 @@
     return plane, line
 
 
-def gather_all(value):
-    part = lax.all_gather(value, "expert", axis=0, tiled=True)
-    return lax.all_gather(part, "fsdp", axis=0, tiled=True)
-
-
-def scatter_all(value):
-    part = lax.psum_scatter(value, "fsdp", scatter_dimension=0, tiled=True)
-    return lax.psum_scatter(part, "expert", scatter_dimension=0, tiled=True)
+def remote(source, target, send, receive, where):
+    return pltpu.make_async_remote_copy(
+        src_ref=source,
+        dst_ref=target,
+        send_sem=send,
+        recv_sem=receive,
+        device_id=where,
+        device_id_type=MESH,
+    )
+
+
+def plane_mates(place):
+    spot = place % PLANE
+    return (place + 1 - 2 * (spot % 2), place + 2 - 4 * (spot // 2))
+
+
+def greet_neighbours(half, place, depth):
+    barrier = pltpu.get_barrier_semaphore()
+    level = place // PLANE
+
+    def greet(where):
+        pl.semaphore_signal(barrier, inc=1, device_id=where, device_id_type=MESH)
+
+    for mate in plane_mates(place):
+        greet((half, mate))
+    greet((1 - half, place))
+
+    @pl.when(level > 0)
+    def _():
+        greet((half, place - PLANE))
+
+    @pl.when(level < depth - 1)
+    def _():
+        greet((half, place + PLANE))
+
+    pl.semaphore_wait(
+        barrier, 3 + jnp.where(level > 0, 1, 0) + jnp.where(level < depth - 1, 1, 0)
+    )
+
+
+def gather_kernel(depth, cut, in_ref, out_ref, own_sem, zs, zr, ps, pr, qs, qr, cs, cr):
+    half = lax.axis_index("fsdp")
+    place = lax.axis_index("expert")
+    level = place // PLANE
+    spot = place % PLANE
+    total = depth * PLANE
+    mates = plane_mates(place)
+    rows, width = in_ref.shape
+    columns = (pl.ds(0, cut), pl.ds(cut, width - cut))
+    greet_neighbours(half, place, depth)
+
+    def at(which, block, count=1):
+        start = pl.multiple_of((half * total + block) * rows, rows)
+        return out_ref.at[pl.ds(start, count * rows), columns[which]]
+
+    def along(which, way, source, own=False):
+        target = at(which, source * PLANE + spot)
+        start = in_ref.at[:, columns[which]] if own else target
+        return remote(
+            start,
+            target,
+            zs.at[which, way, source],
+            zr.at[which, source],
+            (half, place + (2 * way - 1) * PLANE),
+        )
+
+    def plane_one(which, source, own=False):
+        target = at(which, source * PLANE + spot)
+        start = in_ref.at[:, columns[which]] if own else target
+        return remote(
+            start, target, ps.at[which, source], pr.at[which, source], (half, mates[which])
+        )
+
+    def plane_two(which, source, turn):
+        base = source * PLANE
+        if which == 0:
+            block = at(0, base + spot - spot % 2, 2)
+        else:
+            block = at(1, base + (spot + 2 * turn) % PLANE)
+        slot = which + turn
+        return remote(
+            block, block, qs.at[slot, source], qr.at[slot, source], (half, mates[1 - which])
+        )
+
+    def core(which, source):
+        block = at(which, source * PLANE, PLANE)
+        return remote(
+            block, block, cs.at[which, source], cr.at[which, source], (1 - half, place)
+        )
+
+    seconds = ((0, 0), (1, 0), (1, 1))
+
+    def own_copy(which):
+        return pltpu.make_async_copy(
+            in_ref.at[:, columns[which]], at(which, place), own_sem.at[which]
+        )
+
+    for which in range(2):
+
+        @pl.when(level > 0)
+        def _():
+            along(which, 0, level, True).start()
+
+        @pl.when(level < depth - 1)
+        def _():
+            along(which, 1, level, True).start()
+
+        plane_one(which, level, True).start()
+        own_copy(which).start()
+    for which in range(2):
+        own_copy(which).wait()
+
+    def visit(step, act):
+        if step == 0:
+            act(level, None)
+            return
+
+        @pl.when(level - step >= 0)
+        def _():
+            act(level - step, 1)
+
+        @pl.when(level + step < depth)
+        def _():
+            act(level + step, 0)
+
+    def arrive(source, way):
+        for which in range(2):
+            along(which, way, source).wait_recv()
+
+            @pl.when((level < depth - 1) if way == 1 else (level > 0))
+            def _():
+                along(which, way, source).start()
+
+            plane_one(which, source).start()
+
+    def spread(source, way):
+        for which in range(2):
+            plane_one(which, source).wait_recv()
+            for kind, turn in seconds:
+                if kind == which:
+                    plane_two(kind, source, turn).start()
+
+    def share(source, way):
+        for which in range(2):
+            for kind, turn in seconds:
+                if kind == which:
+                    plane_two(kind, source, turn).wait_recv()
+            core(which, source).start()
+
+    for step in range(depth + 2):
+        if 1 <= step <= depth:
+            visit(step - 1, spread)
+        if 1 <= step < depth:
+            visit(step, arrive)
+        if step >= 2:
+            visit(step - 2, share)
+
+    def finish(source, carry):
+        for which in range(2):
+            core(which, source).wait_recv()
+            core(which, source).wait_send()
+            plane_one(which, source).wait_send()
+
+            @pl.when((source <= level) & (level < depth - 1))
+            def _():
+                along(which, 1, source).wait_send()
+
+            @pl.when((source >= level) & (level > 0))
+            def _():
+                along(which, 0, source).wait_send()
+
+        for kind, turn in seconds:
+            plane_two(kind, source, turn).wait_send()
+        return carry
+
+    lax.fori_loop(0, depth, finish, 0)
+
+
+def gather_rows(value, cut):
+    rows, width = value.shape
+    total = lax.axis_size("expert")
+    depth = total // PLANE
+    semaphores = pltpu.SemaphoreType.DMA
+    return pl.pallas_call(
+        functools.partial(gather_kernel, depth, cut),
+        out_shape=jax.ShapeDtypeStruct((2 * total * rows, width), value.dtype),
+        in_specs=[pl.BlockSpec(memory_space=pl.ANY)],
+        out_specs=pl.BlockSpec(memory_space=pl.ANY),
+        scratch_shapes=[
+            semaphores((2,)),
+            semaphores((2, 2, depth)),
+            semaphores((2, depth)),
+            semaphores((2, depth)),
+            semaphores((2, depth)),
+            semaphores((3, depth)),
+            semaphores((3, depth)),
+            semaphores((2, depth)),
+            semaphores((2, depth)),
+        ],
+        compiler_params=pltpu.CompilerParams(collective_id=1, has_side_effects=True),
+    )(value)
+
+
+def reduce_kernel(depth, count, cut, *refs):
+    parts = refs[:count]
+    out_ref = refs[count]
+    acc, inc, one_a, one_b, two_a, two_b, zin = refs[count + 1 : count + 8]
+    own_sem, cs, cr, ps, pr, qs, qr, zs, zr = refs[count + 8 :]
+    half = lax.axis_index("fsdp")
+    place = lax.axis_index("expert")
+    level = place // PLANE
+    spot = place % PLANE
+    total = depth * PLANE
+    mates = plane_mates(place)
+    rows = out_ref.shape[0]
+    group = PLANE * rows
+    width = out_ref.shape[1]
+    greet_neighbours(half, place, depth)
+
+    starts = [sum(part.shape[1] for part in parts[:k]) for k in range(count)]
+
+    def rows_of(k, owner, t):
+        start = pl.multiple_of((owner * total + t * PLANE) * rows, group)
+        return parts[k].at[pl.ds(start, group), :]
+
+    def kept(k, t):
+        return pltpu.make_async_copy(
+            rows_of(k, half, t),
+            acc.at[t, :, pl.ds(starts[k], parts[k].shape[1])],
+            own_sem.at[k, t],
+        )
+
+    def given(k, t):
+        return remote(
+            rows_of(k, 1 - half, t),
+            inc.at[t, :, pl.ds(starts[k], parts[k].shape[1])],
+            cs.at[k, t],
+            cr.at[k, t],
+            (1 - half, place),
+        )
+
+    def block(t, q, n, lo, hi):
+        return acc.at[t, pl.ds(pl.multiple_of(q * rows, rows), n * rows), pl.ds(lo, hi - lo)]
+
+    pair = spot - spot % 2
+
+    def first(t, turn):
+        low = spot % 2
+        if turn == 0:
+            source = block(t, 2 - pair, 2, 0, cut)
+            target, where = one_a.at[t], mates[1]
+        else:
+            source = block(t, 2 * turn - 1 - low, 1, cut, width)
+            target, where = one_b.at[t, turn - 1], mates[0]
+        return remote(source, target, ps.at[turn, t], pr.at[turn, t], (half, where))
+
+    def second(t, turn):
+        if turn == 0:
+            source = block(t, pair + 1 - spot % 2, 1, 0, cut)
+            target, where = two_a.at[t], mates[0]
+        else:
+            source = block(t, (spot + 2) % PLANE, 1, cut, width)
+            target, where = two_b.at[t], mates[1]
+        return remote(source, target, qs.at[turn, t], qr.at[turn, t], (half, where))
+
+    def line(t, way):
+        step = 2 * way - 1
+        return remote(
+            block(t, spot, 1, 0, width),
+            zin.at[way, t],
+            zs.at[way, t],
+            zr.at[way, t],
+            (half, place + step * PLANE),
+        )
+
+    def add_rows(t, start, n, lo, hi, piece):
+        def one(i, carry):
+            r = pl.multiple_of(i * 16, 16)
+            at = (t, pl.ds(pl.multiple_of(start + r, 16), 16), pl.ds(lo, hi - lo))
+            new = piece(pl.ds(r, 16)).astype(jnp.float32)
+            acc[at] = (acc[at].astype(jnp.float32) + new).astype(acc.dtype)
+            return carry
+
+        lax.fori_loop(0, n // 16, one, 0)
+
+    def stage_a(t):
+        for k in range(count):
+            kept(k, t).wait()
+            given(k, t).wait_recv()
+        add_rows(t, 0, group, 0, width, lambda r: inc[t, r, :])
+        for turn in range(3):
+            first(t, turn).start()
+
+    def stage_b(t):
+        first(t, 0).wait_recv()
+        add_rows(t, pair * rows, 2 * rows, 0, cut, lambda r: one_a[t, r, :])
+        second(t, 0).start()
+        for turn in range(2):
+            first(t, 1 + turn).wait_recv()
+            add_rows(
+                t,
+                (spot % 2 + 2 * turn) * rows,
+                rows,
+                cut,
+                width,
+                lambda r: one_b[t, turn, r, :],
+            )
+        second(t, 1).start()
+
+    def stage_c(t):
+        second(t, 0).wait_recv()
+        add_rows(t, spot * rows, rows, 0, cut, lambda r: two_a[t, r, :])
+        second(t, 1).wait_recv()
+        add_rows(t, spot * rows, rows, cut, width, lambda r: two_b[t, r, :])
+
+        def take(way):
+            line(t, way).wait_recv()
+            add_rows(t, spot * rows, rows, 0, width, lambda r: zin[way, t, r, :])
+
+        @pl.when((t >= level) & (level > 0))
+        def _():
+            take(1)
+
+        @pl.when((t <= level) & (level < depth - 1))
+        def _():
+            take(0)
+
+        @pl.when(t > level)
+        def _():
+            line(t, 1).start()
+
+        @pl.when(t < level)
+        def _():
+            line(t, 0).start()
+
+    def visit(index, act):
+        if index >= depth or index < 0:
+            return
+        step = depth - 1 - index
+        if step == 0:
+            act(level)
+            return
+
+        @pl.when(level + step < depth)
+        def _():
+            act(level + step)
+
+        @pl.when(level - step >= 0)
+        def _():
+            act(level - step)
+
+    def begin(t):
+        for k in range(count):
+            given(k, t).start()
+            kept(k, t).start()
+
+    for index in range(depth):
+        visit(index, begin)
+    for index in range(depth + 2):
+        visit(index, stage_a)
+        visit(index - 1, stage_b)
+        visit(index - 2, stage_c)
+
+    def emit(i, carry):
+        r = pl.multiple_of(i * 16, 16)
+        at = pl.ds(pl.multiple_of(spot * rows + r, 16), 16)
+        out_ref[pl.ds(r, 16), :] = acc[level, at, :].astype(out_ref.dtype)
+        return carry
+    lax.fori_loop(0, rows // 16, emit, 0)
+
+    def finish(t, carry):
+        for k in range(count):
+            given(k, t).wait_send()
+        for turn in range(3):
+            first(t, turn).wait_send()
+        for turn in range(2):
+            second(t, turn).wait_send()
+
+        @pl.when(t > level)
+        def _():
+            line(t, 1).wait_send()
+
+        @pl.when(t < level)
+        def _():
+            line(t, 0).wait_send()
+        return carry
+
+    lax.fori_loop(0, depth, finish, 0)
+
+
+def reduce_rows(parts, cut):
+    total = lax.axis_size("expert")
+    depth = total // PLANE
+    rows = parts[0].shape[0] // (2 * total)
+    width = sum(part.shape[1] for part in parts)
+    group = PLANE * rows
+    n = len(parts)
+    semaphores = pltpu.SemaphoreType.DMA
+    low = parts[0].dtype
+    return pl.pallas_call(
+        functools.partial(reduce_kernel, depth, n, cut),
+        out_shape=jax.ShapeDtypeStruct((rows, width), jnp.float32),
+        in_specs=[pl.BlockSpec(memory_space=pl.ANY)] * n,
+        out_specs=pl.BlockSpec(memory_space=pltpu.VMEM),
+        scratch_shapes=[
+            pltpu.VMEM((depth, group, width), low),
+            pltpu.VMEM((depth, group, width), low),
+            pltpu.VMEM((depth, 2 * rows, cut), low),
+            pltpu.VMEM((depth, 2, rows, width - cut), low),
+            pltpu.VMEM((depth, rows, cut), low),
+            pltpu.VMEM((depth, rows, width - cut), low),
+            pltpu.VMEM((2, depth, rows, width), low),
+            semaphores((n, depth)),
+            semaphores((n, depth)),
+            semaphores((n, depth)),
+            semaphores((3, depth)),
+            semaphores((3, depth)),
+            semaphores((2, depth)),
+            semaphores((2, depth)),
+            semaphores((2, depth)),
+            semaphores((2, depth)),
+        ],
+        compiler_params=pltpu.CompilerParams(
+            collective_id=2, has_side_effects=True, vmem_limit_bytes=48 * MEBIBYTE
+        ),
+    )(*parts)
 
 
 def body(
@@ -155,12 +578,10 @@
     line_rows = depth * row_count
     inputs = tokens[0].astype(jnp.float32)
 
+    part_rows = query_weight.shape[0]
     gain_width = attention_norm.shape[0]
     latent_width = latent_norm.shape[0]
-    small = jnp.concatenate(
-        [attention_norm, latent_norm, feed_norm, router_weight.reshape(-1)]
-    )
-    small_full = gather_all(small[None])
+    small = jnp.concatenate([attention_norm, latent_norm, feed_norm, router_weight.reshape(-1)])
     cuts = [
         0,
         gain_width,
@@ -168,16 +589,32 @@
         2 * gain_width + latent_width,
         small.shape[0],
     ]
+    small = jnp.pad(small, (0, 128 * part_rows - small.shape[0])).reshape(part_rows, 128)
+    query_width = query_weight.shape[1]
+    down_width = latent_down.shape[1]
+    entry_width = query_width + down_width + (-down_width) % 128
+    up_width = HEADS * (NOPE + VALUE)
+    packed = jnp.concatenate(
+        [
+            query_weight,
+            jnp.pad(latent_down, ((0, 0), (0, (-down_width) % 128))),
+            latent_up.reshape(part_rows, -1),
+            small,
+        ],
+        axis=1,
+    )
+    cut = packed.shape[1] // 256 * 128
+    packed_full = gather_rows(packed, cut)
+    output_full = lax.all_gather(output_weight, ("fsdp", "expert"), axis=0, tiled=True)
+    entry_full = packed_full[:, :entry_width]
+    up_full = packed_full[:, entry_width:-128].reshape(-1, up_width)
+    small_full = packed_full[:, -128:].reshape(2 * expert_total, -1)
     gain_one, gain_latent, gain_feed, router_full = (
         small_full[:, cuts[0] : cuts[1]].reshape(-1),
         small_full[:, cuts[1] : cuts[2]].reshape(-1),
         small_full[:, cuts[2] : cuts[3]].reshape(-1),
         small_full[:, cuts[3] : cuts[4]].reshape(-1, expert_total),
     )
-    down_full = gather_all(latent_down)
-    query_full = gather_all(query_weight)
-    up_full = gather_all(latent_up)
-    output_full = gather_all(output_weight)
 
     route_rows = routes[0]
     slot_rows = slot_index[0]
@@ -249,7 +686,8 @@
     score_scale = (NOPE + ROPE) ** (-0.5)
     gain_first = gain_one.astype(jnp.float32)
     normed_low = norm_rows(inputs, gain_first).astype(jnp.bfloat16)
-    query_raw = matmul(normed_low, query_full).reshape(row_count, HEADS, NOPE + ROPE)
+    entry = matmul(normed_low, entry_full)
+    query_raw = entry[:, :query_width].reshape(row_count, HEADS, NOPE + ROPE)
     queries = jnp.concatenate(
         [
             query_raw[..., :NOPE],
@@ -257,7 +695,7 @@
         ],
         axis=-1,
     ).astype(jnp.bfloat16)
-    compressed = matmul(normed_low, down_full)
+    compressed = entry[:, query_width : query_width + down_width]
     latent_gain = gain_latent.astype(jnp.float32)
     latent = norm_rows(compressed[:, :LATENT], latent_gain).astype(jnp.bfloat16)
     key_rope = rotate_forward(compressed[:, LATENT:], cosine, sine_table).astype(jnp.bfloat16)
@@ -474,9 +912,11 @@
         .reshape(row_count, HEADS * (NOPE + ROPE))
         .astype(jnp.bfloat16)
     )
-    normed_grad = right_matmul(query_low, query_full) + right_matmul(compressed_low, down_full)
-    query_weight_grad = left_matmul(normed_low, query_low)
-    down_weight_grad = left_matmul(normed_low, compressed_low)
+    entry_low = jnp.concatenate(
+        [query_low, jnp.pad(compressed_low, ((0, 0), (0, (-down_width) % 128)))], axis=1
+    )
+    normed_grad = right_matmul(entry_low, entry_full)
+    entry_grad = left_matmul(normed_low, entry_low).astype(jnp.bfloat16)
     input_add, first_gain_grad = norm_back(inputs, gain_first, normed_grad)
     token_grad = residual_grad + input_add
     small_grad = jnp.concatenate(
@@ -488,20 +928,29 @@
         ],
         axis=1,
     )
-    small_piece = scatter_all(small_grad)[0]
-
-    def shard(value):
-        return scatter_all(value.astype(jnp.bfloat16)).astype(jnp.float32)
+    small_grad = jnp.pad(small_grad, ((0, 0), (0, 128 * part_rows - small_grad.shape[1])))
+    packed_piece = reduce_rows(
+        [
+            entry_grad,
+            up_weight_grad.astype(jnp.bfloat16).reshape(gain_width * 2 * expert_total, -1),
+            small_grad.astype(jnp.bfloat16).reshape(-1, 128),
+        ],
+        cut,
+    )
+    small_piece = packed_piece[:, -128:].reshape(-1)
+    output_piece = lax.psum_scatter(
+        output_grad.astype(jnp.bfloat16), ("fsdp", "expert"), scatter_dimension=0, tiled=True
+    ).astype(jnp.float32)
 
     return (
         output[None],
         token_grad[None],
         small_piece[cuts[0] : cuts[1]],
-        shard(query_weight_grad),
-        shard(down_weight_grad),
+        packed_piece[:, :query_width],
+        packed_piece[:, query_width : query_width + down_width],
         small_piece[cuts[1] : cuts[2]],
-        shard(up_weight_grad),
-        shard(output_grad),
+        packed_piece[:, entry_width:-128].reshape(latent_up.shape),
+        output_piece,
         small_piece[cuts[2] : cuts[3]],
         small_piece[cuts[3] : cuts[4]].reshape(gain_width, expert_total),
         sgate_piece,

time: 1820 us -> 1260 us (0.69)
  waiting for transfers between devices: 1220 us -> 413 us
  Pallas kernels: 0 us -> 305 us
  blocking collectives: 117 us -> 45.4 us
    reduce_scatter x8 -> x1, waiting for transfers between devices: 334 us -> 18.2 us  [body(): lax.psum_scatter(output_grad.astype(jnp.bfloat16), ('fsdp', 'expert'), sc...]
    pallas_call x0 -> x2, Pallas kernels: none -> 305 us  [the longest x1 182 us: reduce_rows(): pl.pallas_call(functools.partial(reduce_kernel, depth, n, cut), out_shape...]
    all_gather x8 -> x1, waiting for transfers between devices: 295 us -> 0.02 us  [body(): lax.all_gather(output_weight, ('fsdp', 'expert'), axis=0, tiled=True)]
    unnamed x46 -> x28, waiting for transfers between devices: 283 us -> 86.9 us
    unnamed x1 -> x0, blocking collectives: 76.3 us -> none
    all_gather x2, waiting for transfers between devices: 51.7 us -> 0.02 us  [columns_to_levels(): across = lax.all_gather(moved, 'expert', axis_index_groups=plane, axis=0)]
    all_to_all x2, waiting for transfers between devices: 14 us -> 55.2 us  [to_experts(): lax.all_to_all(placed, 'expert', split_axis=0, concat_axis=0, axis_index_...]
    all_gather x1, waiting for transfers between devices: 23.3 us -> 62.4 us  [body(): lax.all_gather(mixed_low, 'expert', axis_index_groups=line, axis=0, tiled...]
  transfers between devices with their start and end apart: 54 -> 37, of which waited for: 28 -> 14; matrix products, arithmetic and copies ran while one was open for 22% -> 33% of each run, Pallas kernels for 0% -> 24%
where the time goes in v2:
time: 1260 us; the launch traced here: 1250 us
  waiting for transfers between devices  413 us (33%)
  Pallas kernels  305 us (24%)
  matrix products  255 us (20%)
  local copies, waits for them, and re-layouts  118 us (9%)
  other arithmetic  49.9 us (4%)
  starting transfers between devices  45.6 us (4%)
  blocking collectives  45.4 us (4%)
  between operations  16.3 us (1%)
    pallas_call x1, Pallas kernels, reduce_rows(): pl.pallas_call(functools.partial(reduce_kernel, depth, n, cut), out_shape...  182 us
    pallas_call x1, Pallas kernels, gather_rows(): pl.pallas_call(functools.partial(gather_kernel, depth, cut), out_shape=ja...  122 us
    all_to_all x4, waiting for transfers between devices, from_experts(): lax.all_to_all(rows.reshape(PLANE, depth, capacity, -1), 'expert', split_...  101 us
    unnamed x28, waiting for transfers between devices  86.9 us
    dot_general x10, matrix products, right_matmul(): lax.dot_general(former, latter, (((1,), (1,)), ((), ())), preferred_eleme...  86.4 us
    dot_general x10, matrix products, matmul(): return jnp.dot(former, latter, preferred_element_type=jnp.float32)  73.3 us
    dot_general x10, matrix products, left_matmul(): lax.dot_general(former, latter, (((0,), (0,)), ((), ())), preferred_eleme...  73.3 us
    all_gather x1, waiting for transfers between devices, body(): lax.all_gather(mixed_low, 'expert', axis_index_groups=line, axis=0, tiled...  62.4 us
  transfers between devices with their start and end apart: 37, of which 14 were waited for; matrix products, arithmetic and copies ran while one was open for 33% of the time, Pallas kernels for 24%

profile of v2, /device:TPU:0, one launch (start us, length us, event | category | flops | bytes accessed | tf_op | source)
XLA Modules:
  0.0 1248.0 jit_solution(8548697857199645337)
XLA Ops:
  9.5 17.9 %all_to_all.50 = bf16[4,64,704]{2,1,0:T(8,128)(2,1)} all-to-all(bf16[4,64,704]{2,1,0:T(8,128)(2,1)S(1)} %reshape.445), channel_id=1, replica_groups={{0,4,8,12},{1,5,9,13},{2,6,10,14},{3,7,11,15},{16,20,24,28},{17,21,25,2..., dimensions={0} | all-to-all | bytes 720896 | tf_op jit(solution)/shard_map/all_to_all | solution.py:633
  28.6 13.9 %all_to_all.51 = bf16[4,64,704]{2,1,0:T(8,128)(2,1)} all-to-all(bf16[4,64,704]{2,1,0:T(8,128)(2,1)S(1)} %reshape.448), channel_id=1, replica_groups={{0,4,8,12},{1,5,9,13},{2,6,10,14},{3,7,11,15},{16,20,24,28},{17,21,25,2..., dimensions={0} | all-to-all | bytes 720896 | tf_op jit(solution)/shard_map/all_to_all | solution.py:633
  45.2 122.4 %shard_map.306 = bf16[2048,4864]{1,0:T(8,128)(2,1)} custom-call(bf16[64,4864]{1,0:T(8,128)(2,1)} %fusion.70.in_ref), custom_call_target="tpu_custom_call" | custom-call | tf_op jit(solution)/shard_map/pallas_call | solution.py:304
  170.2 7.5 fusion.2
  188.2 4.7 slice.131
  194.6 7.5 reshape.433
  212.1 4.2 convolution_convert_fusion.7
  227.8 5.6 multiply_reduce_fusion.4
  239.3 3.9 copy.235
  243.2 10.6 all-gather.41.cloned.1.call-done
  253.8 3.9 copy.237
  257.7 62.4 %all-gather.23.cloned.1.call-done = bf16[768,2048]{1,0:T(8,128)(2,1)} async-done(((bf16[192,2048]{1,0:T(8,128)(2,1)}), bf16[768,2048]{1,0:T(8,128)(2,1)}) %all-gather.23.cloned.1.call-update) | async-done | bytes 3145744 | tf_op jit(solution)/shard_map/all_gather | solution.py:730
  320.0 6.8 fusion.126
  326.8 3.9 fusion.127
  330.7 53.1 %all-gather.43.cloned.1.call-done = bf16[1,768,2048]{2,1,0:T(8,128)(2,1)} async-done(((bf16[1,192,2048]{2,1,0:T(8,128)(2,1)}), bf16[1,768,2048]{2,1,0:T(8,128)(2,1)}) %all-gather.43.cloned.1.call-update) | async-done | bytes 3145744 | tf_op jit(solution)/shard_map/all_gather | solution.py:625
  383.8 12.0 all-gather.27.cloned.1.call-done
  395.8 8.6 multiply_convert_fusion.5
  405.3 4.0 convolution_convert_fusion.11
  409.3 4.6 copy.254
  418.5 13.6 %all_gather.53 = s32[4,192,6]{1,2,0:T(8,128)S(1)} all-gather(s32[1,192,6]{1,2,0:T(8,128)S(1)} %fusion.106), channel_id=1, replica_groups={{0,4,8,12},{1,5,9,13},{2,6,10,14},{3,7,11,15},{16,20,24,28},{17,21,25,2..., dimensions={0}, use_global_device_ids=true | all-gather | bytes 23040 | tf_op jit(solution)/shard_map/all_gather | solution.py:624
  437.1 5.0 all-to-all-start
  452.8 5.3 convolution_convert_fusion.10
  463.2 29.7 %all-to-all-done = bf16[4,4,72,2048]{3,2,1,0:T(8,128)(2,1)} async-done(((bf16[4,4,72,2048]{3,2,1,0:T(8,128)(2,1)}), bf16[4,4,72,2048]{3,2,1,0:T(8,128)(2,1)}, u32[]{:S(2)}, u32[]{:S(2)}) %all-to-all-start) | async-done | bytes 4718624 | tf_op jit(solution)/shard_map/all_to_all | solution.py:669
  492.9 5.3 all-to-all-start.4
  498.3 12.7 %fusion.17 = f32[1152,1408]{1,0:T(8,128)} fusion(bf16[1152,2048]{1,0:T(8,128)(2,1)} %bitcast.12, bf16[1,2048,1408]{2,1,0:T(8,128)(2,1)} %all-gather.29.cloned.1.call-done), kind=kOutput, calls=%fused_computation.37 | convolution fusion | flops 6643777536 | bytes 16973824 | tf_op jit(solution)/shard_map/dot_general | solution.py:81
  510.9 14.3 %multiply_convert_fusion.2 = (bf16[1152,1408]{1,0:T(8,128)(2,1)}, f32[1152,1408]{1,0:T(8,128)}) fusion(f32[1152,1408]{1,0:T(8,128)} %fusion.17, bf16[1152,2048]{1,0:T(8,128)(2,1)} %bitcast.12, bf16[1,2048,1408]{2,1,0:T(8,128)(2,1)} %all-gather.31.cloned.1.call-done), kind=kOutput, calls=%fused_computation.20 | convolution fusion | flops 6653509632 | bytes 26705920 | tf_op jit(solution)/shard_map/dot_general | solution.py:81
  525.2 25.5 %all-to-all-done.4 = bf16[4,4,72,2048]{3,2,1,0:T(8,128)(2,1)} async-done(((bf16[4,4,72,2048]{3,2,1,0:T(8,128)(2,1)}), bf16[4,4,72,2048]{3,2,1,0:T(8,128)(2,1)}, u32[]{:S(2)}, u32[]{:S(2)}) %all-to-all-start.4) | async-done | bytes 4718624 | tf_op jit(solution)/shard_map/all_to_all | solution.py:669
  550.7 13.0 %multiply_reduce_fusion = (f32[1152]{0:T(1024)S(1)}, bf16[1152,2048]{1,0:T(8,128)(2,1)}) fusion(bf16[4,4,72,2048]{3,2,1,0:T(8,128)(2,1)} %all-to-all-done.4, bf16[1152,1408]{1,0:T(8,128)(2,1)} %get-tuple-element.139, bf16[1,1408,2048]{2,1,0:T(8,128)(2,1)} %all-gather.33.cloned.1.call-done), kind=kOutput, calls=%fused_computation.8 | convolution fusion | flops 6655572992 | bytes 18452992 | tf_op jit(solution)/shard_map/dot_general | solution.py:81
  567.7 4.6 all-to-all-done.5
  578.1 5.3 convolution_convert_fusion.12
  583.5 17.6 %multiply_convert_fusion.1 = (bf16[1152,1408]{1,0:T(8,128)(2,1)S(1)}, bf16[1152,1408]{1,0:T(8,128)(2,1)}) fusion(f32[1152,1408]{1,0:T(8,128)} %fusion.17, f32[1152,1408]{1,0:T(8,128)} %get-tuple-element.140, f32[1152]{0:T(1024)S(1)} %mul.512, bf16[1152,2048]{1,0:T(8,128)(2,1)} %bitcast.36, bf16[1,1408,2048]{2,1,0:T(8,128)(2,1)} %all-gather.33.cloned.1.call-done), kind=kOutput, calls=%fused_computation.19 | convolution fusion | flops 6668107776 | bytes 29954560 | tf_op jit(solution)/shard_map/dot_general | solution.py:91
  601.1 10.7 fusion.15
  611.8 11.9 add_convert_fusion
  623.7 5.3 all-to-all-start.7
  629.0 6.0 fusion.129
  635.7 44.6 %all-to-all-done.7 = bf16[4,4,72,2048]{3,2,1,0:T(8,128)(2,1)} async-done(((bf16[4,4,72,2048]{3,2,1,0:T(8,128)(2,1)}), bf16[4,4,72,2048]{3,2,1,0:T(8,128)(2,1)}, u32[]{:S(2)}, u32[]{:S(2)}) %all-to-all-start.7) | async-done | bytes 4718624 | tf_op jit(solution)/shard_map/all_to_all | solution.py:674
  686.1 4.8 fusion.8
  690.9 5.0 all-to-all-start.1
  696.1 52.3 %all-to-all-done.1 = bf16[4,4,72,2048]{3,2,1,0:T(8,128)(2,1)} async-done(((bf16[4,4,72,2048]{3,2,1,0:T(8,128)(2,1)}), bf16[4,4,72,2048]{3,2,1,0:T(8,128)(2,1)}, u32[]{:S(2)}, u32[]{:S(2)}) %all-to-all-start.1) | async-done | bytes 4718624 | tf_op jit(solution)/shard_map/all_to_all | solution.py:674
  753.1 4.5 fusion.9
  759.8 12.3 convolution_convert_fusion.3
  774.0 12.8 %convolution_convert_fusion.2 = bf16[2048,1408]{1,0:T(8,128)(2,1)} fusion(bf16[1152,2048]{1,0:T(8,128)(2,1)} %bitcast.12, bf16[1152,1408]{1,0:T(8,128)(2,1)S(1)} %copy-done.90), kind=kOutput, calls=%fused_computation.10 | convolution fusion | flops 6646661120 | bytes 13729792 | tf_op jit(solution)/shard_map/dot_general | solution.py:85
  788.7 11.5 convolution_convert_fusion.1
  804.9 13.2 %reduce-scatter.20.cloned.1.call-done = bf16[192,2048]{1,0:T(8,128)(2,1)} async-done(((bf16[768,2048]{1,0:T(8,128)(2,1)}), bf16[192,2048]{1,0:T(8,128)(2,1)}) %reduce-scatter.20.cloned.1.call-update) | async-done | bytes 786448 | tf_op jit(solution)/shard_map/reduce_scatter | solution.py:818
  821.4 5.7 convolution_convert_fusion.5
  827.2 24.9 %reduce-scatter.40.cloned.1.call-done = bf16[1,4,64,704]{3,2,1,0:T(8,128)(2,1)} async-done(((bf16[4,4,64,704]{3,2,1,0:T(8,128)(2,1)}), bf16[1,4,64,704]{3,2,1,0:T(8,128)(2,1)}) %reduce-scatter.40.cloned.1.call-update) | async-done | bytes 360464
  852.0 4.6 all-to-all-start.8
  856.6 29.2 %reduce-scatter.42.cloned.1.call-done = bf16[1,4,64,704]{3,2,1,0:T(8,128)(2,1)} async-done(((bf16[4,4,64,704]{3,2,1,0:T(8,128)(2,1)}), bf16[1,4,64,704]{3,2,1,0:T(8,128)(2,1)}) %reduce-scatter.42.cloned.1.call-update) | async-done | bytes 360464
  885.8 4.8 all-to-all-start.9
  892.5 26.5 %reduce-scatter.44.cloned.1.call-done = bf16[88,2048]{1,0:T(8,128)(2,1)} async-done(((bf16[352,2048]{1,0:T(8,128)(2,1)}), bf16[88,2048]{1,0:T(8,128)(2,1)}) %reduce-scatter.44.cloned.1.call-update) | async-done | bytes 360464
  926.0 7.4 fusion.51
  943.8 4.1 copy.249
  953.1 5.6 fusion.21
  965.6 3.9 copy.247
  974.0 4.8 convolution_convert_fusion.6
  978.8 7.9 reshape.458.refs_1_
  986.8 4.5 multiply_reduce_fusion.7
  992.6 12.1 fusion.35
  1005.3 11.3 convolution_convert_fusion.refs_0_
  1016.7 182.3 %shard_map.307 = f32[64,4864]{1,0:T(8,128)S(1)} custom-call(bf16[2048,3712]{1,0:T(8,128)(2,1)} %convolution_convert_fusion.refs_0_, bf16[2048,1024]{1,0:T(8,128)(2,1)S(1)} %copy-done, bf16[2048,128]{1,0:T(8,128)(2,1)S(1)} %reshape.463.refs_2_), custom_call_target="tpu_custom_call" | custom-call | tf_op jit(solution)/shard_map/pallas_call | solution.py:520
  1206.4 4.7 bitcast_convert_fusion.2
  1211.2 4.7 bitcast_convert_fusion.1
  1215.9 5.1 bitcast_convert_fusion
  1221.0 18.2 %reduce-scatter.26.cloned.1.call-done = bf16[64,2048]{1,0:T(8,128)(2,1)} async-done(((bf16[2048,2048]{1,0:T(8,128)(2,1)}), bf16[64,2048]{1,0:T(8,128)(2,1)}) %reduce-scatter.26.cloned.1.call-update) | async-done | bytes 262160 | tf_op jit(solution)/shard_map/reduce_scatter | solution.py:941
  (420 shorter events, 155.6 us)
Async XLA Ops:
  7.2 20.3 %copy-start.40 = (bf16[64,2816]{1,0:T(8,128)(2,1)S(1)}, bf16[64,2816]{1,0:T(8,128)(2,1)}, u32[]{:S(2)}) copy-start(bf16[64,2816]{1,0:T(8,128)(2,1)} %param.33) | copy-start | bytes 1081348
  7.2 172.2 %all-gather.35.cloned.1.call-start = ((), (), s32[]{:S(2)}) async-start(), calls=%async_computation.40 | async-start | bytes 1966080 | tf_op jit(solution)/shard_map/all_gather | solution.py:641
  9.1 34.8 %copy-start.77 = (bf16[64,16]{0,1:T(8,128)(2,1)S(1)}, bf16[64,16]{0,1:T(8,128)(2,1)}, u32[]{:S(2)}) copy-start(bf16[64,16]{0,1:T(8,128)(2,1)} %param.31) | copy-start | bytes 6148
  9.1 35.0 %copy-start.82 = (bf16[64]{0:T(256)(128)(2,1)S(1)}, bf16[64]{0:T(256)(128)(2,1)}, u32[]{:S(2)}) copy-start(bf16[64]{0:T(256)(128)(2,1)} %param.24) | copy-start | bytes 388
  9.1 35.0 %copy-start.83 = (bf16[16]{0:T(256)(128)(2,1)S(1)}, bf16[16]{0:T(256)(128)(2,1)}, u32[]{:S(2)}) copy-start(bf16[16]{0:T(256)(128)(2,1)} %param.27) | copy-start | bytes 100
  9.1 35.0 %copy-start.84 = (bf16[64]{0:T(256)(128)(2,1)S(1)}, bf16[64]{0:T(256)(128)(2,1)}, u32[]{:S(2)}) copy-start(bf16[64]{0:T(256)(128)(2,1)} %param.30) | copy-start | bytes 388
  9.1 35.1 %copy-start.57 = (bf16[16,4096]{1,0:T(8,128)(2,1)S(1)}, bf16[16,4096]{1,0:T(8,128)(2,1)}, u32[]{:S(2)}) copy-start(bf16[16,4096]{1,0:T(8,128)(2,1)} %param.28) | copy-start | bytes 393220
  9.1 35.2 %copy-start.39 = (bf16[64,3072]{1,0:T(8,128)(2,1)S(1)}, bf16[64,3072]{1,0:T(8,128)(2,1)}, u32[]{:S(2)}) copy-start(bf16[64,3072]{1,0:T(8,128)(2,1)} %param.25) | copy-start | bytes 1179652
  9.2 35.2 %copy-start.58 = (bf16[64,576]{1,0:T(8,128)(2,1)S(1)}, bf16[64,576]{1,0:T(8,128)(2,1)}, u32[]{:S(2)}) copy-start(bf16[64,576]{1,0:T(8,128)(2,1)} %param.26) | copy-start | bytes 221188
  27.4 191.6 %all-gather.39.cloned.1.call-start = ((), (), s32[]{:S(2)}) async-start(), calls=%async_computation.42 | async-start | bytes 1966080 | tf_op jit(solution)/shard_map/all_gather | solution.py:641
  42.5 185.2 %all-gather.21.cloned.1.call-start = ((), (), s32[]{:S(2)}) async-start(), calls=%async_computation.23 | async-start | bytes 8650752 | tf_op jit(solution)/shard_map/all_gather | solution.py:608
  43.3 193.2 %all-gather.25.cloned.1.call-start = ((), (), s32[]{:S(2)}) async-start(), calls=%async_computation.25 | async-start | bytes 1802240 | tf_op jit(solution)/shard_map/all_gather | solution.py:648
  43.8 195.4 %all-gather.37.cloned.1.call-start = ((), (), s32[]{:S(2)}) async-start(), calls=%async_computation.41 | async-start | bytes 4718592 | tf_op jit(solution)/shard_map/all_gather | solution.py:642
  45.2 124.7 %copy-start.11 = (bf16[1,192,2048]{2,1,0:T(8,128)(2,1)S(1)}, bf16[1,192,2048]{2,1,0:T(8,128)(2,1)}, u32[]{:S(2)}) copy-start(bf16[1,192,2048]{2,1,0:T(8,128)(2,1)} %param.19) | copy-start | bytes 2359300
  169.9 9.6 copy-start.60
  179.3 13.6 %copy-start.70 = (f32[192]{0:T(256)}, f32[192]{0:T(256)S(1)}, u32[]{:S(2)}) copy-start(f32[192]{0:T(256)S(1)} %multiply_reduce_fusion.9) | copy-start | bytes 2308
  179.4 74.3 %all-gather.41.cloned.1.call-start = ((), (), s32[]{:S(2)}) async-start(), calls=%async_computation.43 | async-start | bytes 4718592 | tf_op jit(solution)/shard_map/all_gather | solution.py:642
  181.3 30.8 %collective-permute-start = (bf16[192,512]{1,0:T(8,128)(2,1)}, bf16[192,512]{1,0:T(8,128)(2,1)}, u32[]{:S(2)}, u32[]{:S(2)}) collective-permute-start(bf16[192,512]{1,0:T(8,128)(2,1)} %multiply_convert_fusion.9), channel_id=1, source_target_pairs={{0,16},{1,17},{2,18},{3,19},{4,20},{5,21},{6,22},{7,23},{8,24},{9,... | collective-permute-start | bytes 589832 | tf_op jit(solution)/shard_map/ppermute | solution.py:27
  185.7 26.1 %copy-start.41 = (f32[192,32]{0,1:T(8,128)}, f32[192,32]{0,1:T(8,128)S(1)}, u32[]{:S(2)}) copy-start(f32[192,32]{0,1:T(8,128)S(1)} %get-tuple-element.131) | copy-start | bytes 73732
  185.7 26.1 %copy-start.43 = (f32[192,32]{0,1:T(8,128)}, f32[192,32]{0,1:T(8,128)S(1)}, u32[]{:S(2)}) copy-start(f32[192,32]{0,1:T(8,128)S(1)} %get-tuple-element.132) | copy-start | bytes 73732
  185.7 36.5 %copy-start.45 = (bf16[192,32]{0,1:T(8,128)(2,1)}, bf16[192,32]{0,1:T(8,128)(2,1)S(1)}, u32[]{:S(2)}) copy-start(bf16[192,32]{0,1:T(8,128)(2,1)S(1)} %get-tuple-element.127) | copy-start | bytes 36868
  185.7 36.5 %copy-start.47 = (bf16[192,32]{0,1:T(8,128)(2,1)}, bf16[192,32]{0,1:T(8,128)(2,1)S(1)}, u32[]{:S(2)}) copy-start(bf16[192,32]{0,1:T(8,128)(2,1)S(1)} %get-tuple-element.128) | copy-start | bytes 36868
  186.3 35.8 %collective-permute-start.1 = (bf16[192,64]{0,1:T(8,128)(2,1)}, bf16[192,64]{0,1:T(8,128)(2,1)S(1)}, u32[]{:S(2)}, u32[]{:S(2)}) collective-permute-start(bf16[192,64]{0,1:T(8,128)(2,1)} %pad_maximum_fusion.8), channel_id=1, source_target_pairs={{0,16},{1,17},{2,18},{3,19},{4,20},{5,21},{6,22},{7,23},{8,24},{9,... | collective-permute-start | bytes 73736 | tf_op jit(solution)/shard_map/ppermute | solution.py:27
  211.6 21.8 %copy-start.55 = (f32[2048]{0:T(1024)}, f32[2048]{0:T(1024)S(1)}, u32[]{:S(2)}) copy-start(f32[2048]{0:T(1024)S(1)} %reshape.473) | copy-start | bytes 24580
  211.9 10.2 copy-start.32
  211.9 10.2 copy-start.34
  219.1 101.0 %all-gather.23.cloned.1.call-start = ((), (), s32[]{:S(2)}) async-start(), calls=%async_computation.24 | async-start | bytes 3932160 | tf_op jit(solution)/shard_map/all_gather | solution.py:730
  235.6 148.2 %all-gather.43.cloned.1.call-start = ((), (), s32[]{:S(2)}) async-start(), calls=%async_computation.44 | async-start | bytes 3932160 | tf_op jit(solution)/shard_map/all_gather | solution.py:625
  236.4 159.4 %all-gather.27.cloned.1.call-start = ((), (), s32[]{:S(2)}) async-start(), calls=%async_computation.26 | async-start | bytes 4325376 | tf_op jit(solution)/shard_map/all_gather | solution.py:647
  237.1 261.1 %all-gather.29.cloned.1.call-start = ((), (), s32[]{:S(2)}) async-start(), calls=%async_computation.37 | async-start | bytes 8650752 | tf_op jit(solution)/shard_map/all_gather | solution.py:653
  237.7 273.2 %all-gather.31.cloned.1.call-start = ((), (), s32[]{:S(2)}) async-start(), calls=%async_computation.38 | async-start | bytes 8650752 | tf_op jit(solution)/shard_map/all_gather | solution.py:654
  238.4 286.7 %all-gather.33.cloned.1.call-start = ((), (), s32[]{:S(2)}) async-start(), calls=%async_computation.39 | async-start | bytes 8650752 | tf_op jit(solution)/shard_map/all_gather | solution.py:655
  239.0 518.7 %reduce-scatter.28.cloned.1.call-start = ((), (), s32[]{:S(2)}) async-start(), calls=%async_computation.31 | async-start | bytes 4718592 | tf_op jit(solution)/shard_map/reduce_scatter | solution.py:787
  437.1 55.8 %all-to-all-start = ((bf16[4,4,72,2048]{3,2,1,0:T(8,128)(2,1)}), bf16[4,4,72,2048]{3,2,1,0:T(8,128)(2,1)}, u32[]{:S(2)}, u32[]{:S(2)}) async-start(bf16[4,4,72,2048]{3,2,1,0:T(8,128)(2,1)} %bitcast.249), calls=%async_computation | async-start | bytes 9437184 | tf_op jit(solution)/shard_map/all_to_all | solution.py:669
  442.0 316.4 %reduce-scatter.30.cloned.1.call-start = ((), (), s32[]{:S(2)}) async-start(), calls=%async_computation.32 | async-start | bytes 4718592 | tf_op jit(solution)/shard_map/reduce_scatter | solution.py:787
  492.9 57.8 %all-to-all-start.4 = ((bf16[4,4,72,2048]{3,2,1,0:T(8,128)(2,1)}), bf16[4,4,72,2048]{3,2,1,0:T(8,128)(2,1)}, u32[]{:S(2)}, u32[]{:S(2)}) async-start(bf16[4,4,72,2048]{3,2,1,0:T(8,128)(2,1)} %bitcast.250), calls=%async_computation.5 | async-start | bytes 9437184 | tf_op jit(solution)/shard_map/all_to_all | solution.py:669
  550.7 27.4 %copy-start.17 = (bf16[1,768,2048]{2,1,0:T(8,128)(2,1)S(1)}, bf16[1,768,2048]{2,1,0:T(8,128)(2,1)}, u32[]{:S(2)}) copy-start(bf16[1,768,2048]{2,1,0:T(8,128)(2,1)} %all-gather.43.cloned.1.call-done) | copy-start | bytes 9437188
  564.4 7.9 all-to-all-start.5
  574.8 8.6 all-to-all-start.6
  578.0 181.0 %reduce-scatter.32.cloned.1.call-start = ((), (), s32[]{:S(2)}) async-start(), calls=%async_computation.33 | async-start | bytes 4325376 | tf_op jit(solution)/shard_map/reduce_scatter | solution.py:787
  583.4 17.7 %slice-start.2 = ((s8[5767168]{0:T(1024)(128)(4,1)}), s8[1572864]{0:T(1024)(128)(4,1)S(1)}, s32[]{:S(2)}) async-start(s8[5767168]{0:T(1024)(128)(4,1)} %bitcast.282), calls=%async_computation.50 | async-start | bytes 3145728
  583.5 17.6 %slice-start.3 = ((s8[5767168]{0:T(1024)(128)(4,1)}), s8[4194304]{0:T(1024)(128)(4,1)S(1)}, s32[]{:S(2)}) async-start(s8[5767168]{0:T(1024)(128)(4,1)} %bitcast.282), calls=%async_computation.51 | async-start | bytes 8388608
  601.1 10.7 copy-start.89
  623.7 56.6 %all-to-all-start.7 = ((bf16[4,4,72,2048]{3,2,1,0:T(8,128)(2,1)}), bf16[4,4,72,2048]{3,2,1,0:T(8,128)(2,1)}, u32[]{:S(2)}, u32[]{:S(2)}) async-start(bf16[4,4,72,2048]{3,2,1,0:T(8,128)(2,1)} %bitcast.262), calls=%async_computation.9 | async-start | bytes 9437184 | tf_op jit(solution)/shard_map/all_to_all | solution.py:674
  628.9 171.5 %reduce-scatter.22.cloned.1.call-start = ((), (), s32[]{:S(2)}) async-start(), calls=%async_computation.28 | async-start | bytes 81920 | tf_op jit(solution)/shard_map/reduce_scatter | solution.py:832
  635.7 166.3 %reduce-scatter.24.cloned.1.call-start = ((), (), s32[]{:S(2)}) async-start(), calls=%async_computation.29 | async-start | bytes 3932160 | tf_op jit(solution)/shard_map/reduce_scatter | solution.py:818
  690.9 57.4 %all-to-all-start.1 = ((bf16[4,4,72,2048]{3,2,1,0:T(8,128)(2,1)}), bf16[4,4,72,2048]{3,2,1,0:T(8,128)(2,1)}, u32[]{:S(2)}, u32[]{:S(2)}) async-start(bf16[4,4,72,2048]{3,2,1,0:T(8,128)(2,1)} %bitcast.261), calls=%async_computation.1 | async-start | bytes 9437184 | tf_op jit(solution)/shard_map/all_to_all | solution.py:674
  695.8 122.2 %reduce-scatter.20.cloned.1.call-start = ((), (), s32[]{:S(2)}) async-start(), calls=%async_computation.27 | async-start | bytes 3932160 | tf_op jit(solution)/shard_map/reduce_scatter | solution.py:818
  757.6 94.4 %reduce-scatter.40.cloned.1.call-start = ((), (), s32[]{:S(2)}) async-start(), calls=%async_computation.45 | async-start | bytes 1966080
  758.4 127.4 %reduce-scatter.42.cloned.1.call-start = ((), (), s32[]{:S(2)}) async-start(), calls=%async_computation.46 | async-start | bytes 1966080
  759.0 160.0 %reduce-scatter.44.cloned.1.call-start = ((), (), s32[]{:S(2)}) async-start(), calls=%async_computation.47 | async-start | bytes 1802240
  759.7 446.7 %reduce-scatter.34.cloned.1.call-start = ((), (), s32[]{:S(2)}) async-start(), calls=%async_computation.34 | async-start | bytes 8650752 | tf_op jit(solution)/shard_map/reduce_scatter | solution.py:764
  772.1 439.0 %reduce-scatter.36.cloned.1.call-start = ((), (), s32[]{:S(2)}) async-start(), calls=%async_computation.35 | async-start | bytes 8650752 | tf_op jit(solution)/shard_map/reduce_scatter | solution.py:765
  786.8 429.1 %reduce-scatter.38.cloned.1.call-start = ((), (), s32[]{:S(2)}) async-start(), calls=%async_computation.36 | async-start | bytes 8650752 | tf_op jit(solution)/shard_map/reduce_scatter | solution.py:766
  800.3 438.9 %reduce-scatter.26.cloned.1.call-start = ((), (), s32[]{:S(2)}) async-start(), calls=%async_computation.30 | async-start | bytes 8650752 | tf_op jit(solution)/shard_map/reduce_scatter | solution.py:941
  821.4 104.6 %copy-start.7 = (f32[192,2048]{1,0:T(8,128)}, f32[192,2048]{1,0:T(8,128)S(1)}, u32[]{:S(2)}) copy-start(f32[192,2048]{1,0:T(8,128)S(1)} %get-tuple-element.115) | copy-start | bytes 4718596
  827.1 63.5 %copy-start.18 = (bf16[192,2048]{1,0:T(8,128)(2,1)S(1)}, bf16[192,2048]{1,0:T(8,128)(2,1)}, u32[]{:S(2)}) copy-start(bf16[192,2048]{1,0:T(8,128)(2,1)} %multiply_convert_fusion.8) | copy-start | bytes 2359300
  852.0 33.8 %all-to-all-start.8 = ((bf16[4,64,704]{2,1,0:T(8,128)(2,1)}), bf16[4,64,704]{2,1,0:T(8,128)(2,1)S(1)}, u32[]{:S(2)}, u32[]{:S(2)}) async-start(bf16[4,64,704]{2,1,0:T(8,128)(2,1)} %bitcast.278), calls=%async_computation.13 | async-start | bytes 786432 | tf_op jit(solution)/shard_map/all_to_all | solution.py:796
  885.8 37.6 %all-to-all-start.9 = ((bf16[4,64,704]{2,1,0:T(8,128)(2,1)}), bf16[4,64,704]{2,1,0:T(8,128)(2,1)S(1)}, u32[]{:S(2)}, u32[]{:S(2)}) async-start(bf16[4,64,704]{2,1,0:T(8,128)(2,1)} %bitcast.277), calls=%async_computation.15 | async-start | bytes 786432 | tf_op jit(solution)/shard_map/all_to_all | solution.py:796
  924.6 8.8 slice-start
  937.7 35.8 %collective-permute-start.3 = (bf16[192,64]{0,1:T(8,128)(2,1)S(1)}, bf16[192,64]{0,1:T(8,128)(2,1)S(1)}, u32[]{:S(2)}, u32[]{:S(2)}) collective-permute-start(bf16[192,64]{0,1:T(8,128)(2,1)S(1)} %slice.214), channel_id=1, source_target_pairs={{16,0},{17,1},{18,2},{19,3},{20,4},{21,5},{22,6},{23,7},{24,8},{25... | collective-permute-start | bytes 73736 | tf_op jit(solution)/shard_map/ppermute | solution.py:27
  947.8 26.2 %collective-permute-start.2 = (bf16[192,4096]{1,0:T(8,128)(2,1)}, bf16[192,4096]{1,0:T(8,128)(2,1)}, u32[]{:S(2)}, u32[]{:S(2)}) collective-permute-start(bf16[192,4096]{1,0:T(8,128)(2,1)} %copy.249), channel_id=1, source_target_pairs={{16,0},{17,1},{18,2},{19,3},{20,4},{21,5},{22,6},{23,7},{24,8},{25... | collective-permute-start | bytes 4718600 | tf_op jit(solution)/shard_map/ppermute | solution.py:27
  992.6 12.3 copy-start.49
  1005.3 11.3 copy-start
  (72 other events, 292.4 us)
Sparse Core Ops, SparseCore 0:
  27.5 36.1 all-gather.34
  65.6 39.4 all-gather.38
  108.0 87.1 all-gather.20
  196.9 28.5 all-gather.24
  226.9 12.1 all-gather.36
  240.4 13.2 all-gather.40
  255.3 64.6 all-gather.22
  321.6 62.1 all-gather.42
  385.3 10.3 all-gather.26
  397.1 17.1 all-gather.28
  415.9 17.1 all-gather.30
  434.5 17.1 all-gather.32
  453.9 12.0 reduce-scatter.27
  468.2 12.0 reduce-scatter.29
  583.5 11.7 reduce-scatter.31
  635.8 20.2 reduce-scatter.21
  691.0 60.2 reduce-scatter.23
  757.8 60.2 reduce-scatter.19
  821.1 30.9 reduce-scatter.39
  854.9 30.9 reduce-scatter.41
  888.8 30.1 reduce-scatter.43
  922.0 13.7 reduce-scatter.33
  938.7 16.2 reduce-scatter.35
  957.3 14.3 reduce-scatter.37
  973.9 265.2 reduce-scatter.25

commit v3 on v2

--- a/solution.py
+++ b/solution.py
@@ -109,6 +109,7 @@
 PLANE = 4
 MESH = pl.DeviceIdType.MESH
 MEBIBYTE = 1024 * 1024
+LONG = pl.CostEstimate(flops=100 * 10**9, bytes_accessed=0, transcendentals=0)
 
 
 def groups(count):
@@ -134,31 +135,63 @@
     return (place + 1 - 2 * (spot % 2), place + 2 - 4 * (spot // 2))
 
 
+def greet(partners):
+    barrier = pltpu.get_barrier_semaphore()
+    for where in partners:
+        pl.semaphore_signal(barrier, inc=1, device_id=where, device_id_type=MESH)
+    pl.semaphore_wait(barrier, len(partners))
+
+
+def line_others(half, place, depth):
+    total = depth * PLANE
+    return [(half, (place + offset * PLANE) % total) for offset in range(1, depth)]
+
+
+def plane_others(half, place):
+    spot = place % PLANE
+    return [(half, place - spot + (spot + offset) % PLANE) for offset in range(1, PLANE)]
+
+
 def greet_neighbours(half, place, depth):
-    barrier = pltpu.get_barrier_semaphore()
+    mates = [(half, mate) for mate in plane_mates(place)]
+    greet(line_others(half, place, depth) + mates + [(1 - half, place)])
+
+
+def exchange_along(depth, half, place, in_ref, land, own_sem, send, receive):
     level = place // PLANE
-
-    def greet(where):
-        pl.semaphore_signal(barrier, inc=1, device_id=where, device_id_type=MESH)
-
-    for mate in plane_mates(place):
-        greet((half, mate))
-    greet((1 - half, place))
-
-    @pl.when(level > 0)
-    def _():
-        greet((half, place - PLANE))
-
-    @pl.when(level < depth - 1)
-    def _():
-        greet((half, place + PLANE))
-
-    pl.semaphore_wait(
-        barrier, 3 + jnp.where(level > 0, 1, 0) + jnp.where(level < depth - 1, 1, 0)
-    )
-
-
-def gather_kernel(depth, cut, in_ref, out_ref, own_sem, zs, zr, ps, pr, qs, qr, cs, cr):
+    total = depth * PLANE
+
+    def own():
+        return pltpu.make_async_copy(in_ref.at[level], land(level), own_sem)
+
+    def to(offset):
+        where = (place + offset * PLANE) % total
+        return remote(
+            in_ref.at[where // PLANE],
+            land(level),
+            send.at[offset],
+            receive.at[offset],
+            (half, where),
+        )
+
+    def start():
+        own().start()
+        for offset in range(1, depth):
+            to(offset).start()
+
+    def finish():
+        own().wait()
+        for offset in range(1, depth):
+            to(offset).wait()
+
+    return start, finish
+
+
+def gather_kernel(depth, cut, *refs):
+    in_ref, *line_ins, move_in, down_in = refs[:5]
+    out_ref, *line_outs, shared_out, down_out = refs[5:10]
+    own_sem, zs, zr, ps, pr, qs, qr, cs, cr, ls, lr, ms, mr, *shared_sems = refs[10:]
+    os, ore, ts, tr, us, ur = shared_sems
     half = lax.axis_index("fsdp")
     place = lax.axis_index("expert")
     level = place // PLANE
@@ -208,6 +241,65 @@
             block, block, cs.at[which, source], cr.at[which, source], (1 - half, place)
         )
 
+    def trail(which, way, source, own=False):
+        target = line_outs[which].at[source]
+        return remote(
+            line_ins[which] if own else target,
+            target,
+            ls.at[which, way, source],
+            lr.at[which, source],
+            (half, place + (2 * way - 1) * PLANE),
+        )
+
+    def trail_own(which):
+        return pltpu.make_async_copy(
+            line_ins[which], line_outs[which].at[level], own_sem.at[2 + which]
+        )
+
+    move_start, move_finish = exchange_along(
+        depth,
+        half,
+        place,
+        move_in,
+        lambda source: shared_out.at[half, source, spot],
+        own_sem.at[4],
+        ms,
+        mr,
+    )
+    items = range(depth + 2)
+    down_own = pltpu.make_async_copy(down_in, down_out.at[half, spot], own_sem.at[5])
+
+    def shared_at(item, first, count):
+        if item < depth:
+            return shared_out.at[half, item, pl.ds(first, count)]
+        span = down_in.shape[1] // 2
+        return down_out.at[
+            half, pl.ds(first, count), :, pl.ds((item - depth) * span, span)
+        ]
+
+    def shared_route(item):
+        return (0 if item < depth // 2 else 1) if item < depth else item - depth
+
+    def shared_one(item):
+        block = shared_at(item, spot, 1)
+        mate = mates[shared_route(item)]
+        return remote(block, block, os.at[item], ore.at[item], (half, mate))
+
+    def shared_two(item):
+        if shared_route(item) == 0:
+            blocks = [shared_at(item, spot - spot % 2, 2)]
+        else:
+            blocks = [shared_at(item, (spot + 2 * turn) % PLANE, 1) for turn in range(2)]
+        mate = mates[1 - shared_route(item)]
+        return [
+            remote(block, block, ts.at[turn, item], tr.at[turn, item], (half, mate))
+            for turn, block in enumerate(blocks)
+        ]
+
+    def shared_core(item):
+        block = shared_at(item, 0, PLANE)
+        return remote(block, block, us.at[item], ur.at[item], (1 - half, place))
+
     seconds = ((0, 0), (1, 0), (1, 1))
 
     def own_copy(which):
@@ -227,8 +319,31 @@
 
         plane_one(which, level, True).start()
         own_copy(which).start()
+    move_start()
+    down_own.start()
+    for which in range(2):
+        trail_own(which).start()
     for which in range(2):
         own_copy(which).wait()
+
+    def trail_first():
+        for which in range(2):
+
+            @pl.when(level > 0)
+            def _():
+                trail(which, 0, level, True).start()
+
+            @pl.when(level < depth - 1)
+            def _():
+                trail(which, 1, level, True).start()
+
+    def trail_on(source, way):
+        for which in range(2):
+            trail(which, way, source).wait_recv()
+
+            @pl.when((level < depth - 1) if way == 1 else (level > 0))
+            def _():
+                trail(which, way, source).start()
 
     def visit(step, act):
         if step == 0:
@@ -272,11 +387,45 @@
             visit(step - 1, spread)
         if 1 <= step < depth:
             visit(step, arrive)
+        if step == 1:
+            trail_first()
+            move_finish()
+            down_own.wait()
+            for item in items:
+                shared_one(item).start()
+        if step == 2:
+            for item in items:
+                shared_one(item).wait_recv()
+                for copy in shared_two(item):
+                    copy.start()
+        if step == depth:
+            for item in items:
+                for copy in shared_two(item):
+                    copy.wait_recv()
+                shared_core(item).start()
         if step >= 2:
             visit(step - 2, share)
+            if step <= depth:
+                visit(step - 1, trail_on)
+    for item in items:
+        shared_one(item).wait_send()
+        for copy in shared_two(item):
+            copy.wait_send()
+        shared_core(item).wait()
+    for which in range(2):
+        trail_own(which).wait()
 
     def finish(source, carry):
         for which in range(2):
+
+            @pl.when((source <= level) & (level < depth - 1))
+            def _():
+                trail(which, 1, source).wait_send()
+
+            @pl.when((source >= level) & (level > 0))
+            def _():
+                trail(which, 0, source).wait_send()
+
             core(which, source).wait_recv()
             core(which, source).wait_send()
             plane_one(which, source).wait_send()
@@ -296,18 +445,24 @@
     lax.fori_loop(0, depth, finish, 0)
 
 
-def gather_rows(value, cut):
+def gather_rows(value, first, second, moved, down, cut):
     rows, width = value.shape
     total = lax.axis_size("expert")
     depth = total // PLANE
     semaphores = pltpu.SemaphoreType.DMA
     return pl.pallas_call(
         functools.partial(gather_kernel, depth, cut),
-        out_shape=jax.ShapeDtypeStruct((2 * total * rows, width), value.dtype),
-        in_specs=[pl.BlockSpec(memory_space=pl.ANY)],
-        out_specs=pl.BlockSpec(memory_space=pl.ANY),
+        out_shape=[
+            jax.ShapeDtypeStruct((2 * total * rows, width), value.dtype),
+            jax.ShapeDtypeStruct((depth,) + first.shape, first.dtype),
+            jax.ShapeDtypeStruct((depth,) + second.shape, second.dtype),
+            jax.ShapeDtypeStruct((2, depth, PLANE) + moved.shape[1:], moved.dtype),
+            jax.ShapeDtypeStruct((2, PLANE) + down.shape, down.dtype),
+        ],
+        in_specs=[pl.BlockSpec(memory_space=pl.ANY)] * 5,
+        out_specs=[pl.BlockSpec(memory_space=pl.ANY)] * 5,
         scratch_shapes=[
-            semaphores((2,)),
+            semaphores((6,)),
             semaphores((2, 2, depth)),
             semaphores((2, depth)),
             semaphores((2, depth)),
@@ -316,16 +471,678 @@
             semaphores((3, depth)),
             semaphores((2, depth)),
             semaphores((2, depth)),
+            semaphores((2, 2, depth)),
+            semaphores((2, depth)),
+            semaphores((depth,)),
+            semaphores((depth,)),
+            semaphores((depth + 2,)),
+            semaphores((depth + 2,)),
+            semaphores((2, depth + 2)),
+            semaphores((2, depth + 2)),
+            semaphores((depth + 2,)),
+            semaphores((depth + 2,)),
         ],
         compiler_params=pltpu.CompilerParams(collective_id=1, has_side_effects=True),
-    )(value)
+        cost_estimate=LONG,
+    )(value, first, second, moved, down)
+
+
+def dot_nt(former, latter):
+    return lax.dot_general(
+        former, latter, (((1,), (1,)), ((), ())), preferred_element_type=jnp.float32
+    )
+
+
+def dot_tn(former, latter):
+    return lax.dot_general(
+        former, latter, (((0,), (0,)), ((), ())), preferred_element_type=jnp.float32
+    )
+
+
+def dispatch_kernel(depth, *refs):
+    x_ref, choose_ref, grad_in, shared_in, down_in = refs[:5]
+    rows_out, forth_out, back_out, wide_out, tall_out = refs[5:10]
+    lines, placed, grads, weights, downs, low_ref, hidden_ref, forth_ref, back_ref = refs[10:19]
+    wide_ref, tall_ref, load_sem, out_sem, zs, zr, es, er, own_sem, done_sem = refs[19:]
+    half = lax.axis_index("fsdp")
+    place = lax.axis_index("expert")
+    level = place // PLANE
+    spot = place % PLANE
+    padded, width = downs.shape
+    true = down_in.shape[0]
+    chunk = 256 if padded % 256 == 0 else 128
+    greet(line_others(half, place, depth) + plane_others(half, place))
+
+    def along(way, source):
+        block = lines.at[source]
+        where = (half, place + (2 * way - 1) * PLANE)
+        return remote(block, block, zs.at[way, source], zr.at[source], where)
+
+    loads = [
+        pltpu.make_async_copy(shared_in, weights, load_sem.at[0]),
+        pltpu.make_async_copy(down_in, downs.at[pl.ds(0, true), :], load_sem.at[1]),
+        pltpu.make_async_copy(grad_in, grads, load_sem.at[2]),
+    ]
+    lines[level] = x_ref[...]
+
+    def pass_on(way, source):
+        @pl.when((level < depth - 1) if way == 1 else (level > 0))
+        def _():
+            along(way, source).start()
+
+    for way in range(2):
+        pass_on(way, level)
+    for load in loads:
+        load.start()
+    if padded > true:
+        downs[pl.ds(true, padded - true), :] = jnp.zeros((padded - true, width), downs.dtype)
+
+    def own_rows(source):
+        return pltpu.make_async_copy(
+            placed.at[source, spot], rows_out.at[spot, source], own_sem.at[source]
+        )
+
+    def to_mate(offset, source):
+        mate = (spot + offset) % PLANE
+        return remote(
+            placed.at[source, mate],
+            rows_out.at[spot, source],
+            es.at[offset, source],
+            er.at[offset, source],
+            (half, place - spot + mate),
+        )
+
+    def from_mate(offset, source):
+        mate = (spot + PLANE - offset) % PLANE
+        block = rows_out.at[mate, source]
+        return remote(
+            block,
+            block,
+            es.at[offset, source],
+            er.at[offset, source],
+            (half, place - spot + mate),
+        )
+
+    def give(source):
+        def columns(n, carry):
+            at = pl.ds(pl.multiple_of(n * 512, 512), 512)
+            for mate in range(PLANE):
+                placed[source, mate, :, at] = jnp.dot(
+                    choose_ref[source, mate],
+                    lines[source, :, at],
+                    preferred_element_type=jnp.float32,
+                ).astype(placed.dtype)
+            return carry
+
+        lax.fori_loop(0, width // 512, columns, 0)
+        for offset in range(1, PLANE):
+            to_mate(offset, source).start()
+        own_rows(source).start()
+
+    def shared(source):
+        def inner(n, carry):
+            at = pl.ds(pl.multiple_of(n * chunk, chunk), chunk)
+            after = pl.ds(pl.multiple_of(padded + n * chunk, 128), chunk)
+            x = lines[source]
+            gate = jnp.dot(x, weights[:, at], preferred_element_type=jnp.float32)
+            up = jnp.dot(x, weights[:, after], preferred_element_type=jnp.float32)
+            dh = dot_nt(grads[source], downs[at, :])
+            sig = 1.0 / (1.0 + jnp.exp(-gate))
+            act = gate * sig
+            hidden_ref[source, :, at] = (act * up).astype(hidden_ref.dtype)
+            low_ref[source, :, at] = (dh * up * (sig + act * (1.0 - sig))).astype(low_ref.dtype)
+            low_ref[source, :, after] = (dh * act).astype(low_ref.dtype)
+            return carry
+
+        lax.fori_loop(0, padded // chunk, inner, 0)
+
+        def outer(n, carry):
+            at = pl.ds(pl.multiple_of(n * 512, 512), 512)
+            forth_ref[:, at] = jnp.dot(
+                hidden_ref[source], downs[:, at], preferred_element_type=jnp.float32
+            ).astype(forth_ref.dtype)
+            back_ref[:, at] = dot_nt(low_ref[source], weights[at, :]).astype(back_ref.dtype)
+            return carry
+
+        lax.fori_loop(0, width // 512, outer, 0)
+        outs = [
+            pltpu.make_async_copy(forth_ref, forth_out.at[source], out_sem.at[0]),
+            pltpu.make_async_copy(back_ref, back_out.at[source], out_sem.at[1]),
+        ]
+        for out in outs:
+            out.start()
+        for out in outs:
+            out.wait()
+
+    give(level)
+    for load in loads:
+        load.wait()
+    shared(level)
+
+    def step(s, carry):
+        @pl.when(level - s >= 0)
+        def _():
+            along(1, level - s).wait_recv()
+            pass_on(1, level - s)
+
+        @pl.when(level + s < depth)
+        def _():
+            along(0, level + s).wait_recv()
+            pass_on(0, level + s)
+
+        def one(way, act):
+            source = level + (1 - 2 * way) * s
+
+            @pl.when((source >= 0) & (source < depth))
+            def _():
+                act(source)
+
+        def both(way, carry):
+            one(way, give)
+            return carry
+
+        def both_shared(way, carry):
+            one(way, shared)
+            return carry
+
+        lax.fori_loop(0, 2, both, 0)
+        lax.fori_loop(0, 2, both_shared, 0)
+        return carry
+
+    lax.fori_loop(1, depth, step, 0)
+
+    tokens = x_ref.shape[0]
+
+    def all_lines(ref, at):
+        return ref[:, :, at].reshape(depth * tokens, -1)
+
+    def write(kind, k):
+        slot = k % 2
+        staged, target = ((wide_ref, wide_out), (tall_ref, tall_out))[kind]
+        size = staged.shape[1]
+        at = pl.ds(pl.multiple_of(k * size, size), size)
+        return pltpu.make_async_copy(
+            staged.at[slot], target.at[at, :], done_sem.at[kind, slot]
+        )
+
+    def tile(kind, k, ref, others):
+        staged = (wide_ref, tall_ref)[kind]
+        size = staged.shape[1]
+
+        @pl.when(k >= 2)
+        def _():
+            write(kind, k - 2).wait()
+
+        at = pl.ds(pl.multiple_of(k * size, size), size)
+        staged[k % 2] = dot_tn(
+            all_lines(ref, at), others[...].reshape(depth * tokens, -1)
+        ).astype(staged.dtype)
+        write(kind, k).start()
+
+    def wide_tile(k, carry):
+        tile(0, k, lines, low_ref)
+        return carry
+
+    def tall_tile(k, carry):
+        tile(1, k, hidden_ref, grads)
+        return carry
+
+    wide_count = width // wide_ref.shape[1]
+    tall_count = padded // tall_ref.shape[1]
+    lax.fori_loop(0, wide_count, wide_tile, 0)
+    lax.fori_loop(0, tall_count, tall_tile, 0)
+    for kind, total in ((0, wide_count), (1, tall_count)):
+        for k in range(max(0, total - 2), total):
+            write(kind, k).wait()
+
+    def finish(source, carry):
+        own_rows(source).wait()
+        for offset in range(1, PLANE):
+            from_mate(offset, source).wait_recv()
+            to_mate(offset, source).wait_send()
+
+        @pl.when((source <= level) & (level < depth - 1))
+        def _():
+            along(1, source).wait_send()
+
+        @pl.when((source >= level) & (level > 0))
+        def _():
+            along(0, source).wait_send()
+
+        return carry
+
+    lax.fori_loop(0, depth, finish, 0)
+
+
+def dispatch(x, choose, grad_line, shared_full, down_full):
+    depth = choose.shape[0]
+    tokens, width = x.shape
+    capacity = choose.shape[2]
+    padded = shared_full.shape[1] // 2
+    semaphores = pltpu.SemaphoreType.DMA
+    low = x.dtype
+    anywhere = pl.BlockSpec(memory_space=pl.ANY)
+    local = pl.BlockSpec(memory_space=pltpu.VMEM)
+    return pl.pallas_call(
+        functools.partial(dispatch_kernel, depth),
+        out_shape=[
+            jax.ShapeDtypeStruct((PLANE, depth, capacity, width), low),
+            jax.ShapeDtypeStruct((depth, tokens, width), low),
+            jax.ShapeDtypeStruct((depth, tokens, width), low),
+            jax.ShapeDtypeStruct((width, 2 * padded), low),
+            jax.ShapeDtypeStruct((padded, width), low),
+        ],
+        in_specs=[local, local, anywhere, anywhere, anywhere],
+        out_specs=[anywhere] * 5,
+        scratch_shapes=[
+            pltpu.VMEM((depth, tokens, width), low),
+            pltpu.VMEM((depth, PLANE, capacity, width), low),
+            pltpu.VMEM((depth, tokens, width), low),
+            pltpu.VMEM((width, 2 * padded), low),
+            pltpu.VMEM((padded, width), low),
+            pltpu.VMEM((depth, tokens, 2 * padded), low),
+            pltpu.VMEM((depth, tokens, padded), low),
+            pltpu.VMEM((tokens, width), low),
+            pltpu.VMEM((tokens, width), low),
+            pltpu.VMEM((2, 256, 2 * padded), low),
+            pltpu.VMEM((2, 128, width), low),
+            semaphores((3,)),
+            semaphores((2,)),
+            semaphores((2, depth)),
+            semaphores((depth,)),
+            semaphores((PLANE, depth)),
+            semaphores((PLANE, depth)),
+            semaphores((depth,)),
+            semaphores((2, 2)),
+        ],
+        compiler_params=pltpu.CompilerParams(
+            collective_id=3, has_side_effects=True, vmem_limit_bytes=56 * MEBIBYTE
+        ),
+        cost_estimate=LONG,
+    )(x, choose, grad_line, shared_full, down_full)
+
+
+def return_kernel(depth, *refs):
+    rows_in, scalars_in, choose_ref, shared_in = refs[:4]
+    operands_in = refs[4:9]
+    back_ref, prob_ref, gate_out, up_out, down_out = refs[9:14]
+    came, scalars, shared, onward, incoming, prob_send, prob_land = refs[14:21]
+    held = refs[21:26]
+    give_wide, give_tall, take_wide, take_tall, done_wide, done_tall = refs[26:32]
+    own_sem, es, er, ss, sr, load_sem, shared_sem, cs, cr, ps, pr = refs[32:43]
+    ws, wr, ts, tr, wide_sem, tall_sem = refs[43:]
+    x_held, gate_held, up_held, hidden_held, grad_held = held
+    half = lax.axis_index("fsdp")
+    place = lax.axis_index("expert")
+    level = place // PLANE
+    spot = place % PLANE
+    other = (1 - half, place)
+    tokens, width = back_ref.shape
+    capacity = choose_ref.shape[2]
+    wide_count, wide_rows = take_wide.shape[1:3]
+    tall_count, tall_rows, tall_width = take_tall.shape
+    greet(line_others(half, place, depth) + plane_others(half, place) + [other])
+
+    def rows_to(offset, source):
+        mate = (spot + offset) % PLANE
+        where = (half, place - spot + mate)
+        return (
+            remote(
+                rows_in.at[mate, source],
+                came.at[spot, source],
+                es.at[offset, source],
+                er.at[offset, source],
+                where,
+            ),
+            remote(
+                scalars_in.at[mate, source],
+                scalars.at[spot, source],
+                ss.at[offset, source],
+                sr.at[offset, source],
+                where,
+            ),
+        )
+
+    def rows_from(offset, source):
+        mate = (spot + PLANE - offset) % PLANE
+        where = (half, place - spot + mate)
+        block, small = came.at[mate, source], scalars.at[mate, source]
+        return (
+            remote(block, block, es.at[offset, source], er.at[offset, source], where),
+            remote(small, small, ss.at[offset, source], sr.at[offset, source], where),
+        )
+
+    def own_rows(source):
+        return (
+            pltpu.make_async_copy(
+                rows_in.at[spot, source], came.at[spot, source], own_sem.at[0, source]
+            ),
+            pltpu.make_async_copy(
+                scalars_in.at[spot, source], scalars.at[spot, source], own_sem.at[1, source]
+            ),
+        )
+
+    def shared_load(slot, source):
+        return pltpu.make_async_copy(shared_in.at[source], shared.at[slot], shared_sem.at[slot])
+
+    def each_way(s, act):
+        def one(way, carry):
+            source = level + (2 * way - 1) * s
+
+            @pl.when((source >= 0) & (source < depth) & ((s > 0) | (way == 0)))
+            def _():
+                act(way, source)
+
+            return carry
+
+        lax.fori_loop(0, 2, one, 0)
+
+    def begin(way, source):
+        for offset in range(1, PLANE):
+            for copy in rows_to(offset, source):
+                copy.start()
+        for copy in own_rows(source):
+            copy.start()
+
+    def begin_step(i, carry):
+        each_way(depth - 1 - i, begin)
+        return carry
+
+    lax.fori_loop(0, depth, begin_step, 0)
+    loads = [
+        pltpu.make_async_copy(source, target, load_sem.at[k])
+        for k, (source, target) in enumerate(zip(operands_in, held))
+    ]
+    for load in loads:
+        load.start()
+    for load in loads:
+        load.wait()
+
+    def wide_tiles(owner, k):
+        at = pl.ds(pl.multiple_of((owner * wide_count + k) * wide_rows, wide_rows), wide_rows)
+        x = x_held[:, at]
+        return dot_tn(x, gate_held[...]), dot_tn(x, up_held[...])
+
+    def tall_tile(owner, k):
+        at = pl.ds(pl.multiple_of(k * tall_rows, tall_rows), tall_rows)
+        over = pl.ds(pl.multiple_of(owner * tall_width, tall_width), tall_width)
+        return dot_tn(hidden_held[:, at], grad_held[:, over])
+
+    def wide_send(which, k):
+        slot = k % 2
+        return remote(
+            give_wide.at[slot, which],
+            take_wide.at[which, k],
+            ws.at[slot, which],
+            wr.at[which, k],
+            other,
+        )
+
+    def tall_send(k):
+        slot = k % 2
+        return remote(give_tall.at[slot], take_tall.at[k], ts.at[slot], tr.at[k], other)
+
+    def wide_write(which, k):
+        target = (gate_out, up_out)[which]
+        at = pl.ds(pl.multiple_of(k * wide_rows, wide_rows), wide_rows)
+        return pltpu.make_async_copy(done_wide.at[which], target.at[at, :], wide_sem.at[which])
+
+    def tall_write(k):
+        slot = k % 2
+        at = pl.ds(pl.multiple_of(k * tall_rows, tall_rows), tall_rows)
+        return pltpu.make_async_copy(done_tall.at[slot], down_out.at[at, :], tall_sem.at[slot])
+
+    def give_wide_tile(k):
+        @pl.when(k >= 2)
+        def _():
+            for which in range(2):
+                wide_send(which, k - 2).wait_send()
+
+        for which, tile in enumerate(wide_tiles(1 - half, k)):
+            give_wide[k % 2, which] = tile.astype(give_wide.dtype)
+            wide_send(which, k).start()
+
+    def give_tall_tile(k):
+        @pl.when(k >= 2)
+        def _():
+            tall_send(k - 2).wait_send()
+
+        give_tall[k % 2] = tall_tile(1 - half, k).astype(give_tall.dtype)
+        tall_send(k).start()
+
+    def keep_wide_tile(k):
+        @pl.when(k >= 1)
+        def _():
+            for which in range(2):
+                wide_write(which, k - 1).wait()
+
+        for which, tile in enumerate(wide_tiles(half, k)):
+            wide_send(which, k).wait_recv()
+            tile = tile + take_wide[which, k].astype(jnp.float32)
+            done_wide[which] = tile.astype(done_wide.dtype)
+            wide_write(which, k).start()
+
+    def keep_tall_tile(k):
+        @pl.when(k >= 2)
+        def _():
+            tall_write(k - 2).wait()
+
+        tile = tall_tile(half, k)
+        tall_send(k).wait_recv()
+        tile = tile + take_tall[k].astype(jnp.float32)
+        done_tall[k % 2] = tile.astype(done_tall.dtype)
+        tall_write(k).start()
+
+    units = 2 * (wide_count + tall_count)
+    each = -(-units // depth)
+    bounds = (0, wide_count, wide_count + tall_count, units - tall_count, units)
+    acts = (give_wide_tile, give_tall_tile, keep_wide_tile, keep_tall_tile)
+
+    def fill(unit, carry):
+        for act, low, high in zip(acts, bounds[:-1], bounds[1:]):
+
+            @pl.when((unit >= low) & (unit < high))
+            def _():
+                act(unit - low)
+
+        return carry
+
+    def chain_out(source):
+        up = jnp.where(source > level, 1, 0)
+        step = 2 * up - 1
+        slot = jnp.where(source == level - 1, depth, source)
+        return remote(
+            onward.at[up],
+            incoming.at[slot],
+            cs.at[source],
+            cr.at[slot],
+            (half, place + step * PLANE),
+        )
+
+    def chain_in(slot):
+        block = incoming.at[slot]
+        return remote(block, block, cs.at[0], cr.at[slot], (half, place))
+
+    def prob_to(source):
+        return remote(
+            prob_send.at[source],
+            prob_land.at[level],
+            ps.at[source],
+            pr.at[level],
+            (half, source * PLANE + spot),
+        )
+
+    def prob_from(source):
+        block = prob_land.at[source]
+        return remote(block, block, ps.at[source], pr.at[source], (half, source * PLANE + spot))
+
+    def add_incoming(slot):
+        chain_in(slot).wait_recv()
+        back_ref[...] += incoming[slot].astype(jnp.float32)
+
+    def settle(way, source):
+        for copy in own_rows(source):
+            copy.wait()
+        for offset in range(1, PLANE):
+            for copy in rows_from(offset, source):
+                copy.wait_recv()
+        shared_load(way, source).wait()
+
+        def columns(n, carry):
+            at = pl.ds(pl.multiple_of(n * 512, 512), 512)
+            total = shared[way, :, at].astype(jnp.float32)
+            for mate in range(PLANE):
+                total = total + dot_tn(choose_ref[source, mate], came[mate, source, :, at])
+            back_ref[:, at] = total
+            return carry
+
+        lax.fori_loop(0, width // 512, columns, 0)
+        lines = lax.broadcasted_iota(jnp.int32, (8, tokens), 0)
+        probs = jnp.zeros((8, tokens), jnp.float32)
+        for mate in range(PLANE):
+            part = jnp.dot(
+                scalars[mate, source, :, :capacity],
+                choose_ref[source, mate].astype(jnp.float32),
+                preferred_element_type=jnp.float32,
+                precision=lax.Precision.HIGHEST,
+            )
+            probs = jnp.where(lines == mate, part, probs)
+
+        @pl.when((source >= level) & (level > 0))
+        def _():
+            add_incoming(source)
+
+        @pl.when((source < level) & (level < depth - 1))
+        def _():
+            add_incoming(source)
+
+        @pl.when((source == level) & (level < depth - 1))
+        def _():
+            add_incoming(depth)
+
+        @pl.when(source == level)
+        def _():
+            prob_land[level] = probs
+
+        @pl.when(source != level)
+        def _():
+            prob_send[source] = probs
+            prob_to(source).start()
+            former = source + 2 * way - 1
+
+            @pl.when((former >= 0) & (former < depth))
+            def _():
+                chain_out(former).wait_send()
+
+            onward[way] = back_ref[...].astype(onward.dtype)
+            chain_out(source).start()
+
+    def step(i, carry):
+        s = depth - 1 - i
+        each_way(s, lambda way, source: shared_load(way, source).start())
+        lax.fori_loop(i * each, jnp.minimum((i + 1) * each, units), fill, 0)
+        each_way(s, settle)
+        return carry
+
+    lax.fori_loop(0, depth, step, 0)
+    for which in range(2):
+        wide_write(which, wide_count - 1).wait()
+        for k in (wide_count - 2, wide_count - 1):
+            wide_send(which, k).wait_send()
+    for k in (tall_count - 2, tall_count - 1):
+        tall_write(k).wait()
+        tall_send(k).wait_send()
+
+    def finish(source, carry):
+        for offset in range(1, PLANE):
+            for copy in rows_to(offset, source):
+                copy.wait_send()
+
+        @pl.when((source == level - 1) | (source == level + 1))
+        def _():
+            chain_out(source).wait_send()
+
+        @pl.when(source != level)
+        def _():
+            prob_to(source).wait_send()
+            prob_from(source).wait_recv()
+
+        prob_ref[source] = prob_land[source]
+        return carry
+
+    lax.fori_loop(0, depth, finish, 0)
+
+
+def give_back(rows, scalars, choose, shared_back, operands):
+    depth, _, capacity, tokens = choose.shape
+    width = rows.shape[-1]
+    slots, inner = operands[1].shape
+    wide_rows, tall_rows = 256 if depth <= PLANE else 128, 128
+    wide_count = width // 2 // wide_rows
+    tall_count = inner // tall_rows
+    semaphores = pltpu.SemaphoreType.DMA
+    low = rows.dtype
+    wide = jnp.float32
+    anywhere = pl.BlockSpec(memory_space=pl.ANY)
+    local = pl.BlockSpec(memory_space=pltpu.VMEM)
+    return pl.pallas_call(
+        functools.partial(return_kernel, depth),
+        out_shape=[
+            jax.ShapeDtypeStruct((tokens, width), wide),
+            jax.ShapeDtypeStruct((depth, 8, tokens), wide),
+            jax.ShapeDtypeStruct((width // 2, inner), low),
+            jax.ShapeDtypeStruct((width // 2, inner), low),
+            jax.ShapeDtypeStruct((inner, width // 2), low),
+        ],
+        in_specs=[anywhere, anywhere, local, anywhere] + [anywhere] * 5,
+        out_specs=[local, local, anywhere, anywhere, anywhere],
+        scratch_shapes=[
+            pltpu.VMEM((PLANE, depth, capacity, width), low),
+            pltpu.VMEM((PLANE, depth, 8, 128), wide),
+            pltpu.VMEM((2, tokens, width), low),
+            pltpu.VMEM((2, tokens, width), low),
+            pltpu.VMEM((depth + 1, tokens, width), low),
+            pltpu.VMEM((depth, 8, tokens), wide),
+            pltpu.VMEM((depth, 8, tokens), wide),
+        ]
+        + [pltpu.VMEM(operand.shape, low) for operand in operands]
+        + [
+            pltpu.VMEM((2, 2, wide_rows, inner), low),
+            pltpu.VMEM((2, tall_rows, width // 2), low),
+            pltpu.VMEM((2, wide_count, wide_rows, inner), low),
+            pltpu.VMEM((tall_count, tall_rows, width // 2), low),
+            pltpu.VMEM((2, wide_rows, inner), low),
+            pltpu.VMEM((2, tall_rows, width // 2), low),
+            semaphores((2, depth)),
+            semaphores((PLANE, depth)),
+            semaphores((PLANE, depth)),
+            semaphores((PLANE, depth)),
+            semaphores((PLANE, depth)),
+            semaphores((5,)),
+            semaphores((2,)),
+            semaphores((depth,)),
+            semaphores((depth + 1,)),
+            semaphores((depth,)),
+            semaphores((depth,)),
+            semaphores((2, 2)),
+            semaphores((2, wide_count)),
+            semaphores((2,)),
+            semaphores((tall_count,)),
+            semaphores((2,)),
+            semaphores((2,)),
+        ],
+        compiler_params=pltpu.CompilerParams(
+            collective_id=4, has_side_effects=True, vmem_limit_bytes=62 * MEBIBYTE
+        ),
+        cost_estimate=LONG,
+    )(rows, scalars, choose, shared_back, *operands)
 
 
 def reduce_kernel(depth, count, cut, *refs):
     parts = refs[:count]
-    out_ref = refs[count]
-    acc, inc, one_a, one_b, two_a, two_b, zin = refs[count + 1 : count + 8]
-    own_sem, cs, cr, ps, pr, qs, qr, zs, zr = refs[count + 8 :]
+    move_in, out_ref, move_out = refs[count : count + 3]
+    acc, inc, one_a, one_b, two_a, two_b, zin = refs[count + 3 : count + 10]
+    own_sem, cs, cr, ps, pr, qs, qr, zs, zr, move_sem, ms, mr = refs[count + 10 :]
     half = lax.axis_index("fsdp")
     place = lax.axis_index("expert")
     level = place // PLANE
@@ -476,6 +1293,17 @@
 
     for index in range(depth):
         visit(index, begin)
+    move_start, move_finish = exchange_along(
+        depth,
+        half,
+        place,
+        move_in,
+        lambda source: move_out.at[source],
+        move_sem.at[0],
+        ms,
+        mr,
+    )
+    move_start()
     for index in range(depth + 2):
         visit(index, stage_a)
         visit(index - 1, stage_b)
@@ -487,6 +1315,7 @@
         out_ref[pl.ds(r, 16), :] = acc[level, at, :].astype(out_ref.dtype)
         return carry
     lax.fori_loop(0, rows // 16, emit, 0)
+    move_finish()
 
     def finish(t, carry):
         for k in range(count):
@@ -508,7 +1337,7 @@
     lax.fori_loop(0, depth, finish, 0)
 
 
-def reduce_rows(parts, cut):
+def reduce_rows(parts, moved, cut):
     total = lax.axis_size("expert")
     depth = total // PLANE
     rows = parts[0].shape[0] // (2 * total)
@@ -519,9 +1348,15 @@
     low = parts[0].dtype
     return pl.pallas_call(
         functools.partial(reduce_kernel, depth, n, cut),
-        out_shape=jax.ShapeDtypeStruct((rows, width), jnp.float32),
-        in_specs=[pl.BlockSpec(memory_space=pl.ANY)] * n,
-        out_specs=pl.BlockSpec(memory_space=pltpu.VMEM),
+        out_shape=[
+            jax.ShapeDtypeStruct((rows, width), jnp.float32),
+            jax.ShapeDtypeStruct(moved.shape, moved.dtype),
+        ],
+        in_specs=[pl.BlockSpec(memory_space=pl.ANY)] * (n + 1),
+        out_specs=[
+            pl.BlockSpec(memory_space=pltpu.VMEM),
+            pl.BlockSpec(memory_space=pl.ANY),
+        ],
         scratch_shapes=[
             pltpu.VMEM((depth, group, width), low),
             pltpu.VMEM((depth, group, width), low),
@@ -539,11 +1374,15 @@
             semaphores((2, depth)),
             semaphores((2, depth)),
             semaphores((2, depth)),
+            semaphores((1,)),
+            semaphores((depth,)),
+            semaphores((depth,)),
         ],
+        cost_estimate=LONG,
         compiler_params=pltpu.CompilerParams(
-            collective_id=2, has_side_effects=True, vmem_limit_bytes=48 * MEBIBYTE
+            collective_id=2, has_side_effects=True, vmem_limit_bytes=60 * MEBIBYTE
         ),
-    )(*parts)
+    )(*parts, moved)
 
 
 def body(
@@ -594,20 +1433,64 @@
     down_width = latent_down.shape[1]
     entry_width = query_width + down_width + (-down_width) % 128
     up_width = HEADS * (NOPE + VALUE)
+    quarters = part_rows // latent_up.shape[0]
     packed = jnp.concatenate(
         [
             query_weight,
             jnp.pad(latent_down, ((0, 0), (0, (-down_width) % 128))),
-            latent_up.reshape(part_rows, -1),
+            latent_up.reshape(latent_up.shape[0], quarters, -1)
+            .transpose(1, 0, 2)
+            .reshape(part_rows, -1),
             small,
         ],
         axis=1,
     )
     cut = packed.shape[1] // 256 * 128
-    packed_full = gather_rows(packed, cut)
-    output_full = lax.all_gather(output_weight, ("fsdp", "expert"), axis=0, tiled=True)
+    route_rows = routes[0]
+    slot_rows = slot_index[0]
+    target = jnp.where(
+        slot_rows >= 0, route_rows * capacity + slot_rows, expert_total * capacity
+    )
+    target = jnp.pad(target, ((0, 0), (0, 8 - TOPK)), constant_values=expert_total * capacity).T
+    shared_width = shared_gate.shape[1] // (2 * depth)
+    shared_both = jnp.stack([shared_gate, shared_up]).reshape(
+        2, part_rows, 2, depth, shared_width
+    )
+    shared_both = shared_both.transpose(3, 1, 0, 2, 4)
+    shared_both = shared_both.reshape(depth, part_rows, 2, 2 * shared_width)
+    shared_padded = 2 * shared_width + (-2 * shared_width) % 128
+    shared_both = jnp.pad(
+        shared_both, ((0, 0), (0, 0), (0, 0), (0, shared_padded - 2 * shared_width))
+    ).reshape(depth, part_rows, 2 * shared_padded)
+    packed_full, grad_line, target_line, shared_full, sdown_full = gather_rows(
+        packed, cotangent[0], target, shared_both, shared_down, cut
+    )
+    shared_full = shared_full.reshape(D, 2 * shared_padded)
+    sdown_full = sdown_full.reshape(2 * shared_width, D)
+    expert_gate_full = lax.all_gather(expert_gate[0], "fsdp", axis=0, tiled=True)
+    expert_up_full = lax.all_gather(expert_up[0], "fsdp", axis=0, tiled=True)
+    expert_down_full = lax.all_gather(expert_down[0], "fsdp", axis=1, tiled=True)
+    packed_full, grad_line, target_line, expert_gate_full, expert_up_full, expert_down_full = (
+        lax.optimization_barrier(
+            (
+                packed_full,
+                grad_line,
+                target_line,
+                expert_gate_full,
+                expert_up_full,
+                expert_down_full,
+            )
+        )
+    )
+    output_rows, packed_full = lax.optimization_barrier((output_weight, packed_full))
+    output_full = lax.all_gather(output_rows, ("fsdp", "expert"), axis=0, tiled=True)
+    grad_line = grad_line.reshape(line_rows, D)
     entry_full = packed_full[:, :entry_width]
-    up_full = packed_full[:, entry_width:-128].reshape(-1, up_width)
+    up_parts = packed_full.reshape(2 * expert_total, quarters, latent_up.shape[0], -1)
+    up_full = jnp.concatenate(
+        [up_parts[:, k, :, entry_width:-128].reshape(LATENT, -1) for k in range(quarters)],
+        axis=1,
+    )
     small_full = packed_full[:, -128:].reshape(2 * expert_total, -1)
     gain_one, gain_latent, gain_feed, router_full = (
         small_full[:, cuts[0] : cuts[1]].reshape(-1),
@@ -616,47 +1499,9 @@
         small_full[:, cuts[3] : cuts[4]].reshape(-1, expert_total),
     )
 
-    route_rows = routes[0]
-    slot_rows = slot_index[0]
-    target = jnp.where(
-        slot_rows >= 0, route_rows * capacity + slot_rows, expert_total * capacity
-    )
-    target_line = lax.all_gather(target, "expert", axis_index_groups=line, axis=0)
-    grad_line = lax.all_gather(
-        cotangent[0], "expert", axis_index_groups=line, axis=0, tiled=True
-    )
-    shared_width = shared_gate.shape[1] // (2 * depth)
-
-    def columns_to_levels(weight):
-        rows = weight.shape[0]
-        pieces = weight.reshape(rows, 2, depth, shared_width).transpose(2, 0, 1, 3)
-        moved = lax.all_to_all(
-            pieces.reshape(depth, rows, 2 * shared_width),
-            "expert",
-            split_axis=0,
-            concat_axis=0,
-            axis_index_groups=line,
-            tiled=True,
-        )
-        across = lax.all_gather(moved, "expert", axis_index_groups=plane, axis=0)
-        whole = lax.all_gather(across, "fsdp", axis=0)
-        return whole.transpose(0, 2, 1, 3, 4).reshape(-1, 2 * shared_width)
-
-    sgate_full = columns_to_levels(shared_gate)
-    sup_full = columns_to_levels(shared_up)
-    sdown_full = lax.all_gather(
-        lax.all_gather(shared_down, "expert", axis_index_groups=plane, axis=0, tiled=True),
-        "fsdp",
-        axis=0,
-        tiled=True,
-    )
-    expert_gate_full = lax.all_gather(expert_gate[0], "fsdp", axis=0, tiled=True)
-    expert_up_full = lax.all_gather(expert_up[0], "fsdp", axis=0, tiled=True)
-    expert_down_full = lax.all_gather(expert_down[0], "fsdp", axis=1, tiled=True)
-
     slot_names = level * PLANE * capacity + jnp.arange(PLANE * capacity)
-    hits = target_line[:, None, :, :] == slot_names[None, :, None, None]
-    choose_rows = jnp.any(hits, axis=-1).astype(jnp.bfloat16)
+    hits = target_line[:, :TOPK, None, :] == slot_names[None, None, :, None]
+    choose_rows = jnp.any(hits, axis=1).astype(jnp.bfloat16)
 
     def to_experts(rows_line):
         placed = jnp.einsum(
@@ -679,8 +1524,6 @@
             axis_index_groups=plane,
             tiled=True,
         )
-
-    grad_rows = to_experts(grad_line)
 
     cosine, sine_table = rotary_table(row_count, device_half * row_count, ROPE)
     score_scale = (NOPE + ROPE) ** (-0.5)
@@ -727,61 +1570,46 @@
     residual = inputs + matmul(mixed_heads, output_full)
     feed_gain = gain_feed.astype(jnp.float32)
     mixed_low = norm_rows(residual, feed_gain).astype(jnp.bfloat16)
-    mixed_line = lax.all_gather(mixed_low, "expert", axis_index_groups=line, axis=0, tiled=True)
-    mixed_rows = to_experts(mixed_line)
-    probabilities_line = jax.nn.softmax(matmul(mixed_line, router_full), axis=-1).reshape(
-        depth, row_count, expert_total
-    )
-    level_probs = lax.dynamic_slice_in_dim(probabilities_line, level * PLANE, PLANE, axis=2)
-    hit_weights = choose_rows.astype(jnp.float32).reshape(depth, PLANE, capacity, row_count)
-    weighted = hit_weights * level_probs.transpose(0, 2, 1)[:, :, None, :]
-    slot_gate = jnp.sum(weighted, axis=-1).transpose(1, 0, 2).reshape(PLANE, depth, capacity, 1)
-    gate_column = from_experts(slot_gate).reshape(expert_total * capacity, 1)
+    grad_rows = to_experts(grad_line)
+    choose_slots = choose_rows.reshape(depth, PLANE, capacity, row_count)
+    mixed_low, grad_rows = lax.optimization_barrier((mixed_low, grad_rows))
+    mixed_rows, shared_out, shared_back, shared_grad, sdown_grad = dispatch(
+        mixed_low, choose_slots, grad_line.reshape(depth, row_count, D), shared_full, sdown_full
+    )
+    mixed_rows = mixed_rows.reshape(expert_total * capacity, D)
+    shared_out = shared_out.reshape(line_rows, D)
+    hidden_grad_raw = right_matmul(grad_rows, expert_down_full)
+    slot_probs = jax.nn.softmax(matmul(mixed_rows, router_full), axis=-1)
+    gate_column = lax.dynamic_slice_in_dim(slot_probs, place, 1, axis=1)
 
     gate_part = matmul(mixed_rows, expert_gate_full)
     up_portion = matmul(mixed_rows, expert_up_full)
     hidden_wide = jax.nn.silu(gate_part) * up_portion
     hidden = hidden_wide.astype(jnp.bfloat16)
-    expert_out = matmul(hidden, expert_down_full).astype(jnp.bfloat16)
-    returned = from_experts(expert_out)
-    slot_grad = jnp.sum(
-        expert_out.astype(jnp.float32) * grad_rows.astype(jnp.float32), axis=-1, keepdims=True
-    )
-    slot_grad_back = from_experts(slot_grad)
-    hidden_grad = right_matmul(grad_rows, expert_down_full) * gate_column
+    slot_grad = jnp.sum(hidden.astype(jnp.float32) * hidden_grad_raw, axis=-1)
+    hidden_grad = hidden_grad_raw * gate_column
     gate_part_grad, up_part_grad = swiglu_back(gate_part, up_portion, hidden_grad)
     gate_low = gate_part_grad.astype(jnp.bfloat16)
     up_low = up_part_grad.astype(jnp.bfloat16)
     input_grad = (
         right_matmul(gate_low, expert_gate_full) + right_matmul(up_low, expert_up_full)
     ).astype(jnp.bfloat16)
-    back_rows = from_experts(input_grad)
     hidden_scaled = (hidden.astype(jnp.float32) * gate_column).astype(jnp.bfloat16)
-    egate_grad = left_matmul(mixed_rows, gate_low).astype(jnp.bfloat16)
-    eup_grad = left_matmul(mixed_rows, up_low).astype(jnp.bfloat16)
-    edown_grad = left_matmul(hidden_scaled, grad_rows).astype(jnp.bfloat16)
-    expert_gate_piece, expert_up_piece, expert_down_piece = (
-        lax.psum_scatter(egate_grad, "fsdp", scatter_dimension=0, tiled=True),
-        lax.psum_scatter(eup_grad, "fsdp", scatter_dimension=0, tiled=True),
-        lax.psum_scatter(edown_grad, "fsdp", scatter_dimension=1, tiled=True),
-    )
-
-    shared_gate_part = matmul(mixed_line, sgate_full)
-    shared_up_part = matmul(mixed_line, sup_full)
-    shared_hidden = (jax.nn.silu(shared_gate_part) * shared_up_part).astype(jnp.bfloat16)
-    shared_out = matmul(shared_hidden, sdown_full)
-    shared_hidden_grad = right_matmul(grad_line, sdown_full)
-    shared_gate_grad, shared_up_grad = swiglu_back(
-        shared_gate_part, shared_up_part, shared_hidden_grad
-    )
-    shared_gate_low = shared_gate_grad.astype(jnp.bfloat16)
-    shared_up_low = shared_up_grad.astype(jnp.bfloat16)
-    shared_back = right_matmul(shared_gate_low, sgate_full) + right_matmul(
-        shared_up_low, sup_full
-    )
-    sdown_grad = left_matmul(shared_hidden, grad_line).astype(jnp.bfloat16)
-    sgate_grad = left_matmul(mixed_line, shared_gate_low).astype(jnp.bfloat16)
-    sup_grad = left_matmul(mixed_line, shared_up_low).astype(jnp.bfloat16)
+    slot_grad = jnp.pad(
+        slot_grad.reshape(PLANE, depth, 1, capacity), ((0, 0), (0, 0), (0, 0), (0, 128 - capacity))
+    )
+    back_and_shared, prob_parts, expert_gate_piece, expert_up_piece, expert_down_piece = give_back(
+        input_grad.reshape(PLANE, depth, capacity, D),
+        jnp.broadcast_to(slot_grad, (PLANE, depth, 8, 128)),
+        choose_slots,
+        shared_back,
+        [mixed_rows, gate_low, up_low, hidden_scaled, grad_rows],
+    )
+    back_and_shared, hidden = lax.optimization_barrier((back_and_shared, hidden))
+    expert_out = (matmul(hidden, expert_down_full) * gate_column).astype(jnp.bfloat16)
+    returned = from_experts(expert_out)
+
+    sdown_grad = sdown_grad[: 2 * shared_width]
 
     def scatter_plane(value):
         part = lax.psum_scatter(value, "fsdp", scatter_dimension=0, tiled=True)
@@ -789,50 +1617,13 @@
             part, "expert", scatter_dimension=0, axis_index_groups=plane, tiled=True
         )
 
-    def levels_to_columns(weight):
-        rows = D // (2 * expert_total)
-        pieces = weight.reshape(2, depth, PLANE, rows, 2 * shared_width).transpose(0, 2, 1, 3, 4)
-        summed = scatter_plane(pieces.reshape(2 * PLANE, depth, rows, 2 * shared_width))[0]
-        moved = lax.all_to_all(
-            summed, "expert", split_axis=0, concat_axis=0, axis_index_groups=line, tiled=True
-        )
-        return (
-            moved.reshape(depth, rows, 2, shared_width)
-            .transpose(1, 2, 0, 3)
-            .reshape(rows, -1)
-            .astype(jnp.float32)
-        )
-
-    sgate_piece = levels_to_columns(sgate_grad)
-    sup_piece = levels_to_columns(sup_grad)
+    shared_grad = shared_grad.reshape(2, depth, PLANE, part_rows, -1).transpose(0, 2, 1, 3, 4)
+    shared_summed = scatter_plane(shared_grad.reshape(2 * PLANE, depth, part_rows, -1))[0]
     sdown_piece = scatter_plane(sdown_grad).astype(jnp.float32)
 
-    choose_weighted = (
-        weighted.reshape(depth, PLANE * capacity, row_count).astype(jnp.bfloat16)
-    )
-
-    def combine(matrix, rows, add):
-        gathered = rows.transpose(1, 0, 2, 3).reshape(depth, PLANE * capacity, D)
-        mixed = jnp.einsum("zst,zsd->ztd", matrix, gathered, preferred_element_type=jnp.float32)
-        total = (mixed.reshape(line_rows, D) + add).astype(jnp.bfloat16)
-        return lax.psum_scatter(
-            total, "expert", scatter_dimension=0, axis_index_groups=line, tiled=True
-        ).astype(jnp.float32)
-
-    routed_and_shared = combine(choose_weighted, returned, shared_out)
-    back_and_shared = combine(choose_rows, back_rows, shared_back)
-    output = (residual + routed_and_shared).astype(jnp.bfloat16)
     out_grad = cotangent[0].astype(jnp.float32)
-
-    slot_grads = slot_grad_back.transpose(1, 0, 2, 3).reshape(depth, PLANE, capacity, 1)
-    prob_part = jnp.sum(hit_weights * slot_grads, axis=2)
-    prob_wide = lax.dynamic_update_slice_in_dim(
-        jnp.zeros((depth, expert_total, row_count), jnp.float32), prob_part, level * PLANE, axis=1
-    )
-    prob_grad = lax.psum_scatter(
-        prob_wide, "expert", scatter_dimension=0, axis_index_groups=line, tiled=True
-    )[0].T
-    probabilities = lax.dynamic_index_in_dim(probabilities_line, level, axis=0, keepdims=False)
+    probabilities = jax.nn.softmax(matmul(mixed_low, router_full), axis=-1)
+    prob_grad = prob_parts[:, :PLANE].reshape(expert_total, row_count).T
     logit_low = (
         probabilities * (prob_grad - jnp.sum(probabilities * prob_grad, axis=-1, keepdims=True))
     ).astype(jnp.bfloat16)
@@ -894,7 +1685,16 @@
     expanded_low = (expanded_grad[row_count:] + returned_expanded).astype(jnp.bfloat16)
     own_rope = key_rope_grad[row_count:] + returned_rope
     latent_grad = right_matmul(expanded_low, up_full)
-    up_weight_grad = left_matmul(latent, expanded_low)
+    quarter = up_width // quarters
+    up_weight_grad = jnp.stack(
+        [
+            left_matmul(latent, expanded_low[:, k * quarter : (k + 1) * quarter])
+            .astype(jnp.bfloat16)
+            .reshape(2 * expert_total, latent_up.shape[0], quarter)
+            for k in range(quarters)
+        ],
+        axis=1,
+    ).reshape(2 * expert_total * part_rows, quarter)
     compressed_latent_grad, latent_gain_grad = norm_back(
         compressed[:, :LATENT], latent_gain, latent_grad
     )
@@ -919,6 +1719,22 @@
     entry_grad = left_matmul(normed_low, entry_low).astype(jnp.bfloat16)
     input_add, first_gain_grad = norm_back(inputs, gain_first, normed_grad)
     token_grad = residual_grad + input_add
+    late = entry_low[0, 0].astype(jnp.float32) * 0.0
+    routed = jnp.einsum(
+        "zst,zsd->ztd",
+        choose_rows,
+        returned.transpose(1, 0, 2, 3).reshape(depth, PLANE * capacity, D),
+        preferred_element_type=jnp.float32,
+    )
+    routed_and_shared = lax.psum_scatter(
+        (routed.reshape(line_rows, D) + shared_out + late).astype(jnp.bfloat16),
+        "expert",
+        scatter_dimension=0,
+        axis_index_groups=line,
+        tiled=True,
+    ).astype(jnp.float32)
+    output = (residual + routed_and_shared).astype(jnp.bfloat16)
+
     small_grad = jnp.concatenate(
         [
             first_gain_grad.reshape(-1, gain_width),
@@ -929,18 +1745,25 @@
         axis=1,
     )
     small_grad = jnp.pad(small_grad, ((0, 0), (0, 128 * part_rows - small_grad.shape[1])))
-    packed_piece = reduce_rows(
+    packed_piece, shared_back_moved = reduce_rows(
         [
             entry_grad,
-            up_weight_grad.astype(jnp.bfloat16).reshape(gain_width * 2 * expert_total, -1),
+            up_weight_grad,
+            output_grad.astype(jnp.bfloat16),
             small_grad.astype(jnp.bfloat16).reshape(-1, 128),
         ],
-        cut,
+        shared_summed,
+        (packed.shape[1] + D) // 256 * 128,
     )
     small_piece = packed_piece[:, -128:].reshape(-1)
-    output_piece = lax.psum_scatter(
-        output_grad.astype(jnp.bfloat16), ("fsdp", "expert"), scatter_dimension=0, tiled=True
-    ).astype(jnp.float32)
+    shared_pieces = (
+        shared_back_moved.reshape(depth, part_rows, 2, shared_padded)[..., : 2 * shared_width]
+        .reshape(depth, part_rows, 2, 2, shared_width)
+        .transpose(2, 1, 3, 0, 4)
+        .reshape((2,) + shared_gate.shape)
+        .astype(jnp.float32)
+    )
+    output_piece = packed_piece[:, -128 - D : -128]
 
     return (
         output[None],
@@ -949,12 +1772,15 @@
         packed_piece[:, :query_width],
         packed_piece[:, query_width : query_width + down_width],
         small_piece[cuts[1] : cuts[2]],
-        packed_piece[:, entry_width:-128].reshape(latent_up.shape),
+        packed_piece[:, entry_width : -128 - D]
+        .reshape(quarters, latent_up.shape[0], -1)
+        .transpose(1, 0, 2)
+        .reshape(latent_up.shape),
         output_piece,
         small_piece[cuts[2] : cuts[3]],
         small_piece[cuts[3] : cuts[4]].reshape(gain_width, expert_total),
-        sgate_piece,
-        sup_piece,
+        shared_pieces[0],
+        shared_pieces[1],
         sdown_piece,
         expert_gate_piece.astype(jnp.float32)[None],
         expert_up_piece.astype(jnp.float32)[None],

time: 1260 us -> 888 us (0.70)
  waiting for transfers between devices: 413 us -> 111 us
  Pallas kernels: 305 us -> 452 us
  matrix products: 255 us -> 161 us
  blocking collectives: 45.4 us -> 0 us
  local copies, waits for them, and re-layouts: 118 us -> 87.3 us
  starting transfers between devices: 45.6 us -> 18.4 us
    pallas_call x1 -> x3, Pallas kernels: 122 us -> 311 us  [the longest x1 145 us: gather_rows(): pl.pallas_call(functools.partial(gather_kernel, depth, cut), out_shape=[j...]
    all_gather x9 -> x1, waiting for transfers between devices: 138 us -> 51.6 us  [body(): lax.all_gather(output_rows, ('fsdp', 'expert'), axis=0, tiled=True)]
    all_to_all x4 -> x1, waiting for transfers between devices: 101 us -> 31.1 us  [from_experts(): lax.all_to_all(rows.reshape(PLANE, depth, capacity, -1), 'expert', split_...]
    unnamed x28 -> x11, waiting for transfers between devices: 86.9 us -> 27.8 us
    dot_general x10 -> x7, matrix products: 73.3 us -> 17.2 us  [left_matmul(): lax.dot_general(former, latter, (((0,), (0,)), ((), ())), preferred_eleme...]
    all_to_all x2 -> x1, waiting for transfers between devices: 55.2 us -> 0.01 us  [to_experts(): lax.all_to_all(placed, 'expert', split_axis=0, concat_axis=0, axis_index_...]
    pallas_call x1, Pallas kernels: 182 us -> 141 us  [reduce_rows(): pl.pallas_call(functools.partial(reduce_kernel, depth, n, cut), out_shape...]
    all_to_all x2 -> x0, blocking collectives: 31.8 us -> none  [columns_to_levels(): lax.all_to_all(pieces.reshape(depth, rows, 2 * shared_width), 'expert', s...]
  transfers between devices with their start and end apart: 37 -> 15, of which waited for: 14 -> 3; matrix products, arithmetic and copies ran while one was open for 33% -> 29% of each run, Pallas kernels for 24% -> 25%
where the time goes in v3:
time: 888 us
  Pallas kernels  452 us (51%)
  matrix products  161 us (18%)
  waiting for transfers between devices  111 us (12%)
  local copies, waits for them, and re-layouts  87.3 us (10%)
  other arithmetic  41.8 us (5%)
  starting transfers between devices  18.4 us (2%)
  between operations  16.7 us (2%)
    pallas_call x1, Pallas kernels, gather_rows(): pl.pallas_call(functools.partial(gather_kernel, depth, cut), out_shape=[j...  145 us
    pallas_call x1, Pallas kernels, reduce_rows(): pl.pallas_call(functools.partial(reduce_kernel, depth, n, cut), out_shape...  141 us
    pallas_call x1, Pallas kernels, dispatch(): pl.pallas_call(functools.partial(dispatch_kernel, depth), out_shape=[jax....  87.5 us
    pallas_call x1, Pallas kernels, give_back(): pl.pallas_call(functools.partial(return_kernel, depth), out_shape=[jax.Sh...  78.3 us
    dot_general x7, matrix products, right_matmul(): lax.dot_general(former, latter, (((1,), (1,)), ((), ())), preferred_eleme...  60.4 us
    dot_general x8, matrix products, matmul(): return jnp.dot(former, latter, preferred_element_type=jnp.float32)  57.8 us
    all_gather x1, waiting for transfers between devices, body(): lax.all_gather(output_rows, ('fsdp', 'expert'), axis=0, tiled=True)  51.6 us
    all_to_all x1, waiting for transfers between devices, from_experts(): lax.all_to_all(rows.reshape(PLANE, depth, capacity, -1), 'expert', split_...  31.1 us
  transfers between devices with their start and end apart: 15, of which 3 were waited for; matrix products, arithmetic and copies ran while one was open for 29% of the time, Pallas kernels for 25%

profile of v3, /device:TPU:0, one launch (start us, length us, event | category | flops | bytes accessed | tf_op | source)
XLA Modules:
  0.0 887.6 jit_solution(18036674610315757926)
XLA Ops:
  16.9 145.3 %shard_map.306 = (bf16[2048,4864]{1,0:T(8,128)(2,1)}, bf16[4,192,2048]{2,1,0:T(8,128)(2,1)}, s32[4,8,192]{2,1,0:T(8,128)}, bf16[2,4,4,64,1536]{4,3,2,1,0:T(8,128)(2,1)}, bf16[2,4,88,2048]{3,2,1,0:T(8,128)(2,1)}) custom-call(bf16[64,4864]{1,0:T(8,128)(2,1)} %fusion.54.refs_0_, bf16[192,2048]{1,0:T(8,128)(2,1)} %bitcast.222, ...), custom_call_target="tpu_custom_call" | custom-call | flops 99999997952 | tf_op jit(solution)/shard_map/pallas_call | solution.py:453
  169.2 7.4 fusion.2
  176.6 1.8 slice.223
  180.2 2.3 collective-permute-start.1
  184.7 2.2 collective-permute-start
  186.9 3.1 reshape.421
  191.1 2.2 fusion.110
  193.3 3.0 copy.214
  196.3 2.9 copy.213
  199.2 2.3 convolution_convert_fusion.3
  201.5 2.6 copy.273
  204.1 5.0 all-to-all-start
  209.1 2.7 fusion.109
  212.2 4.4 convolution_convert_fusion.2
  219.9 1.8 fusion.116
  223.9 1.5 fusion.36
  225.4 51.6 %all-gather.8.cloned.1.call-done = bf16[2048,2048]{1,0:T(8,128)(2,1)} async-done(((bf16[64,2048]{1,0:T(8,128)(2,1)}), bf16[2048,2048]{1,0:T(8,128)(2,1)}) %all-gather.8.cloned.1.call-update) | async-done | bytes 8388624 | tf_op jit(solution)/shard_map/all_gather | solution.py:1486
  277.0 5.3 multiply_reduce_fusion.3
  284.6 87.5 %shard_map.307 = (bf16[4,4,72,2048]{3,2,1,0:T(8,128)(2,1)}, bf16[4,192,2048]{2,1,0:T(8,128)(2,1)}, bf16[4,192,2048]{2,1,0:T(8,128)(2,1)}, bf16[2048,1536]{1,0:T(8,128)(2,1)}, bf16[768,2048]{1,0:T(8,128)(2,1)}) custom-call(bf16[192,2048]{1,0:T(8,128)(2,1)} %multiply_convert_fusion.4.refs_0_, bf16[4,4,72,192]{3,2,1,0:T(8,128)(2,1)} %bitcast.223, ...), custom_call_target="tpu_custom_call" | custom-call | flops 99999997952 | tf_op jit(solution)/shard_map/pallas_call | solution.py:726
  372.0 3.8 slice.221
  375.9 6.4 copy.205
  383.7 11.6 %fusion.120 = f32[1152,1408]{1,0:T(8,128)} fusion(bf16[1152,2048]{1,0:T(8,128)(2,1)S(1)} %bitcast.197, bf16[2048,1408]{1,0:T(8,128)(2,1)} %bitcast.236), kind=kOutput, calls=%fused_computation.221 | convolution fusion | flops 6643777536 | bytes 16973824 | tf_op jit(solution)/shard_map/dot_general | solution.py:81
  395.3 9.4 %fusion.119 = f32[1152,1408]{1,0:T(8,128)S(1)} fusion(bf16[1152,2048]{1,0:T(8,128)(2,1)} %bitcast.23.refs_8_, bf16[1408,2048]{1,0:T(8,128)(2,1)S(1)} %bitcast.233), kind=kOutput, calls=%fused_computation.220 | convolution fusion | flops 6643777536 | bytes 16973824 | tf_op jit(solution)/shard_map/dot_general | solution.py:91
  404.8 15.3 %fusion.6 = (bf16[1152,1408]{1,0:T(8,128)(2,1)}, bf16[1152,1408]{1,0:T(8,128)(2,1)}, bf16[1152,1408]{1,0:T(8,128)(2,1)}, bf16[1152,1408]{1,0:T(8,128)(2,1)}) fusion(f32[1152]{0:T(1024)S(1)} %divide_reduce_fusion, f32[1152,1408]{1,0:T(8,128)} %fusion.120, f32[1152,1408]{1,0:T(8,128)S(1)} %fusion.119, bf16[1152,2048]{1,0:T(8,128)(2,1)S(1)} %bitcast.198, ...), kind=kOutput, calls=%fused_computation.14 | convolution fusion | flops 6676217856 | bytes 36442624 | tf_op jit(solution)/shard_map/dot_general | solution.py:81
  420.1 2.6 fusion.5
  422.8 13.2 %fusion.121 = f32[1152,2048]{1,0:T(8,128)} fusion(bf16[1152,1408]{1,0:T(8,128)(2,1)} %get-tuple-element.152.refs_5_, bf16[2048,1408]{1,0:T(8,128)(2,1)} %bitcast.237), kind=kOutput, calls=%fused_computation.222 | convolution fusion | flops 6643777536 | bytes 18448384 | tf_op jit(solution)/shard_map/dot_general | solution.py:91
  436.0 13.3 %add_convert_fusion = bf16[1152,2048]{1,0:T(8,128)(2,1)} fusion(f32[1152,2048]{1,0:T(8,128)} %fusion.121, bf16[1152,1408]{1,0:T(8,128)(2,1)} %get-tuple-element.153.refs_6_, bf16[2048,1408]{1,0:T(8,128)(2,1)} %bitcast.235), kind=kOutput, calls=%fused_computation.7 | convolution fusion | flops 6648496128 | bytes 23166976 | tf_op jit(solution)/shard_map/dot_general | solution.py:91
  450.0 78.3 %shard_map.308 = (f32[192,2048]{1,0:T(8,128)}, f32[4,8,192]{2,1,0:T(8,128)}, bf16[1024,1408]{1,0:T(8,128)(2,1)}, bf16[1024,1408]{1,0:T(8,128)(2,1)}, bf16[1408,1024]{1,0:T(8,128)(2,1)}) custom-call(bf16[4,4,72,2048]{3,2,1,0:T(8,128)(2,1)} %bitcast.240, f32[4,4,8,128]{3,2,1,0:T(8,128)} %broadcast_in_dim.53.refs_1_, bf16[4,4,72,192]{3,2,1,0:T(8,128)(2,1)} %bitcast.224, ...), custom_call_target="tpu_custom_call" | custom-call | flops 99999997952 | tf_op jit(solution)/shard_map/pallas_call | solution.py:1088
  528.3 12.1 %fusion.4 = bf16[1152,2048]{1,0:T(8,128)(2,1)} fusion(bf16[1152,1408]{1,0:T(8,128)(2,1)} %get-tuple-element.63, bf16[1408,2048]{1,0:T(8,128)(2,1)} %bitcast.230, f32[1152]{0:T(1024)S(1)} %divide_reduce_fusion), kind=kOutput, calls=%fused_computation.10 | convolution fusion | flops 6648496128 | bytes 13734400 | tf_op jit(solution)/shard_map/dot_general | solution.py:81
  540.4 5.3 all-to-all-start.1
  546.3 2.7 multiply_reduce_fusion.1
  549.6 6.8 fusion.35
  556.5 4.2 multiply_reduce_fusion
  566.6 2.4 fusion.32
  569.6 2.0 copy.194
  571.6 3.0 convert_element_type.236
  575.8 31.1 %all-to-all-done.1 = bf16[4,4,72,2048]{3,2,1,0:T(8,128)(2,1)} async-done(((bf16[4,4,72,2048]{3,2,1,0:T(8,128)(2,1)}), bf16[4,4,72,2048]{3,2,1,0:T(8,128)(2,1)}, u32[]{:S(2)}, u32[]{:S(2)}) %all-to-all-start.1) | async-done | bytes 4718624 | tf_op jit(solution)/shard_map/all_to_all | solution.py:1519
  606.9 2.9 copy.189
  610.3 3.8 add_convert_fusion.1
  615.1 1.5 fusion.41
  618.9 4.8 convolution_bitcast_fusion
  623.8 1.6 fusion.14
  625.4 3.9 copy.196
  629.3 1.9 collective-permute-start.2
  631.2 7.3 convolution_convert_fusion.1.refs_2_
  638.5 2.9 bitcast_convert_fusion.2
  641.6 3.2 bitcast_convert_fusion.1
  645.4 3.2 bitcast_convert_fusion
  648.7 3.1 fusion.13
  653.6 3.8 copy.197
  658.0 1.9 add_convert_fusion.2
  660.7 3.1 multiply_reduce_fusion.4
  665.1 11.8 %fusion.19 = (bf16[2048]{0:T(1024)(128)(2,1)S(1)}, f32[192]{0:T(256)S(1)}, f32[192,2048]{1,0:T(8,128)}) fusion(bf16[1,192,2048]{2,1,0:T(8,128)(2,1)S(1)} %copy-done.14, f32[192]{0:T(256)S(1)} %copy-done.82, f32[2048]{0:T(1024)S(1)} %copy-done.69, bf16[2048,4864]{1,0:T(8,128)(2,1)} %get-tuple-element.49, bf16[192,640]{1,0:T(8,128)(2,1)S(1)} %fusion.71, ...), kind=kOutput, calls=%fused_computation.62 | convolution fusion | flops 2924836608 | bytes 19002880 | tf_op jit(solution)/shard_map/dot_general | solution.py:91
  680.3 2.4 pad_maximum_fusion.2
  683.7 1.6 fusion.22
  685.3 7.8 convolution_convert_fusion.refs_0_
  693.1 1.9 convert_element_type.255
  695.1 2.3 fusion.42
  697.4 25.6 %reduce-scatter.16.cloned.1.call-done = bf16[1,4,64,1536]{3,2,1,0:T(8,128)(2,1)} async-done(((bf16[4,4,64,1536]{3,2,1,0:T(8,128)(2,1)}), bf16[1,4,64,1536]{3,2,1,0:T(8,128)(2,1)}) %reduce-scatter.16.cloned.1.call-update) | async-done | bytes 786448
  723.0 140.9 %shard_map.309 = (f32[64,6912]{1,0:T(8,128)}, bf16[4,64,1536]{2,1,0:T(8,128)(2,1)}) custom-call(bf16[2048,3712]{1,0:T(8,128)(2,1)} %convolution_convert_fusion.refs_0_, bf16[2048,1024]{1,0:T(8,128)(2,1)} %bitcast.205, bf16[2048,2048]{1,0:T(8,128)(2,1)} %convolution_convert_fusion.1.refs_2_, bf16[2048,128]{1,0:T(8,128)(2,1)} %reshape.439.refs_3_, ...), custom_call_target="tpu_custom_call" | custom-call | flops 99999997952 | tf_op jit(solution)/shard_map/pallas_call | solution.py:1349
  865.9 1.6 slice.211
  868.4 1.9 slice.214
  870.3 2.1 slice.210
  874.6 2.2 reshape.454
  (371 shorter events, 61.4 us)
Async XLA Ops:
  7.2 155.1 %all-gather.10.cloned.1.call-start = ((), (), s32[]{:S(2)}) async-start(), calls=%async_computation.11 | async-start | bytes 8650752 | tf_op jit(solution)/shard_map/all_gather | solution.py:1470
  8.0 154.3 %all-gather.12.cloned.1.call-start = ((), (), s32[]{:S(2)}) async-start(), calls=%async_computation.12 | async-start | bytes 8650752 | tf_op jit(solution)/shard_map/all_gather | solution.py:1471
  8.8 153.5 %all-gather.14.cloned.1.call-start = ((), (), s32[]{:S(2)}) async-start(), calls=%async_computation.13 | async-start | bytes 8650752 | tf_op jit(solution)/shard_map/all_gather | solution.py:1472
  9.5 267.5 %all-gather.8.cloned.1.call-start = ((), (), s32[]{:S(2)}) async-start(), calls=%async_computation.7 | async-start | bytes 8650752 | tf_op jit(solution)/shard_map/all_gather | solution.py:1486
  16.9 145.4 %copy-start.95 = (s32[1,384]{1,0:T(1,128)S(1)}, s32[1,384]{1,0:T(1,128)}, u32[]{:S(2)}) copy-start(s32[1,384]{1,0:T(1,128)} %param.20) | copy-start | bytes 4612
  16.9 145.7 %copy-start.12 = (bf16[1,192,2048]{2,1,0:T(8,128)(2,1)S(1)}, bf16[1,192,2048]{2,1,0:T(8,128)(2,1)}, u32[]{:S(2)}) copy-start(bf16[1,192,2048]{2,1,0:T(8,128)(2,1)} %param.19) | copy-start | bytes 2359300
  162.4 16.9 %copy-start.101 = (f32[32]{0:T(128)}, f32[32]{0:T(128)S(1)}, u32[]{:S(2)}) copy-start(f32[32]{0:T(128)S(1)} %multiply_exponential_fusion) | copy-start | bytes 388
  162.4 16.9 %copy-start.96 = (f32[192]{0:T(256)}, f32[192]{0:T(256)S(1)}, u32[]{:S(2)}) copy-start(f32[192]{0:T(256)S(1)} %fusion.100) | copy-start | bytes 2308
  162.9 13.7 %copy-start.81 = (f32[192]{0:T(256)}, f32[192]{0:T(256)S(1)}, u32[]{:S(2)}) copy-start(f32[192]{0:T(256)S(1)} %fusion.97) | copy-start | bytes 2308
  165.1 18.5 %copy-start.79 = (f32[512]{0:T(512)}, f32[512]{0:T(512)S(1)}, u32[]{:S(2)}) copy-start(f32[512]{0:T(512)S(1)} %reshape.448) | copy-start | bytes 6148
  165.3 117.1 %copy-start.72 = (f32[2048]{0:T(1024)}, f32[2048]{0:T(1024)S(1)}, u32[]{:S(2)}) copy-start(f32[2048]{0:T(1024)S(1)} %reshape.449) | copy-start | bytes 24580
  165.3 11.3 %copy-start.68 = (f32[2048]{0:T(1024)}, f32[2048]{0:T(1024)S(1)}, u32[]{:S(2)}) copy-start(f32[2048]{0:T(1024)S(1)} %reshape.447) | copy-start | bytes 24580
  179.5 32.4 %copy-start.59 = (f32[192,32]{0,1:T(8,128)}, f32[192,32]{0,1:T(8,128)S(1)}, u32[]{:S(2)}) copy-start(f32[192,32]{0,1:T(8,128)S(1)} %get-tuple-element.176) | copy-start | bytes 73732
  179.5 32.4 %copy-start.61 = (f32[192,32]{0,1:T(8,128)}, f32[192,32]{0,1:T(8,128)S(1)}, u32[]{:S(2)}) copy-start(f32[192,32]{0,1:T(8,128)S(1)} %get-tuple-element.177) | copy-start | bytes 73732
  179.5 40.3 %copy-start.63 = (bf16[192,32]{0,1:T(8,128)(2,1)}, bf16[192,32]{0,1:T(8,128)(2,1)S(1)}, u32[]{:S(2)}) copy-start(bf16[192,32]{0,1:T(8,128)(2,1)S(1)} %get-tuple-element.172) | copy-start | bytes 36868
  179.5 40.3 %copy-start.65 = (bf16[192,32]{0,1:T(8,128)(2,1)}, bf16[192,32]{0,1:T(8,128)(2,1)S(1)}, u32[]{:S(2)}) copy-start(bf16[192,32]{0,1:T(8,128)(2,1)S(1)} %get-tuple-element.173) | copy-start | bytes 36868
  180.2 39.6 %collective-permute-start.1 = (bf16[192,64]{0,1:T(8,128)(2,1)}, bf16[192,64]{0,1:T(8,128)(2,1)S(1)}, u32[]{:S(2)}, u32[]{:S(2)}) collective-permute-start(bf16[192,64]{0,1:T(8,128)(2,1)} %pad_maximum_fusion.12), channel_id=1, source_target_pairs={{0,16},{1,17},{2,18},{3,19},{4,20},{5,21},{6,22},{7,23},{8,24},{9,... | collective-permute-start | bytes 73736 | tf_op jit(solution)/shard_map/ppermute | solution.py:27
  184.7 27.4 %copy-start.23 = (bf16[192,512]{1,0:T(8,128)(2,1)}, bf16[192,512]{1,0:T(8,128)(2,1)S(1)}, u32[]{:S(2)}) copy-start(bf16[192,512]{1,0:T(8,128)(2,1)S(1)} %multiply_convert_fusion.5) | copy-start | bytes 589828
  184.7 27.4 %collective-permute-start = (bf16[192,512]{1,0:T(8,128)(2,1)S(1)}, bf16[192,512]{1,0:T(8,128)(2,1)}, u32[]{:S(2)}, u32[]{:S(2)}) collective-permute-start(bf16[192,512]{1,0:T(8,128)(2,1)S(1)} %multiply_convert_fusion.5), channel_id=1, source_target_pairs={{0,16},{1,17},{2,18},{3,19},{4,20},{5,21},{6,22},{7,23},{8,24},{9,... | collective-permute-start | bytes 589832 | tf_op jit(solution)/shard_map/ppermute | solution.py:27
  193.3 5.9 copy-start.17
  204.1 80.5 %all-to-all-start = ((bf16[4,4,72,2048]{3,2,1,0:T(8,128)(2,1)}), bf16[4,4,72,2048]{3,2,1,0:T(8,128)(2,1)}, u32[]{:S(2)}, u32[]{:S(2)}) async-start(bf16[4,4,72,2048]{3,2,1,0:T(8,128)(2,1)} %bitcast.191), calls=%async_computation | async-start | bytes 9437184 | tf_op jit(solution)/shard_map/all_to_all | solution.py:1514
  209.1 340.4 %reduce-scatter.14.cloned.1.call-start = ((), (), s32[]{:S(2)}) async-start(), calls=%async_computation.10 | async-start | bytes 4325376 | tf_op jit(solution)/shard_map/reduce_scatter | solution.py:1615
  211.9 4.7 copy-start.44
  211.9 4.7 copy-start.46
  211.9 4.7 copy-start.48
  211.9 4.7 copy-start.50
  212.1 7.7 copy-start.38
  212.1 7.7 copy-start.40
  218.2 4.9 copy-start.8
  223.9 53.1 %copy-start.13 = (bf16[1,192,2048]{2,1,0:T(8,128)(2,1)S(1)}, bf16[1,192,2048]{2,1,0:T(8,128)(2,1)}, u32[]{:S(2)}) copy-start(bf16[1,192,2048]{2,1,0:T(8,128)(2,1)} %param.19) | copy-start | bytes 2359300
  225.4 56.9 %copy-start.25 = (bf16[16,24,8,128]{3,2,1,0:T(8,128)(2,1)}, bf16[16,24,8,128]{3,2,1,0:T(8,128)(2,1)S(1)}, u32[]{:S(2)}) copy-start(bf16[16,24,8,128]{3,2,1,0:T(8,128)(2,1)S(1)} %fusion.36) | copy-start | bytes 2359300
  282.3 89.7 %copy-start.99 = (f32[192]{0:T(256)}, f32[192]{0:T(256)S(1)}, u32[]{:S(2)}) copy-start(f32[192]{0:T(256)S(1)} %get-tuple-element.180) | copy-start | bytes 2308
  375.8 6.5 slice-start.2
  375.9 282.1 %reduce-scatter.12.cloned.1.call-start = ((), (), s32[]{:S(2)}) async-start(), calls=%async_computation.9 | async-start | bytes 9437184 | tf_op jit(solution)/shard_map/reduce_scatter | solution.py:1615
  375.9 6.4 slice-start.3
  375.9 6.4 copy-start.10
  382.3 13.0 %slice-start.4 = ((s8[5767168]{0:T(1024)(128)(4,1)}), s8[4194304]{0:T(1024)(128)(4,1)S(1)}, s32[]{:S(2)}) async-start(s8[5767168]{0:T(1024)(128)(4,1)} %bitcast.231), calls=%async_computation.20 | async-start | bytes 8388608
  383.7 11.6 %slice-start.5 = ((s8[5767168]{0:T(1024)(128)(4,1)}), s8[1572864]{0:T(1024)(128)(4,1)S(1)}, s32[]{:S(2)}) async-start(s8[5767168]{0:T(1024)(128)(4,1)} %bitcast.231), calls=%async_computation.21 | async-start | bytes 3145728
  540.3 5.4 copy-start.92
  540.3 5.4 copy-start.11
  540.3 5.4 copy-start.18
  540.4 5.9 copy-start.4
  540.4 5.9 copy-start.73
  540.4 5.9 copy-start.85
  540.4 66.5 %all-to-all-start.1 = ((bf16[4,4,72,2048]{3,2,1,0:T(8,128)(2,1)}), bf16[4,4,72,2048]{3,2,1,0:T(8,128)(2,1)}, u32[]{:S(2)}, u32[]{:S(2)}) async-start(bf16[4,4,72,2048]{3,2,1,0:T(8,128)(2,1)} %bitcast.203), calls=%async_computation.1 | async-start | bytes 9437184 | tf_op jit(solution)/shard_map/all_to_all | solution.py:1519
  545.7 147.5 %reduce-scatter.18.cloned.1.call-start = ((), (), s32[]{:S(2)}) async-start(), calls=%async_computation.15 | async-start | bytes 1802240
  549.5 7.0 copy-start.6
  549.5 6.9 copy-start.9
  549.5 6.9 copy-start.55
  549.5 145.5 %reduce-scatter.10.cloned.1.call-start = ((), (), s32[]{:S(2)}) async-start(), calls=%async_computation.8 | async-start | bytes 3932160 | tf_op jit(solution)/shard_map/reduce_scatter | solution.py:1729
  549.6 11.2 %slice-start = ((s8[4718592]{0:T(1024)(128)(4,1)}), s8[524288]{0:T(1024)(128)(4,1)S(1)}, s32[]{:S(2)}) async-start(s8[4718592]{0:T(1024)(128)(4,1)} %bitcast.187), calls=%async_computation.16 | async-start | bytes 1048576
  574.6 35.2 %copy-start.27 = (bf16[192,3072]{1,0:T(8,128)(2,1)}, bf16[192,3072]{1,0:T(8,128)(2,1)S(1)}, u32[]{:S(2)}) copy-start(bf16[192,3072]{1,0:T(8,128)(2,1)S(1)} %convert_element_type.236) | copy-start | bytes 3538948
  614.2 108.8 %reduce-scatter.16.cloned.1.call-start = ((), (), s32[]{:S(2)}) async-start(), calls=%async_computation.14 | async-start | bytes 3932160
  616.6 40.7 %collective-permute-start.3 = (bf16[192,64]{0,1:T(8,128)(2,1)S(1)}, bf16[192,64]{0,1:T(8,128)(2,1)S(1)}, u32[]{:S(2)}, u32[]{:S(2)}) collective-permute-start(bf16[192,64]{0,1:T(8,128)(2,1)S(1)} %slice.297), channel_id=1, source_target_pairs={{16,0},{17,1},{18,2},{19,3},{20,4},{21,5},{22,6},{23,7},{24,8},{25... | collective-permute-start | bytes 73736 | tf_op jit(solution)/shard_map/ppermute | solution.py:27
  618.9 4.9 copy-start.1
  629.3 9.3 %copy-start.37 = (bf16[1024,1408]{1,0:T(8,128)(2,1)S(1)}, bf16[1024,1408]{1,0:T(8,128)(2,1)}, u32[]{:S(2)}) copy-start(bf16[1024,1408]{1,0:T(8,128)(2,1)} %get-tuple-element.71) | copy-start | bytes 8650756
  629.3 28.8 %collective-permute-start.2 = (bf16[192,4096]{1,0:T(8,128)(2,1)}, bf16[192,4096]{1,0:T(8,128)(2,1)}, u32[]{:S(2)}, u32[]{:S(2)}) collective-permute-start(bf16[192,4096]{1,0:T(8,128)(2,1)} %copy.196), channel_id=1, source_target_pairs={{16,0},{17,1},{18,2},{19,3},{20,4},{21,5},{22,6},{23,7},{24,8},{25... | collective-permute-start | bytes 4718600 | tf_op jit(solution)/shard_map/ppermute | solution.py:27
  660.6 4.4 copy-start.14
  665.1 12.1 %copy-start.67 = (bf16[32,1024]{1,0:T(8,128)(2,1)S(1)}, bf16[32,1024]{1,0:T(8,128)(2,1)}, u32[]{:S(2)}) copy-start(bf16[32,1024]{1,0:T(8,128)(2,1)} %reshape.438) | copy-start | bytes 196612
  665.1 13.3 %copy-start.87 = (f32[192]{0:T(256)S(1)}, f32[192]{0:T(256)}, u32[]{:S(2)}) copy-start(f32[192]{0:T(256)} %copy-done.86) | copy-start | bytes 2308
  665.1 13.3 %copy-start.22 = (bf16[192,4096]{1,0:T(8,128)(2,1)S(1)}, bf16[192,4096]{1,0:T(8,128)(2,1)}, u32[]{:S(2)}) copy-start(bf16[192,4096]{1,0:T(8,128)(2,1)} %copy-done.21) | copy-start | bytes 4718596
  665.1 13.3 %copy-start.24 = (bf16[192,512]{1,0:T(8,128)(2,1)S(1)}, bf16[192,512]{1,0:T(8,128)(2,1)}, u32[]{:S(2)}) copy-start(bf16[192,512]{1,0:T(8,128)(2,1)} %copy-done.23) | copy-start | bytes 589828
  685.3 9.8 %copy-start.5 = (f32[192,2048]{1,0:T(8,128)S(1)}, f32[192,2048]{1,0:T(8,128)}, u32[]{:S(2)}) copy-start(f32[192,2048]{1,0:T(8,128)} %copy-done.3) | copy-start | bytes 4718596
  863.9 8.5 copy-start.53
  (64 other events, 163.3 us)
Sparse Core Ops, SparseCore 0:
  9.6 18.6 all-gather.9
  29.8 17.1 all-gather.11
  48.6 17.1 all-gather.13
  162.4 114.5 all-gather.7
  376.0 8.2 reduce-scatter.13
  436.1 12.7 reduce-scatter.11
  549.6 54.2 reduce-scatter.17
  614.3 61.3 reduce-scatter.9
  679.0 43.9 reduce-scatter.15

commit v4 on v3

--- a/solution.py
+++ b/solution.py
@@ -21,12 +21,6 @@
 FLOOR_SCORE = -1e30
 
 
-def passed_along(value, axis, steps):
-    count = lax.axis_size(axis)
-    first, last = (max(0, -steps), min(count, count - steps))
-    return lax.ppermute(value, axis, [(source, source + steps) for source in range(first, last)])
-
-
 def norm_rows(values, gain):
     return values * lax.rsqrt(jnp.mean(values * values, axis=-1, keepdims=True) + EPSILON) * gain
 
@@ -51,32 +45,6 @@
     return (jnp.cos(angles), jnp.sin(angles))
 
 
-def rotate_forward(values, cosine, sine_table):
-    middle = values.shape[-1] // 2
-    front_half = values[..., :middle]
-    back_half = values[..., middle:]
-    return jnp.concatenate(
-        [
-            front_half * cosine - back_half * sine_table,
-            back_half * cosine + front_half * sine_table,
-        ],
-        axis=-1,
-    )
-
-
-def rotate_backward(values, cosine, sine_table):
-    middle = values.shape[-1] // 2
-    front_half = values[..., :middle]
-    back_half = values[..., middle:]
-    return jnp.concatenate(
-        [
-            front_half * cosine + back_half * sine_table,
-            back_half * cosine - front_half * sine_table,
-        ],
-        axis=-1,
-    )
-
-
 def matmul(former, latter):
     return jnp.dot(former, latter, preferred_element_type=jnp.float32)
 
@@ -91,25 +59,13 @@
     return lax.dot_general(
         former, latter, (((1,), (1,)), ((), ())), preferred_element_type=jnp.float32
     )
-
-
-def attention_scores(queries, expanded, keys_rope, visible, score_scale):
-    scores = jnp.einsum(
-        "qhd,khd->hqk",
-        queries[..., :NOPE],
-        expanded[..., :NOPE],
-        preferred_element_type=jnp.float32,
-    )
-    scores = scores + jnp.einsum(
-        "qhd,kd->hqk", queries[..., NOPE:], keys_rope, preferred_element_type=jnp.float32
-    )
-    return jnp.where(visible[None], scores * score_scale, FLOOR_SCORE)
 
 
 PLANE = 4
 MESH = pl.DeviceIdType.MESH
 MEBIBYTE = 1024 * 1024
 LONG = pl.CostEstimate(flops=100 * 10**9, bytes_accessed=0, transcendentals=0)
+MIDDLE = pl.CostEstimate(flops=40 * 10**9, bytes_accessed=0, transcendentals=0)
 
 
 def groups(count):
@@ -185,6 +141,61 @@
             to(offset).wait()
 
     return start, finish
+
+
+def exchange_plane(half, place, source_of, target_of, own_sem, send, receive):
+    spot = place % PLANE
+
+    def to(offset, level):
+        mate = (spot + offset) % PLANE
+        return remote(
+            source_of(mate, level),
+            target_of(spot, level),
+            send.at[offset, level],
+            receive.at[offset, level],
+            (half, place - spot + mate),
+        )
+
+    def came(offset, level):
+        mate = (spot + PLANE - offset) % PLANE
+        block = target_of(mate, level)
+        return remote(
+            block,
+            block,
+            send.at[offset, level],
+            receive.at[offset, level],
+            (half, place - spot + mate),
+        )
+
+    def own(level):
+        return pltpu.make_async_copy(
+            source_of(spot, level), target_of(spot, level), own_sem.at[level]
+        )
+
+    def start(level):
+        for offset in range(1, PLANE):
+            to(offset, level).start()
+        own(level).start()
+
+    def finish(level):
+        own(level).wait()
+        for offset in range(1, PLANE):
+            came(offset, level).wait_recv()
+            to(offset, level).wait_send()
+
+    return start, finish
+
+
+def place_rows(choose_ref, source, block, placed):
+    def columns(n, carry):
+        at = lanes_at(n * 512, 512)
+        for mate in range(PLANE):
+            placed[mate, :, at] = jnp.dot(
+                choose_ref[source, mate], block[:, at], preferred_element_type=jnp.float32
+            ).astype(placed.dtype)
+        return carry
+
+    lax.fori_loop(0, block.shape[1] // 512, columns, 0)
 
 
 def gather_kernel(depth, cut, *refs):
@@ -382,31 +393,37 @@
                     plane_two(kind, source, turn).wait_recv()
             core(which, source).start()
 
-    for step in range(depth + 2):
-        if 1 <= step <= depth:
-            visit(step - 1, spread)
-        if 1 <= step < depth:
-            visit(step, arrive)
+    visit(0, spread)
+    for step in range(1, depth):
+        visit(step, arrive)
         if step == 1:
-            trail_first()
             move_finish()
             down_own.wait()
             for item in items:
                 shared_one(item).start()
         if step == 2:
+            trail_first()
+        if step >= 3:
+            visit(step - 2, trail_on)
+        if step >= 2:
+            visit(step - 1, spread)
+        if step == 2:
             for item in items:
                 shared_one(item).wait_recv()
                 for copy in shared_two(item):
                     copy.start()
-        if step == depth:
-            for item in items:
-                for copy in shared_two(item):
-                    copy.wait_recv()
-                shared_core(item).start()
-        if step >= 2:
-            visit(step - 2, share)
-            if step <= depth:
-                visit(step - 1, trail_on)
+        if step >= 3:
+            visit(step - 3, share)
+    visit(depth - 1, spread)
+    visit(depth - 2, trail_on)
+    visit(depth - 3, share)
+    for item in items:
+        for copy in shared_two(item):
+            copy.wait_recv()
+        shared_core(item).start()
+    visit(depth - 2, share)
+    visit(depth - 1, trail_on)
+    visit(depth - 1, share)
     for item in items:
         shared_one(item).wait_send()
         for copy in shared_two(item):
@@ -501,9 +518,10 @@
 
 def dispatch_kernel(depth, *refs):
     x_ref, choose_ref, grad_in, shared_in, down_in = refs[:5]
-    rows_out, forth_out, back_out, wide_out, tall_out = refs[5:10]
-    lines, placed, grads, weights, downs, low_ref, hidden_ref, forth_ref, back_ref = refs[10:19]
-    wide_ref, tall_ref, load_sem, out_sem, zs, zr, es, er, own_sem, done_sem = refs[19:]
+    rows_out, forth_out, back_out, wide_out, tall_out, grad_out = refs[6:12]
+    lines, placed, grads, weights, downs, low_ref, hidden_ref, forth_ref, back_ref = refs[12:21]
+    wide_ref, tall_ref, grad_placed, load_sem, out_sem, zs, zr, es, er, own_sem = refs[21:31]
+    done_sem, gs, gr, grad_sem = refs[31:]
     half = lax.axis_index("fsdp")
     place = lax.axis_index("expert")
     level = place // PLANE
@@ -537,47 +555,34 @@
     if padded > true:
         downs[pl.ds(true, padded - true), :] = jnp.zeros((padded - true, width), downs.dtype)
 
-    def own_rows(source):
-        return pltpu.make_async_copy(
-            placed.at[source, spot], rows_out.at[spot, source], own_sem.at[source]
-        )
-
-    def to_mate(offset, source):
-        mate = (spot + offset) % PLANE
-        return remote(
-            placed.at[source, mate],
-            rows_out.at[spot, source],
-            es.at[offset, source],
-            er.at[offset, source],
-            (half, place - spot + mate),
-        )
-
-    def from_mate(offset, source):
-        mate = (spot + PLANE - offset) % PLANE
-        block = rows_out.at[mate, source]
-        return remote(
-            block,
-            block,
-            es.at[offset, source],
-            er.at[offset, source],
-            (half, place - spot + mate),
-        )
+    rows_start, rows_finish = exchange_plane(
+        half,
+        place,
+        lambda mate, source: placed.at[source, mate],
+        lambda mate, source: rows_out.at[mate, source],
+        own_sem,
+        es,
+        er,
+    )
+    grad_start, grad_finish = exchange_plane(
+        half,
+        place,
+        lambda mate, source: grad_placed.at[source // 2, mate],
+        lambda mate, source: grad_out.at[mate, source],
+        grad_sem,
+        gs,
+        gr,
+    )
 
     def give(source):
-        def columns(n, carry):
-            at = pl.ds(pl.multiple_of(n * 512, 512), 512)
-            for mate in range(PLANE):
-                placed[source, mate, :, at] = jnp.dot(
-                    choose_ref[source, mate],
-                    lines[source, :, at],
-                    preferred_element_type=jnp.float32,
-                ).astype(placed.dtype)
-            return carry
-
-        lax.fori_loop(0, width // 512, columns, 0)
-        for offset in range(1, PLANE):
-            to_mate(offset, source).start()
-        own_rows(source).start()
+        place_rows(choose_ref, source, lines.at[source], placed.at[source])
+        rows_start(source)
+
+    def give_grad(n, carry):
+        source = 2 * n + 1
+        place_rows(choose_ref, source, grads.at[source], grad_placed.at[n])
+        grad_start(source)
+        return carry
 
     def shared(source):
         def inner(n, carry):
@@ -617,6 +622,7 @@
     give(level)
     for load in loads:
         load.wait()
+    lax.fori_loop(0, depth // 2, give_grad, 0)
     shared(level)
 
     def step(s, carry):
@@ -656,50 +662,67 @@
     def all_lines(ref, at):
         return ref[:, :, at].reshape(depth * tokens, -1)
 
-    def write(kind, k):
-        slot = k % 2
-        staged, target = ((wide_ref, wide_out), (tall_ref, tall_out))[kind]
-        size = staged.shape[1]
-        at = pl.ds(pl.multiple_of(k * size, size), size)
+    part = wide_ref.shape[2]
+    chunk_rows = max(PLANE * part, 128)
+    per_chunk = chunk_rows // (PLANE * part)
+
+    def write_wide(k):
         return pltpu.make_async_copy(
-            staged.at[slot], target.at[at, :], done_sem.at[kind, slot]
-        )
-
-    def tile(kind, k, ref, others):
-        staged = (wide_ref, tall_ref)[kind]
-        size = staged.shape[1]
-
-        @pl.when(k >= 2)
-        def _():
-            write(kind, k - 2).wait()
-
-        at = pl.ds(pl.multiple_of(k * size, size), size)
-        staged[k % 2] = dot_tn(
-            all_lines(ref, at), others[...].reshape(depth * tokens, -1)
-        ).astype(staged.dtype)
-        write(kind, k).start()
-
-    def wide_tile(k, carry):
-        tile(0, k, lines, low_ref)
+            wide_ref.at[k % 2], wide_out.at[k // depth, :, k % depth], done_sem.at[0, k % 2]
+        )
+
+    def wide_tile(n, carry):
+        at = pl.ds(pl.multiple_of(n * chunk_rows, chunk_rows), chunk_rows)
+        value = dot_tn(
+            all_lines(lines, at), low_ref[...].reshape(depth * tokens, -1)
+        ).astype(wide_ref.dtype)
+        for j in range(per_chunk):
+            k = n * per_chunk + j
+
+            @pl.when(k >= 2)
+            def _():
+                write_wide(k - 2).wait()
+
+            for spot_at in range(PLANE):
+                first = (j * PLANE + spot_at) * part
+                wide_ref[k % 2, spot_at] = value[first : first + part]
+            write_wide(k).start()
         return carry
 
-    def tall_tile(k, carry):
-        tile(1, k, hidden_ref, grads)
+    lax.fori_loop(0, width // chunk_rows, wide_tile, 0)
+    for k in (2 * depth - 2, 2 * depth - 1):
+        write_wide(k).wait()
+    tall_rows = tall_ref.shape[1]
+    tall_count = -(-true // tall_rows)
+
+    def write_tall(k, size):
+        return pltpu.make_async_copy(
+            tall_ref.at[k % 2, pl.ds(0, size), :],
+            tall_out.at[pl.ds(k * tall_rows, size), :],
+            done_sem.at[1, k % 2],
+        )
+
+    writes = []
+    for k in range(tall_count):
+        if k >= 2:
+            writes[k - 2].wait()
+        tall_ref[k % 2] = dot_tn(
+            all_lines(hidden_ref, pl.ds(k * tall_rows, tall_rows)),
+            grads[...].reshape(depth * tokens, -1),
+        ).astype(tall_ref.dtype)
+        writes.append(write_tall(k, min(tall_rows, true - k * tall_rows)))
+        writes[k].start()
+    for write in writes[-2:]:
+        write.wait()
+
+    def finish_grad(n, carry):
+        grad_finish(2 * n + 1)
         return carry
 
-    wide_count = width // wide_ref.shape[1]
-    tall_count = padded // tall_ref.shape[1]
-    lax.fori_loop(0, wide_count, wide_tile, 0)
-    lax.fori_loop(0, tall_count, tall_tile, 0)
-    for kind, total in ((0, wide_count), (1, tall_count)):
-        for k in range(max(0, total - 2), total):
-            write(kind, k).wait()
+    lax.fori_loop(0, depth // 2, finish_grad, 0)
 
     def finish(source, carry):
-        own_rows(source).wait()
-        for offset in range(1, PLANE):
-            from_mate(offset, source).wait_recv()
-            to_mate(offset, source).wait_send()
+        rows_finish(source)
 
         @pl.when((source <= level) & (level < depth - 1))
         def _():
@@ -714,11 +737,12 @@
     lax.fori_loop(0, depth, finish, 0)
 
 
-def dispatch(x, choose, grad_line, shared_full, down_full):
+def dispatch(x, choose, grad_line, shared_full, down_full, grad_rows):
     depth = choose.shape[0]
     tokens, width = x.shape
     capacity = choose.shape[2]
     padded = shared_full.shape[1] // 2
+    part = width // (2 * PLANE * depth)
     semaphores = pltpu.SemaphoreType.DMA
     low = x.dtype
     anywhere = pl.BlockSpec(memory_space=pl.ANY)
@@ -729,11 +753,13 @@
             jax.ShapeDtypeStruct((PLANE, depth, capacity, width), low),
             jax.ShapeDtypeStruct((depth, tokens, width), low),
             jax.ShapeDtypeStruct((depth, tokens, width), low),
-            jax.ShapeDtypeStruct((width, 2 * padded), low),
-            jax.ShapeDtypeStruct((padded, width), low),
+            jax.ShapeDtypeStruct((2, PLANE, depth, part, 2 * padded), low),
+            jax.ShapeDtypeStruct(down_full.shape, low),
+            jax.ShapeDtypeStruct(grad_rows.shape, low),
         ],
-        in_specs=[local, local, anywhere, anywhere, anywhere],
-        out_specs=[anywhere] * 5,
+        in_specs=[local, local] + [anywhere] * 4,
+        out_specs=[anywhere] * 6,
+        input_output_aliases={5: 5},
         scratch_shapes=[
             pltpu.VMEM((depth, tokens, width), low),
             pltpu.VMEM((depth, PLANE, capacity, width), low),
@@ -744,8 +770,9 @@
             pltpu.VMEM((depth, tokens, padded), low),
             pltpu.VMEM((tokens, width), low),
             pltpu.VMEM((tokens, width), low),
-            pltpu.VMEM((2, 256, 2 * padded), low),
+            pltpu.VMEM((2, PLANE, part, 2 * padded), low),
             pltpu.VMEM((2, 128, width), low),
+            pltpu.VMEM((depth // 2, PLANE, capacity, width), low),
             semaphores((3,)),
             semaphores((2,)),
             semaphores((2, depth)),
@@ -754,12 +781,15 @@
             semaphores((PLANE, depth)),
             semaphores((depth,)),
             semaphores((2, 2)),
+            semaphores((PLANE, depth)),
+            semaphores((PLANE, depth)),
+            semaphores((depth,)),
         ],
         compiler_params=pltpu.CompilerParams(
             collective_id=3, has_side_effects=True, vmem_limit_bytes=56 * MEBIBYTE
         ),
         cost_estimate=LONG,
-    )(x, choose, grad_line, shared_full, down_full)
+    )(x, choose, grad_line, shared_full, down_full, grad_rows)
 
 
 def return_kernel(depth, *refs):
@@ -1385,6 +1415,518 @@
     )(*parts, moved)
 
 
+def turned(values):
+    width = values.shape[1]
+    lanes = lax.broadcasted_iota(jnp.int32, values.shape, 1)
+    return jnp.where(
+        lanes % ROPE < ROPE // 2,
+        pltpu.roll(values, width - ROPE // 2, 1),
+        pltpu.roll(values, ROPE // 2, 1),
+    )
+
+
+def row_scale(values):
+    return lax.rsqrt(jnp.mean(values * values, axis=-1, keepdims=True) + EPSILON)
+
+
+def head_lanes(values, head):
+    lanes = lax.broadcasted_iota(jnp.int32, values.shape, 1)
+    return jnp.where(lanes // ROPE == head % 2, values, jnp.zeros_like(values))
+
+
+def lanes_at(start, size):
+    return pl.ds(pl.multiple_of(start, 128), size)
+
+
+def attend_kernel(layout, *refs):
+    x_ref, packed, up_in, first_gain, latent_gain, feed_gain, cosine, sine, mask = refs[:9]
+    choose_ref, grad_in = refs[9:11]
+    normed, residual, mixed, queries, latent, compressed = refs[11:17]
+    expanded, keys_rope, log_total, heads, grad_out = refs[17:22]
+    entry, ups, outs, prior_latent, prior_rope, grads, grad_placed = refs[22:29]
+    load_sem, up_sem, send_sem, receive_sem, gl, gs, gr, grad_sem = refs[29:]
+    entry_width, out_start = layout
+    half = lax.axis_index("fsdp")
+    place = lax.axis_index("expert")
+    other = (1 - half, place)
+    rows, width = x_ref.shape
+    low = x_ref.dtype
+    scale = (NOPE + ROPE) ** (-0.5)
+    loads = [
+        pltpu.make_async_copy(packed.at[:, pl.ds(0, entry_width)], entry, load_sem.at[0]),
+        pltpu.make_async_copy(packed.at[:, pl.ds(out_start, width)], outs, load_sem.at[1]),
+    ]
+    up_loads = load_ups(up_in, ups, up_sem, layout)
+    depth = grad_in.shape[0]
+
+    def grad_load(n):
+        return pltpu.make_async_copy(grad_in.at[2 * n], grads.at[n], gl.at[n])
+
+    grad_start, grad_finish = exchange_plane(
+        half,
+        place,
+        lambda mate, source: grad_placed.at[source // 2, mate],
+        lambda mate, source: grad_out.at[mate, source],
+        grad_sem,
+        gs,
+        gr,
+    )
+
+    def each_grad(act):
+        def one(n, carry):
+            act(n)
+            return carry
+
+        lax.fori_loop(0, depth // 2, one, 0)
+
+    def give_grad(n):
+        grad_load(n).wait()
+        place_rows(choose_ref, 2 * n, grads.at[n], grad_placed.at[n])
+        grad_start(2 * n)
+
+    each_grad(lambda n: grad_load(n).start())
+    for load in loads[:1] + up_loads + loads[1:]:
+        load.start()
+    greet([other] + plane_others(half, place))
+    each_grad(give_grad)
+    x = x_ref[...].astype(jnp.float32)
+    normed[...] = (x * row_scale(x) * first_gain[...]).astype(low)
+    loads[0].wait()
+    nope_width = HEADS * NOPE
+    query_width = HEADS * (NOPE + ROPE)
+
+    def through(start, size):
+        return jnp.dot(
+            normed[...], entry[:, lanes_at(start, size)], preferred_element_type=jnp.float32
+        )
+
+    def rotary(values):
+        return values * cosine[...] + turned(values) * sine[...]
+
+    squeezed = through(query_width, LATENT)
+    compressed[...] = squeezed
+    latent[...] = (squeezed * row_scale(squeezed) * latent_gain[...]).astype(low)
+    key = rotary(through(query_width + LATENT, 128))
+    keys_rope[pl.ds(rows, rows), :] = (key + pltpu.roll(key, ROPE, 1)).astype(low)
+    sends = [
+        remote(latent, prior_latent, send_sem.at[0], receive_sem.at[0], other),
+        remote(
+            keys_rope.at[pl.ds(rows, rows), :],
+            prior_rope,
+            send_sem.at[1],
+            receive_sem.at[1],
+            other,
+        ),
+    ]
+
+    @pl.when(half == 0)
+    def _():
+        for send in sends:
+            send.start()
+
+    def nope_part(n, carry):
+        queries[:, lanes_at(n * 512, 512)] = through(n * 512, 512).astype(low)
+        return carry
+
+    lax.fori_loop(0, nope_width // 512, nope_part, 0)
+
+    def rope_part(n, carry):
+        values = through(nope_width + n * 512, 512)
+        for k in range(4):
+            tile = rotary(values[:, k * 128 : (k + 1) * 128])
+            queries[:, lanes_at(nope_width + n * 512 + k * 128, 128)] = tile.astype(low)
+        return carry
+
+    lax.fori_loop(0, HEADS * ROPE // 512, rope_part, 0)
+    for load in up_loads:
+        load.wait()
+    quarters, span = ups.shape[0], ups.shape[-1]
+
+    def expand(source, first):
+        def one(n, carry):
+            expanded[pl.ds(first, rows), lanes_at(n * span, span)] = jnp.dot(
+                source[...], whole(ups[n]), preferred_element_type=jnp.float32
+            ).astype(low)
+            return carry
+
+        lax.fori_loop(0, quarters, one, 0)
+
+    expand(latent, rows)
+
+    @pl.when(half == 0)
+    def _():
+        expanded[pl.ds(0, rows), :] = jnp.zeros((rows, quarters * span), low)
+        keys_rope[pl.ds(0, rows), :] = jnp.zeros((rows, 128), low)
+        for send in sends:
+            send.wait_send()
+
+    @pl.when(half == 1)
+    def _():
+        for send in sends:
+            send.wait_recv()
+        keys_rope[pl.ds(0, rows), :] = prior_rope[...]
+        expand(prior_latent, 0)
+
+    def head(h, totals):
+        pair = queries[:, lanes_at(nope_width + (h // 2) * 128, 128)]
+        scores = dot_nt(
+            queries[:, lanes_at(h * NOPE, NOPE)], expanded[:, lanes_at(h * 256, NOPE)]
+        )
+        scores = scores + dot_nt(head_lanes(pair, h), keys_rope[...])
+        scores = jnp.where(mask[...] > 0, scores * scale, FLOOR_SCORE)
+        top = jnp.max(scores, axis=-1, keepdims=True)
+        weights = jnp.exp(scores - top)
+        total = jnp.sum(weights, axis=-1, keepdims=True)
+        heads[:, lanes_at(h * VALUE, VALUE)] = jnp.dot(
+            (weights / total).astype(low),
+            expanded[:, lanes_at(h * 256 + NOPE, VALUE)],
+            preferred_element_type=jnp.float32,
+        ).astype(low)
+        lanes = lax.broadcasted_iota(jnp.int32, totals.shape, 1)
+        return jnp.where(lanes == h, top + jnp.log(total), totals)
+
+    log_total[...] = lax.fori_loop(0, HEADS, head, jnp.zeros((rows, 128), jnp.float32))
+    loads[1].wait()
+
+    def project(n, carry):
+        at = lanes_at(n * 512, 512)
+        residual[:, at] = x_ref[:, at].astype(jnp.float32) + jnp.dot(
+            heads[...], outs[:, at], preferred_element_type=jnp.float32
+        )
+        return carry
+
+    lax.fori_loop(0, width // 512, project, 0)
+    total = residual[...]
+    mixed[...] = (total * row_scale(total) * feed_gain[...]).astype(low)
+    each_grad(lambda n: grad_finish(2 * n))
+
+
+def attend(x, packed, ups, ups_shape, gains, tables, mask, choose, grad_line, layout):
+    rows, width = x.shape
+    low, wide = x.dtype, jnp.float32
+    semaphores = pltpu.SemaphoreType.DMA
+    anywhere = pl.BlockSpec(memory_space=pl.ANY)
+    local = pl.BlockSpec(memory_space=pltpu.VMEM)
+    expanded_width = HEADS * (NOPE + VALUE)
+    depth, _, capacity, _ = choose.shape
+    shapes = [
+        ((rows, width), low),
+        ((rows, width), wide),
+        ((rows, width), low),
+        ((rows, HEADS * (NOPE + ROPE)), low),
+        ((rows, LATENT), low),
+        ((rows, LATENT), wide),
+        ((2 * rows, expanded_width), low),
+        ((2 * rows, 128), low),
+        ((rows, 128), wide),
+        ((rows, HEADS * VALUE), low),
+        ((PLANE, depth, capacity, width), low),
+    ]
+    return pl.pallas_call(
+        functools.partial(attend_kernel, layout),
+        out_shape=[jax.ShapeDtypeStruct(shape, dtype) for shape, dtype in shapes],
+        in_specs=[local, anywhere, anywhere] + [local] * 7 + [anywhere],
+        out_specs=[local] * (len(shapes) - 1) + [anywhere],
+        scratch_shapes=[
+            pltpu.VMEM((packed.shape[0], layout[0]), low),
+            pltpu.VMEM(ups_shape, low),
+            pltpu.VMEM((packed.shape[0], width), low),
+            pltpu.VMEM((rows, LATENT), low),
+            pltpu.VMEM((rows, 128), low),
+            pltpu.VMEM((depth // 2, rows, width), low),
+            pltpu.VMEM((depth // 2, PLANE, capacity, width), low),
+            semaphores((2,)),
+            semaphores((ups_shape[0],)),
+            semaphores((2,)),
+            semaphores((2,)),
+            semaphores((depth // 2,)),
+            semaphores((PLANE, depth)),
+            semaphores((PLANE, depth)),
+            semaphores((depth,)),
+        ],
+        compiler_params=pltpu.CompilerParams(
+            collective_id=5, has_side_effects=True, vmem_limit_bytes=56 * MEBIBYTE
+        ),
+        cost_estimate=MIDDLE,
+    )(x, packed, ups, *gains, *tables, mask, choose, grad_line)
+
+
+def load_ups(up_in, ups, sem, layout):
+    if up_in.shape == ups.shape:
+        return [pltpu.make_async_copy(up_in, ups, sem.at[0])]
+    span = ups.shape[-1]
+    return [
+        pltpu.make_async_copy(
+            up_in.at[:, k, :, pl.ds(layout[0], span)], ups.at[k], sem.at[k]
+        )
+        for k in range(ups.shape[0])
+    ]
+
+
+def whole(block):
+    return block.reshape(-1, block.shape[-1])
+
+
+def attend_back_kernel(layout, count, *refs):
+    d_ref, packed, up_in, queries, expanded, keys_rope, log_total = refs[:7]
+    latent, compressed, normed, heads, x_ref, above = refs[7:13]
+    latent_gain, first_gain, cosine, sine, mask, rows_in = refs[13:19]
+    refs = refs[19 + count :]
+    token_grad, up_grad, gain_grad, first_grad, entry_grad, out_grad, rows_out = refs[:7]
+    outs, ups, d_heads, own, prior, came, prior_rope, came_rope, total_low = refs[7:16]
+    entry, entry_low, up_tile, entry_tile, out_tile = refs[16:21]
+    load_sem, up_sem, send_sem, receive_sem, write_sem, es, er, own_sem = refs[21:]
+    entry_width, out_start = layout
+    half = lax.axis_index("fsdp")
+    place = lax.axis_index("expert")
+    other = (1 - half, place)
+    rows, width = d_ref.shape
+    low = d_ref.dtype
+    wide = jnp.float32
+    scale = (NOPE + ROPE) ** (-0.5)
+    nope_width = HEADS * NOPE
+    query_width = HEADS * (NOPE + ROPE)
+    loads = [
+        pltpu.make_async_copy(packed.at[:, pl.ds(out_start, width)], outs, load_sem.at[0]),
+        pltpu.make_async_copy(packed.at[:, pl.ds(0, entry_width)], entry, load_sem.at[1]),
+    ]
+    up_loads = load_ups(up_in, ups, up_sem, layout)
+    for load in loads + up_loads:
+        load.start()
+    greet([other] + plane_others(half, place))
+    rows_start, rows_finish = exchange_plane(
+        half,
+        place,
+        lambda mate, level: rows_in.at[mate, level],
+        lambda mate, level: rows_out.at[mate, level],
+        own_sem,
+        es,
+        er,
+    )
+
+    def each_level(act):
+        def one(level, carry):
+            act(level)
+            return carry
+
+        lax.fori_loop(0, rows_in.shape[1], one, 0)
+
+    each_level(rows_start)
+
+    def write(kind, k):
+        staged, target = ((out_tile, out_grad), (entry_tile, entry_grad), (up_tile, up_grad))[kind]
+        size = staged.shape[1]
+        if kind == 2:
+            place_at = up_grad.at[k] if up_grad.shape[0] == ups.shape[0] else up_grad.at[:, k]
+        else:
+            place_at = target.at[pl.ds(pl.multiple_of(k * size, size), size), :]
+        return pltpu.make_async_copy(
+            staged.at[k % 2], place_at, write_sem.at[kind, k % 2]
+        )
+
+    def put(kind, k, value):
+        staged = (out_tile, entry_tile, up_tile)[kind]
+
+        @pl.when(k >= 2)
+        def _():
+            write(kind, k - 2).wait()
+
+        staged[k % 2] = value.astype(low).reshape(staged.shape[1:])
+        write(kind, k).start()
+
+    def settle(kind, total):
+        for k in range(max(0, total - 2), total):
+            write(kind, k).wait()
+
+    def out_part(k, carry):
+        size = out_tile.shape[1]
+        put(0, k, dot_tn(heads[:, lanes_at(k * size, size)], d_ref[...]))
+        return carry
+
+    out_count = heads.shape[1] // out_tile.shape[1]
+    lax.fori_loop(0, out_count, out_part, 0)
+    loads[0].wait()
+
+    def head_part(n, carry):
+        at = lanes_at(n * 512, 512)
+        d_heads[:, at] = dot_nt(d_ref[...], outs[at, :]).astype(low)
+        return carry
+
+    lax.fori_loop(0, width // 512, head_part, 0)
+
+    def turn_back(values):
+        return values * cosine[...] - turned(values) * sine[...]
+
+    def pair_of_heads(n, rope_sum):
+        pair = queries[:, lanes_at(nope_width + n * 128, 128)]
+        query_rope = jnp.zeros((rows, 128), wide)
+        for k in range(2):
+            h = 2 * n + k
+            query = queries[:, lanes_at(h * NOPE, NOPE)]
+            key = expanded[:, lanes_at(h * 256, NOPE)]
+            value = expanded[:, lanes_at(h * 256 + NOPE, VALUE)]
+            d_head = d_heads[:, lanes_at(h * VALUE, VALUE)]
+            own_pair = head_lanes(pair, k)
+            scores = dot_nt(query, key) + dot_nt(own_pair, keys_rope[...])
+            scores = jnp.where(mask[...] > 0, scores * scale, FLOOR_SCORE)
+            lanes = lax.broadcasted_iota(jnp.int32, log_total.shape, 1)
+            log_sum = jnp.sum(
+                jnp.where(lanes == h, log_total[...], 0.0), axis=-1, keepdims=True
+            )
+            probs = jnp.exp(scores - log_sum)
+            d_probs = dot_nt(d_head, value)
+            delta = jnp.sum(probs * d_probs, axis=-1, keepdims=True)
+            d_scores = (probs * (d_probs - delta)).astype(low)
+            entry_low[:, lanes_at(h * NOPE, NOPE)] = (
+                jnp.dot(d_scores, key, preferred_element_type=wide) * scale
+            ).astype(low)
+            query_rope = query_rope + head_lanes(
+                jnp.dot(d_scores, keys_rope[...], preferred_element_type=wide), k
+            )
+            d_key = dot_tn(d_scores, query) * scale
+            d_value = dot_tn(probs.astype(low), d_head)
+            own[:, lanes_at(h * 256, NOPE)] = d_key[rows:]
+            own[:, lanes_at(h * 256 + NOPE, VALUE)] = d_value[rows:]
+            prior[:, lanes_at(h * 256, NOPE)] = d_key[:rows].astype(low)
+            prior[:, lanes_at(h * 256 + NOPE, VALUE)] = d_value[:rows].astype(low)
+            rope_sum = rope_sum + dot_tn(d_scores, own_pair)
+        entry_low[:, lanes_at(nope_width + n * 128, 128)] = (
+            turn_back(query_rope) * scale
+        ).astype(low)
+        return rope_sum
+
+    rope_sum = lax.fori_loop(
+        0, HEADS // 2, pair_of_heads, jnp.zeros((2 * rows, 128), wide)
+    )
+    rope_sum = (rope_sum + pltpu.roll(rope_sum, ROPE, 1)) * scale
+    prior_rope[...] = rope_sum[:rows].astype(low)
+    sends = [
+        remote(prior, came, send_sem.at[0], receive_sem.at[0], other),
+        remote(prior_rope, came_rope, send_sem.at[1], receive_sem.at[1], other),
+    ]
+
+    @pl.when(half == 1)
+    def _():
+        for send in sends:
+            send.start()
+        came_rope[...] = jnp.zeros((rows, 128), low)
+        total_low[...] = own[...].astype(low)
+        for send in sends:
+            send.wait_send()
+
+    @pl.when(half == 0)
+    def _():
+        for send in sends:
+            send.wait_recv()
+        total_low[...] = (own[...] + came[...].astype(wide)).astype(low)
+
+    for load in up_loads:
+        load.wait()
+    quarters, span = ups.shape[0], ups.shape[-1]
+
+    def spread(n, d_latent):
+        part = total_low[:, lanes_at(n * span, span)]
+        put(2, n, dot_tn(latent[...], part))
+        return d_latent + dot_nt(part, whole(ups[n]))
+
+    d_latent = lax.fori_loop(0, quarters, spread, jnp.zeros((rows, LATENT), wide))
+    values = compressed[...]
+    root = row_scale(values)
+    gain_grad[...] = jnp.broadcast_to(
+        jnp.sum(d_latent * values * root, axis=0, keepdims=True), gain_grad.shape
+    )
+    scaled = latent_gain[...] * d_latent
+    inner = jnp.mean(values * scaled, axis=-1, keepdims=True)
+    entry_low[:, lanes_at(query_width, LATENT)] = (
+        root * scaled - values * (root * root * root) * inner
+    ).astype(low)
+    key = rope_sum[rows:] + came_rope[...].astype(wide)
+    entry_low[:, lanes_at(query_width + LATENT, 128)] = turn_back(head_lanes(key, 0)).astype(low)
+
+    def entry_part(k, carry):
+        size = entry_tile.shape[1]
+        put(1, k, dot_tn(normed[:, lanes_at(k * size, size)], entry_low[...]))
+        return carry
+
+    entry_count = width // entry_tile.shape[1]
+    lax.fori_loop(0, entry_count, entry_part, 0)
+    loads[1].wait()
+
+    def normed_part(n, carry):
+        at = lanes_at(n * 512, 512)
+        token_grad[:, at] = dot_nt(entry_low[...], entry[at, :])
+        return carry
+
+    lax.fori_loop(0, width // 512, normed_part, 0)
+    x = x_ref[...].astype(wide)
+    root = row_scale(x)
+    scaled = first_gain[...] * token_grad[...]
+    first_grad[...] = jnp.broadcast_to(
+        jnp.sum(token_grad[...] * x * root, axis=0, keepdims=True), first_grad.shape
+    )
+    inner = jnp.mean(x * scaled, axis=-1, keepdims=True)
+    token_grad[...] = above[...] + root * scaled - x * (root * root * root) * inner
+    settle(0, out_count)
+    settle(1, entry_count)
+    settle(2, quarters)
+    each_level(rows_finish)
+
+
+def attend_back(
+    d, packed, ups, ups_shape, kept, gains, tables, mask, returning, before, layout
+):
+    rows, width = d.shape
+    low, wide = d.dtype, jnp.float32
+    semaphores = pltpu.SemaphoreType.DMA
+    anywhere = pl.BlockSpec(memory_space=pl.ANY)
+    local = pl.BlockSpec(memory_space=pltpu.VMEM)
+    expanded_width = HEADS * (NOPE + VALUE)
+    quarters, blocks, part, span = ups_shape
+    up_grad = (blocks, quarters, part, span) if blocks > 1 else ups_shape
+    return pl.pallas_call(
+        functools.partial(attend_back_kernel, layout, len(before)),
+        out_shape=[
+            jax.ShapeDtypeStruct((rows, width), wide),
+            jax.ShapeDtypeStruct(up_grad, low),
+            jax.ShapeDtypeStruct((8, LATENT), wide),
+            jax.ShapeDtypeStruct((8, width), wide),
+            jax.ShapeDtypeStruct((width, layout[0]), low),
+            jax.ShapeDtypeStruct((HEADS * VALUE, width), low),
+            jax.ShapeDtypeStruct(returning.shape, low),
+        ],
+        in_specs=[local, anywhere, anywhere] + [local] * 15 + [anywhere] * (1 + len(before)),
+        out_specs=[local, anywhere, local, local] + [anywhere] * 3,
+        scratch_shapes=[
+            pltpu.VMEM((packed.shape[0], width), low),
+            pltpu.VMEM(ups_shape, low),
+            pltpu.VMEM((rows, HEADS * VALUE), low),
+            pltpu.VMEM((rows, expanded_width), wide),
+            pltpu.VMEM((rows, expanded_width), low),
+            pltpu.VMEM((rows, expanded_width), low),
+            pltpu.VMEM((rows, 128), low),
+            pltpu.VMEM((rows, 128), low),
+            pltpu.VMEM((rows, expanded_width), low),
+            pltpu.VMEM((packed.shape[0], layout[0]), low),
+            pltpu.VMEM((rows, layout[0]), low),
+            pltpu.VMEM((2,) + ups_shape[1:], low),
+            pltpu.VMEM((2, 128, layout[0]), low),
+            pltpu.VMEM((2, 256, width), low),
+            semaphores((2,)),
+            semaphores((quarters,)),
+            semaphores((2,)),
+            semaphores((2,)),
+            semaphores((3, 2)),
+            semaphores((PLANE, returning.shape[1])),
+            semaphores((PLANE, returning.shape[1])),
+            semaphores((returning.shape[1],)),
+        ],
+        compiler_params=pltpu.CompilerParams(
+            collective_id=6, has_side_effects=True, vmem_limit_bytes=62 * MEBIBYTE
+        ),
+        cost_estimate=LONG,
+    )(d, packed, ups, *kept, *gains, *tables, mask, returning, *before)
+
+
 def body(
     tokens,
     segments,
@@ -1434,13 +1976,16 @@
     entry_width = query_width + down_width + (-down_width) % 128
     up_width = HEADS * (NOPE + VALUE)
     quarters = part_rows // latent_up.shape[0]
+    by_head = query_weight.reshape(part_rows, HEADS, NOPE + ROPE)
     packed = jnp.concatenate(
         [
-            query_weight,
+            by_head[..., :NOPE].reshape(part_rows, -1),
+            by_head[..., NOPE:].reshape(part_rows, -1),
             jnp.pad(latent_down, ((0, 0), (0, (-down_width) % 128))),
             latent_up.reshape(latent_up.shape[0], quarters, -1)
             .transpose(1, 0, 2)
             .reshape(part_rows, -1),
+            output_weight,
             small,
         ],
         axis=1,
@@ -1482,15 +2027,15 @@
             )
         )
     )
-    output_rows, packed_full = lax.optimization_barrier((output_weight, packed_full))
-    output_full = lax.all_gather(output_rows, ("fsdp", "expert"), axis=0, tiled=True)
-    grad_line = grad_line.reshape(line_rows, D)
-    entry_full = packed_full[:, :entry_width]
-    up_parts = packed_full.reshape(2 * expert_total, quarters, latent_up.shape[0], -1)
-    up_full = jnp.concatenate(
-        [up_parts[:, k, :, entry_width:-128].reshape(LATENT, -1) for k in range(quarters)],
-        axis=1,
-    )
+    up_rows = latent_up.shape[0]
+    up_parts = packed_full.reshape(2 * expert_total, quarters, up_rows, -1)
+    if up_rows % 16 == 0:
+        up_full = up_parts
+        ups_shape = (quarters, 2 * expert_total, up_rows, up_width // quarters)
+    else:
+        up_full = up_parts[..., entry_width : -128 - D].transpose(1, 0, 2, 3)
+        up_full = up_full.reshape(quarters, 1, LATENT, -1)
+        ups_shape = up_full.shape
     small_full = packed_full[:, -128:].reshape(2 * expert_total, -1)
     gain_one, gain_latent, gain_feed, router_full = (
         small_full[:, cuts[0] : cuts[1]].reshape(-1),
@@ -1503,51 +2048,17 @@
     hits = target_line[:, :TOPK, None, :] == slot_names[None, None, :, None]
     choose_rows = jnp.any(hits, axis=1).astype(jnp.bfloat16)
 
-    def to_experts(rows_line):
-        placed = jnp.einsum(
-            "zst,ztd->zsd",
-            choose_rows,
-            rows_line.reshape(depth, row_count, D),
-            preferred_element_type=jnp.float32,
-        ).astype(jnp.bfloat16)
-        placed = placed.reshape(depth, PLANE, capacity, D).transpose(1, 0, 2, 3)
-        return lax.all_to_all(
-            placed, "expert", split_axis=0, concat_axis=0, axis_index_groups=plane, tiled=True
-        ).reshape(expert_total * capacity, D)
-
-    def from_experts(rows):
-        return lax.all_to_all(
-            rows.reshape(PLANE, depth, capacity, -1),
-            "expert",
-            split_axis=0,
-            concat_axis=0,
-            axis_index_groups=plane,
-            tiled=True,
-        )
+    choose_slots = choose_rows.reshape(depth, PLANE, capacity, row_count)
+    grad_line = grad_line.reshape(depth, row_count, D)
 
     cosine, sine_table = rotary_table(row_count, device_half * row_count, ROPE)
-    score_scale = (NOPE + ROPE) ** (-0.5)
+    tables = (
+        jnp.concatenate([cosine] * 4, axis=1),
+        jnp.concatenate([-sine_table, sine_table] * 2, axis=1),
+    )
     gain_first = gain_one.astype(jnp.float32)
-    normed_low = norm_rows(inputs, gain_first).astype(jnp.bfloat16)
-    entry = matmul(normed_low, entry_full)
-    query_raw = entry[:, :query_width].reshape(row_count, HEADS, NOPE + ROPE)
-    queries = jnp.concatenate(
-        [
-            query_raw[..., :NOPE],
-            rotate_forward(query_raw[..., NOPE:], cosine[:, None, :], sine_table[:, None, :]),
-        ],
-        axis=-1,
-    ).astype(jnp.bfloat16)
-    compressed = entry[:, query_width : query_width + down_width]
     latent_gain = gain_latent.astype(jnp.float32)
-    latent = norm_rows(compressed[:, :LATENT], latent_gain).astype(jnp.bfloat16)
-    key_rope = rotate_forward(compressed[:, LATENT:], cosine, sine_table).astype(jnp.bfloat16)
-    prior_latent, prior_rope = passed_along((latent, key_rope), "fsdp", 1)
-    key_latent = jnp.concatenate([prior_latent, latent], axis=0)
-    keys_rope = jnp.concatenate([prior_rope, key_rope], axis=0)
-    expanded = (
-        matmul(key_latent, up_full).astype(jnp.bfloat16).reshape(2 * row_count, HEADS, NOPE + VALUE)
-    )
+    feed_gain = gain_feed.astype(jnp.float32)
     query_place = device_half * row_count + jnp.arange(row_count)
     key_place = (device_half - 1) * row_count + jnp.arange(2 * row_count)
     padded_segments = jnp.concatenate([jnp.full((row_count,), -1, jnp.int32), segments[0]])
@@ -1556,26 +2067,36 @@
     visible = (key_place[None, :] <= query_place[:, None]) & (
         key_segment[None, :] == query_segment[:, None]
     )
-    scores = attention_scores(queries, expanded, keys_rope, visible, score_scale)
-    top_score = jnp.max(scores, axis=-1, keepdims=True)
-    log_total = top_score + jnp.log(jnp.sum(jnp.exp(scores - top_score), axis=-1, keepdims=True))
-    weight_low = jnp.exp(scores - log_total).astype(jnp.bfloat16)
-    mixed_heads = (
-        jnp.einsum(
-            "hqk,khd->qhd", weight_low, expanded[..., NOPE:], preferred_element_type=jnp.float32
-        )
-        .reshape(row_count, HEADS * VALUE)
-        .astype(jnp.bfloat16)
-    )
-    residual = inputs + matmul(mixed_heads, output_full)
-    feed_gain = gain_feed.astype(jnp.float32)
-    mixed_low = norm_rows(residual, feed_gain).astype(jnp.bfloat16)
-    grad_rows = to_experts(grad_line)
-    choose_slots = choose_rows.reshape(depth, PLANE, capacity, row_count)
-    mixed_low, grad_rows = lax.optimization_barrier((mixed_low, grad_rows))
-    mixed_rows, shared_out, shared_back, shared_grad, sdown_grad = dispatch(
-        mixed_low, choose_slots, grad_line.reshape(depth, row_count, D), shared_full, sdown_full
-    )
+    mask = visible.astype(jnp.float32)
+    layout = (entry_width, packed.shape[1] - 128 - D)
+    (
+        normed_low,
+        residual,
+        mixed_low,
+        queries,
+        latent,
+        compressed,
+        expanded,
+        keys_rope,
+        log_total,
+        mixed_heads,
+        grad_rows,
+    ) = attend(
+        tokens[0],
+        packed_full,
+        up_full,
+        ups_shape,
+        (gain_first[None], latent_gain[None], feed_gain[None]),
+        tables,
+        mask,
+        choose_slots,
+        grad_line,
+        layout,
+    )
+    mixed_rows, shared_out, shared_back, shared_grad, sdown_grad, grad_rows = dispatch(
+        mixed_low, choose_slots, grad_line, shared_full, sdown_full, grad_rows
+    )
+    grad_rows = grad_rows.reshape(expert_total * capacity, D)
     mixed_rows = mixed_rows.reshape(expert_total * capacity, D)
     shared_out = shared_out.reshape(line_rows, D)
     hidden_grad_raw = right_matmul(grad_rows, expert_down_full)
@@ -1607,19 +2128,14 @@
     )
     back_and_shared, hidden = lax.optimization_barrier((back_and_shared, hidden))
     expert_out = (matmul(hidden, expert_down_full) * gate_column).astype(jnp.bfloat16)
-    returned = from_experts(expert_out)
-
-    sdown_grad = sdown_grad[: 2 * shared_width]
-
     def scatter_plane(value):
         part = lax.psum_scatter(value, "fsdp", scatter_dimension=0, tiled=True)
         return lax.psum_scatter(
             part, "expert", scatter_dimension=0, axis_index_groups=plane, tiled=True
         )
 
-    shared_grad = shared_grad.reshape(2, depth, PLANE, part_rows, -1).transpose(0, 2, 1, 3, 4)
     shared_summed = scatter_plane(shared_grad.reshape(2 * PLANE, depth, part_rows, -1))[0]
-    sdown_piece = scatter_plane(sdown_grad).astype(jnp.float32)
+    sdown_summed = scatter_plane(sdown_grad)
 
     out_grad = cotangent[0].astype(jnp.float32)
     probabilities = jax.nn.softmax(matmul(mixed_low, router_full), axis=-1)
@@ -1632,94 +2148,43 @@
     residual_add, feed_gain_grad = norm_back(residual, feed_gain, mixed_grad)
     residual_grad = out_grad + residual_add
     attended_low = residual_grad.astype(jnp.bfloat16)
-    output_grad = left_matmul(mixed_heads, attended_low)
-    heads_low = (
-        right_matmul(attended_low, output_full)
-        .astype(jnp.bfloat16)
-        .reshape(row_count, HEADS, VALUE)
-    )
-    scores_again = attention_scores(queries, expanded, keys_rope, visible, score_scale)
-    probs_again = jnp.exp(scores_again - log_total)
-    weights_again = probs_again.astype(jnp.bfloat16)
-    weight_grad = jnp.einsum(
-        "qhd,khd->hqk", heads_low, expanded[..., NOPE:], preferred_element_type=jnp.float32
-    )
-    value_grad = jnp.einsum(
-        "hqk,qhd->khd", weights_again, heads_low, preferred_element_type=jnp.float32
-    )
-    delta_rows = jnp.sum(probs_again * weight_grad, axis=-1, keepdims=True)
-    score_low = (probs_again * (weight_grad - delta_rows)).astype(jnp.bfloat16)
-    query_nope_grad = (
-        jnp.einsum(
-            "hqk,khd->qhd", score_low, expanded[..., :NOPE], preferred_element_type=jnp.float32
-        )
-        * score_scale
-    )
-    query_rope_grad = (
-        jnp.einsum("hqk,kd->qhd", score_low, keys_rope, preferred_element_type=jnp.float32)
-        * score_scale
-    )
-    key_nope_grad = (
-        jnp.einsum(
-            "hqk,qhd->khd", score_low, queries[..., :NOPE], preferred_element_type=jnp.float32
-        )
-        * score_scale
-    )
-    key_rope_grad = (
-        jnp.einsum(
-            "hqk,qhd->kd", score_low, queries[..., NOPE:], preferred_element_type=jnp.float32
-        )
-        * score_scale
-    )
-    expanded_grad = jnp.concatenate([key_nope_grad, value_grad], axis=-1).reshape(
-        2 * row_count, HEADS * (NOPE + VALUE)
-    )
-    returned_expanded, returned_rope = (
-        passed_along(expanded_grad[:row_count].astype(jnp.bfloat16), "fsdp", -1).astype(
-            jnp.float32
+    (
+        token_grad,
+        up_weight_grad,
+        latent_gain_grad,
+        first_gain_grad,
+        entry_grad,
+        output_grad,
+        returned,
+    ) = attend_back(
+        attended_low,
+        packed_full,
+        up_full,
+        ups_shape,
+        (
+            queries,
+            expanded,
+            keys_rope,
+            log_total,
+            latent,
+            compressed,
+            normed_low,
+            mixed_heads,
+            tokens[0],
+            residual_grad,
         ),
-        passed_along(key_rope_grad[:row_count].astype(jnp.bfloat16), "fsdp", -1).astype(
-            jnp.float32
-        ),
-    )
-    expanded_low = (expanded_grad[row_count:] + returned_expanded).astype(jnp.bfloat16)
-    own_rope = key_rope_grad[row_count:] + returned_rope
-    latent_grad = right_matmul(expanded_low, up_full)
-    quarter = up_width // quarters
-    up_weight_grad = jnp.stack(
-        [
-            left_matmul(latent, expanded_low[:, k * quarter : (k + 1) * quarter])
-            .astype(jnp.bfloat16)
-            .reshape(2 * expert_total, latent_up.shape[0], quarter)
-            for k in range(quarters)
-        ],
-        axis=1,
-    ).reshape(2 * expert_total * part_rows, quarter)
-    compressed_latent_grad, latent_gain_grad = norm_back(
-        compressed[:, :LATENT], latent_gain, latent_grad
-    )
-    compressed_low = jnp.concatenate(
-        [compressed_latent_grad, rotate_backward(own_rope, cosine, sine_table)], axis=-1
-    ).astype(jnp.bfloat16)
-    query_low = (
-        jnp.concatenate(
-            [
-                query_nope_grad,
-                rotate_backward(query_rope_grad, cosine[:, None, :], sine_table[:, None, :]),
-            ],
-            axis=-1,
-        )
-        .reshape(row_count, HEADS * (NOPE + ROPE))
-        .astype(jnp.bfloat16)
-    )
-    entry_low = jnp.concatenate(
-        [query_low, jnp.pad(compressed_low, ((0, 0), (0, (-down_width) % 128)))], axis=1
-    )
-    normed_grad = right_matmul(entry_low, entry_full)
-    entry_grad = left_matmul(normed_low, entry_low).astype(jnp.bfloat16)
-    input_add, first_gain_grad = norm_back(inputs, gain_first, normed_grad)
-    token_grad = residual_grad + input_add
-    late = entry_low[0, 0].astype(jnp.float32) * 0.0
+        (latent_gain[None], gain_first[None]),
+        tables,
+        mask,
+        expert_out.reshape(PLANE, depth, capacity, D),
+        (shared_summed, sdown_summed),
+        layout,
+    )
+    if up_rows % 16 != 0:
+        up_weight_grad = up_weight_grad.reshape(quarters, 2 * expert_total, up_rows, -1)
+        up_weight_grad = up_weight_grad.transpose(1, 0, 2, 3)
+    latent_gain_grad = latent_gain_grad[0]
+    first_gain_grad = first_gain_grad[0]
     routed = jnp.einsum(
         "zst,zsd->ztd",
         choose_rows,
@@ -1727,7 +2192,7 @@
         preferred_element_type=jnp.float32,
     )
     routed_and_shared = lax.psum_scatter(
-        (routed.reshape(line_rows, D) + shared_out + late).astype(jnp.bfloat16),
+        (routed.reshape(line_rows, D) + shared_out).astype(jnp.bfloat16),
         "expert",
         scatter_dimension=0,
         axis_index_groups=line,
@@ -1748,12 +2213,12 @@
     packed_piece, shared_back_moved = reduce_rows(
         [
             entry_grad,
-            up_weight_grad,
-            output_grad.astype(jnp.bfloat16),
+            up_weight_grad.reshape(2 * expert_total * part_rows, -1),
+            output_grad,
             small_grad.astype(jnp.bfloat16).reshape(-1, 128),
         ],
         shared_summed,
-        (packed.shape[1] + D) // 256 * 128,
+        cut,
     )
     small_piece = packed_piece[:, -128:].reshape(-1)
     shared_pieces = (
@@ -1764,12 +2229,20 @@
         .astype(jnp.float32)
     )
     output_piece = packed_piece[:, -128 - D : -128]
+    nope_width = HEADS * NOPE
+    query_piece = jnp.concatenate(
+        [
+            packed_piece[:, :nope_width].reshape(part_rows, HEADS, NOPE),
+            packed_piece[:, nope_width:query_width].reshape(part_rows, HEADS, ROPE),
+        ],
+        axis=2,
+    ).reshape(part_rows, query_width)
 
     return (
         output[None],
         token_grad[None],
         small_piece[cuts[0] : cuts[1]],
-        packed_piece[:, :query_width],
+        query_piece,
         packed_piece[:, query_width : query_width + down_width],
         small_piece[cuts[1] : cuts[2]],
         packed_piece[:, entry_width : -128 - D]
@@ -1781,7 +2254,7 @@
         small_piece[cuts[3] : cuts[4]].reshape(gain_width, expert_total),
         shared_pieces[0],
         shared_pieces[1],
-        sdown_piece,
+        sdown_summed.astype(jnp.float32),
         expert_gate_piece.astype(jnp.float32)[None],
         expert_up_piece.astype(jnp.float32)[None],
         expert_down_piece.astype(jnp.float32)[None],

time: 888 us -> 771 us (0.87)
  Pallas kernels: 452 us -> 579 us
  waiting for transfers between devices: 111 us -> 17.3 us
  matrix products: 161 us -> 81.3 us
  local copies, waits for them, and re-layouts: 87.3 us -> 42.7 us
  starting transfers between devices: 18.4 us -> 0.31 us
  other arithmetic: 41.8 us -> 27.7 us
    pallas_call x0 -> x2, Pallas kernels: none -> 95.6 us  [the longest x1 59.9 us: attend_back(): pl.pallas_call(functools.partial(attend_back_kernel, layout, len(before))...]
    all_gather x1 -> x0, waiting for transfers between devices: 51.6 us -> none  [body(): lax.all_gather(output_rows, ('fsdp', 'expert'), axis=0, tiled=True)]
    pallas_call x1, Pallas kernels: 145 us -> 184 us  [gather_rows(): pl.pallas_call(functools.partial(gather_kernel, depth, cut), out_shape=[j...]
    all_to_all x2 -> x0, waiting for transfers between devices: 31.1 us -> none  [the longest x1 31.1 us: from_experts(): lax.all_to_all(rows.reshape(PLANE, depth, capacity, -1), 'expert', split_...]
    dot_general x7 -> x4, matrix products: 60.4 us -> 33.3 us  [right_matmul(): lax.dot_general(former, latter, (((1,), (1,)), ((), ())), preferred_eleme...]
    dot_general x10 -> x0, matrix products: 21.6 us -> none  [the longest x1 4.84 us: body(): jnp.einsum('hqk,qhd->khd', weights_again, heads_low, preferred_element_ty...]
    dot_general x7 -> x1, matrix products: 17.2 us -> 0.21 us  [left_matmul(): lax.dot_general(former, latter, (((0,), (0,)), ((), ())), preferred_eleme...]
    slice x11 -> x4, local copies, waits for them, and re-layouts: 18.6 us -> 1.7 us  [the longest x1 0.87 us: body(): first_gain_grad = first_gain_grad[0]]
  transfers between devices with their start and end apart: 15 -> 8, of which waited for: 3 -> 1; matrix products, arithmetic and copies ran while one was open for 29% -> 17% of each run, Pallas kernels for 25% -> 53%
where the time goes in v4:
time: 771 us; the launch traced here: 763 us
  Pallas kernels  579 us (75%)
  matrix products  81.3 us (11%)
  local copies, waits for them, and re-layouts  42.7 us (6%)
  other arithmetic  27.7 us (4%)
  waiting for transfers between devices  17.3 us (2%)
  between operations  15.2 us (2%)
    pallas_call x1, Pallas kernels, gather_rows(): pl.pallas_call(functools.partial(gather_kernel, depth, cut), out_shape=[j...  184 us
    pallas_call x1, Pallas kernels, reduce_rows(): pl.pallas_call(functools.partial(reduce_kernel, depth, n, cut), out_shape...  138 us
    pallas_call x1, Pallas kernels, dispatch(): pl.pallas_call(functools.partial(dispatch_kernel, depth), out_shape=[jax....  82.3 us
    pallas_call x1, Pallas kernels, give_back(): pl.pallas_call(functools.partial(return_kernel, depth), out_shape=[jax.Sh...  79.4 us
    pallas_call x1, Pallas kernels, attend_back(): pl.pallas_call(functools.partial(attend_back_kernel, layout, len(before))...  59.9 us
    dot_general x5, matrix products, matmul(): return jnp.dot(former, latter, preferred_element_type=jnp.float32)  44.2 us
    pallas_call x1, Pallas kernels, attend(): pl.pallas_call(functools.partial(attend_kernel, layout), out_shape=[jax.S...  35.7 us
    dot_general x4, matrix products, right_matmul(): lax.dot_general(former, latter, (((1,), (1,)), ((), ())), preferred_eleme...  33.3 us
  transfers between devices with their start and end apart: 8, of which 1 were waited for; matrix products, arithmetic and copies ran while one was open for 17% of the time, Pallas kernels for 53%

profile of v4, /device:TPU:0, one launch (start us, length us, event | category | flops | bytes accessed | tf_op | source)
XLA Modules:
  0.0 763.4 jit_solution(12420531128913653693)
XLA Ops:
  7.3 0.7 all-gather.7.cloned.1.call-update
  8.0 0.7 all-gather.9.cloned.1.call-update
  8.8 0.7 all-gather.11.cloned.1.call-update
  10.4 0.6 pad_bitcast_fusion.1.refs_2_
  11.7 0.8 pad_maximum_fusion.1.refs_6_.refs_15_
  13.6 0.6 maximum_bitcast_fusion
  14.2 0.6 copy.74
  14.8 1.2 reshape.265
  16.0 0.6 pad.29
  16.6 1.4 reshape.266.refs_3_
  18.3 0.8 pad_maximum_fusion.2.refs_7_.refs_16_
  19.4 0.9 and_convert_fusion.refs_8_.refs_17_
  20.3 184.0 %shard_map.306 = (bf16[2048,6912]{1,0:T(8,128)(2,1)}, bf16[4,192,2048]{2,1,0:T(8,128)(2,1)}, s32[4,8,192]{2,1,0:T(8,128)}, bf16[2,4,4,64,1536]{4,3,2,1,0:T(8,128)(2,1)}, bf16[2,4,88,2048]{3,2,1,0:T(8,128)(2,1)}) custom-call(bf16[64,6912]{1,0:T(8,128)(2,1)} %copy-done.20, bf16[192,2048]{1,0:T(8,128)(2,1)} %bitcast.115, s32[8,192]{1,0:T(8,128)} %pad_bitcast_fusion.1.refs_2_, ...), custom_call_target="tpu_custom_call" | custom-call | flops 99999997952 | tf_op jit(solution)/shard_map/pallas_call | solution.py:470
  204.4 1.1 slice.81
  205.9 0.7 reshape.292.refs_4_.refs_13_
  206.6 0.7 reshape.291.refs_3_.refs_14_
  207.2 0.7 reshape.293.refs_5_
  207.9 1.7 compare_reduce_fusion
  209.6 0.7 copy-done.10
  210.3 0.9 convert_element_type.170
  211.2 35.7 %shard_map.307 = (bf16[192,2048]{1,0:T(8,128)(2,1)}, f32[192,2048]{1,0:T(8,128)}, bf16[192,2048]{1,0:T(8,128)(2,1)}, bf16[192,3072]{1,0:T(8,128)(2,1)}, bf16[192...) custom-call(bf16[192,2048]{1,0:T(8,128)(2,1)} %bitcast.136, ...), custom_call_target="tpu_custom_call" | custom-call | flops 40000000000 | tf_op jit(solution)/shard_map/pallas_call | solution.py:1625
  247.0 82.3 %shard_map.308 = (bf16[4,4,72,2048]{3,2,1,0:T(8,128)(2,1)}, bf16[4,192,2048]{2,1,0:T(8,128)(2,1)}, bf16[4,192,2048]{2,1,0:T(8,128)(2,1)}, bf16[2,4,4,64,1536]{4,...) custom-call(bf16[192,2048]{1,0:T(8,128)(2,1)} %get-tuple-element.67., ...), custom_call_target="tpu_custom_call", output_to_operand_aliasing={{5}: (5, {})} | custom-call | flops 99999997952 | tf_op jit(solution)/shard_map/pallas_call | solution.py:750
  330.0 3.9 fusion.29
  334.0 13.4 %fusion.32 = f32[1152,1408]{1,0:T(8,128)} fusion(bf16[1152,2048]{1,0:T(8,128)(2,1)S(1)} %bitcast.105, bf16[2048,1408]{1,0:T(8,128)(2,1)} %bitcast.132), kind=kOutput, calls=%fused_computation.92 | convolution fusion | flops 6643777536 | bytes 16973824 | tf_op jit(solution)/shard_map/dot_general | solution.py:49
  347.4 7.5 fusion.31
  355.0 15.9 %fusion.2 = (bf16[1152,1408]{1,0:T(8,128)(2,1)}, bf16[1152,1408]{1,0:T(8,128)(2,1)}, bf16[1152,1408]{1,0:T(8,128)(2,1)}, bf16[1152,1408]{1,0:T(8,128)(2,1)}) fusion(f32[1152]{0:T(1024)S(1)} %divide_reduce_fusion, f32[1152,1408]{1,0:T(8,128)} %fusion.32, f32[1152,1408]{1,0:T(8,128)S(1)} %fusion.31, bf16[1152,2048]{1,0:T(8,128)(2,1)S(1)} %bitcast.106, ...), kind=kOutput, calls=%fused_computation.8 | convolution fusion | flops 6676217856 | bytes 36442624 | tf_op jit(solution)/shard_map/dot_general | solution.py:49
  370.8 2.6 fusion.1
  373.6 10.8 %fusion.33 = f32[1152,2048]{1,0:T(8,128)S(1)} fusion(bf16[1152,1408]{1,0:T(8,128)(2,1)} %get-tuple-element.160.refs_5_, bf16[2048,1408]{1,0:T(8,128)(2,1)} %bitcast.133), kind=kOutput, calls=%fused_computation.93 | convolution fusion | flops 6643777536 | bytes 18448384 | tf_op jit(solution)/shard_map/dot_general | solution.py:59
  384.4 11.9 %add_convert_fusion = bf16[1152,2048]{1,0:T(8,128)(2,1)} fusion(f32[1152,2048]{1,0:T(8,128)S(1)} %fusion.33, bf16[1152,1408]{1,0:T(8,128)(2,1)S(1)} %copy-done.28, bf16[2048,1408]{1,0:T(8,128)(2,1)} %bitcast.135), kind=kOutput, calls=%fused_computation.2 | convolution fusion | flops 6648496128 | bytes 23166976 | tf_op jit(solution)/shard_map/dot_general | solution.py:59
  396.3 0.6 broadcast_in_dim.31.refs_1_
  397.0 79.4 %shard_map.309 = (f32[192,2048]{1,0:T(8,128)}, f32[4,8,192]{2,1,0:T(8,128)}, bf16[1024,1408]{1,0:T(8,128)(2,1)}, bf16[1024,1408]{1,0:T(8,128)(2,1)}, bf16[1408,1024]{1,0:T(8,128)(2,1)}) custom-call(bf16[4,4,72,2048]{3,2,1,0:T(8,128)(2,1)} %bitcast.142, f32[4,4,8,128]{3,2,1,0:T(8,128)} %broadcast_in_dim.31.refs_1_, bf16[4,4,72,192]{3,2,1,0:T(8,128)(2,1)} %bitcast.118, ...), custom_call_target="tpu_custom_call" | custom-call | flops 99999997952 | tf_op jit(solution)/shard_map/pallas_call | solution.py:1118
  476.3 0.8 slice.87
  477.2 1.6 fusion.30
  479.3 3.1 multiply_reduce_fusion
  483.0 0.8 reshape.282
  483.8 3.7 fusion.21
  487.5 3.3 bitcast_convert_fusion.2
  490.8 3.4 bitcast_convert_fusion.1
  494.2 1.3 copy-done.7
  495.5 3.2 bitcast_convert_fusion
  498.8 9.4 %fusion = bf16[1152,2048]{1,0:T(8,128)(2,1)} fusion(bf16[1152,1408]{1,0:T(8,128)(2,1)S(1)} %copy-done.4, bf16[1408,2048]{1,0:T(8,128)(2,1)S(1)} %bitcast.131, f32[1152]{0:T(1024)S(1)} %divide_reduce_fusion), kind=kOutput, calls=%fused_computation.5 | convolution fusion | flops 6648496128 | bytes 13734400 | tf_op jit(solution)/shard_map/dot_general | solution.py:49
  508.2 1.9 convert_element_type.166
  510.1 15.1 %reduce-scatter.16.cloned.1.call-done = bf16[1,4,64,1536]{3,2,1,0:T(8,128)(2,1)} async-done(((bf16[4,4,64,1536]{3,2,1,0:T(8,128)(2,1)}), bf16[1,4,64,1536]{3,2,1,0:T(8,128)(2,1)}) %reduce-scatter.16.cloned.1.call-update) | async-done | bytes 786448
  525.2 59.9 %shard_map.310 = (f32[192,2048]{1,0:T(8,128)}, bf16[32,4,16,1024]{3,2,1,0:T(8,128)(2,1)}, f32[8,512]{1,0:T(8,128)}, f32[8,2048]{1,0:T(8,128)}, bf16[2048,3712]{1...) custom-call(bf16[192,2048]{1,0:T(8,128)(2,1)} %get-tuple-element.154.refs_0_, ...), custom_call_target="tpu_custom_call" | custom-call | flops 99999997952 | tf_op jit(solution)/shard_map/pallas_call | solution.py:1886
  585.1 2.9 copy.75
  588.4 3.6 add_convert_fusion.1
  592.0 0.7 fusion.18
  592.7 0.9 fusion.17
  594.0 1.0 reshape.283.refs_3_
  595.0 137.5 %shard_map.311 = (f32[64,6912]{1,0:T(8,128)}, bf16[4,64,1536]{2,1,0:T(8,128)(2,1)}) custom-call(bf16[2048,3712]{1,0:T(8,128)(2,1)} %get-tuple-element.94.refs_0_, bf16[2048,1024]{1,0:T(8,128)(2,1)} %bitcast.147, bf16[2048,2048]{1,0:T(8,128)(2,1)} %get-tuple-element.96.refs_2_, bf16[2048,128]{1,0:T(8,128)(2,1)} %reshape.283.refs_3_, ...), custom_call_target="tpu_custom_call" | custom-call | flops 99999997952 | tf_op jit(solution)/shard_map/pallas_call | solution.py:1379
  732.5 2.3 reshape.290
  734.8 1.6 slice.94
  736.4 0.8 fusion.24
  737.9 0.7 copy.80
  738.6 1.1 fusion.26
  739.6 0.7 copy.83
  740.5 2.1 fusion.25
  742.8 1.3 reshape.287
  744.6 2.2 reshape.299
  746.8 1.0 copy.100
  748.1 1.4 squeeze.40
  749.5 1.4 squeeze.39
  751.4 2.2 fusion.8
  753.6 2.7 copy.109
  (153 shorter events, 8.7 us)
Async XLA Ops:
  7.2 2.4 copy-start.12
  7.2 3.1 copy-start.23
  7.2 3.2 copy-start.21
  7.2 3.2 copy-start.22
  7.2 3.8 copy-start.24
  7.2 4.0 copy-start.18
  7.2 197.1 %all-gather.7.cloned.1.call-start = ((), (), s32[]{:S(2)}) async-start(), calls=%async_computation.8 | async-start | bytes 8650752 | tf_op jit(solution)/shard_map/all_gather | solution.py:2015
  8.0 4.5 copy-start.13
  8.0 5.0 copy-start.14
  8.0 196.4 %all-gather.9.cloned.1.call-start = ((), (), s32[]{:S(2)}) async-start(), calls=%async_computation.9 | async-start | bytes 8650752 | tf_op jit(solution)/shard_map/all_gather | solution.py:2016
  8.7 195.7 %all-gather.11.cloned.1.call-start = ((), (), s32[]{:S(2)}) async-start(), calls=%async_computation.10 | async-start | bytes 8650752 | tf_op jit(solution)/shard_map/all_gather | solution.py:2017
  9.5 386.8 %reduce-scatter.12.cloned.1.call-start = ((), (), s32[]{:S(2)}) async-start(), calls=%async_computation.6 | async-start | bytes 4325376 | tf_op jit(solution)/shard_map/reduce_scatter | solution.py:2132
  13.5 5.5 copy-start.19
  13.5 5.6 copy-start.15
  14.2 5.0 copy-start.25
  14.2 5.0 copy-start.26
  14.2 5.0 copy-start.27
  19.3 1.0 copy-start.20
  205.9 41.1 %copy-start.16 = (f32[32,64]{1,0:T(8,128)}, f32[32,64]{1,0:T(8,128)S(1)}, u32[]{:S(2)}) copy-start(f32[32,64]{1,0:T(8,128)S(1)} %get-tuple-element.170) | copy-start | bytes 24580
  209.6 0.7 copy-start.10
  329.3 149.8 %reduce-scatter.10.cloned.1.call-start = ((), (), s32[]{:S(2)}) async-start(), calls=%async_computation.5 | async-start | bytes 9437184 | tf_op jit(solution)/shard_map/reduce_scatter | solution.py:2132
  329.8 4.1 copy-start.2
  329.9 4.1 slice-start
  329.9 178.3 %reduce-scatter.18.cloned.1.call-start = ((), (), s32[]{:S(2)}) async-start(), calls=%async_computation.12 | async-start | bytes 1802240
  329.9 4.0 slice-start.1
  329.9 17.4 %slice-start.2 = ((s8[5767168]{0:T(1024)(128)(4,1)}), s8[4194304]{0:T(1024)(128)(4,1)S(1)}, s32[]{:S(2)}) async-start(s8[5767168]{0:T(1024)(128)(4,1)} %bitcast.126), calls=%async_computation.15 | async-start | bytes 8388608
  330.0 17.4 %slice-start.6 = ((s8[4718592]{0:T(1024)(128)(4,1)}), s8[4194304]{0:T(1024)(128)(4,1)S(1)}, s32[]{:S(2)}) async-start(s8[4718592]{0:T(1024)(128)(4,1)} %bitcast.144), calls=%async_computation.19 | async-start | bytes 8388608
  334.0 13.4 %slice-start.3 = ((s8[5767168]{0:T(1024)(128)(4,1)}), s8[1572864]{0:T(1024)(128)(4,1)S(1)}, s32[]{:S(2)}) async-start(s8[5767168]{0:T(1024)(128)(4,1)} %bitcast.126), calls=%async_computation.16 | async-start | bytes 3145728
  334.0 13.4 %slice-start.7 = ((s8[4718592]{0:T(1024)(128)(4,1)}), s8[524288]{0:T(1024)(128)(4,1)S(1)}, s32[]{:S(2)}) async-start(s8[4718592]{0:T(1024)(128)(4,1)} %bitcast.144), calls=%async_computation.20 | async-start | bytes 1048576
  373.6 10.8 %copy-start.28 = (bf16[1152,1408]{1,0:T(8,128)(2,1)S(1)}, bf16[1152,1408]{1,0:T(8,128)(2,1)}, u32[]{:S(2)}) copy-start(bf16[1152,1408]{1,0:T(8,128)(2,1)} %get-tuple-element.161.refs_6_) | copy-start | bytes 9732100
  396.3 128.9 %reduce-scatter.16.cloned.1.call-start = ((), (), s32[]{:S(2)}) async-start(), calls=%async_computation.11 | async-start | bytes 3932160
  397.0 81.9 %copy-start = (f32[192,2048]{1,0:T(8,128)S(1)}, f32[192,2048]{1,0:T(8,128)}, u32[]{:S(2)}) copy-start(f32[192,2048]{1,0:T(8,128)} %get-tuple-element.66) | copy-start | bytes 4718596
  476.3 2.9 copy-start.17
  476.3 3.0 copy-start.3
  478.9 3.7 copy-start.5
  479.1 272.3 %reduce-scatter.14.cloned.1.call-start = ((), (), s32[]{:S(2)}) async-start(), calls=%async_computation.7 | async-start | bytes 3932160 | tf_op jit(solution)/shard_map/reduce_scatter | solution.py:2194
  483.8 3.7 copy-start.9
  487.5 3.3 copy-start.8
  487.5 11.3 %slice-start.4 = ((s8[5767168]{0:T(1024)(128)(4,1)}), s8[4194304]{0:T(1024)(128)(4,1)S(1)}, s32[]{:S(2)}) async-start(s8[5767168]{0:T(1024)(128)(4,1)} %bitcast.129), calls=%async_computation.17 | async-start | bytes 8388608
  490.8 4.7 copy-start.7
  490.8 8.0 %slice-start.5 = ((s8[5767168]{0:T(1024)(128)(4,1)}), s8[1572864]{0:T(1024)(128)(4,1)S(1)}, s32[]{:S(2)}) async-start(s8[5767168]{0:T(1024)(128)(4,1)} %bitcast.129), calls=%async_computation.18 | async-start | bytes 3145728
  494.2 4.6 copy-start.4
  585.1 3.3 copy-start.6
  585.1 3.3 copy-start.11
  746.8 4.7 copy-start.1
Sparse Core Ops, SparseCore 0:
  9.6 18.6 all-gather.6
  29.9 17.1 all-gather.8
  48.6 17.1 all-gather.10
  329.4 10.2 reduce-scatter.11
  341.9 15.7 reduce-scatter.9
  396.4 54.6 reduce-scatter.17
  479.2 45.9 reduce-scatter.15
  592.1 76.8 reduce-scatter.13

commit v5 on v4

--- a/solution.py
+++ b/solution.py
@@ -64,6 +64,7 @@
 PLANE = 4
 MESH = pl.DeviceIdType.MESH
 MEBIBYTE = 1024 * 1024
+GROUPS = 4
 LONG = pl.CostEstimate(flops=100 * 10**9, bytes_accessed=0, transcendentals=0)
 MIDDLE = pl.CostEstimate(flops=40 * 10**9, bytes_accessed=0, transcendentals=0)
 
@@ -143,7 +144,7 @@
     return start, finish
 
 
-def exchange_plane(half, place, source_of, target_of, own_sem, send, receive):
+def exchange_plane(half, place, source_of, target_of, own_sem, send, receive, own_there=False):
     spot = place % PLANE
 
     def to(offset, level):
@@ -175,10 +176,12 @@
     def start(level):
         for offset in range(1, PLANE):
             to(offset, level).start()
-        own(level).start()
+        if not own_there:
+            own(level).start()
 
     def finish(level):
-        own(level).wait()
+        if not own_there:
+            own(level).wait()
         for offset in range(1, PLANE):
             came(offset, level).wait_recv()
             to(offset, level).wait_send()
@@ -198,7 +201,11 @@
     lax.fori_loop(0, block.shape[1] // 512, columns, 0)
 
 
-def gather_kernel(depth, cut, *refs):
+def cuts_of(width, count):
+    return [width * k // count // 128 * 128 for k in range(count)] + [width]
+
+
+def gather_kernel(depth, cuts, *refs):
     in_ref, *line_ins, move_in, down_in = refs[:5]
     out_ref, *line_outs, shared_out, down_out = refs[5:10]
     own_sem, zs, zr, ps, pr, qs, qr, cs, cr, ls, lr, ms, mr, *shared_sems = refs[10:]
@@ -210,7 +217,8 @@
     total = depth * PLANE
     mates = plane_mates(place)
     rows, width = in_ref.shape
-    columns = (pl.ds(0, cut), pl.ds(cut, width - cut))
+    columns = [pl.ds(low, high - low) for low, high in zip(cuts[:-1], cuts[1:])]
+    count = len(columns)
     greet_neighbours(half, place, depth)
 
     def at(which, block, count=1):
@@ -232,18 +240,25 @@
         target = at(which, source * PLANE + spot)
         start = in_ref.at[:, columns[which]] if own else target
         return remote(
-            start, target, ps.at[which, source], pr.at[which, source], (half, mates[which])
+            start,
+            target,
+            ps.at[which, source],
+            pr.at[which, source],
+            (half, mates[which % 2]),
         )
 
     def plane_two(which, source, turn):
         base = source * PLANE
-        if which == 0:
-            block = at(0, base + spot - spot % 2, 2)
+        if which % 2 == 0:
+            block = at(which, base + spot - spot % 2, 2)
         else:
-            block = at(1, base + (spot + 2 * turn) % PLANE)
-        slot = which + turn
+            block = at(which, base + (spot + 2 * turn) % PLANE)
         return remote(
-            block, block, qs.at[slot, source], qr.at[slot, source], (half, mates[1 - which])
+            block,
+            block,
+            qs.at[which, turn, source],
+            qr.at[which, turn, source],
+            (half, mates[1 - which % 2]),
         )
 
     def core(which, source):
@@ -264,7 +279,7 @@
 
     def trail_own(which):
         return pltpu.make_async_copy(
-            line_ins[which], line_outs[which].at[level], own_sem.at[2 + which]
+            line_ins[which], line_outs[which].at[level], own_sem.at[count + which]
         )
 
     move_start, move_finish = exchange_along(
@@ -273,12 +288,12 @@
         place,
         move_in,
         lambda source: shared_out.at[half, source, spot],
-        own_sem.at[4],
+        own_sem.at[count + 2],
         ms,
         mr,
     )
     items = range(depth + 2)
-    down_own = pltpu.make_async_copy(down_in, down_out.at[half, spot], own_sem.at[5])
+    down_own = pltpu.make_async_copy(down_in, down_out.at[half, spot], own_sem.at[count + 3])
 
     def shared_at(item, first, count):
         if item < depth:
@@ -311,14 +326,14 @@
         block = shared_at(item, 0, PLANE)
         return remote(block, block, us.at[item], ur.at[item], (1 - half, place))
 
-    seconds = ((0, 0), (1, 0), (1, 1))
+    seconds = [(which, turn) for which in range(count) for turn in range(1 + which % 2)]
 
     def own_copy(which):
         return pltpu.make_async_copy(
             in_ref.at[:, columns[which]], at(which, place), own_sem.at[which]
         )
 
-    for which in range(2):
+    for which in range(count):
 
         @pl.when(level > 0)
         def _():
@@ -334,8 +349,6 @@
     down_own.start()
     for which in range(2):
         trail_own(which).start()
-    for which in range(2):
-        own_copy(which).wait()
 
     def trail_first():
         for which in range(2):
@@ -370,7 +383,7 @@
             act(level + step, 0)
 
     def arrive(source, way):
-        for which in range(2):
+        for which in range(count):
             along(which, way, source).wait_recv()
 
             @pl.when((level < depth - 1) if way == 1 else (level > 0))
@@ -380,19 +393,21 @@
             plane_one(which, source).start()
 
     def spread(source, way):
-        for which in range(2):
+        for which in range(count):
             plane_one(which, source).wait_recv()
             for kind, turn in seconds:
                 if kind == which:
                     plane_two(kind, source, turn).start()
 
     def share(source, way):
-        for which in range(2):
+        for which in range(count):
             for kind, turn in seconds:
                 if kind == which:
                     plane_two(kind, source, turn).wait_recv()
             core(which, source).start()
 
+    for which in range(count):
+        own_copy(which).wait()
     visit(0, spread)
     for step in range(1, depth):
         visit(step, arrive)
@@ -443,6 +458,7 @@
             def _():
                 trail(which, 0, source).wait_send()
 
+        for which in range(count):
             core(which, source).wait_recv()
             core(which, source).wait_send()
             plane_one(which, source).wait_send()
@@ -462,13 +478,14 @@
     lax.fori_loop(0, depth, finish, 0)
 
 
-def gather_rows(value, first, second, moved, down, cut):
+def gather_rows(value, first, second, moved, down, cuts):
     rows, width = value.shape
     total = lax.axis_size("expert")
     depth = total // PLANE
+    count = len(cuts) - 1
     semaphores = pltpu.SemaphoreType.DMA
     return pl.pallas_call(
-        functools.partial(gather_kernel, depth, cut),
+        functools.partial(gather_kernel, depth, cuts),
         out_shape=[
             jax.ShapeDtypeStruct((2 * total * rows, width), value.dtype),
             jax.ShapeDtypeStruct((depth,) + first.shape, first.dtype),
@@ -476,18 +493,18 @@
             jax.ShapeDtypeStruct((2, depth, PLANE) + moved.shape[1:], moved.dtype),
             jax.ShapeDtypeStruct((2, PLANE) + down.shape, down.dtype),
         ],
-        in_specs=[pl.BlockSpec(memory_space=pl.ANY)] * 5,
+        in_specs=[pl.BlockSpec(memory_space=pltpu.VMEM)] * 5,
         out_specs=[pl.BlockSpec(memory_space=pl.ANY)] * 5,
         scratch_shapes=[
-            semaphores((6,)),
-            semaphores((2, 2, depth)),
-            semaphores((2, depth)),
-            semaphores((2, depth)),
-            semaphores((2, depth)),
-            semaphores((3, depth)),
-            semaphores((3, depth)),
-            semaphores((2, depth)),
-            semaphores((2, depth)),
+            semaphores((count + 4,)),
+            semaphores((count, 2, depth)),
+            semaphores((count, depth)),
+            semaphores((count, depth)),
+            semaphores((count, depth)),
+            semaphores((count, 2, depth)),
+            semaphores((count, 2, depth)),
+            semaphores((count, depth)),
+            semaphores((count, depth)),
             semaphores((2, 2, depth)),
             semaphores((2, depth)),
             semaphores((depth,)),
@@ -520,16 +537,19 @@
     x_ref, choose_ref, grad_in, shared_in, down_in = refs[:5]
     rows_out, forth_out, back_out, wide_out, tall_out, grad_out = refs[6:12]
     lines, placed, grads, weights, downs, low_ref, hidden_ref, forth_ref, back_ref = refs[12:21]
-    wide_ref, tall_ref, grad_placed, load_sem, out_sem, zs, zr, es, er, own_sem = refs[21:31]
-    done_sem, gs, gr, grad_sem = refs[31:]
+    wide_ref, tall_ref, grad_placed, wide_give, wide_take, tall_give, tall_take = refs[21:28]
+    load_sem, out_sem, zs, zr, es, er, own_sem, done_sem, gs, gr, grad_sem = refs[28:39]
+    ws, wr, ts, tr = refs[39:]
     half = lax.axis_index("fsdp")
     place = lax.axis_index("expert")
+    other = (1 - half, place)
     level = place // PLANE
     spot = place % PLANE
     padded, width = downs.shape
-    true = down_in.shape[0]
-    chunk = 256 if padded % 256 == 0 else 128
-    greet(line_others(half, place, depth) + plane_others(half, place))
+    share = padded // 2
+    true = down_in.shape[1]
+    chunk = padded
+    greet(line_others(half, place, depth) + plane_others(half, place) + [other])
 
     def along(way, source):
         block = lines.at[source]
@@ -538,8 +558,12 @@
 
     loads = [
         pltpu.make_async_copy(shared_in, weights, load_sem.at[0]),
-        pltpu.make_async_copy(down_in, downs.at[pl.ds(0, true), :], load_sem.at[1]),
-        pltpu.make_async_copy(grad_in, grads, load_sem.at[2]),
+        pltpu.make_async_copy(grad_in, grads, load_sem.at[1]),
+    ] + [
+        pltpu.make_async_copy(
+            down_in.at[k], downs.at[pl.ds(k * share, true), :], load_sem.at[2 + k]
+        )
+        for k in range(2)
     ]
     lines[level] = x_ref[...]
 
@@ -552,14 +576,17 @@
         pass_on(way, level)
     for load in loads:
         load.start()
-    if padded > true:
-        downs[pl.ds(true, padded - true), :] = jnp.zeros((padded - true, width), downs.dtype)
+    if share > true:
+        for k in range(2):
+            downs[pl.ds(k * share + true, share - true), :] = jnp.zeros(
+                (share - true, width), downs.dtype
+            )
 
     rows_start, rows_finish = exchange_plane(
         half,
         place,
         lambda mate, source: placed.at[source, mate],
-        lambda mate, source: rows_out.at[mate, source],
+        lambda mate, source: rows_out.at[source, mate],
         own_sem,
         es,
         er,
@@ -568,7 +595,7 @@
         half,
         place,
         lambda mate, source: grad_placed.at[source // 2, mate],
-        lambda mate, source: grad_out.at[mate, source],
+        lambda mate, source: grad_out.at[source, mate],
         grad_sem,
         gs,
         gr,
@@ -602,14 +629,14 @@
         lax.fori_loop(0, padded // chunk, inner, 0)
 
         def outer(n, carry):
-            at = pl.ds(pl.multiple_of(n * 512, 512), 512)
+            at = pl.ds(pl.multiple_of(n * 1024, 1024), 1024)
             forth_ref[:, at] = jnp.dot(
                 hidden_ref[source], downs[:, at], preferred_element_type=jnp.float32
             ).astype(forth_ref.dtype)
             back_ref[:, at] = dot_nt(low_ref[source], weights[at, :]).astype(back_ref.dtype)
             return carry
 
-        lax.fori_loop(0, width // 512, outer, 0)
+        lax.fori_loop(0, width // 1024, outer, 0)
         outs = [
             pltpu.make_async_copy(forth_ref, forth_out.at[source], out_sem.at[0]),
             pltpu.make_async_copy(back_ref, back_out.at[source], out_sem.at[1]),
@@ -665,55 +692,94 @@
     part = wide_ref.shape[2]
     chunk_rows = max(PLANE * part, 128)
     per_chunk = chunk_rows // (PLANE * part)
+    core_rows = width // 2
+    tall_rows = tall_ref.shape[1]
+    tall_count = share // tall_rows
+
+    def wide_value(owner, n):
+        at = pl.ds(pl.multiple_of(owner * core_rows + n * chunk_rows, chunk_rows), chunk_rows)
+        return dot_tn(all_lines(lines, at), low_ref[...].reshape(depth * tokens, -1))
+
+    def tall_value(owner, k):
+        at = pl.ds(pl.multiple_of(owner * share + k * tall_rows, tall_rows), tall_rows)
+        return dot_tn(all_lines(hidden_ref, at), grads[...].reshape(depth * tokens, -1))
+
+    def wide_send(k):
+        return remote(wide_give.at[k], wide_take.at[k], ws.at[k], wr.at[k], other)
+
+    def tall_send(k):
+        return remote(tall_give.at[k], tall_take.at[k], ts.at[k], tr.at[k], other)
+
+    def split(value, j):
+        first = j * PLANE * part
+        return [value[first + k * part : first + (k + 1) * part] for k in range(PLANE)]
+
+    def give_wide(n, carry):
+        value = wide_value(1 - half, n)
+        for j in range(per_chunk):
+            for k, block in enumerate(split(value, j)):
+                wide_give[n * per_chunk + j, k] = block.astype(wide_give.dtype)
+            wide_send(n * per_chunk + j).start()
+        return carry
+
+    def give_tall(k, carry):
+        tall_give[k] = tall_value(1 - half, k).astype(tall_give.dtype)
+        tall_send(k).start()
+        return carry
 
     def write_wide(k):
         return pltpu.make_async_copy(
-            wide_ref.at[k % 2], wide_out.at[k // depth, :, k % depth], done_sem.at[0, k % 2]
-        )
-
-    def wide_tile(n, carry):
-        at = pl.ds(pl.multiple_of(n * chunk_rows, chunk_rows), chunk_rows)
-        value = dot_tn(
-            all_lines(lines, at), low_ref[...].reshape(depth * tokens, -1)
-        ).astype(wide_ref.dtype)
+            wide_ref.at[k % 2], wide_out.at[:, k], done_sem.at[0, k % 2]
+        )
+
+    def keep_wide(n, carry):
+        value = wide_value(half, n)
         for j in range(per_chunk):
-            k = n * per_chunk + j
-
-            @pl.when(k >= 2)
+            at = n * per_chunk + j
+
+            @pl.when(at >= 2)
             def _():
-                write_wide(k - 2).wait()
-
-            for spot_at in range(PLANE):
-                first = (j * PLANE + spot_at) * part
-                wide_ref[k % 2, spot_at] = value[first : first + part]
-            write_wide(k).start()
+                write_wide(at - 2).wait()
+
+            wide_send(at).wait_recv()
+            for k, block in enumerate(split(value, j)):
+                total = block + wide_take[at, k].astype(jnp.float32)
+                wide_ref[at % 2, k] = total.astype(wide_ref.dtype)
+            write_wide(at).start()
         return carry
 
-    lax.fori_loop(0, width // chunk_rows, wide_tile, 0)
-    for k in (2 * depth - 2, 2 * depth - 1):
+    lax.fori_loop(0, core_rows // chunk_rows, give_wide, 0)
+    lax.fori_loop(0, tall_count, give_tall, 0)
+    lax.fori_loop(0, core_rows // chunk_rows, keep_wide, 0)
+    for k in range(max(0, depth - 2), depth):
         write_wide(k).wait()
-    tall_rows = tall_ref.shape[1]
-    tall_count = -(-true // tall_rows)
-
-    def write_tall(k, size):
-        return pltpu.make_async_copy(
-            tall_ref.at[k % 2, pl.ds(0, size), :],
-            tall_out.at[pl.ds(k * tall_rows, size), :],
-            done_sem.at[1, k % 2],
-        )
-
     writes = []
     for k in range(tall_count):
         if k >= 2:
             writes[k - 2].wait()
-        tall_ref[k % 2] = dot_tn(
-            all_lines(hidden_ref, pl.ds(k * tall_rows, tall_rows)),
-            grads[...].reshape(depth * tokens, -1),
-        ).astype(tall_ref.dtype)
-        writes.append(write_tall(k, min(tall_rows, true - k * tall_rows)))
+        value = tall_value(half, k)
+        tall_send(k).wait_recv()
+        total = value + tall_take[k].astype(jnp.float32)
+        tall_ref[k % 2] = total.astype(tall_ref.dtype)
+        size = min(tall_rows, true - k * tall_rows)
+        writes.append(
+            pltpu.make_async_copy(
+                tall_ref.at[k % 2, pl.ds(0, size), :],
+                tall_out.at[pl.ds(k * tall_rows, size), :],
+                done_sem.at[1, k % 2],
+            )
+        )
         writes[k].start()
     for write in writes[-2:]:
         write.wait()
+
+    def given(k, carry):
+        wide_send(k).wait_send()
+        return carry
+
+    lax.fori_loop(0, depth, given, 0)
+    for k in range(tall_count):
+        tall_send(k).wait_send()
 
     def finish_grad(n, carry):
         grad_finish(2 * n + 1)
@@ -750,11 +816,11 @@
     return pl.pallas_call(
         functools.partial(dispatch_kernel, depth),
         out_shape=[
-            jax.ShapeDtypeStruct((PLANE, depth, capacity, width), low),
+            jax.ShapeDtypeStruct((depth, PLANE, capacity, width), low),
             jax.ShapeDtypeStruct((depth, tokens, width), low),
             jax.ShapeDtypeStruct((depth, tokens, width), low),
-            jax.ShapeDtypeStruct((2, PLANE, depth, part, 2 * padded), low),
-            jax.ShapeDtypeStruct(down_full.shape, low),
+            jax.ShapeDtypeStruct((PLANE, depth, part, 2 * padded), low),
+            jax.ShapeDtypeStruct(down_full.shape[1:], low),
             jax.ShapeDtypeStruct(grad_rows.shape, low),
         ],
         in_specs=[local, local] + [anywhere] * 4,
@@ -773,7 +839,11 @@
             pltpu.VMEM((2, PLANE, part, 2 * padded), low),
             pltpu.VMEM((2, 128, width), low),
             pltpu.VMEM((depth // 2, PLANE, capacity, width), low),
-            semaphores((3,)),
+            pltpu.VMEM((depth, PLANE, part, 2 * padded), low),
+            pltpu.VMEM((depth, PLANE, part, 2 * padded), low),
+            pltpu.VMEM((padded // 256, 128, width), low),
+            pltpu.VMEM((padded // 256, 128, width), low),
+            semaphores((4,)),
             semaphores((2,)),
             semaphores((2, depth)),
             semaphores((depth,)),
@@ -784,12 +854,114 @@
             semaphores((PLANE, depth)),
             semaphores((PLANE, depth)),
             semaphores((depth,)),
+            semaphores((depth,)),
+            semaphores((depth,)),
+            semaphores((padded // 256,)),
+            semaphores((padded // 256,)),
         ],
         compiler_params=pltpu.CompilerParams(
-            collective_id=3, has_side_effects=True, vmem_limit_bytes=56 * MEBIBYTE
+            collective_id=3, has_side_effects=True, vmem_limit_bytes=62 * MEBIBYTE
         ),
         cost_estimate=LONG,
     )(x, choose, grad_line, shared_full, down_full, grad_rows)
+
+
+def expert_kernel(total, *refs):
+    x_ref, grad_ref, gate_in, up_in, down_in, router_ref = refs[:6]
+    scaled_ref, d_gate_ref, d_up_ref, back_ref, out_ref, slot_ref = refs[6:12]
+    gates, ups, downs, hidden, sem = refs[12:]
+    rows = x_ref.shape[0]
+    width, inner = gates.shape
+    wide = jnp.float32
+    loads = [
+        pltpu.make_async_copy(source, target, sem.at[k])
+        for k, (source, target) in enumerate(zip((gate_in, up_in, down_in), (gates, ups, downs)))
+    ]
+    first = pl.program_id(0) == 0
+
+    @pl.when(first)
+    def _():
+        for load in loads:
+            load.start()
+
+    logits = jnp.dot(x_ref[...], router_ref[...], preferred_element_type=wide)
+    lanes = lax.broadcasted_iota(jnp.int32, logits.shape, 1)
+    logits = jnp.where(lanes < total, logits, FLOOR_SCORE)
+    powers = jnp.exp(logits - jnp.max(logits, axis=-1, keepdims=True))
+    probs = powers / jnp.sum(powers, axis=-1, keepdims=True)
+    mine = jnp.where(lanes == lax.axis_index("expert"), probs, 0.0)
+    gate = jnp.sum(mine, axis=-1, keepdims=True)
+
+    @pl.when(first)
+    def _():
+        for load in loads:
+            load.wait()
+
+    def columns(start, size, slots):
+        at = lanes_at(start, size)
+        former = jnp.dot(x_ref[...], gates[:, at], preferred_element_type=wide)
+        latter = jnp.dot(x_ref[...], ups[:, at], preferred_element_type=wide)
+        raw = dot_nt(grad_ref[...], downs[at, :])
+        sig = 1.0 / (1.0 + jnp.exp(-former))
+        act = former * sig
+        low = (act * latter).astype(hidden.dtype)
+        hidden[:, at] = low
+        low = low.astype(wide)
+        scaled_ref[:, at] = (low * gate).astype(hidden.dtype)
+        grad = raw * gate
+        d_gate_ref[:, at] = (grad * latter * (sig + act * (1.0 - sig))).astype(hidden.dtype)
+        d_up_ref[:, at] = (grad * act).astype(hidden.dtype)
+        return slots + jnp.sum(low * raw, axis=-1, keepdims=True)
+
+    full = inner // 256
+    slots = lax.fori_loop(
+        0, full, lambda n, slots: columns(n * 256, 256, slots), jnp.zeros((rows, 1), wide)
+    )
+    if inner % 256:
+        slots = columns(full * 256, inner % 256, slots)
+    slot_ref[...] = jnp.broadcast_to(slots, slot_ref.shape)
+
+    def outward(n, carry):
+        at = lanes_at(n * 256, 256)
+        back = dot_nt(d_gate_ref[...], gates[at, :]) + dot_nt(d_up_ref[...], ups[at, :])
+        back_ref[:, at] = back.astype(back_ref.dtype)
+        out = jnp.dot(hidden[...], downs[:, at], preferred_element_type=wide)
+        out_ref[:, at] = (out * gate).astype(out_ref.dtype)
+        return carry
+
+    lax.fori_loop(0, width // 256, outward, 0)
+
+
+def run_expert(rows, grads, gate_full, up_full, down_full, router, total):
+    count, width = rows.shape
+    inner = gate_full.shape[1]
+    low, wide = rows.dtype, jnp.float32
+    tile = count // 2
+    anywhere = pl.BlockSpec(memory_space=pl.ANY)
+
+    def tiles(span):
+        return pl.BlockSpec((tile, span), lambda i: (i, 0))
+
+    spans = (inner, inner, inner, width, width)
+    return pl.pallas_call(
+        functools.partial(expert_kernel, total),
+        grid=(2,),
+        out_shape=[jax.ShapeDtypeStruct((count, span), low) for span in spans]
+        + [jax.ShapeDtypeStruct((count, 128), wide)],
+        in_specs=[tiles(width), tiles(width)]
+        + [anywhere] * 3
+        + [pl.BlockSpec(router.shape, lambda i: (0, 0))],
+        out_specs=[tiles(span) for span in spans] + [tiles(128)],
+        scratch_shapes=[
+            pltpu.VMEM(gate_full.shape, low),
+            pltpu.VMEM(up_full.shape, low),
+            pltpu.VMEM(down_full.shape, low),
+            pltpu.VMEM((tile, inner), low),
+            pltpu.SemaphoreType.DMA((3,)),
+        ],
+        compiler_params=pltpu.CompilerParams(vmem_limit_bytes=62 * MEBIBYTE),
+        cost_estimate=MIDDLE,
+    )(rows, grads, gate_full, up_full, down_full, router)
 
 
 def return_kernel(depth, *refs):
@@ -818,14 +990,14 @@
         where = (half, place - spot + mate)
         return (
             remote(
-                rows_in.at[mate, source],
+                rows_in.at[source, mate],
                 came.at[spot, source],
                 es.at[offset, source],
                 er.at[offset, source],
                 where,
             ),
             remote(
-                scalars_in.at[mate, source],
+                scalars_in.at[source, mate],
                 scalars.at[spot, source],
                 ss.at[offset, source],
                 sr.at[offset, source],
@@ -845,10 +1017,10 @@
     def own_rows(source):
         return (
             pltpu.make_async_copy(
-                rows_in.at[spot, source], came.at[spot, source], own_sem.at[0, source]
+                rows_in.at[source, spot], came.at[spot, source], own_sem.at[0, source]
             ),
             pltpu.make_async_copy(
-                scalars_in.at[spot, source], scalars.at[spot, source], own_sem.at[1, source]
+                scalars_in.at[source, spot], scalars.at[spot, source], own_sem.at[1, source]
             ),
         )
 
@@ -1030,13 +1202,14 @@
         lines = lax.broadcasted_iota(jnp.int32, (8, tokens), 0)
         probs = jnp.zeros((8, tokens), jnp.float32)
         for mate in range(PLANE):
-            part = jnp.dot(
-                scalars[mate, source, :, :capacity],
+            part = lax.dot_general(
+                scalars[mate, source],
                 choose_ref[source, mate].astype(jnp.float32),
+                (((0,), (0,)), ((), ())),
                 preferred_element_type=jnp.float32,
                 precision=lax.Precision.HIGHEST,
             )
-            probs = jnp.where(lines == mate, part, probs)
+            probs = jnp.where(lines == mate, part[:8], probs)
 
         @pl.when((source >= level) & (level > 0))
         def _():
@@ -1128,7 +1301,7 @@
         out_specs=[local, local, anywhere, anywhere, anywhere],
         scratch_shapes=[
             pltpu.VMEM((PLANE, depth, capacity, width), low),
-            pltpu.VMEM((PLANE, depth, 8, 128), wide),
+            pltpu.VMEM((PLANE, depth, capacity, 128), wide),
             pltpu.VMEM((2, tokens, width), low),
             pltpu.VMEM((2, tokens, width), low),
             pltpu.VMEM((depth + 1, tokens, width), low),
@@ -1466,7 +1639,7 @@
         half,
         place,
         lambda mate, source: grad_placed.at[source // 2, mate],
-        lambda mate, source: grad_out.at[mate, source],
+        lambda mate, source: grad_out.at[source, mate],
         grad_sem,
         gs,
         gr,
@@ -1525,10 +1698,10 @@
             send.start()
 
     def nope_part(n, carry):
-        queries[:, lanes_at(n * 512, 512)] = through(n * 512, 512).astype(low)
+        queries[:, lanes_at(n * 1024, 1024)] = through(n * 1024, 1024).astype(low)
         return carry
 
-    lax.fori_loop(0, nope_width // 512, nope_part, 0)
+    lax.fori_loop(0, nope_width // 1024, nope_part, 0)
 
     def rope_part(n, carry):
         values = through(nope_width + n * 512, 512)
@@ -1589,13 +1762,13 @@
     loads[1].wait()
 
     def project(n, carry):
-        at = lanes_at(n * 512, 512)
+        at = lanes_at(n * 1024, 1024)
         residual[:, at] = x_ref[:, at].astype(jnp.float32) + jnp.dot(
             heads[...], outs[:, at], preferred_element_type=jnp.float32
         )
         return carry
 
-    lax.fori_loop(0, width // 512, project, 0)
+    lax.fori_loop(0, width // 1024, project, 0)
     total = residual[...]
     mixed[...] = (total * row_scale(total) * feed_gain[...]).astype(low)
     each_grad(lambda n: grad_finish(2 * n))
@@ -1620,7 +1793,7 @@
         ((2 * rows, 128), low),
         ((rows, 128), wide),
         ((rows, HEADS * VALUE), low),
-        ((PLANE, depth, capacity, width), low),
+        ((depth, PLANE, capacity, width), low),
     ]
     return pl.pallas_call(
         functools.partial(attend_kernel, layout),
@@ -1668,14 +1841,15 @@
 
 
 def attend_back_kernel(layout, count, *refs):
-    d_ref, packed, up_in, queries, expanded, keys_rope, log_total = refs[:7]
-    latent, compressed, normed, heads, x_ref, above = refs[7:13]
-    latent_gain, first_gain, cosine, sine, mask, rows_in = refs[13:19]
-    refs = refs[19 + count :]
-    token_grad, up_grad, gain_grad, first_grad, entry_grad, out_grad, rows_out = refs[:7]
-    outs, ups, d_heads, own, prior, came, prior_rope, came_rope, total_low = refs[7:16]
-    entry, entry_low, up_tile, entry_tile, out_tile = refs[16:21]
-    load_sem, up_sem, send_sem, receive_sem, write_sem, es, er, own_sem = refs[21:]
+    back_in, packed, up_in, queries, expanded, keys_rope, log_total = refs[:7]
+    latent, compressed, normed, heads, x_ref, residual, cotangent = refs[7:14]
+    d_logits, router, latent_gain, first_gain, feed_gain, cosine, sine, mask = refs[14:22]
+    rows_in = refs[22]
+    refs = refs[24 + count :]
+    token_grad, up_grad, gain_grad, first_grad, feed_grad, entry_grad, out_grad = refs[:7]
+    rows_out, outs, ups, d_heads, own, prior, came, prior_rope, came_rope = refs[7:16]
+    entry, entry_low, up_tile, entry_tile, out_tile, d_ref = refs[16:22]
+    load_sem, up_sem, send_sem, receive_sem, write_sem, es, er = refs[22:]
     entry_width, out_start = layout
     half = lax.axis_index("fsdp")
     place = lax.axis_index("expert")
@@ -1684,6 +1858,14 @@
     low = d_ref.dtype
     wide = jnp.float32
     scale = (NOPE + ROPE) ** (-0.5)
+
+    def norm_back(values, gain, incoming):
+        root = row_scale(values)
+        scaled = gain * incoming
+        inner = jnp.mean(values * scaled, axis=-1, keepdims=True)
+        gain_sum = jnp.sum(incoming * values * root, axis=0, keepdims=True)
+        return root * scaled - values * (root * root * root) * inner, gain_sum
+
     nope_width = HEADS * NOPE
     query_width = HEADS * (NOPE + ROPE)
     loads = [
@@ -1697,11 +1879,12 @@
     rows_start, rows_finish = exchange_plane(
         half,
         place,
-        lambda mate, level: rows_in.at[mate, level],
-        lambda mate, level: rows_out.at[mate, level],
-        own_sem,
+        lambda mate, level: rows_in.at[level, mate],
+        lambda mate, level: rows_out.at[level, mate],
+        None,
         es,
         er,
+        own_there=True,
     )
 
     def each_level(act):
@@ -1709,9 +1892,14 @@
             act(level)
             return carry
 
-        lax.fori_loop(0, rows_in.shape[1], one, 0)
+        lax.fori_loop(0, rows_in.shape[0], one, 0)
 
     each_level(rows_start)
+    mixed_grad = back_in[...] + dot_nt(d_logits[...], router[...])
+    through_norm, gain_sum = norm_back(residual[...], feed_gain[...], mixed_grad)
+    feed_grad[...] = jnp.broadcast_to(gain_sum, feed_grad.shape)
+    token_grad[...] = cotangent[...].astype(wide) + through_norm
+    d_ref[...] = token_grad[...].astype(low)
 
     def write(kind, k):
         staged, target = ((out_tile, out_grad), (entry_tile, entry_grad), (up_tile, up_grad))[kind]
@@ -1748,11 +1936,11 @@
     loads[0].wait()
 
     def head_part(n, carry):
-        at = lanes_at(n * 512, 512)
+        at = lanes_at(n * 1024, 1024)
         d_heads[:, at] = dot_nt(d_ref[...], outs[at, :]).astype(low)
         return carry
 
-    lax.fori_loop(0, width // 512, head_part, 0)
+    lax.fori_loop(0, width // 1024, head_part, 0)
 
     def turn_back(values):
         return values * cosine[...] - turned(values) * sine[...]
@@ -1810,36 +1998,29 @@
         for send in sends:
             send.start()
         came_rope[...] = jnp.zeros((rows, 128), low)
-        total_low[...] = own[...].astype(low)
         for send in sends:
             send.wait_send()
+        prior[...] = own[...].astype(low)
 
     @pl.when(half == 0)
     def _():
         for send in sends:
             send.wait_recv()
-        total_low[...] = (own[...] + came[...].astype(wide)).astype(low)
+        prior[...] = (own[...] + came[...].astype(wide)).astype(low)
 
     for load in up_loads:
         load.wait()
     quarters, span = ups.shape[0], ups.shape[-1]
 
     def spread(n, d_latent):
-        part = total_low[:, lanes_at(n * span, span)]
+        part = prior[:, lanes_at(n * span, span)]
         put(2, n, dot_tn(latent[...], part))
         return d_latent + dot_nt(part, whole(ups[n]))
 
     d_latent = lax.fori_loop(0, quarters, spread, jnp.zeros((rows, LATENT), wide))
-    values = compressed[...]
-    root = row_scale(values)
-    gain_grad[...] = jnp.broadcast_to(
-        jnp.sum(d_latent * values * root, axis=0, keepdims=True), gain_grad.shape
-    )
-    scaled = latent_gain[...] * d_latent
-    inner = jnp.mean(values * scaled, axis=-1, keepdims=True)
-    entry_low[:, lanes_at(query_width, LATENT)] = (
-        root * scaled - values * (root * root * root) * inner
-    ).astype(low)
+    d_squeezed, gain_sum = norm_back(compressed[...], latent_gain[...], d_latent)
+    gain_grad[...] = jnp.broadcast_to(gain_sum, gain_grad.shape)
+    entry_low[:, lanes_at(query_width, LATENT)] = d_squeezed.astype(low)
     key = rope_sum[rows:] + came_rope[...].astype(wide)
     entry_low[:, lanes_at(query_width + LATENT, 128)] = turn_back(head_lanes(key, 0)).astype(low)
 
@@ -1853,19 +2034,16 @@
     loads[1].wait()
 
     def normed_part(n, carry):
-        at = lanes_at(n * 512, 512)
-        token_grad[:, at] = dot_nt(entry_low[...], entry[at, :])
+        at = lanes_at(n * 1024, 1024)
+        own[:, at] = dot_nt(entry_low[...], entry[at, :])
         return carry
 
-    lax.fori_loop(0, width // 512, normed_part, 0)
-    x = x_ref[...].astype(wide)
-    root = row_scale(x)
-    scaled = first_gain[...] * token_grad[...]
-    first_grad[...] = jnp.broadcast_to(
-        jnp.sum(token_grad[...] * x * root, axis=0, keepdims=True), first_grad.shape
-    )
-    inner = jnp.mean(x * scaled, axis=-1, keepdims=True)
-    token_grad[...] = above[...] + root * scaled - x * (root * root * root) * inner
+    lax.fori_loop(0, width // 1024, normed_part, 0)
+    through_norm, gain_sum = norm_back(
+        x_ref[...].astype(wide), first_gain[...], own[:, pl.ds(0, width)]
+    )
+    first_grad[...] = jnp.broadcast_to(gain_sum, first_grad.shape)
+    token_grad[...] += through_norm
     settle(0, out_count)
     settle(1, entry_count)
     settle(2, quarters)
@@ -1873,10 +2051,10 @@
 
 
 def attend_back(
-    d, packed, ups, ups_shape, kept, gains, tables, mask, returning, before, layout
+    back, packed, ups, ups_shape, kept, gains, tables, mask, returning, before, layout
 ):
-    rows, width = d.shape
-    low, wide = d.dtype, jnp.float32
+    rows, width = back.shape
+    low, wide = packed.dtype, jnp.float32
     semaphores = pltpu.SemaphoreType.DMA
     anywhere = pl.BlockSpec(memory_space=pl.ANY)
     local = pl.BlockSpec(memory_space=pltpu.VMEM)
@@ -1890,12 +2068,16 @@
             jax.ShapeDtypeStruct(up_grad, low),
             jax.ShapeDtypeStruct((8, LATENT), wide),
             jax.ShapeDtypeStruct((8, width), wide),
+            jax.ShapeDtypeStruct((8, width), wide),
             jax.ShapeDtypeStruct((width, layout[0]), low),
             jax.ShapeDtypeStruct((HEADS * VALUE, width), low),
-            jax.ShapeDtypeStruct(returning.shape, low),
+            jax.ShapeDtypeStruct(returning[0].shape, low),
         ],
-        in_specs=[local, anywhere, anywhere] + [local] * 15 + [anywhere] * (1 + len(before)),
-        out_specs=[local, anywhere, local, local] + [anywhere] * 3,
+        in_specs=[local, anywhere, anywhere]
+        + [local] * (len(kept) + len(gains) + len(tables) + 1)
+        + [anywhere] * (2 + len(before)),
+        out_specs=[local, anywhere] + [local] * 3 + [anywhere] * 3,
+        input_output_aliases={23: 7},
         scratch_shapes=[
             pltpu.VMEM((packed.shape[0], width), low),
             pltpu.VMEM(ups_shape, low),
@@ -1905,26 +2087,535 @@
             pltpu.VMEM((rows, expanded_width), low),
             pltpu.VMEM((rows, 128), low),
             pltpu.VMEM((rows, 128), low),
-            pltpu.VMEM((rows, expanded_width), low),
             pltpu.VMEM((packed.shape[0], layout[0]), low),
             pltpu.VMEM((rows, layout[0]), low),
             pltpu.VMEM((2,) + ups_shape[1:], low),
             pltpu.VMEM((2, 128, layout[0]), low),
-            pltpu.VMEM((2, 256, width), low),
+            pltpu.VMEM((2, 128, width), low),
+            pltpu.VMEM((rows, width), low),
             semaphores((2,)),
             semaphores((quarters,)),
             semaphores((2,)),
             semaphores((2,)),
             semaphores((3, 2)),
-            semaphores((PLANE, returning.shape[1])),
-            semaphores((PLANE, returning.shape[1])),
-            semaphores((returning.shape[1],)),
+            semaphores((PLANE, returning[0].shape[0])),
+            semaphores((PLANE, returning[0].shape[0])),
         ],
         compiler_params=pltpu.CompilerParams(
             collective_id=6, has_side_effects=True, vmem_limit_bytes=62 * MEBIBYTE
         ),
         cost_estimate=LONG,
-    )(d, packed, ups, *kept, *gains, *tables, mask, returning, *before)
+    )(back, packed, ups, *kept, *gains, *tables, mask, *returning, *before)
+
+
+def run_and_return_kernel(depth, total, *refs):
+    x_in, grad_in, gate_in, up_in, down_in, router_ref, choose_ref, shared_in = refs[:8]
+    back_ref, prob_ref, gate_out, up_out, down_out, y_out, y_own = refs[8:15]
+    came, scalars, shared, onward, incoming, prob_send, prob_land = refs[15:22]
+    x_held, gate_held, up_held, hidden_held, grad_held, hidden = refs[22:28]
+    gates, ups, downs, sent, scalars_sent, y_stage = refs[28:34]
+    es, er, ss, sr, load_sem, shared_sem, cs, cr, ps, pr = refs[34:44]
+    ws, wr, ts, tr, wide_sem, tall_sem, y_sem, free_sem = refs[44:]
+    half = lax.axis_index("fsdp")
+    place = lax.axis_index("expert")
+    level = place // PLANE
+    spot = place % PLANE
+    other = (1 - half, place)
+    tokens, width = back_ref.shape
+    capacity = choose_ref.shape[2]
+    inner = gates.shape[1]
+    wide_rows, tall_rows, tall_width = 256, 128, width // 2
+    wide_count, tall_count = width // 2 // wide_rows, inner // tall_rows
+    wide = jnp.float32
+
+    def take_wide(which, k):
+        at = pl.multiple_of((which * wide_count + k) * wide_rows, wide_rows)
+        return gates.at[pl.ds(at, wide_rows), :]
+
+    def take_tall(k):
+        at = pl.multiple_of(k * tall_rows, tall_rows)
+        return ups.at[pl.ds(at, tall_rows), pl.ds(0, tall_width)]
+
+    def give_wide(slot, which):
+        at = pl.multiple_of((slot * 2 + which) * wide_rows, wide_rows)
+        return downs.at[pl.ds(at, wide_rows), pl.ds(0, inner)]
+
+    def give_tall(slot):
+        at = pl.multiple_of(4 * wide_rows + slot * tall_rows, tall_rows)
+        return downs.at[pl.ds(at, tall_rows), pl.ds(0, tall_width)]
+
+    def done_wide(which):
+        return ups.at[pl.ds(tall_count * tall_rows + which * wide_rows, wide_rows), :]
+
+    def done_tall(slot):
+        at = pl.multiple_of(slot * tall_width, tall_width)
+        return downs.at[pl.ds(4 * wide_rows + 2 * tall_rows, tall_rows), pl.ds(at, tall_width)]
+
+    greet(line_others(half, place, depth) + plane_others(half, place) + [other])
+
+    def rows_to(offset, way, source):
+        mate = (spot + offset) % PLANE
+        where = (half, place - spot + mate)
+        return (
+            remote(
+                sent.at[way, mate],
+                came.at[spot, source],
+                es.at[offset, source],
+                er.at[offset, source],
+                where,
+            ),
+            remote(
+                scalars_sent.at[way, mate],
+                scalars.at[spot, source],
+                ss.at[offset, source],
+                sr.at[offset, source],
+                where,
+            ),
+        )
+
+    def rows_from(offset, source):
+        mate = (spot + PLANE - offset) % PLANE
+        where = (half, place - spot + mate)
+        block, small = came.at[mate, source], scalars.at[mate, source]
+        return (
+            remote(block, block, es.at[offset, source], er.at[offset, source], where),
+            remote(small, small, ss.at[offset, source], sr.at[offset, source], where),
+        )
+
+    def shared_load(slot, source):
+        return pltpu.make_async_copy(shared_in.at[source], shared.at[slot], shared_sem.at[slot])
+
+    def each_way(s, act):
+        def one(way, carry):
+            source = level + (2 * way - 1) * s
+
+            @pl.when((source >= 0) & (source < depth) & ((s > 0) | (way == 0)))
+            def _():
+                act(way, source)
+
+            return carry
+
+        lax.fori_loop(0, 2, one, 0)
+
+    loads = [
+        pltpu.make_async_copy(source, target, load_sem.at[k])
+        for k, (source, target) in enumerate(
+            (
+                (x_in, x_held),
+                (gate_in, gates),
+                (up_in, ups),
+                (grad_in, grad_held),
+                (down_in, downs),
+            )
+        )
+    ]
+    for load in loads:
+        load.start()
+    earliest = jnp.where(2 * level >= depth - 1, 0, depth - 1)
+
+    def slot_of(way, source):
+        return way + 2 * ((source + level) % 2)
+
+    def compute(way, source):
+        def need(*which):
+            @pl.when(source == earliest)
+            def _():
+                for k in which:
+                    loads[k].wait()
+
+        need(0)
+        slot = slot_of(way, source)
+        x = x_held.at[source]
+        logits = jnp.dot(x[...], router_ref[...], preferred_element_type=wide)
+        lanes = lax.broadcasted_iota(jnp.int32, logits.shape, 1)
+        logits = jnp.where(lanes < total, logits, FLOOR_SCORE)
+        powers = jnp.exp(logits - jnp.max(logits, axis=-1, keepdims=True))
+        probs = powers / jnp.sum(powers, axis=-1, keepdims=True)
+        gate = jnp.sum(jnp.where(lanes == place, probs, 0.0), axis=-1, keepdims=True)
+
+        def columns(start, size, slots):
+            at = lanes_at(start, size)
+            if start == 0:
+                need(1)
+            former_part = jnp.dot(x[...], gates[:, at], preferred_element_type=wide)
+            if start == 0:
+                need(2)
+            latter_part = jnp.dot(x[...], ups[:, at], preferred_element_type=wide)
+            if start == 0:
+                need(3, 4)
+            raw = dot_nt(grad_held[source], downs[at, :])
+            sig = 1.0 / (1.0 + jnp.exp(-former_part))
+            act = former_part * sig
+            low = (act * latter_part).astype(hidden.dtype)
+            hidden[:, at] = low
+            low = low.astype(wide)
+            hidden_held[source, :, at] = (low * gate).astype(hidden.dtype)
+            grad = raw * gate
+            d_gate = grad * latter_part * (sig + act * (1.0 - sig))
+            gate_held[source, :, at] = d_gate.astype(hidden.dtype)
+            up_held[source, :, at] = (grad * act).astype(hidden.dtype)
+            return slots + jnp.sum(low * raw, axis=-1, keepdims=True)
+
+        slots = jnp.zeros((PLANE * capacity, 1), wide)
+        step_size = 640
+        for start in range(0, inner, step_size):
+            slots = columns(start, min(step_size, inner - start), slots)
+
+        def blocks(value):
+            return [value[m * capacity : (m + 1) * capacity] for m in range(PLANE)]
+
+        former = source + 2 * (2 * way - 1)
+
+        @pl.when((former >= 0) & (former < depth))
+        def _():
+            for offset in range(1, PLANE):
+                for copy in rows_to(offset, slot, former):
+                    copy.wait_send()
+
+        for m, block in enumerate(blocks(slots)):
+            spread = jnp.broadcast_to(block, (capacity, 128))
+            scalars_sent[slot, m] = spread
+
+            @pl.when(spot == m)
+            def _():
+                scalars[m, source] = spread
+
+        def outward(n, carry):
+            at = lanes_at(n * 1024, 1024)
+            back = dot_nt(gate_held[source], gates[at, :]) + dot_nt(up_held[source], ups[at, :])
+            for m, block in enumerate(blocks(back)):
+                sent[slot, m, :, at] = block.astype(sent.dtype)
+
+                @pl.when(spot == m)
+                def _():
+                    came[m, source, :, at] = block.astype(came.dtype)
+
+            return carry
+
+        lax.fori_loop(0, width // 1024, outward, 0)
+        for offset in range(1, PLANE):
+            for copy in rows_to(offset, slot, source):
+                copy.start()
+
+        def finally_out(n, carry):
+            at = lanes_at(n * 1024, 1024)
+            out = jnp.dot(hidden[...], downs[:, at], preferred_element_type=wide) * gate
+            for m, block in enumerate(blocks(out)):
+                y_stage[m, :, at] = block.astype(y_stage.dtype)
+            return carry
+
+        lax.fori_loop(0, width // 1024, finally_out, 0)
+        writes = [
+            pltpu.make_async_copy(y_stage, y_out.at[source], y_sem.at[0]),
+            pltpu.make_async_copy(y_stage.at[spot], y_own.at[source, spot], y_sem.at[1]),
+        ]
+        for write in writes:
+            write.start()
+        for write in writes:
+            write.wait()
+
+    def wide_tiles(owner, k):
+        at = pl.ds(pl.multiple_of((owner * wide_count + k) * wide_rows, wide_rows), wide_rows)
+        x = whole(x_held[:, :, at])
+        return dot_tn(x, whole(gate_held[...])), dot_tn(x, whole(up_held[...]))
+
+    def tall_tile(owner, k):
+        at = pl.ds(pl.multiple_of(k * tall_rows, tall_rows), tall_rows)
+        over = pl.ds(pl.multiple_of(owner * tall_width, tall_width), tall_width)
+        return dot_tn(whole(hidden_held[:, :, at]), whole(grad_held[:, :, over]))
+
+    def wide_send(which, k):
+        slot = k % 2
+        return remote(
+            give_wide(slot, which),
+            take_wide(which, k),
+            ws.at[slot, which],
+            wr.at[which, k],
+            other,
+        )
+
+    def tall_send(k):
+        slot = k % 2
+        return remote(give_tall(slot), take_tall(k), ts.at[slot], tr.at[k], other)
+
+    def wide_write(which, k):
+        target = (gate_out, up_out)[which]
+        at = pl.ds(pl.multiple_of(k * wide_rows, wide_rows), wide_rows)
+        return pltpu.make_async_copy(done_wide(which), target.at[at, :], wide_sem.at[which])
+
+    def tall_write(k):
+        slot = k % 2
+        at = pl.ds(pl.multiple_of(k * tall_rows, tall_rows), tall_rows)
+        return pltpu.make_async_copy(done_tall(slot), down_out.at[at, :], tall_sem.at[slot])
+
+    def give_wide_tile(k):
+        @pl.when(k >= 2)
+        def _():
+            for which in range(2):
+                wide_send(which, k - 2).wait_send()
+
+        for which, tile in enumerate(wide_tiles(1 - half, k)):
+            give_wide(k % 2, which)[...] = tile.astype(gates.dtype)
+            wide_send(which, k).start()
+
+    def give_tall_tile(k):
+        @pl.when(k >= 2)
+        def _():
+            tall_send(k - 2).wait_send()
+
+        give_tall(k % 2)[...] = tall_tile(1 - half, k).astype(gates.dtype)
+        tall_send(k).start()
+
+    def keep_wide_tile(k):
+        @pl.when(k >= 1)
+        def _():
+            for which in range(2):
+                wide_write(which, k - 1).wait()
+
+        for which, tile in enumerate(wide_tiles(half, k)):
+            wide_send(which, k).wait_recv()
+            tile = tile + take_wide(which, k)[...].astype(wide)
+            done_wide(which)[...] = tile.astype(gates.dtype)
+            wide_write(which, k).start()
+
+    def keep_tall_tile(k):
+        @pl.when(k >= 2)
+        def _():
+            tall_write(k - 2).wait()
+
+        tile = tall_tile(half, k)
+        tall_send(k).wait_recv()
+        tile = tile + take_tall(k)[...].astype(wide)
+        done_tall(k % 2)[...] = tile.astype(gates.dtype)
+        tall_write(k).start()
+
+    units = 2 * (wide_count + tall_count)
+    bounds = (0, wide_count, wide_count + tall_count, units - tall_count, units)
+    acts = (give_wide_tile, give_tall_tile, keep_wide_tile, keep_tall_tile)
+
+    def fill(unit, carry):
+        for act, low, high in zip(acts, bounds[:-1], bounds[1:]):
+
+            @pl.when((unit >= low) & (unit < high))
+            def _():
+                act(unit - low)
+
+        return carry
+
+    def chain_out(source):
+        up = jnp.where(source > level, 1, 0)
+        step = 2 * up - 1
+        slot = jnp.where(source == level - 1, depth, source)
+        return remote(
+            onward.at[up],
+            incoming.at[slot],
+            cs.at[source],
+            cr.at[slot],
+            (half, place + step * PLANE),
+        )
+
+    def chain_in(slot):
+        block = incoming.at[slot]
+        return remote(block, block, cs.at[0], cr.at[slot], (half, place))
+
+    def prob_to(source):
+        return remote(
+            prob_send.at[source],
+            prob_land.at[level],
+            ps.at[source],
+            pr.at[level],
+            (half, source * PLANE + spot),
+        )
+
+    def prob_from(source):
+        block = prob_land.at[source]
+        return remote(block, block, ps.at[source], pr.at[source], (half, source * PLANE + spot))
+
+    def add_incoming(slot):
+        chain_in(slot).wait_recv()
+        back_ref[...] += incoming[slot].astype(jnp.float32)
+
+    def settle(way, source):
+        load = shared_load(0, source)
+        load.start()
+        for offset in range(1, PLANE):
+            for copy in rows_from(offset, source):
+                copy.wait_recv()
+        load.wait()
+
+        def columns(n, carry):
+            at = pl.ds(pl.multiple_of(n * 512, 512), 512)
+            total = shared[0, :, at].astype(jnp.float32)
+            for mate in range(PLANE):
+                total = total + dot_tn(choose_ref[source, mate], came[mate, source, :, at])
+            back_ref[:, at] = total
+            return carry
+
+        lax.fori_loop(0, width // 512, columns, 0)
+        lines = lax.broadcasted_iota(jnp.int32, (8, tokens), 0)
+        probs = jnp.zeros((8, tokens), jnp.float32)
+        for mate in range(PLANE):
+            part = lax.dot_general(
+                scalars[mate, source],
+                choose_ref[source, mate].astype(jnp.float32),
+                (((0,), (0,)), ((), ())),
+                preferred_element_type=jnp.float32,
+                precision=lax.Precision.HIGHEST,
+            )
+            probs = jnp.where(lines == mate, part[:8], probs)
+
+        @pl.when((source >= level) & (level > 0))
+        def _():
+            add_incoming(source)
+
+        @pl.when((source < level) & (level < depth - 1))
+        def _():
+            add_incoming(source)
+
+        @pl.when((source == level) & (level < depth - 1))
+        def _():
+            add_incoming(depth)
+
+        @pl.when(source == level)
+        def _():
+            prob_land[level] = probs
+
+        @pl.when(source != level)
+        def _():
+            prob_send[source] = probs
+            prob_to(source).start()
+            former = source + 2 * way - 1
+
+            @pl.when((former >= 0) & (former < depth))
+            def _():
+                chain_out(former).wait_send()
+
+            onward[way] = back_ref[...].astype(onward.dtype)
+            chain_out(source).start()
+
+    def step(i, carry):
+        s = depth - 1 - i
+        each_way(s, compute)
+
+        @pl.when(i > 0)
+        def _():
+            each_way(s + 1, settle)
+
+        return carry
+
+    lax.fori_loop(0, depth, step, 0)
+    pl.semaphore_signal(free_sem, inc=1, device_id=other, device_id_type=MESH)
+    pl.semaphore_wait(free_sem, 1)
+    lax.fori_loop(0, units // 2, fill, 0)
+    each_way(0, settle)
+    lax.fori_loop(units // 2, units, fill, 0)
+    for which in range(2):
+        wide_write(which, wide_count - 1).wait()
+        for k in (wide_count - 2, wide_count - 1):
+            wide_send(which, k).wait_send()
+    for k in (tall_count - 2, tall_count - 1):
+        tall_write(k).wait()
+        tall_send(k).wait_send()
+
+    def finish(source, carry):
+        ahead = jnp.where(source > level, 1, 0)
+        near = (source >= level - 1) & (source <= level + 2)
+
+        @pl.when(near)
+        def _():
+            for offset in range(1, PLANE):
+                for copy in rows_to(offset, slot_of(ahead, source), source):
+                    copy.wait_send()
+
+        @pl.when((source == level - 1) | (source == level + 1))
+        def _():
+            chain_out(source).wait_send()
+
+        @pl.when(source != level)
+        def _():
+            prob_to(source).wait_send()
+            prob_from(source).wait_recv()
+
+        prob_ref[source] = prob_land[source]
+        return carry
+
+    lax.fori_loop(0, depth, finish, 0)
+
+
+def run_and_return(rows, grads, weights, router, choose, shared_back, total):
+    depth, _, capacity, width = rows.shape
+    tokens = choose.shape[3]
+    inner = weights[0].shape[1]
+    tile = PLANE * capacity
+    wide_count, tall_count = width // 512, inner // 128
+    semaphores = pltpu.SemaphoreType.DMA
+    low, wide = rows.dtype, jnp.float32
+    anywhere = pl.BlockSpec(memory_space=pl.ANY)
+    local = pl.BlockSpec(memory_space=pltpu.VMEM)
+    return pl.pallas_call(
+        functools.partial(run_and_return_kernel, depth, total),
+        out_shape=[
+            jax.ShapeDtypeStruct((tokens, width), wide),
+            jax.ShapeDtypeStruct((depth, 8, tokens), wide),
+            jax.ShapeDtypeStruct((width // 2, inner), low),
+            jax.ShapeDtypeStruct((width // 2, inner), low),
+            jax.ShapeDtypeStruct((inner, width // 2), low),
+            jax.ShapeDtypeStruct(rows.shape, low),
+            jax.ShapeDtypeStruct(rows.shape, low),
+        ],
+        in_specs=[anywhere] * 5 + [local, local, anywhere],
+        out_specs=[local, local] + [anywhere] * 5,
+        scratch_shapes=[
+            pltpu.VMEM((PLANE, depth, capacity, width), low),
+            pltpu.VMEM((PLANE, depth, capacity, 128), wide),
+            pltpu.VMEM((1, tokens, width), low),
+            pltpu.VMEM((2, tokens, width), low),
+            pltpu.VMEM((depth + 1, tokens, width), low),
+            pltpu.VMEM((depth, 8, tokens), wide),
+            pltpu.VMEM((depth, 8, tokens), wide),
+            pltpu.VMEM((depth, tile, width), low),
+            pltpu.VMEM((depth, tile, inner), low),
+            pltpu.VMEM((depth, tile, inner), low),
+            pltpu.VMEM((depth, tile, inner), low),
+            pltpu.VMEM((depth, tile, width), low),
+            pltpu.VMEM((tile, inner), low),
+            pltpu.VMEM(weights[0].shape, low),
+            pltpu.VMEM(weights[1].shape, low),
+            pltpu.VMEM(weights[2].shape, low),
+            pltpu.VMEM((4, PLANE, capacity, width), low),
+            pltpu.VMEM((4, PLANE, capacity, 128), wide),
+            pltpu.VMEM((PLANE, capacity, width), low),
+            semaphores((PLANE, depth)),
+            semaphores((PLANE, depth)),
+            semaphores((PLANE, depth)),
+            semaphores((PLANE, depth)),
+            semaphores((5,)),
+            semaphores((2,)),
+            semaphores((depth,)),
+            semaphores((depth + 1,)),
+            semaphores((depth,)),
+            semaphores((depth,)),
+            semaphores((2, 2)),
+            semaphores((2, wide_count)),
+            semaphores((2,)),
+            semaphores((tall_count,)),
+            semaphores((2,)),
+            semaphores((2,)),
+            semaphores((2,)),
+            pltpu.SemaphoreType.REGULAR,
+        ],
+        compiler_params=pltpu.CompilerParams(
+            collective_id=7, has_side_effects=True, vmem_limit_bytes=63 * MEBIBYTE
+        ),
+        cost_estimate=LONG,
+    )(
+        rows.reshape(depth, tile, width),
+        grads.reshape(depth, tile, width),
+        *weights,
+        router,
+        choose,
+        shared_back,
+    )
 
 
 def body(
@@ -2002,16 +2693,14 @@
         2, part_rows, 2, depth, shared_width
     )
     shared_both = shared_both.transpose(3, 1, 0, 2, 4)
-    shared_both = shared_both.reshape(depth, part_rows, 2, 2 * shared_width)
-    shared_padded = 2 * shared_width + (-2 * shared_width) % 128
-    shared_both = jnp.pad(
-        shared_both, ((0, 0), (0, 0), (0, 0), (0, shared_padded - 2 * shared_width))
-    ).reshape(depth, part_rows, 2 * shared_padded)
+    spare = (-shared_width) % 128
+    shared_both = jnp.pad(shared_both, ((0, 0),) * 4 + ((0, spare),))
+    shared_both = shared_both.reshape(depth, part_rows, -1)
     packed_full, grad_line, target_line, shared_full, sdown_full = gather_rows(
-        packed, cotangent[0], target, shared_both, shared_down, cut
-    )
-    shared_full = shared_full.reshape(D, 2 * shared_padded)
-    sdown_full = sdown_full.reshape(2 * shared_width, D)
+        packed, cotangent[0], target, shared_both, shared_down, cuts_of(packed.shape[1], GROUPS)
+    )
+    shared_full = shared_full.reshape(D, -1)
+    sdown_full = sdown_full.reshape(2, shared_width, D)
     expert_gate_full = lax.all_gather(expert_gate[0], "fsdp", axis=0, tiled=True)
     expert_up_full = lax.all_gather(expert_up[0], "fsdp", axis=0, tiled=True)
     expert_down_full = lax.all_gather(expert_down[0], "fsdp", axis=1, tiled=True)
@@ -2096,68 +2785,65 @@
     mixed_rows, shared_out, shared_back, shared_grad, sdown_grad, grad_rows = dispatch(
         mixed_low, choose_slots, grad_line, shared_full, sdown_full, grad_rows
     )
-    grad_rows = grad_rows.reshape(expert_total * capacity, D)
-    mixed_rows = mixed_rows.reshape(expert_total * capacity, D)
     shared_out = shared_out.reshape(line_rows, D)
-    hidden_grad_raw = right_matmul(grad_rows, expert_down_full)
-    slot_probs = jax.nn.softmax(matmul(mixed_rows, router_full), axis=-1)
-    gate_column = lax.dynamic_slice_in_dim(slot_probs, place, 1, axis=1)
-
-    gate_part = matmul(mixed_rows, expert_gate_full)
-    up_portion = matmul(mixed_rows, expert_up_full)
-    hidden_wide = jax.nn.silu(gate_part) * up_portion
-    hidden = hidden_wide.astype(jnp.bfloat16)
-    slot_grad = jnp.sum(hidden.astype(jnp.float32) * hidden_grad_raw, axis=-1)
-    hidden_grad = hidden_grad_raw * gate_column
-    gate_part_grad, up_part_grad = swiglu_back(gate_part, up_portion, hidden_grad)
-    gate_low = gate_part_grad.astype(jnp.bfloat16)
-    up_low = up_part_grad.astype(jnp.bfloat16)
-    input_grad = (
-        right_matmul(gate_low, expert_gate_full) + right_matmul(up_low, expert_up_full)
-    ).astype(jnp.bfloat16)
-    hidden_scaled = (hidden.astype(jnp.float32) * gate_column).astype(jnp.bfloat16)
-    slot_grad = jnp.pad(
-        slot_grad.reshape(PLANE, depth, 1, capacity), ((0, 0), (0, 0), (0, 0), (0, 128 - capacity))
-    )
-    back_and_shared, prob_parts, expert_gate_piece, expert_up_piece, expert_down_piece = give_back(
-        input_grad.reshape(PLANE, depth, capacity, D),
-        jnp.broadcast_to(slot_grad, (PLANE, depth, 8, 128)),
-        choose_slots,
-        shared_back,
-        [mixed_rows, gate_low, up_low, hidden_scaled, grad_rows],
-    )
-    back_and_shared, hidden = lax.optimization_barrier((back_and_shared, hidden))
-    expert_out = (matmul(hidden, expert_down_full) * gate_column).astype(jnp.bfloat16)
-    def scatter_plane(value):
-        part = lax.psum_scatter(value, "fsdp", scatter_dimension=0, tiled=True)
-        return lax.psum_scatter(
-            part, "expert", scatter_dimension=0, axis_index_groups=plane, tiled=True
-        )
-
-    shared_summed = scatter_plane(shared_grad.reshape(2 * PLANE, depth, part_rows, -1))[0]
-    sdown_summed = scatter_plane(sdown_grad)
-
-    out_grad = cotangent[0].astype(jnp.float32)
+    router_wide = jnp.pad(router_full, ((0, 0), (0, (-expert_total) % 128)))
+    shared_summed = lax.psum_scatter(
+        shared_grad, "expert", scatter_dimension=0, axis_index_groups=plane, tiled=True
+    )[0]
+    sdown_summed = lax.psum_scatter(
+        sdown_grad, "expert", scatter_dimension=0, axis_index_groups=plane, tiled=True
+    )
+    weights = (expert_gate_full, expert_up_full, expert_down_full)
+    if depth <= PLANE:
+        (
+            back_and_shared,
+            prob_parts,
+            expert_gate_piece,
+            expert_up_piece,
+            expert_down_piece,
+            expert_out,
+            own_out,
+        ) = run_and_return(
+            mixed_rows, grad_rows, weights, router_wide, choose_slots, shared_back, expert_total
+        )
+    else:
+        flat_rows = mixed_rows.reshape(expert_total * capacity, D)
+        flat_grads = grad_rows.reshape(expert_total * capacity, D)
+        hidden_scaled, gate_low, up_low, input_grad, expert_out, slot_grad = run_expert(
+            flat_rows, flat_grads, *weights, router_wide, expert_total
+        )
+        (
+            back_and_shared,
+            prob_parts,
+            expert_gate_piece,
+            expert_up_piece,
+            expert_down_piece,
+        ) = give_back(
+            input_grad.reshape(mixed_rows.shape),
+            slot_grad.reshape(depth, PLANE, capacity, 128),
+            choose_slots,
+            shared_back,
+            [flat_rows, gate_low, up_low, hidden_scaled, flat_grads],
+        )
+        own_out = expert_out
+    prob_grad = prob_parts[:, :PLANE].reshape(expert_total, row_count).T
     probabilities = jax.nn.softmax(matmul(mixed_low, router_full), axis=-1)
     prob_grad = prob_parts[:, :PLANE].reshape(expert_total, row_count).T
     logit_low = (
         probabilities * (prob_grad - jnp.sum(probabilities * prob_grad, axis=-1, keepdims=True))
     ).astype(jnp.bfloat16)
     router_grad = left_matmul(mixed_low, logit_low)
-    mixed_grad = right_matmul(logit_low, router_full) + back_and_shared
-    residual_add, feed_gain_grad = norm_back(residual, feed_gain, mixed_grad)
-    residual_grad = out_grad + residual_add
-    attended_low = residual_grad.astype(jnp.bfloat16)
     (
         token_grad,
         up_weight_grad,
         latent_gain_grad,
         first_gain_grad,
+        feed_gain_grad,
         entry_grad,
         output_grad,
         returned,
     ) = attend_back(
-        attended_low,
+        back_and_shared,
         packed_full,
         up_full,
         ups_shape,
@@ -2171,12 +2857,15 @@
             normed_low,
             mixed_heads,
             tokens[0],
-            residual_grad,
+            residual,
+            cotangent[0],
+            jnp.pad(logit_low, ((0, 0), (0, (-expert_total) % 128))),
+            router_wide,
         ),
-        (latent_gain[None], gain_first[None]),
+        (latent_gain[None], gain_first[None], feed_gain[None]),
         tables,
         mask,
-        expert_out.reshape(PLANE, depth, capacity, D),
+        (expert_out.reshape(mixed_rows.shape), own_out.reshape(mixed_rows.shape)),
         (shared_summed, sdown_summed),
         layout,
     )
@@ -2185,10 +2874,11 @@
         up_weight_grad = up_weight_grad.transpose(1, 0, 2, 3)
     latent_gain_grad = latent_gain_grad[0]
     first_gain_grad = first_gain_grad[0]
+    feed_gain_grad = feed_gain_grad[0]
     routed = jnp.einsum(
         "zst,zsd->ztd",
         choose_rows,
-        returned.transpose(1, 0, 2, 3).reshape(depth, PLANE * capacity, D),
+        returned.reshape(depth, PLANE * capacity, D),
         preferred_element_type=jnp.float32,
     )
     routed_and_shared = lax.psum_scatter(
@@ -2222,8 +2912,7 @@
     )
     small_piece = packed_piece[:, -128:].reshape(-1)
     shared_pieces = (
-        shared_back_moved.reshape(depth, part_rows, 2, shared_padded)[..., : 2 * shared_width]
-        .reshape(depth, part_rows, 2, 2, shared_width)
+        shared_back_moved.reshape(depth, part_rows, 2, 2, -1)[..., :shared_width]
         .transpose(2, 1, 3, 0, 4)
         .reshape((2,) + shared_gate.shape)
         .astype(jnp.float32)

time: 771 us -> 715 us (0.927)
  matrix products: 81.3 us -> 9.7 us
  Pallas kernels: 579 us -> 625 us
  waiting for transfers between devices: 17.3 us -> 2.17 us
  local copies, waits for them, and re-layouts: 42.7 us -> 34.4 us
    dot_general x5 -> x1, matrix products: 44.2 us -> 1.48 us  [matmul(): return jnp.dot(former, latter, preferred_element_type=jnp.float32)]
    pallas_call x2, Pallas kernels: 263 us -> 304 us  [the longest x1 166 us: gather_rows(): pl.pallas_call(functools.partial(gather_kernel, depth, cuts), out_shape=[...]
    dot_general x5 -> x1, matrix products: 36.9 us -> 6.83 us  [body(): jnp.einsum('zst,zsd->ztd', choose_rows, returned.reshape(depth, PLANE * c...]
    unnamed x10 -> x8, waiting for transfers between devices: 17.2 us -> 2.11 us
  transfers between devices with their start and end apart: 8 -> 6, of which waited for: 1 -> 0; matrix products, arithmetic and copies ran while one was open for 17% -> 7% of each run, Pallas kernels for 53% -> 63%
where the time goes in v5:
time: 715 us; the launch traced here: 708 us
  Pallas kernels  625 us (87%)
  local copies, waits for them, and re-layouts  34.4 us (5%)
  other arithmetic  21.3 us (3%)
  between operations  15.3 us (2%)
  matrix products  9.7 us (1%)
    pallas_call x1, Pallas kernels, gather_rows(): pl.pallas_call(functools.partial(gather_kernel, depth, cuts), out_shape=[...  166 us
    pallas_call x1, Pallas kernels, reduce_rows(): pl.pallas_call(functools.partial(reduce_kernel, depth, n, cut), out_shape...  141 us
    pallas_call x1, Pallas kernels, run_and_return(): pl.pallas_call(functools.partial(run_and_return_kernel, depth, total), ou...  138 us
    pallas_call x1, Pallas kernels, dispatch(): pl.pallas_call(functools.partial(dispatch_kernel, depth), out_shape=[jax....  82.5 us
    pallas_call x1, Pallas kernels, attend_back(): pl.pallas_call(functools.partial(attend_back_kernel, layout, len(before))...  61.5 us
    pallas_call x1, Pallas kernels, attend(): pl.pallas_call(functools.partial(attend_kernel, layout), out_shape=[jax.S...  35.9 us
  transfers between devices with their start and end apart: 6, of which 0 were waited for; matrix products, arithmetic and copies ran while one was open for 7% of the time, Pallas kernels for 63%

profile of v5, /device:TPU:0, one launch (start us, length us, event | category | flops | bytes accessed | tf_op | source)
XLA Modules:
  0.0 708.1 jit_solution(8499768871712030712)
XLA Ops:
  7.2 0.7 all-gather.7.cloned.1.call-update
  8.0 0.7 all-gather.9.cloned.1.call-update
  8.8 0.7 all-gather.11.cloned.1.call-update
  9.6 0.6 reshape.211
  10.4 0.6 pad_bitcast_fusion.refs_2_
  11.3 0.4 fusion.6
  11.7 0.8 pad_maximum_fusion.1.refs_6_.refs_19_
  12.5 0.5 stack.9
  13.0 0.3 copy.85
  13.3 0.5 stack.10
  13.8 0.3 copy.86
  14.2 1.1 maximum_bitcast_fusion
  15.3 0.7 pad.33
  16.0 1.4 reshape.218.refs_3_
  17.7 0.8 pad_maximum_fusion.2.refs_7_.refs_20_
  18.8 0.9 and_convert_fusion.refs_8_.refs_21_
  19.7 166.1 %shard_map.306 = (bf16[2048,6912]{1,0:T(8,128)(2,1)}, bf16[4,192,2048]{2,1,0:T(8,128)(2,1)}, s32[4,8,192]{2,1,0:T(8,128)}, bf16[2,4,4,64,1536]{4,3,2,1,0:T(8,128)(2,1)}, bf16[2,4,88,2048]{3,2,1,0:T(8,128)(2,1)}) custom-call(bf16[64,6912]{1,0:T(8,128)(2,1)} %copy-done.14, bf16[192,2048]{1,0:T(8,128)(2,1)} %bitcast.96, s32[8,192]{1,0:T(8,128)} %pad_bitcast_fusion.refs_2_, ...), custom_call_target="tpu_custom_call" | custom-call | flops 99999997952 | tf_op jit(solution)/shard_map/pallas_call | solution.py:487
  185.9 1.1 slice.85
  187.3 0.7 reshape.239.refs_4_.refs_16_
  188.0 0.7 reshape.240.refs_5_.refs_18_
  188.7 0.7 reshape.238.refs_3_.refs_17_
  189.4 1.7 compare_reduce_fusion
  191.0 0.7 copy-done.3
  191.8 0.9 convert_element_type.123
  192.7 35.9 %shard_map.307 = (bf16[192,2048]{1,0:T(8,128)(2,1)}, f32[192,2048]{1,0:T(8,128)}, bf16[192,2048]{1,0:T(8,128)(2,1)}, bf16[192,3072]{1,0:T(8,128)(2,1)}, bf16[192...) custom-call(bf16[192,2048]{1,0:T(8,128)(2,1)} %bitcast.94, ...), custom_call_target="tpu_custom_call" | custom-call | flops 40000000000 | tf_op jit(solution)/shard_map/pallas_call | solution.py:1798
  228.6 82.5 %shard_map.308 = (bf16[4,4,72,2048]{3,2,1,0:T(8,128)(2,1)}, bf16[4,192,2048]{2,1,0:T(8,128)(2,1)}, bf16[4,192,2048]{2,1,0:T(8,128)(2,1)}, bf16[4,4,64,1536]{3,2,...) custom-call(bf16[192,2048]{1,0:T(8,128)(2,1)} %get-tuple-element.68., ...), custom_call_target="tpu_custom_call", output_to_operand_aliasing={{5}: (5, {})} | custom-call | flops 99999997952 | tf_op jit(solution)/shard_map/pallas_call | solution.py:816
  311.3 0.4 reshape.225
  311.7 0.9 pad.34.refs_5_.refs_15_
  312.6 0.5 reduce-scatter.8.cloned.1.call-start
  313.1 137.8 %shard_map.309 = (f32[192,2048]{1,0:T(8,128)}, f32[4,8,192]{2,1,0:T(8,128)}, bf16[1024,1408]{1,0:T(8,128)(2,1)}, bf16[1024,1408]{1,0:T(8,128)(2,1)}, bf16[1408,1...) custom-call(bf16[4,288,2048]{2,1,0:T(8,128)(2,1)} %bitcast.101, ...), custom_call_target="tpu_custom_call" | custom-call | flops 99999997952 | tf_op jit(solution)/shard_map/pallas_call | solution.py:2555
  451.0 1.5 fusion.18
  452.6 0.9 slice.91
  454.2 0.6 pad.35.refs_14_
  454.8 1.4 convolution_convert_fusion
  456.5 0.8 reshape.229
  457.3 2.9 bitcast_convert_fusion.2
  460.2 2.9 bitcast_convert_fusion.1
  463.2 3.2 bitcast_convert_fusion
  466.5 1.9 convert_element_type.119
  468.4 61.5 %shard_map.310 = (f32[192,2048]{1,0:T(8,128)}, bf16[32,4,16,1024]{3,2,1,0:T(8,128)(2,1)}, f32[8,512]{1,0:T(8,128)}, f32[8,2048]{1,0:T(8,128)}, f32[8,2048]{1,0:T...) custom-call(f32[192,2048]{1,0:T(8,128)} %get-tuple-element.78.refs_0, ...), custom_call_target="tpu_custom_call", output_to_operand_aliasing={{7}: (23, {})} | custom-call | flops 99999997952 | tf_op jit(solution)/shard_map/pallas_call | solution.py:2064
  529.8 6.8 add_convert_fusion
  536.7 0.7 fusion.11
  537.4 0.9 fusion.10
  538.4 0.9 fusion.9
  539.6 1.0 reshape.230.refs_3_
  540.6 140.8 %shard_map.311 = (f32[64,6912]{1,0:T(8,128)}, bf16[4,64,1536]{2,1,0:T(8,128)(2,1)}) custom-call(bf16[2048,3712]{1,0:T(8,128)(2,1)} %get-tuple-element.95.refs_0_, bf16[2048,1024]{1,0:T(8,128)(2,1)} %bitcast.103, bf16[2048,2048]{1,0:T(8,128)(2,1)} %get-tuple-element.97.refs_2_, bf16[2048,128]{1,0:T(8,128)(2,1)} %reshape.230.refs_3_, bf16[4,64,1536]{2,1,0:T(8,128)(2,1)} %bitcast.99), custom_call_target="tpu_custom_call" | custom-call | flops 99999997952 | tf_op jit(solution)/shard_map/pallas_call | solution.py:1552
  681.5 2.4 reshape.237
  683.9 1.6 slice.99
  685.4 0.8 fusion.13
  686.2 0.6 slice.119
  686.9 0.7 copy.94
  687.6 1.1 fusion.15
  688.7 0.7 copy.97
  689.5 0.9 fusion.14
  690.6 1.3 reshape.234
  691.9 0.5 convert_bitcast_fusion
  692.5 0.5 fusion.16
  693.0 0.5 copy.93
  693.5 1.4 squeeze.40
  694.9 0.5 copy.92
  695.4 1.4 squeeze.39
  696.8 0.6 fusion.17
  697.4 2.2 fusion
  699.6 1.1 copy.122
  (98 shorter events, 3.9 us)
Async XLA Ops:
  7.2 178.6 %all-gather.7.cloned.1.call-start = ((), (), s32[]{:S(2)}) async-start(), calls=%async_computation.4 | async-start | bytes 8650752 | tf_op jit(solution)/shard_map/all_gather | solution.py:2704
  7.9 1.7 copy-start.8
  7.9 177.9 %all-gather.9.cloned.1.call-start = ((), (), s32[]{:S(2)}) async-start(), calls=%async_computation.5 | async-start | bytes 8650752 | tf_op jit(solution)/shard_map/all_gather | solution.py:2705
  8.7 1.6 copy-start.17
  8.7 1.7 copy-start.15
  8.7 1.7 copy-start.16
  8.7 2.3 copy-start.18
  8.7 2.5 copy-start.12
  8.7 3.8 copy-start.9
  8.7 4.6 copy-start.10
  8.7 177.1 %all-gather.11.cloned.1.call-start = ((), (), s32[]{:S(2)}) async-start(), calls=%async_computation.6 | async-start | bytes 8650752 | tf_op jit(solution)/shard_map/all_gather | solution.py:2706
  9.5 457.0 %reduce-scatter.12.cloned.1.call-start = ((), (), s32[]{:S(2)}) async-start(), calls=%async_computation.8 | async-start | bytes 1802240
  14.2 4.3 copy-start.13
  14.2 4.4 copy-start.11
  15.3 3.3 copy-start.19
  15.3 3.3 copy-start.20
  15.3 3.2 copy-start.21
  18.7 1.0 copy-start.14
  191.0 0.7 copy-start.3
  311.1 157.2 %reduce-scatter.10.cloned.1.call-start = ((), (), s32[]{:S(2)}) async-start(), calls=%async_computation.7 | async-start | bytes 3932160
  312.6 384.8 %reduce-scatter.8.cloned.1.call-start = ((), (), s32[]{:S(2)}) async-start(), calls=%async_computation.3 | async-start | bytes 3932160 | tf_op jit(solution)/shard_map/reduce_scatter | solution.py:2884
  452.4 4.8 copy-start.2
  457.2 3.0 copy-start.1
  460.2 3.0 copy-start
  468.4 61.5 %copy-start.4 = (pred[4,288,192]{2,1,0:T(8,128)(4,1)S(1)}, pred[4,288,192]{2,1,0:T(8,128)(4,1)}, u32[]{:S(2)}) copy-start(pred[4,288,192]{2,1,0:T(8,128)(4,1)} %copy-done.3) | copy-start | bytes 663556
  681.5 8.1 %copy-start.5 = (f32[64,6912]{1,0:T(8,128)S(1)}, f32[64,6912]{1,0:T(8,128)}, u32[]{:S(2)}) copy-start(f32[64,6912]{1,0:T(8,128)} %get-tuple-element.101) | copy-start | bytes 5308420
  693.0 4.4 copy-start.6
  696.8 2.8 copy-start.7
Sparse Core Ops, SparseCore 0:
  9.6 18.6 all-gather.6
  29.8 17.1 all-gather.8
  48.6 17.1 all-gather.10
  311.3 39.9 reduce-scatter.11
  354.4 72.6 reduce-scatter.9
  536.8 76.3 reduce-scatter.7

commit v6 on v5

--- a/solution.py
+++ b/solution.py
@@ -65,6 +65,7 @@
 MESH = pl.DeviceIdType.MESH
 MEBIBYTE = 1024 * 1024
 GROUPS = 4
+PARTS = 2
 LONG = pl.CostEstimate(flops=100 * 10**9, bytes_accessed=0, transcendentals=0)
 MIDDLE = pl.CostEstimate(flops=40 * 10**9, bytes_accessed=0, transcendentals=0)
 
@@ -551,10 +552,10 @@
     chunk = padded
     greet(line_others(half, place, depth) + plane_others(half, place) + [other])
 
-    def along(way, source):
-        block = lines.at[source]
+    def along(part, way, source):
+        block = lines.at[source, :, pl.ds(part * (width // PARTS), width // PARTS)]
         where = (half, place + (2 * way - 1) * PLANE)
-        return remote(block, block, zs.at[way, source], zr.at[source], where)
+        return remote(block, block, zs.at[part, way, source], zr.at[part, source], where)
 
     loads = [
         pltpu.make_async_copy(shared_in, weights, load_sem.at[0]),
@@ -567,13 +568,14 @@
     ]
     lines[level] = x_ref[...]
 
-    def pass_on(way, source):
+    def pass_on(part, way, source):
         @pl.when((level < depth - 1) if way == 1 else (level > 0))
         def _():
-            along(way, source).start()
-
-    for way in range(2):
-        pass_on(way, level)
+            along(part, way, source).start()
+
+    for part in range(PARTS):
+        for way in range(2):
+            pass_on(part, way, level)
     for load in loads:
         load.start()
     if share > true:
@@ -653,15 +655,17 @@
     shared(level)
 
     def step(s, carry):
-        @pl.when(level - s >= 0)
-        def _():
-            along(1, level - s).wait_recv()
-            pass_on(1, level - s)
-
-        @pl.when(level + s < depth)
-        def _():
-            along(0, level + s).wait_recv()
-            pass_on(0, level + s)
+        for part in range(PARTS):
+
+            @pl.when(level - s >= 0)
+            def _():
+                along(part, 1, level - s).wait_recv()
+                pass_on(part, 1, level - s)
+
+            @pl.when(level + s < depth)
+            def _():
+                along(part, 0, level + s).wait_recv()
+                pass_on(part, 0, level + s)
 
         def one(way, act):
             source = level + (1 - 2 * way) * s
@@ -790,13 +794,15 @@
     def finish(source, carry):
         rows_finish(source)
 
-        @pl.when((source <= level) & (level < depth - 1))
-        def _():
-            along(1, source).wait_send()
-
-        @pl.when((source >= level) & (level > 0))
-        def _():
-            along(0, source).wait_send()
+        for part in range(PARTS):
+
+            @pl.when((source <= level) & (level < depth - 1))
+            def _():
+                along(part, 1, source).wait_send()
+
+            @pl.when((source >= level) & (level > 0))
+            def _():
+                along(part, 0, source).wait_send()
 
         return carry
 
@@ -845,8 +851,8 @@
             pltpu.VMEM((padded // 256, 128, width), low),
             semaphores((4,)),
             semaphores((2,)),
-            semaphores((2, depth)),
-            semaphores((depth,)),
+            semaphores((PARTS, 2, depth)),
+            semaphores((PARTS, depth)),
             semaphores((PLANE, depth)),
             semaphores((PLANE, depth)),
             semaphores((depth,)),
@@ -2506,9 +2512,8 @@
     lax.fori_loop(0, depth, step, 0)
     pl.semaphore_signal(free_sem, inc=1, device_id=other, device_id_type=MESH)
     pl.semaphore_wait(free_sem, 1)
-    lax.fori_loop(0, units // 2, fill, 0)
+    lax.fori_loop(0, units, fill, 0)
     each_way(0, settle)
-    lax.fori_loop(units // 2, units, fill, 0)
     for which in range(2):
         wide_write(which, wide_count - 1).wait()
         for k in (wide_count - 2, wide_count - 1):
@@ -2618,6 +2623,67 @@
     )
 
 
+def finish_kernel(layout, *refs):
+    piece, moved, residual, added, sdown, token = refs[:6]
+    query_ref, down_ref, up_ref, out_ref, gate_ref, shared_up_ref = refs[6:12]
+    sdown_ref, output_ref, token_ref = refs[12:]
+    entry_width, out_start = layout
+    rows = piece.shape[0]
+    nope_width = HEADS * NOPE
+    query_width = HEADS * (NOPE + ROPE)
+    low_half = lax.broadcasted_iota(jnp.int32, (rows, 128), 1) < ROPE
+    for pair in range(HEADS // 2):
+        start = pair * 2 * NOPE
+        rope = piece[:, nope_width + pair * 128 : nope_width + (pair + 1) * 128]
+        latter = pltpu.roll(piece[:, start + NOPE : start + 2 * NOPE], NOPE // 2, 1)
+        at = pair * 2 * (NOPE + ROPE)
+        query_ref[:, at : at + 128] = piece[:, start : start + NOPE]
+        query_ref[:, at + 128 : at + 256] = jnp.where(low_half, rope, latter)
+        query_ref[:, at + 256 : at + 384] = jnp.where(low_half, latter, rope)
+    down_ref[...] = piece[:, query_width : query_width + down_ref.shape[1]]
+    up_rows = up_ref.shape[0]
+    span = out_start - entry_width
+    for k in range(rows // up_rows):
+        up_ref[:, k * span : (k + 1) * span] = piece[
+            k * up_rows : (k + 1) * up_rows, entry_width:out_start
+        ]
+    out_ref[...] = piece[:, out_start : out_start + out_ref.shape[1]]
+    depth = moved.shape[0]
+    share = gate_ref.shape[1] // (2 * depth)
+    padded = moved.shape[2] // 4
+    for which, target in enumerate((gate_ref, shared_up_ref)):
+        target[...] = jnp.concatenate(
+            [
+                moved[t, :, (2 * which + k) * padded : (2 * which + k + 1) * padded].astype(
+                    jnp.float32
+                )[:, :share]
+                for k in range(2)
+                for t in range(depth)
+            ],
+            axis=1,
+        )
+    sdown_ref[...] = sdown[...].astype(jnp.float32)
+    output_ref[...] = (residual[...] + added[...].astype(jnp.float32)).astype(output_ref.dtype)
+    token_ref[...] = token[...]
+
+
+def finish(piece, moved, residual, added, sdown, token, shapes, layout):
+    wide = jnp.float32
+    local = pl.BlockSpec(memory_space=pltpu.VMEM)
+    spans = list(shapes) + [sdown.shape]
+    return pl.pallas_call(
+        functools.partial(finish_kernel, layout),
+        out_shape=[jax.ShapeDtypeStruct(shape, wide) for shape in spans]
+        + [
+            jax.ShapeDtypeStruct(residual.shape, added.dtype),
+            jax.ShapeDtypeStruct(token.shape, wide),
+        ],
+        in_specs=[local] * 6,
+        out_specs=[local] * 9,
+        compiler_params=pltpu.CompilerParams(vmem_limit_bytes=48 * MEBIBYTE),
+    )(piece, moved, residual, added, sdown, token)
+
+
 def body(
     tokens,
     segments,
@@ -2735,7 +2801,7 @@
 
     slot_names = level * PLANE * capacity + jnp.arange(PLANE * capacity)
     hits = target_line[:, :TOPK, None, :] == slot_names[None, None, :, None]
-    choose_rows = jnp.any(hits, axis=1).astype(jnp.bfloat16)
+    choose_rows = jnp.sum(hits.astype(jnp.float32), axis=1).astype(jnp.bfloat16)
 
     choose_slots = choose_rows.reshape(depth, PLANE, capacity, row_count)
     grad_line = grad_line.reshape(depth, row_count, D)
@@ -2887,8 +2953,7 @@
         scatter_dimension=0,
         axis_index_groups=line,
         tiled=True,
-    ).astype(jnp.float32)
-    output = (residual + routed_and_shared).astype(jnp.bfloat16)
+    )
 
     small_grad = jnp.concatenate(
         [
@@ -2911,39 +2976,48 @@
         cut,
     )
     small_piece = packed_piece[:, -128:].reshape(-1)
-    shared_pieces = (
-        shared_back_moved.reshape(depth, part_rows, 2, 2, -1)[..., :shared_width]
-        .transpose(2, 1, 3, 0, 4)
-        .reshape((2,) + shared_gate.shape)
-        .astype(jnp.float32)
-    )
-    output_piece = packed_piece[:, -128 - D : -128]
-    nope_width = HEADS * NOPE
-    query_piece = jnp.concatenate(
-        [
-            packed_piece[:, :nope_width].reshape(part_rows, HEADS, NOPE),
-            packed_piece[:, nope_width:query_width].reshape(part_rows, HEADS, ROPE),
-        ],
-        axis=2,
-    ).reshape(part_rows, query_width)
+    (
+        query_piece,
+        down_piece,
+        up_piece,
+        output_piece,
+        sgate_piece,
+        sup_piece,
+        sdown_piece,
+        output,
+        token_grad,
+    ) = finish(
+        packed_piece,
+        shared_back_moved,
+        residual,
+        routed_and_shared,
+        sdown_summed,
+        token_grad,
+        (
+            query_weight.shape,
+            latent_down.shape,
+            latent_up.shape,
+            output_weight.shape,
+            shared_gate.shape,
+            shared_up.shape,
+        ),
+        layout,
+    )
 
     return (
         output[None],
         token_grad[None],
         small_piece[cuts[0] : cuts[1]],
         query_piece,
-        packed_piece[:, query_width : query_width + down_width],
+        down_piece,
         small_piece[cuts[1] : cuts[2]],
-        packed_piece[:, entry_width : -128 - D]
-        .reshape(quarters, latent_up.shape[0], -1)
-        .transpose(1, 0, 2)
-        .reshape(latent_up.shape),
+        up_piece,
         output_piece,
         small_piece[cuts[2] : cuts[3]],
         small_piece[cuts[3] : cuts[4]].reshape(gain_width, expert_total),
-        shared_pieces[0],
-        shared_pieces[1],
-        sdown_summed.astype(jnp.float32),
+        sgate_piece,
+        sup_piece,
+        sdown_piece,
         expert_gate_piece.astype(jnp.float32)[None],
         expert_up_piece.astype(jnp.float32)[None],
         expert_down_piece.astype(jnp.float32)[None],

time: 715 us -> 709 us (level)
  transfers between devices with their start and end apart: 6 -> 6, of which waited for: 0 -> 0; matrix products, arithmetic and copies ran while one was open for 7% -> 6% of each run, Pallas kernels for 63% -> 63%
where the time goes in v6:
time: 709 us; the launch traced here: 702 us
  Pallas kernels  628 us (89%)
  local copies, waits for them, and re-layouts  28.9 us (4%)
  other arithmetic  18.4 us (3%)
  between operations  14.8 us (2%)
  matrix products  9.69 us (1%)
    pallas_call x1, Pallas kernels, gather_rows(): pl.pallas_call(functools.partial(gather_kernel, depth, cuts), out_shape=[...  166 us
    pallas_call x1, Pallas kernels, reduce_rows(): pl.pallas_call(functools.partial(reduce_kernel, depth, n, cut), out_shape...  141 us
    pallas_call x1, Pallas kernels, run_and_return(): pl.pallas_call(functools.partial(run_and_return_kernel, depth, total), ou...  137 us
    pallas_call x1, Pallas kernels, dispatch(): pl.pallas_call(functools.partial(dispatch_kernel, depth), out_shape=[jax....  82.7 us
    pallas_call x1, Pallas kernels, attend_back(): pl.pallas_call(functools.partial(attend_back_kernel, layout, len(before))...  61.4 us
    pallas_call x1, Pallas kernels, attend(): pl.pallas_call(functools.partial(attend_kernel, layout), out_shape=[jax.S...  35.8 us
  transfers between devices with their start and end apart: 6, of which 0 were waited for; matrix products, arithmetic and copies ran while one was open for 6% of the time, Pallas kernels for 63%

profile of v6, /device:TPU:0, one launch (start us, length us, event | category | flops | bytes accessed | tf_op | source)
XLA Modules:
  0.0 702.3 jit_solution(14645409959932952314)
XLA Ops:
  7.3 0.7 all-gather.7.cloned.1.call-update
  8.0 0.7 all-gather.9.cloned.1.call-update
  8.8 0.7 all-gather.11.cloned.1.call-update
  9.6 0.6 reshape.186
  10.4 0.6 pad_bitcast_fusion.refs_2_
  11.3 0.4 fusion.5
  11.7 0.8 pad_maximum_fusion.refs_6_.refs_19_
  12.5 0.5 stack.9
  13.1 0.3 copy.76
  13.4 0.5 stack.10
  13.9 0.3 copy.77
  14.2 1.1 maximum_bitcast_fusion
  15.3 0.7 pad.33
  16.0 1.4 reshape.193.refs_3_
  17.4 0.2 reshape.188
  17.6 0.8 bitcast_dynamic-update-slice_fusion
  18.4 0.8 pad_maximum_fusion.1.refs_7_.refs_20_
  19.1 0.7 constant_dynamic-update-slice_fusion.2
  19.8 0.6 pad_dynamic-update-slice_fusion
  20.5 0.7 constant_dynamic-update-slice_fusion.1
  21.1 0.7 constant_dynamic-update-slice_fusion
  21.9 0.6 bitcast_dynamic-update-slice_fusion.1.refs_0_
  22.6 0.8 and_convert_fusion.refs_8_.refs_21_
  23.5 165.7 %shard_map.306 = (bf16[2048,6912]{1,0:T(8,128)(2,1)}, bf16[4,192,2048]{2,1,0:T(8,128)(2,1)}, s32[4,8,192]{2,1,0:T(8,128)}, bf16[2,4,4,64,1536]{4,3,2,1,0:T(8,128)(2,1)}, bf16[2,4,88,2048]{3,2,1,0:T(8,128)(2,1)}) custom-call(bf16[64,6912]{1,0:T(8,128)(2,1)} %bitcast_dynamic-update-slice_fusion.1.refs_0_, bf16[192,2048]{1,0:T(8,128)(2,1)} %bitcast.82, ...), custom_call_target="tpu_custom_call" | custom-call | flops 99999997952 | tf_op jit(solution)/shard_map/pallas_call | solution.py:488
  189.3 1.1 slice.59
  190.3 0.2 reshape.195
  190.7 0.7 reshape.208.refs_4_.refs_16_
  191.4 0.7 reshape.209.refs_5_.refs_18_
  192.1 0.7 reshape.207.refs_3_.refs_17_
  192.8 2.6 convert_reduce_fusion
  195.4 35.8 %shard_map.307 = (bf16[192,2048]{1,0:T(8,128)(2,1)}, f32[192,2048]{1,0:T(8,128)}, bf16[192,2048]{1,0:T(8,128)(2,1)}, bf16[192,3072]{1,0:T(8,128)(2,1)}, bf16[192...) custom-call(bf16[192,2048]{1,0:T(8,128)(2,1)} %bitcast.80, ...), custom_call_target="tpu_custom_call" | custom-call | flops 40000000000 | tf_op jit(solution)/shard_map/pallas_call | solution.py:1804
  231.2 82.7 %shard_map.308 = (bf16[4,4,72,2048]{3,2,1,0:T(8,128)(2,1)}, bf16[4,192,2048]{2,1,0:T(8,128)(2,1)}, bf16[4,192,2048]{2,1,0:T(8,128)(2,1)}, bf16[4,4,64,1536]{3,2,...) custom-call(bf16[192,2048]{1,0:T(8,128)(2,1)} %get-tuple-element.76., ...), custom_call_target="tpu_custom_call", output_to_operand_aliasing={{5}: (5, {})} | custom-call | flops 99999997952 | tf_op jit(solution)/shard_map/pallas_call | solution.py:822
  314.1 0.4 reshape.200
  314.5 0.9 pad.34.refs_5_.refs_15_
  315.4 0.4 reduce-scatter.8.cloned.1.call-start
  315.8 137.1 %shard_map.309 = (f32[192,2048]{1,0:T(8,128)}, f32[4,8,192]{2,1,0:T(8,128)}, bf16[1024,1408]{1,0:T(8,128)(2,1)}, bf16[1024,1408]{1,0:T(8,128)(2,1)}, bf16[1408,1...) custom-call(bf16[4,288,2048]{2,1,0:T(8,128)(2,1)} %bitcast.88, ...), custom_call_target="tpu_custom_call" | custom-call | flops 99999997952 | tf_op jit(solution)/shard_map/pallas_call | solution.py:2560
  452.9 1.5 fusion.14
  454.5 0.8 slice.65
  455.4 0.2 fusion.4
  455.6 0.2 fusion
  456.0 0.6 pad.35.refs_14_
  456.6 1.4 convolution_convert_fusion
  458.0 0.3 copy.80
  458.3 0.8 reshape.203
  459.0 4.8 bitcast_convert_fusion.2
  463.9 2.9 bitcast_convert_fusion.1
  466.9 3.2 bitcast_convert_fusion
  470.1 61.4 %shard_map.310 = (f32[192,2048]{1,0:T(8,128)}, bf16[32,4,16,1024]{3,2,1,0:T(8,128)(2,1)}, f32[8,512]{1,0:T(8,128)}, f32[8,2048]{1,0:T(8,128)}, f32[8,2048]{1,0:T...) custom-call(f32[192,2048]{1,0:T(8,128)} %get-tuple-element.86.refs_0, ...), custom_call_target="tpu_custom_call", output_to_operand_aliasing={{7}: (23, {})} | custom-call | flops 99999997952 | tf_op jit(solution)/shard_map/pallas_call | solution.py:2070
  531.6 6.8 add_convert_fusion
  538.4 0.7 fusion.10
  539.2 0.9 fusion.9
  540.1 0.9 fusion.8
  541.3 1.0 reshape.204.refs_3_
  542.4 140.6 %shard_map.311 = (f32[64,6912]{1,0:T(8,128)}, bf16[4,64,1536]{2,1,0:T(8,128)(2,1)}) custom-call(bf16[2048,3712]{1,0:T(8,128)(2,1)} %get-tuple-element.101.refs_0_, bf16[2048,1024]{1,0:T(8,128)(2,1)} %bitcast.90, bf16[2048,2048]{1,0:T(8,128)(2,1)} %get-tuple-element.103.refs_2_, bf16[2048,128]{1,0:T(8,128)(2,1)} %reshape.204.refs_3_, ...), custom_call_target="tpu_custom_call" | custom-call | flops 99999997952 | tf_op jit(solution)/shard_map/pallas_call | solution.py:1558
  682.9 0.8 fusion.12
  683.7 0.6 copy-done.14
  684.3 0.6 slice.85
  684.9 0.8 slice.73
  685.7 0.8 slice.87
  686.5 0.7 copy.82
  687.2 1.3 fusion.13
  688.5 1.1 copy-done.2
  689.7 1.1 copy-done.3
  690.8 4.4 shard_map.312
  (80 shorter events, 2.1 us)
Async XLA Ops:
  7.2 2.4 copy-start.8
  7.2 3.1 copy-start.17
  7.2 3.2 copy-start.15
  7.2 3.2 copy-start.16
  7.2 3.8 copy-start.18
  7.2 4.0 copy-start.12
  7.2 182.0 %all-gather.7.cloned.1.call-start = ((), (), s32[]{:S(2)}) async-start(), calls=%async_computation.4 | async-start | bytes 8650752 | tf_op jit(solution)/shard_map/all_gather | solution.py:2770
  8.0 4.5 copy-start.9
  8.0 5.4 copy-start.10
  8.0 181.2 %all-gather.9.cloned.1.call-start = ((), (), s32[]{:S(2)}) async-start(), calls=%async_computation.5 | async-start | bytes 8650752 | tf_op jit(solution)/shard_map/all_gather | solution.py:2771
  8.7 180.5 %all-gather.11.cloned.1.call-start = ((), (), s32[]{:S(2)}) async-start(), calls=%async_computation.6 | async-start | bytes 8650752 | tf_op jit(solution)/shard_map/all_gather | solution.py:2772
  9.5 460.6 %reduce-scatter.12.cloned.1.call-start = ((), (), s32[]{:S(2)}) async-start(), calls=%async_computation.8 | async-start | bytes 1802240
  11.7 8.1 %copy-start.13 = (bf16[64,576]{1,0:T(8,128)(2,1)S(1)}, bf16[64,576]{1,0:T(8,128)(2,1)}, u32[]{:S(2)}) copy-start(bf16[64,576]{1,0:T(8,128)(2,1)} %param.26) | copy-start | bytes 221188
  12.5 8.6 %copy-start.11 = (bf16[64,2048]{1,0:T(8,128)(2,1)S(1)}, bf16[64,2048]{1,0:T(8,128)(2,1)}, u32[]{:S(2)}) copy-start(bf16[64,2048]{1,0:T(8,128)(2,1)} %param.29) | copy-start | bytes 786436
  13.0 8.8 %copy-start.19 = (bf16[64]{0:T(256)(128)(2,1)S(1)}, bf16[64]{0:T(256)(128)(2,1)}, u32[]{:S(2)}) copy-start(bf16[64]{0:T(256)(128)(2,1)} %param.24) | copy-start | bytes 388
  13.0 8.8 %copy-start.20 = (bf16[16]{0:T(256)(128)(2,1)S(1)}, bf16[16]{0:T(256)(128)(2,1)}, u32[]{:S(2)}) copy-start(bf16[16]{0:T(256)(128)(2,1)} %param.27) | copy-start | bytes 100
  13.0 8.8 %copy-start.21 = (bf16[64]{0:T(256)(128)(2,1)S(1)}, bf16[64]{0:T(256)(128)(2,1)}, u32[]{:S(2)}) copy-start(bf16[64]{0:T(256)(128)(2,1)} %param.30) | copy-start | bytes 388
  313.9 156.2 %reduce-scatter.10.cloned.1.call-start = ((), (), s32[]{:S(2)}) async-start(), calls=%async_computation.7 | async-start | bytes 3932160
  315.4 373.1 %reduce-scatter.8.cloned.1.call-start = ((), (), s32[]{:S(2)}) async-start(), calls=%async_computation.3 | async-start | bytes 3932160 | tf_op jit(solution)/shard_map/reduce_scatter | solution.py:2950
  458.3 5.6 copy-start.7
  463.9 3.0 copy-start.6
  470.1 61.4 %copy-start.5 = (bf16[4,288,192]{2,1,0:T(8,128)(2,1)S(1)}, bf16[4,288,192]{2,1,0:T(8,128)(2,1)}, u32[]{:S(2)}) copy-start(bf16[4,288,192]{2,1,0:T(8,128)(2,1)} %convert_reduce_fusion) | copy-start | bytes 1327108
  542.3 146.2 %copy-start = (f32[192,2048]{1,0:T(8,128)S(1)}, f32[192,2048]{1,0:T(8,128)}, u32[]{:S(2)}) copy-start(f32[192,2048]{1,0:T(8,128)} %get-tuple-element.95.refs_12_.refs_2_) | copy-start | bytes 4718596
  542.4 146.2 %copy-start.1 = (f32[192,2048]{1,0:T(8,128)S(1)}, f32[192,2048]{1,0:T(8,128)}, u32[]{:S(2)}) copy-start(f32[192,2048]{1,0:T(8,128)} %get-tuple-element.111.refs_5_) | copy-start | bytes 4718596
  542.4 146.2 %copy-start.4 = (bf16[88,2048]{1,0:T(8,128)(2,1)S(1)}, bf16[88,2048]{1,0:T(8,128)(2,1)}, u32[]{:S(2)}) copy-start(bf16[88,2048]{1,0:T(8,128)(2,1)} %reduce-scatter.12.cloned.1.call-done.refs_25_.refs_4_) | copy-start | bytes 1081348
  683.7 0.6 copy-start.14
  688.5 1.1 copy-start.2
  689.7 1.1 copy-start.3
Sparse Core Ops, SparseCore 0:
  9.6 18.6 all-gather.6
  29.9 17.1 all-gather.8
  48.6 17.1 all-gather.10
  314.0 39.9 reduce-scatter.11
  357.1 72.6 reduce-scatter.9
  538.5 76.2 reduce-scatter.7

commit v7 on v6

--- a/solution.py
+++ b/solution.py
@@ -2801,7 +2801,7 @@
 
     slot_names = level * PLANE * capacity + jnp.arange(PLANE * capacity)
     hits = target_line[:, :TOPK, None, :] == slot_names[None, None, :, None]
-    choose_rows = jnp.sum(hits.astype(jnp.float32), axis=1).astype(jnp.bfloat16)
+    choose_rows = jnp.any(hits, axis=1).astype(jnp.bfloat16)
 
     choose_slots = choose_rows.reshape(depth, PLANE, capacity, row_count)
     grad_line = grad_line.reshape(depth, row_count, D)

time: 709 us -> 705 us (level)
  transfers between devices with their start and end apart: 6 -> 6, of which waited for: 0 -> 0; matrix products, arithmetic and copies ran while one was open for 6% -> 5% of each run, Pallas kernels for 63% -> 64%
where the time goes in v7:
time: 705 us; the launch traced here: 698 us
  Pallas kernels  628 us (89%)
  local copies, waits for them, and re-layouts  25.9 us (4%)
  other arithmetic  16.5 us (2%)
  between operations  14.9 us (2%)
  matrix products  9.7 us (1%)
    pallas_call x1, Pallas kernels, gather_rows(): pl.pallas_call(functools.partial(gather_kernel, depth, cuts), out_shape=[...  166 us
    pallas_call x1, Pallas kernels, reduce_rows(): pl.pallas_call(functools.partial(reduce_kernel, depth, n, cut), out_shape...  141 us
    pallas_call x1, Pallas kernels, run_and_return(): pl.pallas_call(functools.partial(run_and_return_kernel, depth, total), ou...  137 us
    pallas_call x1, Pallas kernels, dispatch(): pl.pallas_call(functools.partial(dispatch_kernel, depth), out_shape=[jax....  82.7 us
    pallas_call x1, Pallas kernels, attend_back(): pl.pallas_call(functools.partial(attend_back_kernel, layout, len(before))...  61.4 us
    pallas_call x1, Pallas kernels, attend(): pl.pallas_call(functools.partial(attend_kernel, layout), out_shape=[jax.S...  35.9 us
  transfers between devices with their start and end apart: 6, of which 0 were waited for; matrix products, arithmetic and copies ran while one was open for 5% of the time, Pallas kernels for 64%

profile of v7, /device:TPU:0, one launch (start us, length us, event | category | flops | bytes accessed | tf_op | source)
XLA Modules:
  0.0 698.0 jit_solution(12294003159449670573)
XLA Ops:
  7.2 0.7 all-gather.7.cloned.1.call-update
  8.0 0.7 all-gather.9.cloned.1.call-update
  8.8 0.7 all-gather.11.cloned.1.call-update
  9.6 0.6 reshape.187
  10.4 0.6 pad_bitcast_fusion.refs_2_
  11.3 0.4 fusion.5
  11.7 0.8 pad_maximum_fusion.refs_6_.refs_19_
  12.5 0.5 stack.9
  13.0 0.3 copy.76
  13.4 0.5 stack.10
  13.9 0.3 copy.77
  14.2 1.1 maximum_bitcast_fusion
  15.3 0.7 pad.33
  16.0 1.4 reshape.194.refs_3_
  17.4 0.2 reshape.189
  17.7 0.8 pad_maximum_fusion.1.refs_7_.refs_20_
  18.8 0.9 and_convert_fusion.refs_8_.refs_21_
  19.7 166.1 %shard_map.306 = (bf16[2048,6912]{1,0:T(8,128)(2,1)}, bf16[4,192,2048]{2,1,0:T(8,128)(2,1)}, s32[4,8,192]{2,1,0:T(8,128)}, bf16[2,4,4,64,1536]{4,3,2,1,0:T(8,128)(2,1)}, bf16[2,4,88,2048]{3,2,1,0:T(8,128)(2,1)}) custom-call(bf16[64,6912]{1,0:T(8,128)(2,1)} %copy-done.16, bf16[192,2048]{1,0:T(8,128)(2,1)} %bitcast.82, s32[8,192]{1,0:T(8,128)} %pad_bitcast_fusion.refs_2_, ...), custom_call_target="tpu_custom_call" | custom-call | flops 99999997952 | tf_op jit(solution)/shard_map/pallas_call | solution.py:488
  185.9 1.1 slice.59
  187.0 0.2 reshape.196
  187.3 0.7 reshape.209.refs_4_.refs_16_
  188.0 0.7 reshape.210.refs_5_.refs_18_
  188.7 0.7 reshape.208.refs_3_.refs_17_
  189.4 1.7 compare_reduce_fusion
  191.0 0.7 copy-done.8
  191.8 0.9 convert_element_type.102
  192.7 35.9 %shard_map.307 = (bf16[192,2048]{1,0:T(8,128)(2,1)}, f32[192,2048]{1,0:T(8,128)}, bf16[192,2048]{1,0:T(8,128)(2,1)}, bf16[192,3072]{1,0:T(8,128)(2,1)}, bf16[192...) custom-call(bf16[192,2048]{1,0:T(8,128)(2,1)} %bitcast.80, ...), custom_call_target="tpu_custom_call" | custom-call | flops 40000000000 | tf_op jit(solution)/shard_map/pallas_call | solution.py:1804
  228.5 82.7 %shard_map.308 = (bf16[4,4,72,2048]{3,2,1,0:T(8,128)(2,1)}, bf16[4,192,2048]{2,1,0:T(8,128)(2,1)}, bf16[4,192,2048]{2,1,0:T(8,128)(2,1)}, bf16[4,4,64,1536]{3,2,...) custom-call(bf16[192,2048]{1,0:T(8,128)(2,1)} %get-tuple-element.76., ...), custom_call_target="tpu_custom_call", output_to_operand_aliasing={{5}: (5, {})} | custom-call | flops 99999997952 | tf_op jit(solution)/shard_map/pallas_call | solution.py:822
  311.4 0.4 reshape.201
  311.8 0.9 pad.34.refs_5_.refs_15_
  312.7 0.4 reduce-scatter.8.cloned.1.call-start
  313.2 137.1 %shard_map.309 = (f32[192,2048]{1,0:T(8,128)}, f32[4,8,192]{2,1,0:T(8,128)}, bf16[1024,1408]{1,0:T(8,128)(2,1)}, bf16[1024,1408]{1,0:T(8,128)(2,1)}, bf16[1408,1...) custom-call(bf16[4,288,2048]{2,1,0:T(8,128)(2,1)} %bitcast.88, ...), custom_call_target="tpu_custom_call" | custom-call | flops 99999997952 | tf_op jit(solution)/shard_map/pallas_call | solution.py:2560
  450.3 1.5 fusion.14
  451.8 0.1 copy.78
  451.9 0.9 slice.65
  452.8 0.1 copy.79
  452.9 0.2 fusion.4
  453.1 0.2 fusion
  453.4 0.2 fusion.2
  453.5 0.6 pad.35.refs_14_
  454.2 1.4 convolution_convert_fusion
  455.5 0.3 copy.80
  455.8 0.8 reshape.204
  456.6 2.9 bitcast_convert_fusion.2
  459.6 2.9 bitcast_convert_fusion.1
  462.6 3.2 bitcast_convert_fusion
  465.8 61.4 %shard_map.310 = (f32[192,2048]{1,0:T(8,128)}, bf16[32,4,16,1024]{3,2,1,0:T(8,128)(2,1)}, f32[8,512]{1,0:T(8,128)}, f32[8,2048]{1,0:T(8,128)}, f32[8,2048]{1,0:T...) custom-call(f32[192,2048]{1,0:T(8,128)} %get-tuple-element.86.refs_0, ...), custom_call_target="tpu_custom_call", output_to_operand_aliasing={{7}: (23, {})} | custom-call | flops 99999997952 | tf_op jit(solution)/shard_map/pallas_call | solution.py:2070
  527.3 6.8 add_convert_fusion
  534.1 0.7 fusion.10
  534.9 0.9 fusion.9
  535.8 0.9 fusion.8
  536.9 0.1 concatenate.25
  537.0 1.0 reshape.205.refs_3_
  538.1 140.5 %shard_map.311 = (f32[64,6912]{1,0:T(8,128)}, bf16[4,64,1536]{2,1,0:T(8,128)(2,1)}) custom-call(bf16[2048,3712]{1,0:T(8,128)(2,1)} %get-tuple-element.101.refs_0_, bf16[2048,1024]{1,0:T(8,128)(2,1)} %bitcast.90, bf16[2048,2048]{1,0:T(8,128)(2,1)} %get-tuple-element.103.refs_2_, bf16[2048,128]{1,0:T(8,128)(2,1)} %reshape.205.refs_3_, ...), custom_call_target="tpu_custom_call" | custom-call | flops 99999997952 | tf_op jit(solution)/shard_map/pallas_call | solution.py:1558
  678.6 0.8 fusion.12
  679.4 0.6 copy-done.17
  680.0 0.6 slice.85
  680.6 0.8 slice.73
  681.4 0.8 slice.87
  682.2 0.7 copy.82
  682.9 1.3 fusion.13
  684.2 1.1 copy-done.2
  685.4 1.1 copy-done.3
  686.5 4.4 shard_map.312
  (87 shorter events, 1.8 us)
Async XLA Ops:
  7.2 2.4 copy-start.10
  7.2 178.6 %all-gather.7.cloned.1.call-start = ((), (), s32[]{:S(2)}) async-start(), calls=%async_computation.4 | async-start | bytes 8650752 | tf_op jit(solution)/shard_map/all_gather | solution.py:2770
  7.9 2.4 copy-start.20
  7.9 2.5 copy-start.18
  7.9 2.5 copy-start.19
  8.0 3.1 copy-start.21
  8.0 3.3 copy-start.14
  8.0 4.5 copy-start.11
  8.0 177.9 %all-gather.9.cloned.1.call-start = ((), (), s32[]{:S(2)}) async-start(), calls=%async_computation.5 | async-start | bytes 8650752 | tf_op jit(solution)/shard_map/all_gather | solution.py:2771
  8.7 4.6 copy-start.12
  8.7 177.1 %all-gather.11.cloned.1.call-start = ((), (), s32[]{:S(2)}) async-start(), calls=%async_computation.6 | async-start | bytes 8650752 | tf_op jit(solution)/shard_map/all_gather | solution.py:2772
  9.5 456.3 %reduce-scatter.12.cloned.1.call-start = ((), (), s32[]{:S(2)}) async-start(), calls=%async_computation.8 | async-start | bytes 1802240
  13.0 5.5 copy-start.15
  13.3 5.2 copy-start.13
  13.4 5.2 copy-start.22
  13.4 5.2 copy-start.23
  13.4 5.2 copy-start.24
  18.7 1.0 copy-start.16
  191.0 0.7 copy-start.8
  311.2 154.6 %reduce-scatter.10.cloned.1.call-start = ((), (), s32[]{:S(2)}) async-start(), calls=%async_computation.7 | async-start | bytes 3932160
  312.7 371.5 %reduce-scatter.8.cloned.1.call-start = ((), (), s32[]{:S(2)}) async-start(), calls=%async_computation.3 | async-start | bytes 3932160 | tf_op jit(solution)/shard_map/reduce_scatter | solution.py:2950
  451.8 4.8 copy-start.7
  456.6 3.0 copy-start.6
  459.6 3.0 copy-start.5
  465.8 61.4 %copy-start.9 = (pred[4,288,192]{2,1,0:T(8,128)(4,1)S(1)}, pred[4,288,192]{2,1,0:T(8,128)(4,1)}, u32[]{:S(2)}) copy-start(pred[4,288,192]{2,1,0:T(8,128)(4,1)} %copy-done.8) | copy-start | bytes 663556
  538.1 146.1 %copy-start = (f32[192,2048]{1,0:T(8,128)S(1)}, f32[192,2048]{1,0:T(8,128)}, u32[]{:S(2)}) copy-start(f32[192,2048]{1,0:T(8,128)} %get-tuple-element.95.refs_12_.refs_2_) | copy-start | bytes 4718596
  538.1 146.1 %copy-start.1 = (f32[192,2048]{1,0:T(8,128)S(1)}, f32[192,2048]{1,0:T(8,128)}, u32[]{:S(2)}) copy-start(f32[192,2048]{1,0:T(8,128)} %get-tuple-element.111.refs_5_) | copy-start | bytes 4718596
  538.1 146.2 %copy-start.4 = (bf16[88,2048]{1,0:T(8,128)(2,1)S(1)}, bf16[88,2048]{1,0:T(8,128)(2,1)}, u32[]{:S(2)}) copy-start(bf16[88,2048]{1,0:T(8,128)(2,1)} %reduce-scatter.12.cloned.1.call-done.refs_25_.refs_4_) | copy-start | bytes 1081348
  679.4 0.6 copy-start.17
  684.2 1.1 copy-start.2
  685.4 1.1 copy-start.3
Sparse Core Ops, SparseCore 0:
  9.6 18.6 all-gather.6
  29.8 17.1 all-gather.8
  48.6 17.1 all-gather.10
  311.4 39.9 reduce-scatter.11
  354.5 72.5 reduce-scatter.9
  534.3 76.3 reduce-scatter.7
